TPU v7x, 128 devices: a whole 4x4x4 slice. The times are simulated.
128 devices in a mesh: group: 16 (over y, z), local: 8 (over x, core).
Axes of the slice: x: 4, y: 4, z: 4, core: 2. Of those that a mesh axis runs over, the one named last changes fastest.
Arguments:
- features: float32 [131072, 512], P(('group', 'local'))
- aggregated: float32 [131072, 512], P(('group', 'local')), may hold values from -6 to 6
- preact: float32 [131072, 512], P(('group', 'local')), may hold values from -6 to 6
- grad_out: float32 [131072, 512], P(('group', 'local')), may hold values from -6 to 6
- w_self: float32 [512, 512], replicated, may hold values from -0.25 to 0.25
- w_neigh: float32 [512, 512], replicated, may hold values from -0.25 to 0.25
- tile_vals: float32 [8192, 128, 128], P(('group', 'local')), as said below
- tile_col: int32 [8192], P(('group', 'local')), may hold values from 0 to 39, as said below
- halo_count: int32 [16, 16], replicated, may hold values from 0 to 2, as said below
- halo_target: int32 [16, 32], replicated, may hold values from 0 to 63, as said below
Outputs:
- node_grad: float32 [131072, 512], P(('group', 'local'))
- self_grad: float32 [512, 512], replicated
- neigh_grad: float32 [512, 512], replicated
Inputs may be any that keep to these rules, and one draw needn't show every extreme that they name: `halo_count`: no partition sends to itself; for every partition some owner receives 2 slots from it, and one owner partition receives 2 slots from every other partition. `halo_target`: entries of slots that are not live are in range but unused. `tile_col`: A tile's column names a row block of its own device (0 to 7) or 8 plus a live halo slot of its own partition. `tile_vals`: each tile is sparse with nonnegative weights; a row's weights over its 8 tiles sum to about one.
All inputs are finite; a program needn't handle non-finite values.
Results may differ from a plain program's by a relative error of at most 0.0003.
Values sent between devices are 32-bit elements; how exact they have to be, the bound alone decides.
No kernel may reach another device: no remote copies, remote signals or barrier semaphores. Data moves between devices by JAX's collectives and lax.ppermute only.
A program may use at most 192 MiB of HBM per device.

v0:
```python
import jax
import jax.numpy as jnp
from jax import lax
from jax.sharding import PartitionSpec as P


def on_device(
    features,
    aggregated,
    preact,
    grad_out,
    w_self,
    w_neigh,
    tile_vals,
    tile_col,
    halo_count,
    halo_target,
):
    precise = lax.Precision.HIGHEST
    node_rows, feat_width = features.shape
    blocks = node_rows // 128
    groups = lax.axis_size("group")
    members = lax.axis_size("local")
    slot_count = halo_target.shape[1]
    capacity = slot_count // groups
    group_id = lax.axis_index("group")
    pre_grad = jnp.where(preact > 0, grad_out, jnp.zeros_like(grad_out))
    neigh_rows = jnp.dot(pre_grad, w_neigh.T, precision=precise, preferred_element_type=jnp.float32)
    tile_blocks = tile_vals.reshape(blocks, -1, 128, 128)
    contrib = jnp.einsum(
        "rkab,raf->rkbf",
        tile_blocks,
        neigh_rows.reshape(blocks, 128, feat_width),
        precision=precise,
    ).reshape(-1, 128, feat_width)
    own_pick = (tile_col[:, None] == jnp.arange(blocks, dtype=jnp.int32)[None, :]).astype(
        jnp.float32
    )
    local_sum = jnp.einsum("tr,tbf->rbf", own_pick, contrib, precision=precise)
    slot_ids = jnp.arange(slot_count, dtype=jnp.int32)
    my_counts = lax.dynamic_index_in_dim(halo_count, group_id, 0, keepdims=False)
    live_mask = (slot_ids % capacity < my_counts[slot_ids // capacity]).astype(jnp.float32)
    halo_pick = (tile_col[:, None] - blocks == slot_ids[None, :]).astype(jnp.float32) * live_mask[
        None, :
    ]
    halo_terms = jnp.einsum("ts,tbf->sbf", halo_pick, contrib, precision=precise)
    source = slot_ids // capacity
    offset = slot_ids % capacity
    recv_target = halo_target[source, group_id * capacity + offset]
    recv_live = offset < halo_count[source, group_id]
    group_blocks = blocks * members
    place_table = (
        (recv_target[:, None] == jnp.arange(group_blocks, dtype=jnp.int32)[None, :])
        & recv_live[:, None]
    ).astype(jnp.float32)
    row_parts = lax.psum_scatter(halo_terms, "local", scatter_dimension=1, tiled=True)
    arrived = lax.all_to_all(row_parts, "group", split_axis=0, concat_axis=0, tiled=True)
    gathered_rows = jnp.einsum("sb,srf->brf", place_table, arrived, precision=precise)
    incoming = lax.all_to_all(gathered_rows, "local", split_axis=0, concat_axis=1, tiled=True)
    node_grad = jnp.dot(pre_grad, w_self.T, precision=precise, preferred_element_type=jnp.float32)
    node_grad = (
        node_grad
        + local_sum.reshape(node_rows, feat_width)
        + incoming.reshape(node_rows, feat_width)
    )
    contract = (((0,), (0,)), ((), ()))
    self_term = lax.dot_general(
        features, pre_grad, contract, precision=precise, preferred_element_type=jnp.float32
    )
    neigh_term = lax.dot_general(
        aggregated, pre_grad, contract, precision=precise, preferred_element_type=jnp.float32
    )
    self_total, neigh_total = lax.psum((self_term, neigh_term), ("group", "local"))
    scale = float(node_rows * groups * members) ** (-0.5)
    return (node_grad, self_total * scale, neigh_total * scale)


def solution(mesh):
    in_specs = (
        P(("group", "local"), None),
        P(("group", "local"), None),
        P(("group", "local"), None),
        P(("group", "local"), None),
        P(),
        P(),
        P(("group", "local"), None, None),
        P(("group", "local")),
        P(),
        P(),
    )
    out_specs = (P(("group", "local"), None), P(), P())
    return jax.shard_map(
        on_device, mesh=mesh, in_specs=in_specs, out_specs=out_specs, check_vma=False
    )
```

profile of v0, /device:TPU:1, one launch (start us, length us, event | category | flops | bytes accessed | tf_op | source)
XLA Modules:
  0.0 337.5 jit_solution(6790897963332100551)
XLA Ops:
  8.0 0.0 copy-start
  8.0 0.0 reduce-scatter.2.cloned.1.call-start
  8.1 0.0 copy-start.9
  8.1 2.9 compare_select_fusion
  11.0 3.5 %fusion.25 = f32[1024,512]{1,0:T(8,128)S(1)} fusion(f32[1024,512]{1,0:T(8,128)S(1)} %compare_select_fusion, f32[512,512]{1,0:T(8,128)S(1)} %copy-done.9), kind=kOutput, calls=%fused_computation.50 | convolution fusion | flops 3221225472 | bytes 5242880 | tf_op jit(solution)/shard_map/dot_general | solution.py:28
  14.5 16.2 %fusion.26 = f32[8,512,8,128]{3,1,2,0:T(8,128)} fusion(f32[8,128,512,1]{2,1,3,0:T(8,128)S(1)} %bitcast.52, f32[8,8,128,128]{3,2,1,0:T(8,128)S(1)} %bitcast.53), kind=kOutput, calls=%fused_computation.51 | convolution fusion | flops 6442450944 | bytes 23068672 | tf_op jit(solution)/shard_map/rkab,raf->rkbf/dot_general | solution.py:30
  30.7 17.5 %copy.26 = f32[64,128,512]{2,0,1:T(8,128)} copy(f32[64,128,512]{1,2,0:T(8,128)} %bitcast.51) | data formatting | bytes 33554432 | tf_op jit(solution)/shard_map/reshape | solution.py:35
  48.2 0.7 gather_fusion.2
  48.9 13.5 %fusion.2 = f32[32,128,512]{2,0,1:T(8,128)} fusion(f32[64,128,512]{2,0,1:T(8,128)} %copy.26, f32[32]{0:T(128)S(1)} %compare_convert_fusion, s32[64]{0:T(128)S(1)} %broadcast_add_fusion), kind=kOutput, calls=%fused_computation.12 | convolution fusion | flops 1610616832 | bytes 25166208 | tf_op jit(solution)/shard_map/ts,tbf->sbf/dot_general | solution.py:46
  62.4 0.0 reduce-scatter.2.cloned.1.call-update
  62.5 55.2 %reduce-scatter.2.cloned.1.call-done = f32[32,16,512]{2,0,1:T(8,128)} async-done(((f32[32,128,512]{2,0,1:T(8,128)}), f32[32,16,512]{2,0,1:T(8,128)}) %reduce-scatter.2.cloned.1.call-update) | async-done | bytes 1048592 | tf_op jit(solution)/shard_map/reduce_scatter | solution.py:56
  117.7 2.8 copy.29
  120.5 6.7 %all-to-all-start = ((f32[32,16,512]{2,1,0:T(8,128)}), f32[32,16,512]{2,1,0:T(8,128)S(1)}, u32[]{:S(2)}, u32[]{:S(2)}) async-start(f32[32,16,512]{2,1,0:T(8,128)} %copy.29), calls=%async_computation.1 | async-start | bytes 2097152 | tf_op jit(solution)/shard_map/all_to_all | solution.py:57
  127.2 0.7 gather_fusion.1
  127.9 0.7 gather_fusion
  128.7 13.7 %all-to-all-done = f32[32,16,512]{2,1,0:T(8,128)S(1)} async-done(((f32[32,16,512]{2,1,0:T(8,128)}), f32[32,16,512]{2,1,0:T(8,128)S(1)}, u32[]{:S(2)}, u32[]{:S(2)}) %all-to-all-start) | async-done | bytes 1048608 | tf_op jit(solution)/shard_map/all_to_all | solution.py:57
  142.4 1.7 fusion
  144.1 2.5 copy.31
  146.6 7.5 %all-to-all-start.1 = ((f32[64,16,512]{2,1,0:T(8,128)}), f32[64,16,512]{2,1,0:T(8,128)}, u32[]{:S(2)}, u32[]{:S(2)}) async-start(f32[64,16,512]{2,1,0:T(8,128)} %copy.31), calls=%async_computation.2 | async-start | bytes 4194304 | tf_op jit(solution)/shard_map/all_to_all | solution.py:59
  154.2 6.2 %convolution_bitcast_fusion.1 = f32[512,512]{0,1:T(8,128)} fusion(f32[1024,512]{1,0:T(8,128)} %copy-done.1, f32[1024,512]{1,0:T(8,128)S(1)} %copy-done), kind=kOutput, calls=%fused_computation.7 | convolution fusion | flops 3221225472 | bytes 5242880 | tf_op jit(solution)/shard_map/dot_general | solution.py:67
  160.4 4.6 %convolution_bitcast_fusion = f32[512,512]{0,1:T(8,128)} fusion(f32[1024,512]{1,0:T(8,128)S(1)} %copy-done.2, f32[1024,512]{1,0:T(8,128)S(1)} %copy-done.8), kind=kOutput, calls=%fused_computation.6 | convolution fusion | flops 3221225472 | bytes 5242880 | tf_op jit(solution)/shard_map/dot_general | solution.py:70
  165.0 0.0 all-reduce.4.cloned.1.call-update
  165.0 9.6 %fusion.14 = f32[8,128,512]{2,0,1:T(8,128)S(1)} fusion(f32[64,128,512]{2,0,1:T(8,128)} %copy.26, s32[64]{0:T(128)S(1)} %copy-done.10), kind=kOutput, calls=%fused_computation.27 | convolution fusion | flops 402653696 | bytes 18874624 | tf_op jit(solution)/shard_map/tr,tbf->rbf/dot_general | solution.py:39
  174.6 2.5 copy.27
  177.1 137.4 %all-reduce.4.cloned.1.call-done = (f32[512,512]{0,1:T(8,128)}, f32[512,512]{0,1:T(8,128)}) async-done(((f32[512,512]{0,1:T(8,128)}, f32[512,512]{0,1:T(8,128)}), (f32[512,512]{0,1:T(8,128)}, f32[512,512]{0,1:T(8,128)})) %all-reduce.4.cloned.1.call-update) | async-done | bytes 2097168 | tf_op jit(solution)/shard_map/psum | solution.py:73
  314.5 2.8 broadcast_multiply_fusion
  317.3 2.5 copy.33
  319.8 1.3 copy.34
  321.1 1.9 copy.32
  323.0 0.3 copy-done.3
  323.3 0.6 copy-done.7
  324.0 6.1 %bitcast_add_fusion = f32[1024,512]{1,0:T(8,128)} fusion(f32[8,8,16,512]{3,2,0,1:T(8,128)S(1)} %copy.32, f32[8,128,512]{2,1,0:T(8,128)S(1)} %copy-done.7, f32[1024,512]{1,0:T(8,128)S(1)} %copy-done.3, f32[512,512]{1,0:T(8,128)} %param.14), kind=kOutput, calls=%fused_computation.3 | convolution fusion | flops 3222274048 | bytes 9437184 | tf_op jit(solution)/shard_map/dot_general | solution.py:60
  (28 shorter events, 0.1 us)
Async XLA Ops:
  8.0 146.2 %copy-start = (f32[1024,512]{1,0:T(8,128)S(1)}, f32[1024,512]{1,0:T(8,128)}, u32[]{:S(2)}) copy-start(f32[1024,512]{1,0:T(8,128)} %param.10) | copy-start | bytes 6291460
  8.0 109.7 %reduce-scatter.2.cloned.1.call-start = ((), (), s32[]{:S(2)}) async-start(), calls=%async_computation.3 | async-start | bytes 9437184 | tf_op jit(solution)/shard_map/reduce_scatter | solution.py:56
  8.1 2.9 copy-start.9
  11.0 3.5 %copy-start.1 = (f32[1024,512]{1,0:T(8,128)}, f32[1024,512]{1,0:T(8,128)S(1)}, u32[]{:S(2)}) copy-start(f32[1024,512]{1,0:T(8,128)S(1)} %compare_select_fusion) | copy-start | bytes 6291460
  11.0 3.5 %copy-start.6 = (f32[64,128,128]{2,1,0:T(8,128)S(1)}, f32[64,128,128]{2,1,0:T(8,128)}, u32[]{:S(2)}) copy-start(f32[64,128,128]{2,1,0:T(8,128)} %param.16) | copy-start | bytes 12582916
  30.7 17.5 %copy-start.4 = (s32[16,16]{1,0:T(8,128)S(1)}, s32[16,16]{1,0:T(8,128)}, u32[]{:S(2)}) copy-start(s32[16,16]{1,0:T(8,128)} %param.18) | copy-start | bytes 3076
  30.7 18.2 %copy-start.10 = (s32[64]{0:T(128)S(1)}, s32[64]{0:T(128)}, u32[]{:S(2)}) copy-start(s32[64]{0:T(128)} %param.17) | copy-start | bytes 772
  62.5 65.5 %copy-start.5 = (s32[16,32]{1,0:T(8,128)S(1)}, s32[16,32]{1,0:T(8,128)}, u32[]{:S(2)}) copy-start(s32[16,32]{1,0:T(8,128)} %param.19) | copy-start | bytes 6148
  120.5 21.9 %all-to-all-start = ((f32[32,16,512]{2,1,0:T(8,128)}), f32[32,16,512]{2,1,0:T(8,128)S(1)}, u32[]{:S(2)}, u32[]{:S(2)}) async-start(f32[32,16,512]{2,1,0:T(8,128)} %copy.29), calls=%async_computation.1 | async-start | bytes 2097152 | tf_op jit(solution)/shard_map/all_to_all | solution.py:57
  146.6 174.5 %all-to-all-start.1 = ((f32[64,16,512]{2,1,0:T(8,128)}), f32[64,16,512]{2,1,0:T(8,128)}, u32[]{:S(2)}, u32[]{:S(2)}) async-start(f32[64,16,512]{2,1,0:T(8,128)} %copy.31), calls=%async_computation.2 | async-start | bytes 4194304 | tf_op jit(solution)/shard_map/all_to_all | solution.py:59
  154.2 160.4 %all-reduce.4.cloned.1.call-start = ((), (), s32[]{:S(2)}) async-start(), calls=%async_computation.4 | async-start | bytes 4194304 | tf_op jit(solution)/shard_map/psum | solution.py:73
  154.2 6.2 %copy-start.2 = (f32[1024,512]{1,0:T(8,128)S(1)}, f32[1024,512]{1,0:T(8,128)}, u32[]{:S(2)}) copy-start(f32[1024,512]{1,0:T(8,128)} %copy-done.1) | copy-start | bytes 6291460
  154.2 6.2 %copy-start.8 = (f32[1024,512]{1,0:T(8,128)S(1)}, f32[1024,512]{1,0:T(8,128)}, u32[]{:S(2)}) copy-start(f32[1024,512]{1,0:T(8,128)} %param.11) | copy-start | bytes 6291460
  321.1 2.2 copy-start.3
  321.1 2.9 copy-start.7
Sparse Core Ops, SparseCore 0:
  62.6 55.0 reduce-scatter.1
Sparse Core Ops, SparseCore 1:
  165.1 149.4 all-reduce.3
where the time goes:
time: 338 us; the launch traced here: 337 us
  waiting for transfers between devices  206 us (61%)
  matrix products  61.3 us (18%)
  local copies, waits for them, and re-layouts  34.2 us (10%)
  between operations  15.7 us (5%)
  starting transfers between devices  14.3 us (4%)
  other arithmetic  5.66 us (2%)
    psum x1, waiting for transfers between devices, on_device(): lax.psum((self_term, neigh_term), ('group', 'local'))  137 us
    reduce_scatter x1, waiting for transfers between devices, on_device(): lax.psum_scatter(halo_terms, 'local', scatter_dimension=1, tiled=True)  55.2 us
    reshape x1, local copies, waits for them, and re-layouts, on_device(): contrib = jnp.einsum('rkab,raf->rkbf', tile_blocks, neigh_rows.reshape(bl...  17.5 us
    dot_general x1, matrix products, on_device(): jnp.einsum('rkab,raf->rkbf', tile_blocks, neigh_rows.reshape(blocks, 128,...  16.2 us
    all_to_all x1, waiting for transfers between devices, on_device(): lax.all_to_all(row_parts, 'group', split_axis=0, concat_axis=0, tiled=True)  13.7 us
    dot_general x1, matrix products, on_device(): jnp.einsum('ts,tbf->sbf', halo_pick, contrib, precision=precise)  13.5 us
    dot_general x1, matrix products, on_device(): local_sum = jnp.einsum('tr,tbf->rbf', own_pick, contrib, precision=precise)  9.55 us
    all_to_all x1, starting transfers between devices, on_device(): lax.all_to_all(gathered_rows, 'local', split_axis=0, concat_axis=1, tiled...  7.52 us
  transfers between devices with their start and end apart: 4, of which 3 were waited for; matrix products, arithmetic and copies ran while one was open for 9% of the time, Pallas kernels for 0%

commit v1 on v0

v1 whole, which is shorter than its diff:
```python
import functools

import jax
import jax.numpy as jnp
from jax import lax
from jax.experimental import pallas as pl
from jax.experimental.pallas import tpu as pltpu
from jax.sharding import PartitionSpec as P

F32 = jnp.float32
BF16 = jnp.bfloat16
BLOCK = 128


def split(x):
    high = x.astype(BF16)
    low = (x - high.astype(F32)).astype(BF16)
    return high, low


def tile_kernel(blocks, col_ref, tiles_ref, rows_ref, local_ref, halo_ref, left, product):
    step = pl.program_id(0)
    tiles_row = tiles_ref.shape[0]

    @pl.when(step == 0)
    def _():
        local_ref[...] = jnp.zeros_like(local_ref)
        halo_ref[...] = jnp.zeros_like(halo_ref)

    for k in range(tiles_row):
        high, low = split(tiles_ref[k].T)
        rows = pl.ds(k * BLOCK, BLOCK)
        left[rows, 0:BLOCK] = high
        left[rows, BLOCK : 2 * BLOCK] = high
        left[rows, 2 * BLOCK : 3 * BLOCK] = low
    high, low = split(rows_ref[...])
    right = jnp.concatenate([high, low, high], axis=0)
    product[...] = jnp.dot(left[...], right, preferred_element_type=F32)
    for k in range(tiles_row):
        col = col_ref[step * tiles_row + k]
        rows = pl.ds(k * BLOCK, BLOCK)

        @pl.when(col < blocks)
        def _():
            local_ref[col] += product[rows, :]

        @pl.when(col >= blocks)
        def _():
            halo_ref[col - blocks] += product[rows, :]


def tile_sums(tile_col, tile_vals, neigh_rows, slot_count):
    node_rows, width = neigh_rows.shape
    blocks = node_rows // BLOCK
    tiles_row = tile_vals.shape[0] // blocks
    return pl.pallas_call(
        functools.partial(tile_kernel, blocks),
        out_shape=(
            jax.ShapeDtypeStruct((blocks, BLOCK, width), F32),
            jax.ShapeDtypeStruct((slot_count, BLOCK, width), F32),
        ),
        grid_spec=pltpu.PrefetchScalarGridSpec(
            num_scalar_prefetch=1,
            grid=(blocks,),
            in_specs=[
                pl.BlockSpec((tiles_row, BLOCK, BLOCK), lambda r, col: (r, 0, 0)),
                pl.BlockSpec((BLOCK, width), lambda r, col: (r, 0)),
            ],
            out_specs=[
                pl.BlockSpec((blocks, BLOCK, width), lambda r, col: (0, 0, 0)),
                pl.BlockSpec((slot_count, BLOCK, width), lambda r, col: (0, 0, 0)),
            ],
            scratch_shapes=[
                pltpu.VMEM((tiles_row * BLOCK, 3 * BLOCK), BF16),
                pltpu.VMEM((tiles_row * BLOCK, width), F32),
            ],
        ),
        compiler_params=pltpu.CompilerParams(
            dimension_semantics=("arbitrary",), vmem_limit_bytes=48 * 1024 * 1024
        ),
        cost_estimate=pl.CostEstimate(
            flops=6 * tile_vals.size * width, bytes_accessed=16 * 1024 * 1024, transcendentals=0
        ),
        name="tile_sums",
    )(tile_col, tile_vals, neigh_rows)


def on_device(
    features,
    aggregated,
    preact,
    grad_out,
    w_self,
    w_neigh,
    tile_vals,
    tile_col,
    halo_count,
    halo_target,
):
    high = lax.Precision.HIGH
    node_rows, width = features.shape
    blocks = node_rows // BLOCK
    groups = lax.axis_size("group")
    members = lax.axis_size("local")
    slot_count = halo_target.shape[1]
    capacity = slot_count // groups
    group_id = lax.axis_index("group")
    core = lax.axis_index("local") % 2

    pre_grad = jnp.where(preact > 0, grad_out, jnp.zeros_like(grad_out))
    neigh_rows = jnp.dot(pre_grad, w_neigh.T, precision=high, preferred_element_type=F32)
    local_sum, halo_terms = tile_sums(tile_col, tile_vals, neigh_rows, slot_count)

    slot_ids = jnp.arange(slot_count, dtype=jnp.int32)
    source = slot_ids // capacity
    offset = slot_ids % capacity
    recv_target = halo_target[source, group_id * capacity + offset]
    recv_live = offset < halo_count[source, group_id]
    group_blocks = blocks * members
    place_table = (
        (recv_target[:, None] == jnp.arange(group_blocks, dtype=jnp.int32)[None, :])
        & recv_live[:, None]
    ).astype(F32)
    row_parts = lax.psum_scatter(halo_terms, "local", scatter_dimension=1, tiled=True)
    arrived = lax.all_to_all(row_parts, "group", split_axis=0, concat_axis=0, tiled=True)
    gathered_rows = jnp.einsum("sb,srf->brf", place_table, arrived, precision=high)
    incoming = lax.all_to_all(gathered_rows, "local", split_axis=0, concat_axis=1, tiled=True)

    contract = (((0,), (0,)), ((), ()))
    self_term = lax.dot_general(
        features, pre_grad, contract, precision=high, preferred_element_type=F32
    )
    neigh_term = lax.dot_general(
        aggregated, pre_grad, contract, precision=high, preferred_element_type=F32
    )
    swap = [(i, i ^ 1) for i in range(members)]
    first = core == 0
    mine = jnp.where(first, self_term, neigh_term) + lax.ppermute(
        jnp.where(first, neigh_term, self_term), "local", swap
    )
    shares = lax.all_to_all(
        mine.reshape(groups, -1, width), "group", split_axis=0, concat_axis=0, tiled=True
    )
    total = jnp.sum(shares, axis=0)
    pairs = [(i, i ^ 2) for i in range(members)]
    total = total + lax.ppermute(total, "local", pairs)
    across = [(i, members - 2 - (i - i % 2) + i % 2) for i in range(members)]
    total = total + lax.ppermute(total, "local", across)
    scale = float(node_rows * groups * members) ** (-0.5)
    whole = lax.all_gather(total * scale, "group", tiled=True)
    other = lax.ppermute(whole, "local", swap)
    self_grad = jnp.where(first, whole, other)
    neigh_grad = jnp.where(first, other, whole)

    node_grad = jnp.dot(pre_grad, w_self.T, precision=high, preferred_element_type=F32)
    node_grad = (
        node_grad + local_sum.reshape(node_rows, width) + incoming.reshape(node_rows, width)
    )
    return (node_grad, self_grad, neigh_grad)


def solution(mesh):
    in_specs = (
        P(("group", "local"), None),
        P(("group", "local"), None),
        P(("group", "local"), None),
        P(("group", "local"), None),
        P(),
        P(),
        P(("group", "local"), None, None),
        P(("group", "local")),
        P(),
        P(),
    )
    out_specs = (P(("group", "local"), None), P(), P())
    return jax.shard_map(
        on_device, mesh=mesh, in_specs=in_specs, out_specs=out_specs, check_vma=False
    )
```

time: 338 us -> 161 us (0.48)
  waiting for transfers between devices: 206 us -> 51.5 us
  matrix products: 61.3 us -> 13 us
  blocking collectives: 0 us -> 23.6 us
  local copies, waits for them, and re-layouts: 34.2 us -> 15 us
  Pallas kernels: 0 us -> 14.1 us
  starting transfers between devices: 14.3 us -> 22 us
    psum x1 -> x0, waiting for transfers between devices: 137 us -> none  [on_device(): lax.psum((self_term, neigh_term), ('group', 'local'))]
    dot_general x8 -> x5, matrix products: 61.3 us -> 13 us  [the longest x1 4.46 us: on_device(): jnp.dot(pre_grad, w_self.T, precision=high, preferred_element_type=F32)]
    reduce_scatter x1, waiting for transfers between devices: 55.2 us -> 12.3 us  [on_device(): lax.psum_scatter(halo_terms, 'local', scatter_dimension=1, tiled=True)]
    all_to_all x0 -> x1, blocking collectives: none -> 23.6 us  [on_device(): lax.all_to_all(mine.reshape(groups, -1, width), 'group', split_axis=0, co...]
    reshape x1 -> x0, local copies, waits for them, and re-layouts: 17.5 us -> none  [on_device(): contrib = jnp.einsum('rkab,raf->rkbf', tile_blocks, neigh_rows.reshape(bl...]
    pallas_call x0 -> x1, Pallas kernels: none -> 14.1 us  [tile_sums(): pl.pallas_call(functools.partial(tile_kernel, blocks), out_shape=(jax.Sha...]
    all_to_all x1, waiting for transfers between devices: 0.01 us -> 12.8 us  [on_device(): lax.all_to_all(gathered_rows, 'local', split_axis=0, concat_axis=1, tiled...]
    ppermute x0 -> x4, waiting for transfers between devices: none -> 10.7 us  [the longest x1 3.09 us: on_device(): total = total + lax.ppermute(total, 'local', pairs)]
  transfers between devices with their start and end apart: 4 -> 8, of which waited for: 3 -> 8; matrix products, arithmetic and copies ran while one was open for 9% -> 12% of each run, Pallas kernels for 0% -> 0%
where the time goes in v1:
time: 161 us
  waiting for transfers between devices  51.5 us (32%)
  blocking collectives  23.6 us (15%)
  starting transfers between devices  22 us (14%)
  between operations  15.7 us (10%)
  local copies, waits for them, and re-layouts  15 us (9%)
  Pallas kernels  14.1 us (9%)
  matrix products  13 us (8%)
  other arithmetic  5.76 us (4%)
    all_to_all x1, blocking collectives, on_device(): lax.all_to_all(mine.reshape(groups, -1, width), 'group', split_axis=0, co...  23.6 us
    pallas_call x1, Pallas kernels, tile_sums(): pl.pallas_call(functools.partial(tile_kernel, blocks), out_shape=(jax.Sha...  14.1 us
    all_to_all x1, waiting for transfers between devices, on_device(): lax.all_to_all(row_parts, 'group', split_axis=0, concat_axis=0, tiled=True)  13.7 us
    all_to_all x1, waiting for transfers between devices, on_device(): lax.all_to_all(gathered_rows, 'local', split_axis=0, concat_axis=1, tiled...  12.8 us
    reduce_scatter x1, waiting for transfers between devices, on_device(): lax.psum_scatter(halo_terms, 'local', scatter_dimension=1, tiled=True)  12.3 us
    unnamed x26, local copies, waits for them, and re-layouts  7.61 us
    all_to_all x1, starting transfers between devices, on_device(): lax.all_to_all(gathered_rows, 'local', split_axis=0, concat_axis=1, tiled...  7.53 us
    all_to_all x1, starting transfers between devices, on_device(): lax.all_to_all(row_parts, 'group', split_axis=0, concat_axis=0, tiled=True)  6.71 us
  transfers between devices with their start and end apart: 8, of which 8 were waited for; matrix products, arithmetic and copies ran while one was open for 12% of the time, Pallas kernels for 0%

profile of v1, /device:TPU:1, one launch (start us, length us, event | category | flops | bytes accessed | tf_op | source)
XLA Modules:
  0.0 160.8 jit_solution(3350373254624406472)
XLA Ops:
  8.1 2.9 %compare_select_fusion = f32[1024,512]{1,0:T(8,128)S(1)} fusion(f32[1024,512]{1,0:T(8,128)} %param.13, f32[1024,512]{1,0:T(8,128)} %param.12), kind=kLoop, calls=%fused_computation.4 | loop fusion | flops 1048576 | bytes 6291456 | tf_op jit(solution)/shard_map/jit(_where)/select_n | solution.py:110
  11.0 1.4 copy-done.4
  12.4 1.8 %fusion.15.rows_ref = f32[1024,512]{1,0:T(8,128)S(1)} fusion(f32[1024,512]{1,0:T(8,128)S(1)} %compare_select_fusion, f32[512,512]{1,0:T(8,128)S(1)} %copy-done.11), kind=kOutput, calls=%fused_computation.34 | convolution fusion | flops 1610612736 | bytes 5242880 | tf_op jit(solution)/shard_map/dot_general | solution.py:111
  14.2 14.1 %tile_sums.1 = (f32[8,128,512]{2,1,0:T(8,128)S(1)}, f32[32,128,512]{2,1,0:T(8,128)}) custom-call(s32[64]{0:T(128)S(1)} %copy-done.3, f32[64,128,128]{2,1,0:T(8,128)} %tiles_ref.1, f32[1024,512]{1,0:T(8,128)S(1)} %fusion.15.rows_ref), custom_call_target="tpu_custom_call" | custom-call | flops 3221225472 | bytes 16777216 | tf_op jit(solution)/shard_map/tile_sums/pallas_call | solution.py:56
  28.4 1.3 copy-done.1
  29.8 3.6 %fusion.17 = f32[512,512]{0,1:T(8,128)S(1)} fusion(f32[1024,512]{1,0:T(8,128)} %copy-done.4, f32[1024,512]{1,0:T(8,128)S(1)} %copy-done), kind=kOutput, calls=%fused_computation.36 | convolution fusion | flops 1610612736 | bytes 5242880 | tf_op jit(solution)/shard_map/dot_general | solution.py:133
  33.4 1.9 %fusion.16 = f32[512,512]{0,1:T(8,128)S(1)} fusion(f32[1024,512]{1,0:T(8,128)S(1)} %copy-done.5, f32[1024,512]{1,0:T(8,128)S(1)} %copy-done.10), kind=kOutput, calls=%fused_computation.35 | convolution fusion | flops 1610612736 | bytes 5242880 | tf_op jit(solution)/shard_map/dot_general | solution.py:130
  35.5 1.5 collective-permute-start
  37.0 2.3 %collective-permute-done = f32[512,512]{1,0:T(8,128)S(1)} collective-permute-done((f32[512,512]{1,0:T(8,128)S(1)}, f32[512,512]{1,0:T(8,128)S(1)}, u32[]{:S(2)}, u32[]{:S(2)}) %collective-permute-start) | collective-permute-done | bytes 1048608 | tf_op jit(solution)/shard_map/ppermute | solution.py:138
  39.7 23.6 %all_to_all.25 = f32[16,32,512]{2,1,0:T(8,128)S(1)} all-to-all(f32[16,32,512]{2,1,0:T(8,128)S(1)} %bitcast.29), channel_id=1, replica_groups=mesh['group'=16,'local'=8] {'group'}, dimensions={0} | all-to-all | bytes 2097152 | tf_op jit(solution)/shard_map/all_to_all | solution.py:141
  63.4 1.3 collective-permute-start.1
  64.7 3.1 %collective-permute-done.1 = f32[32,512]{1,0:T(8,128)S(1)} collective-permute-done((f32[32,512]{1,0:T(8,128)S(1)}, f32[32,512]{1,0:T(8,128)S(1)}, u32[]{:S(2)}, u32[]{:S(2)}) %collective-permute-start.1) | collective-permute-done | bytes 65568 | tf_op jit(solution)/shard_map/ppermute | solution.py:146
  67.8 2.5 %collective-permute-start.2 = (f32[32,512]{1,0:T(8,128)S(1)}, f32[32,512]{1,0:T(8,128)S(1)}, u32[]{:S(2)}, u32[]{:S(2)}) collective-permute-start(f32[32,512]{1,0:T(8,128)S(1)} %add.103), channel_id=1, source_target_pairs={{0,6},{1,7},{2,4},{3,5},{4,2},{5,3},{6,0},{7,1},{8,14},{9,15},{10,... | collective-permute-start | bytes 196616 | tf_op jit(solution)/shard_map/ppermute | solution.py:148
  70.3 3.0 %collective-permute-done.2 = f32[32,512]{1,0:T(8,128)S(1)} collective-permute-done((f32[32,512]{1,0:T(8,128)S(1)}, f32[32,512]{1,0:T(8,128)S(1)}, u32[]{:S(2)}, u32[]{:S(2)}) %collective-permute-start.2) | collective-permute-done | bytes 65568 | tf_op jit(solution)/shard_map/ppermute | solution.py:148
  74.0 12.3 %reduce-scatter.2.cloned.1.call-done = f32[32,16,512]{2,1,0:T(8,128)} async-done(((f32[32,128,512]{2,1,0:T(8,128)}), f32[32,16,512]{2,1,0:T(8,128)}) %reduce-scatter.2.cloned.1.call-update) | async-done | bytes 1048592 | tf_op jit(solution)/shard_map/reduce_scatter | solution.py:124
  86.3 6.7 %all-to-all-start = ((f32[32,16,512]{2,1,0:T(8,128)}), f32[32,16,512]{2,1,0:T(8,128)S(1)}, u32[]{:S(2)}, u32[]{:S(2)}) async-start(f32[32,16,512]{2,1,0:T(8,128)} %reduce-scatter.2.cloned.1.call-done), calls=%async_computation.1 | async-start | bytes 2097152 | tf_op jit(solution)/shard_map/all_to_all | solution.py:125
  93.0 0.7 gather_fusion
  93.8 0.7 gather_fusion.1
  94.5 13.7 %all-to-all-done = f32[32,16,512]{2,1,0:T(8,128)S(1)} async-done(((f32[32,16,512]{2,1,0:T(8,128)}), f32[32,16,512]{2,1,0:T(8,128)S(1)}, u32[]{:S(2)}, u32[]{:S(2)}) %all-to-all-start) | async-done | bytes 1048608 | tf_op jit(solution)/shard_map/all_to_all | solution.py:125
  108.2 1.3 fusion
  109.5 2.5 %copy.22 = f32[64,16,512]{2,1,0:T(8,128)} copy(f32[64,16,512]{2,0,1:T(8,128)S(1)} %fusion) | data formatting | bytes 4194304 | tf_op jit(solution)/shard_map/sb,srf->brf/dot_general | solution.py:126
  112.0 7.5 %all-to-all-start.1 = ((f32[64,16,512]{2,1,0:T(8,128)}), f32[64,16,512]{2,1,0:T(8,128)}, u32[]{:S(2)}, u32[]{:S(2)}) async-start(f32[64,16,512]{2,1,0:T(8,128)} %copy.22), calls=%async_computation.2 | async-start | bytes 4194304 | tf_op jit(solution)/shard_map/all_to_all | solution.py:127
  119.6 1.9 %all-gather.2.cloned.1.call-done = f32[512,512]{1,0:T(8,128)} async-done(((f32[32,512]{1,0:T(8,128)}), f32[512,512]{1,0:T(8,128)}) %all-gather.2.cloned.1.call-update) | async-done | bytes 1048592 | tf_op jit(solution)/shard_map/all_gather | solution.py:150
  121.5 1.6 copy.25
  123.1 2.3 %collective-permute-start.3 = (f32[512,512]{0,1:T(8,128)S(1)}, f32[512,512]{0,1:T(8,128)S(1)}, u32[]{:S(2)}, u32[]{:S(2)}) collective-permute-start(f32[512,512]{0,1:T(8,128)S(1)} %copy.25), channel_id=1, source_target_pairs={{0,1},{1,0},{2,3},{3,2},{4,5},{5,4},{6,7},{7,6},{8,9},{9,8},{10,11... | collective-permute-start | bytes 3145736 | tf_op jit(solution)/shard_map/ppermute | solution.py:151
  125.4 2.3 %collective-permute-done.3 = f32[512,512]{0,1:T(8,128)S(1)} collective-permute-done((f32[512,512]{0,1:T(8,128)S(1)}, f32[512,512]{0,1:T(8,128)S(1)}, u32[]{:S(2)}, u32[]{:S(2)}) %collective-permute-start.3) | collective-permute-done | bytes 1048608 | tf_op jit(solution)/shard_map/ppermute | solution.py:151
  127.7 1.6 broadcast_select_fusion
  129.2 2.6 %copy.27 = f32[512,512]{1,0:T(8,128)} copy(f32[512,512]{0,1:T(8,128)} %get-tuple-element.17) | data formatting | bytes 2097152
  131.9 1.3 copy.28
  133.2 12.8 %all-to-all-done.1 = f32[64,16,512]{2,1,0:T(8,128)} async-done(((f32[64,16,512]{2,1,0:T(8,128)}), f32[64,16,512]{2,1,0:T(8,128)}, u32[]{:S(2)}, u32[]{:S(2)}) %all-to-all-start.1) | async-done | bytes 2097184 | tf_op jit(solution)/shard_map/all_to_all | solution.py:127
  146.0 1.9 %copy.23 = f32[8,8,16,512]{3,2,0,1:T(8,128)S(1)} copy(f32[8,8,16,512]{3,2,1,0:T(8,128)} %bitcast.4) | data formatting | bytes 4194304 | tf_op jit(solution)/shard_map/all_to_all | solution.py:127
  148.9 4.5 %bitcast_add_fusion = f32[1024,512]{1,0:T(8,128)} fusion(f32[8,8,16,512]{3,2,0,1:T(8,128)S(1)} %copy.23, f32[8,128,512]{2,1,0:T(8,128)S(1)} %copy-done.2, f32[1024,512]{1,0:T(8,128)S(1)} %copy-done.6, f32[512,512]{1,0:T(8,128)} %param.14), kind=kOutput, calls=%fused_computation.2 | convolution fusion | flops 1611661312 | bytes 9437184 | tf_op jit(solution)/shard_map/dot_general | solution.py:155
  (34 shorter events, 2.4 us)
Async XLA Ops:
  8.0 21.8 %copy-start = (f32[1024,512]{1,0:T(8,128)S(1)}, f32[1024,512]{1,0:T(8,128)}, u32[]{:S(2)}) copy-start(f32[1024,512]{1,0:T(8,128)} %param.11) | copy-start | bytes 6291460
  8.0 4.3 %copy-start.11 = (f32[512,512]{1,0:T(8,128)S(1)}, f32[512,512]{1,0:T(8,128)}, u32[]{:S(2)}) copy-start(f32[512,512]{1,0:T(8,128)} %param.15) | copy-start | bytes 3145732
  8.0 78.3 %reduce-scatter.2.cloned.1.call-start = ((), (), s32[]{:S(2)}) async-start(), calls=%async_computation.4 | async-start | bytes 9437184 | tf_op jit(solution)/shard_map/reduce_scatter | solution.py:124
  11.0 1.4 copy-start.4
  12.3 1.9 %copy-start.3 = (s32[64]{0:T(128)S(1)}, s32[64]{0:T(128)}, u32[]{:S(2)}) copy-start(s32[64]{0:T(128)} %col_ref.1) | copy-start | bytes 772
  28.4 1.3 copy-start.1
  29.7 91.8 %all-gather.2.cloned.1.call-start = ((), (), s32[]{:S(2)}) async-start(), calls=%async_computation.5 | async-start | bytes 1114112 | tf_op jit(solution)/shard_map/all_gather | solution.py:150
  29.8 3.6 %copy-start.5 = (f32[1024,512]{1,0:T(8,128)S(1)}, f32[1024,512]{1,0:T(8,128)}, u32[]{:S(2)}) copy-start(f32[1024,512]{1,0:T(8,128)} %copy-done.4) | copy-start | bytes 6291460
  29.8 3.6 %copy-start.10 = (f32[1024,512]{1,0:T(8,128)S(1)}, f32[1024,512]{1,0:T(8,128)}, u32[]{:S(2)}) copy-start(f32[1024,512]{1,0:T(8,128)} %param.10) | copy-start | bytes 6291460
  35.5 3.8 %collective-permute-start = (f32[512,512]{1,0:T(8,128)S(1)}, f32[512,512]{1,0:T(8,128)S(1)}, u32[]{:S(2)}, u32[]{:S(2)}) collective-permute-start(f32[512,512]{1,0:T(8,128)S(1)} %select_bitcast_fusion), channel_id=1, source_target_pairs={{0,1},{1,0},{2,3},{3,2},{4,5},{5,4},{6,7},{7,6},{8,9},{9,8},{10,11... | collective-permute-start | bytes 3145736 | tf_op jit(solution)/shard_map/ppermute | solution.py:138
  63.3 29.7 %copy-start.7 = (s32[16,32]{1,0:T(8,128)S(1)}, s32[16,32]{1,0:T(8,128)}, u32[]{:S(2)}) copy-start(s32[16,32]{1,0:T(8,128)} %param.19) | copy-start | bytes 6148
  63.3 30.5 %copy-start.8 = (s32[16,16]{1,0:T(8,128)S(1)}, s32[16,16]{1,0:T(8,128)}, u32[]{:S(2)}) copy-start(s32[16,16]{1,0:T(8,128)} %param.18) | copy-start | bytes 3076
  63.4 4.4 %collective-permute-start.1 = (f32[32,512]{1,0:T(8,128)S(1)}, f32[32,512]{1,0:T(8,128)S(1)}, u32[]{:S(2)}, u32[]{:S(2)}) collective-permute-start(f32[32,512]{1,0:T(8,128)S(1)} %reduce_sum.9), channel_id=1, source_target_pairs={{0,2},{1,3},{2,0},{3,1},{4,6},{5,7},{6,4},{7,5},{8,10},{9,11},{10,... | collective-permute-start | bytes 196616 | tf_op jit(solution)/shard_map/ppermute | solution.py:146
  67.8 5.6 %collective-permute-start.2 = (f32[32,512]{1,0:T(8,128)S(1)}, f32[32,512]{1,0:T(8,128)S(1)}, u32[]{:S(2)}, u32[]{:S(2)}) collective-permute-start(f32[32,512]{1,0:T(8,128)S(1)} %add.103), channel_id=1, source_target_pairs={{0,6},{1,7},{2,4},{3,5},{4,2},{5,3},{6,0},{7,1},{8,14},{9,15},{10,... | collective-permute-start | bytes 196616 | tf_op jit(solution)/shard_map/ppermute | solution.py:148
  86.3 21.9 %all-to-all-start = ((f32[32,16,512]{2,1,0:T(8,128)}), f32[32,16,512]{2,1,0:T(8,128)S(1)}, u32[]{:S(2)}, u32[]{:S(2)}) async-start(f32[32,16,512]{2,1,0:T(8,128)} %reduce-scatter.2.cloned.1.call-done), calls=%async_computation.1 | async-start | bytes 2097152 | tf_op jit(solution)/shard_map/all_to_all | solution.py:125
  112.0 34.0 %all-to-all-start.1 = ((f32[64,16,512]{2,1,0:T(8,128)}), f32[64,16,512]{2,1,0:T(8,128)}, u32[]{:S(2)}, u32[]{:S(2)}) async-start(f32[64,16,512]{2,1,0:T(8,128)} %copy.22), calls=%async_computation.2 | async-start | bytes 4194304 | tf_op jit(solution)/shard_map/all_to_all | solution.py:127
  123.1 4.6 %collective-permute-start.3 = (f32[512,512]{0,1:T(8,128)S(1)}, f32[512,512]{0,1:T(8,128)S(1)}, u32[]{:S(2)}, u32[]{:S(2)}) collective-permute-start(f32[512,512]{0,1:T(8,128)S(1)} %copy.25), channel_id=1, source_target_pairs={{0,1},{1,0},{2,3},{3,2},{4,5},{5,4},{6,7},{7,6},{8,9},{9,8},{10,11... | collective-permute-start | bytes 3145736 | tf_op jit(solution)/shard_map/ppermute | solution.py:151
  129.2 2.6 %copy-start.9 = (f32[512,512]{0,1:T(8,128)S(1)}, f32[512,512]{0,1:T(8,128)}, u32[]{:S(2)}) copy-start(f32[512,512]{0,1:T(8,128)} %get-tuple-element.16) | copy-start | bytes 3145732
  146.0 2.2 %copy-start.2 = (f32[8,128,512]{2,1,0:T(8,128)S(1)}, f32[8,128,512]{2,1,0:T(8,128)}, u32[]{:S(2)}) copy-start(f32[8,128,512]{2,1,0:T(8,128)} %copy-done.1) | copy-start | bytes 6291460
  146.0 2.9 %copy-start.6 = (f32[1024,512]{1,0:T(8,128)S(1)}, f32[1024,512]{1,0:T(8,128)}, u32[]{:S(2)}) copy-start(f32[1024,512]{1,0:T(8,128)} %copy-done.4) | copy-start | bytes 6291460
Sparse Core Ops, SparseCore 0:
  29.8 56.4 reduce-scatter.1
Sparse Core Ops, SparseCore 1:
  74.1 47.3 all-gather.1

commit v2 on v1

v2 whole, which is shorter than its diff:
```python
import functools

import jax
import jax.numpy as jnp
from jax import lax
from jax.experimental import pallas as pl
from jax.experimental.pallas import tpu as pltpu
from jax.sharding import PartitionSpec as P

F32 = jnp.float32
BF16 = jnp.bfloat16
BLOCK = 128


def split(x):
    high = x.astype(BF16)
    low = (x - high.astype(F32)).astype(BF16)
    return high, low


def tile_kernel(
    blocks,
    want_rows,
    info_ref,
    preact_ref,
    grad_ref,
    weight_ref,
    tiles_ref,
    local_ref,
    keep_ref,
    send_ref,
    *rest,
):
    if want_rows:
        pre_ref, *rest = rest
    left, product, halo, weight, sems = rest
    step = pl.program_id(0)
    tiles_row = 8
    step_rows = preact_ref.shape[0]
    width = weight_ref.shape[0]

    @pl.when(step == 0)
    def _():
        local_ref[...] = jnp.zeros_like(local_ref)
        halo[...] = jnp.zeros_like(halo)
        high, low = split(weight_ref[...])
        weight[0] = high
        weight[1] = low

    pre_grad = jnp.where(preact_ref[...] > 0, grad_ref[...], 0.0)
    if want_rows:
        pre_ref[...] = pre_grad
    pre_high, pre_low = split(pre_grad)
    contract = (((1,), (1,)), ((), ()))
    rows = lax.dot_general(pre_high, weight[0], contract, preferred_element_type=F32)
    rows += lax.dot_general(pre_high, weight[1], contract, preferred_element_type=F32)
    rows += lax.dot_general(pre_low, weight[0], contract, preferred_element_type=F32)
    row_high, row_low = split(rows)
    for r in range(step_rows // BLOCK):
        for k in range(tiles_row):
            high, low = split(tiles_ref[r * tiles_row + k].T)
            at = pl.ds(k * BLOCK, BLOCK)
            left[at, 0:BLOCK] = high
            left[at, BLOCK : 2 * BLOCK] = high
            left[at, 2 * BLOCK : 3 * BLOCK] = low
        mine = slice(r * BLOCK, (r + 1) * BLOCK)
        right = jnp.concatenate([row_high[mine], row_low[mine], row_high[mine]], axis=0)
        product[...] = jnp.dot(left[...], right, preferred_element_type=F32)
        for k in range(tiles_row):
            col = info_ref[step * tiles_ref.shape[0] + r * tiles_row + k]
            at = pl.ds(k * BLOCK, BLOCK)

            @pl.when(col < blocks)
            def _():
                local_ref[col] += product[at, :]

            @pl.when(col >= blocks)
            def _():
                halo[col - blocks] += product[at, :]

    @pl.when(step == pl.num_programs(0) - 1)
    def _():
        half = BLOCK // 2
        core = info_ref[info_ref.shape[0] - 1]
        own = pl.ds(pl.multiple_of(core * half, half), half)
        other = pl.ds(pl.multiple_of((1 - core) * half, half), half)
        out = pltpu.make_async_copy(halo.at[:, other], send_ref, sems.at[0])
        stay = pltpu.make_async_copy(halo.at[:, own], keep_ref, sems.at[1])
        out.start()
        stay.start()
        out.wait()
        stay.wait()


def tile_sums(info, preact, grad_out, weight, tile_vals, slot_count, part, parts, want_rows):
    node_rows, feat = preact.shape
    width = weight.shape[0] // parts
    blocks = node_rows // BLOCK
    tiles_row = tile_vals.shape[0] // blocks
    steps = 4
    step_rows = node_rows // steps
    step_tiles = tile_vals.shape[0] // steps
    out_shape = [
        jax.ShapeDtypeStruct((blocks, BLOCK, width), F32),
        jax.ShapeDtypeStruct((slot_count, BLOCK // 2, width), F32),
        jax.ShapeDtypeStruct((slot_count, BLOCK // 2, width), F32),
    ]
    out_specs = [
        pl.BlockSpec((blocks, BLOCK, width), lambda i, info: (0, 0, 0)),
        pl.BlockSpec(memory_space=pl.ANY),
        pl.BlockSpec(memory_space=pl.ANY),
    ]
    if want_rows:
        out_shape.append(jax.ShapeDtypeStruct((node_rows, feat), F32))
        out_specs.append(pl.BlockSpec((step_rows, feat), lambda i, info: (i, 0)))
    return pl.pallas_call(
        functools.partial(tile_kernel, blocks, want_rows),
        out_shape=out_shape,
        grid_spec=pltpu.PrefetchScalarGridSpec(
            num_scalar_prefetch=1,
            grid=(steps,),
            in_specs=[
                pl.BlockSpec((step_rows, feat), lambda i, info: (i, 0)),
                pl.BlockSpec((step_rows, feat), lambda i, info: (i, 0)),
                pl.BlockSpec((width, feat), lambda i, info: (part, 0)),
                pl.BlockSpec((step_tiles, BLOCK, BLOCK), lambda i, info: (i, 0, 0)),
            ],
            out_specs=out_specs,
            scratch_shapes=[
                pltpu.VMEM((tiles_row * BLOCK, 3 * BLOCK), BF16),
                pltpu.VMEM((tiles_row * BLOCK, width), F32),
                pltpu.VMEM((slot_count, BLOCK, width), F32),
                pltpu.VMEM((2, width, feat), BF16),
                pltpu.SemaphoreType.DMA((2,)),
            ],
        ),
        compiler_params=pltpu.CompilerParams(
            dimension_semantics=("arbitrary",), vmem_limit_bytes=40 * 1024 * 1024
        ),
        cost_estimate=pl.CostEstimate(
            flops=6 * (tile_vals.size + node_rows * feat) * width,
            bytes_accessed=14 * 1024 * 1024,
            transcendentals=0,
        ),
        name="tile_sums",
    )(info, preact, grad_out, weight, tile_vals)


ROWS = 16


def first_kernel(info_ref, keep_ref, recv_ref, keep_a, send_a, keep_b, send_b):
    p = info_ref[1]
    q = info_ref[2]
    for p_at in range(2):
        for q_at, out in ((q, keep_a), (1 - q, send_a)):
            at = pl.ds(pl.multiple_of(p_at * 2 * ROWS + q_at * ROWS, ROWS), ROWS)
            out[:, p_at] = keep_ref[0, :, at] + recv_ref[0, :, at]
    for q_at in range(2):
        for p_at, out in ((p, keep_b), (1 - p, send_b)):
            at = pl.ds(pl.multiple_of(p_at * 2 * ROWS + q_at * ROWS, ROWS), ROWS)
            out[:, q_at] = keep_ref[1, :, at] + recv_ref[1, :, at]


def first_sums(info, keep, recv):
    slots, rows, width = keep.shape
    half = slots // 2
    step = half // 4
    piece = jax.ShapeDtypeStruct((half, 2, ROWS, width), F32)
    whole_spec = pl.BlockSpec((2, step, rows, width), lambda i, info: (0, i, 0, 0))
    piece_spec = pl.BlockSpec((step, 2, ROWS, width), lambda i, info: (i, 0, 0, 0))
    return pl.pallas_call(
        first_kernel,
        out_shape=[piece] * 4,
        grid_spec=pltpu.PrefetchScalarGridSpec(
            num_scalar_prefetch=1,
            grid=(4,),
            in_specs=[whole_spec] * 2,
            out_specs=[piece_spec] * 4,
        ),
        cost_estimate=pl.CostEstimate(
            flops=keep.size, bytes_accessed=12 * keep.size, transcendentals=0
        ),
        name="first_sums",
    )(info, keep.reshape(2, half, rows, width), recv.reshape(2, half, rows, width))


def second_kernel(info_ref, keep_a, recv_a, keep_b, recv_b, out_keep, out_send_a, out_send_b):
    p = info_ref[1]
    q = info_ref[2]
    out_keep[0] = keep_a[:, p] + recv_a[:, p]
    out_send_a[...] = keep_a[:, 1 - p] + recv_a[:, 1 - p]
    out_keep[1] = keep_b[:, q] + recv_b[:, q]
    out_send_b[...] = keep_b[:, 1 - q] + recv_b[:, 1 - q]


def second_sums(info, keep_a, recv_a, keep_b, recv_b):
    half, _, rows, width = keep_a.shape
    step = half // 2
    piece_spec = pl.BlockSpec((step, 2, rows, width), lambda i, info: (i, 0, 0, 0))
    send_spec = pl.BlockSpec((step, rows, width), lambda i, info: (i, 0, 0))
    send = jax.ShapeDtypeStruct((half, rows, width), F32)
    return pl.pallas_call(
        second_kernel,
        out_shape=[jax.ShapeDtypeStruct((2, half, rows, width), F32), send, send],
        grid_spec=pltpu.PrefetchScalarGridSpec(
            num_scalar_prefetch=1,
            grid=(2,),
            in_specs=[piece_spec] * 4,
            out_specs=[
                pl.BlockSpec((2, step, rows, width), lambda i, info: (0, i, 0, 0)),
                send_spec,
                send_spec,
            ],
        ),
        cost_estimate=pl.CostEstimate(
            flops=keep_a.size, bytes_accessed=24 * keep_a.size, transcendentals=0
        ),
        name="second_sums",
    )(info, keep_a, recv_a, keep_b, recv_b)


def third_kernel(keep_ref, recv_a, recv_b, out_ref):
    out_ref[0] = keep_ref[0] + recv_a[...]
    out_ref[1] = keep_ref[1] + recv_b[...]


def third_sums(keep, recv_a, recv_b):
    return pl.pallas_call(
        third_kernel,
        out_shape=jax.ShapeDtypeStruct(keep.shape, F32),
        cost_estimate=pl.CostEstimate(
            flops=keep.size, bytes_accessed=12 * keep.size, transcendentals=0
        ),
        name="third_sums",
    )(keep, recv_a, recv_b)


def place_kernel(target_ref, arrived_ref, out_ref):
    out_ref[...] = jnp.zeros_like(out_ref)

    @pl.loop(0, arrived_ref.shape[0])
    def _(s):
        target = target_ref[s]

        @pl.when(target >= 0)
        def _():
            out_ref[target] += arrived_ref[s]


def place(target, arrived, group_blocks):
    _, rows, width = arrived.shape
    return pl.pallas_call(
        place_kernel,
        out_shape=jax.ShapeDtypeStruct((group_blocks, rows, width), F32),
        grid_spec=pltpu.PrefetchScalarGridSpec(
            num_scalar_prefetch=1,
            grid=(1,),
            in_specs=[pl.BlockSpec(arrived.shape, lambda i, t: (0, 0, 0))],
            out_specs=pl.BlockSpec((group_blocks, rows, width), lambda i, t: (0, 0, 0)),
        ),
        cost_estimate=pl.CostEstimate(
            flops=arrived.size, bytes_accessed=12 * arrived.size, transcendentals=0
        ),
        name="place",
    )(target, arrived)


QUARTER = (0, 1, 3, 2)


def finish_kernel(base_ref, *rest):
    *parts, out_ref = rest
    width = out_ref.shape[1] // len(parts)
    for h, part in enumerate(parts):
        for member in range(part.shape[0]):
            start = (member % 2) * (BLOCK // 2) + QUARTER[member // 2] * ROWS
            at = (slice(start, start + ROWS), slice(h * width, (h + 1) * width))
            out_ref[at] = base_ref[at] + part[member, 0]


def finish(base, parts):
    node_rows, feat = base.shape
    members, blocks, rows, width = parts[0].shape
    part_spec = pl.BlockSpec((members, 1, rows, width), lambda i: (0, i, 0, 0))
    row_spec = pl.BlockSpec((BLOCK, feat), lambda i: (i, 0))
    return pl.pallas_call(
        finish_kernel,
        out_shape=jax.ShapeDtypeStruct((node_rows, feat), F32),
        grid=(blocks,),
        in_specs=[row_spec] + [part_spec] * len(parts),
        out_specs=row_spec,
        cost_estimate=pl.CostEstimate(
            flops=base.size, bytes_accessed=12 * base.size, transcendentals=0
        ),
        name="finish",
    )(base, *parts)


PARTS = 2


def on_device(
    features,
    aggregated,
    preact,
    grad_out,
    w_self,
    w_neigh,
    tile_vals,
    tile_col,
    halo_count,
    halo_target,
):
    high = lax.Precision.HIGH
    node_rows, width = features.shape
    blocks = node_rows // BLOCK
    groups = lax.axis_size("group")
    members = lax.axis_size("local")
    slot_count = halo_target.shape[1]
    capacity = slot_count // groups
    group_id = lax.axis_index("group")
    core = lax.axis_index("local") % 2

    member = lax.axis_index("local")
    chip = member // 2
    side = chip // 2
    pair = (chip % 2) ^ side
    place_info = jnp.stack([core, side, pair]).astype(jnp.int32)
    tile_info = jnp.concatenate([tile_col, core[None].astype(jnp.int32)])
    swap = [(i, i ^ 1) for i in range(members)]
    pairs = [(i, i ^ 2) for i in range(members)]
    across = [(i, members - 2 - (i - i % 2) + i % 2) for i in range(members)]

    slot_ids = jnp.arange(slot_count, dtype=jnp.int32)
    source = slot_ids // capacity
    offset = slot_ids % capacity
    recv_target = halo_target[source, group_id * capacity + offset]
    recv_live = offset < halo_count[source, group_id]
    target = jnp.where(recv_live, recv_target, -1)
    group_blocks = blocks * members

    local_parts = []
    incoming = []
    for part in range(PARTS):
        local_part, keep, send, *rows = tile_sums(
            tile_info, preact, grad_out, w_neigh, tile_vals, slot_count, part, PARTS, part == 0
        )
        if part == 0:
            pre_grad = rows[0]
        local_parts.append(local_part.reshape(node_rows, -1))
        recv = lax.ppermute(send, "local", swap)
        keep_a, send_a, keep_b, send_b = first_sums(place_info, keep, recv)
        recv_a = lax.ppermute(send_a, "local", pairs)
        recv_b = lax.ppermute(send_b, "local", across)
        keep, send_a, send_b = second_sums(place_info, keep_a, recv_a, keep_b, recv_b)
        recv_a = lax.ppermute(send_a, "local", across)
        recv_b = lax.ppermute(send_b, "local", pairs)
        row_part = third_sums(keep, recv_a, recv_b).reshape(slot_count, ROWS, -1)
        arrived = lax.all_to_all(row_part, "group", split_axis=0, concat_axis=0, tiled=True)
        placed = place(target, arrived, group_blocks)
        received = lax.all_to_all(placed, "local", split_axis=0, concat_axis=0, tiled=True)
        incoming.append(received.reshape(members, blocks, ROWS, -1))

    contract = (((0,), (0,)), ((), ()))
    self_term = lax.dot_general(
        features, pre_grad, contract, precision=high, preferred_element_type=F32
    )
    neigh_term = lax.dot_general(
        aggregated, pre_grad, contract, precision=high, preferred_element_type=F32
    )
    first = core == 0
    mine = jnp.where(first, self_term, neigh_term) + lax.ppermute(
        jnp.where(first, neigh_term, self_term), "local", swap
    )
    shares = lax.all_to_all(
        mine.reshape(groups, -1, width), "group", split_axis=0, concat_axis=0, tiled=True
    )
    total = jnp.sum(shares, axis=0)
    total = total + lax.ppermute(total, "local", pairs)
    total = total + lax.ppermute(total, "local", across)
    scale = float(node_rows * groups * members) ** (-0.5)
    whole = lax.all_gather(total * scale, "group", tiled=True)
    other = lax.ppermute(whole, "local", swap)
    self_grad = jnp.where(first, whole, other)
    neigh_grad = jnp.where(first, other, whole)

    base = jnp.dot(pre_grad, w_self.T, precision=high, preferred_element_type=F32)
    base = base + jnp.concatenate(local_parts, axis=1)
    node_grad = finish(base, incoming)
    return (node_grad, self_grad, neigh_grad)


def solution(mesh):
    in_specs = (
        P(("group", "local"), None),
        P(("group", "local"), None),
        P(("group", "local"), None),
        P(("group", "local"), None),
        P(),
        P(),
        P(("group", "local"), None, None),
        P(("group", "local")),
        P(),
        P(),
    )
    out_specs = (P(("group", "local"), None), P(), P())
    return jax.shard_map(
        on_device, mesh=mesh, in_specs=in_specs, out_specs=out_specs, check_vma=False
    )
```

time: 161 us -> 214 us (1.33)
  Pallas kernels: 14.1 us -> 57.6 us
  starting transfers between devices: 22 us -> 49 us
  blocking collectives: 23.6 us -> 0 us
  local copies, waits for them, and re-layouts: 15 us -> 21.5 us
  matrix products: 13 us -> 9.1 us
  waiting for transfers between devices: 51.5 us -> 53.7 us
    pallas_call x1 -> x11, Pallas kernels: 14.1 us -> 57.6 us  [the longest x2 24.7 us: tile_sums(): pl.pallas_call(functools.partial(tile_kernel, blocks, want_rows), out_sha...]
    all_to_all x1 -> x0, blocking collectives: 23.6 us -> none  [on_device(): lax.all_to_all(mine.reshape(groups, -1, width), 'group', split_axis=0, co...]
    all_to_all x2 -> x5, starting transfers between devices: 14.2 us -> 36.2 us  [the longest x2 14.6 us: on_device(): lax.all_to_all(placed, 'local', split_axis=0, concat_axis=0, tiled=True)]
    ppermute x0 -> x10, waiting for transfers between devices: none -> 17.3 us  [the longest x2 17.3 us: on_device(): recv_a = lax.ppermute(send_a, 'local', across)]
    reduce_scatter x1 -> x0, waiting for transfers between devices: 12.3 us -> none  [on_device(): lax.psum_scatter(halo_terms, 'local', scatter_dimension=1, tiled=True)]
    unnamed x26 -> x52, local copies, waits for them, and re-layouts: 7.61 us -> 17.5 us
    ppermute x0 -> x10, starting transfers between devices: none -> 8.38 us  [the longest x2 2.55 us: on_device(): recv_b = lax.ppermute(send_b, 'local', across)]
    all_to_all x2 -> x5, waiting for transfers between devices: 26.5 us -> 30.7 us  [the longest x2 19 us: on_device(): lax.all_to_all(placed, 'local', split_axis=0, concat_axis=0, tiled=True)]
  transfers between devices with their start and end apart: 8 -> 20, of which waited for: 8 -> 8; matrix products, arithmetic and copies ran while one was open for 12% -> 8% of each run, Pallas kernels for 0% -> 21%
where the time goes in v2:
time: 214 us; the launch traced here: 212 us
  Pallas kernels  57.6 us (27%)
  waiting for transfers between devices  53.7 us (25%)
  starting transfers between devices  49 us (23%)
  local copies, waits for them, and re-layouts  21.5 us (10%)
  between operations  14.3 us (7%)
  matrix products  9.1 us (4%)
  other arithmetic  7.12 us (3%)
    pallas_call x2, Pallas kernels, tile_sums(): pl.pallas_call(functools.partial(tile_kernel, blocks, want_rows), out_sha...  24.7 us
    all_to_all x2, waiting for transfers between devices, on_device(): lax.all_to_all(placed, 'local', split_axis=0, concat_axis=0, tiled=True)  19 us
    unnamed x52, local copies, waits for them, and re-layouts  17.5 us
    ppermute x2, waiting for transfers between devices, on_device(): recv_a = lax.ppermute(send_a, 'local', across)  17.3 us
    all_to_all x2, starting transfers between devices, on_device(): lax.all_to_all(placed, 'local', split_axis=0, concat_axis=0, tiled=True)  14.6 us
    all_to_all x2, starting transfers between devices, on_device(): lax.all_to_all(row_part, 'group', split_axis=0, concat_axis=0, tiled=True)  13.8 us
    pallas_call x2, Pallas kernels, first_sums(): pl.pallas_call(first_kernel, out_shape=[piece] * 4, grid_spec=pltpu.Prefe...  9.71 us
    all_to_all x1, starting transfers between devices, on_device(): lax.all_to_all(mine.reshape(groups, -1, width), 'group', split_axis=0, co...  7.86 us
  transfers between devices with their start and end apart: 20, of which 8 were waited for; matrix products, arithmetic and copies ran while one was open for 8% of the time, Pallas kernels for 21%

profile of v2, /device:TPU:1, one launch (start us, length us, event | category | flops | bytes accessed | tf_op | source)
XLA Modules:
  0.0 212.3 jit_solution(16779615525728115045)
XLA Ops:
  12.5 12.4 %tile_sums.3 = (f32[8,128,256]{2,1,0:T(8,128)S(1)}, f32[32,64,256]{2,1,0:T(8,128)S(1)}, f32[32,64,256]{2,1,0:T(8,128)}) custom-call(s32[65]{0:T(128)S(1)} %pad_add_fusion.info_ref, f32[1024,512]{1,0:T(8,128)S(1)} %copy-done.2, f32[1024,512]{1,0:T(8,128)S(1)} %copy-done.4, f32[512,512]{1,0:T(8,128)S(1)} %copy-done.6, f32[64,128,128]{2,1,0:T(8,128)} %tiles_ref.3), custom_call_target="tpu_custom_call" | custom-call | flops 2415919104 | bytes 14680064 | tf_op jit(solution)/shard_map/tile_sums/pallas_call | solution.py:116
  31.8 12.4 %tile_sums.2 = (f32[8,128,256]{2,1,0:T(8,128)S(1)}, f32[32,64,256]{2,1,0:T(8,128)S(1)}, f32[32,64,256]{2,1,0:T(8,128)}, f32[1024,512]{1,0:T(8,128)S(1)}) custom-call(s32[65]{0:T(128)S(1)} %pad_add_fusion.info_ref, f32[1024,512]{1,0:T(8,128)S(1)} %copy-done.3, f32[1024,512]{1,0:T(8,128)S(1)} %copy-done.5, f32[512,512]{1,0:T(8,128)S(1)} %copy-done.7, ...), custom_call_target="tpu_custom_call" | custom-call | flops 2415919104 | bytes 14680064 | tf_op jit(solution)/shard_map/tile_sums/pallas_call | solution.py:116
  44.2 1.8 fusion.8
  47.4 1.9 fusion.7
  50.1 2.7 %collective-permute-done.10 = f32[512,512]{1,0:T(8,128)S(1)} collective-permute-done((f32[512,512]{1,0:T(8,128)S(1)}, f32[512,512]{1,0:T(8,128)S(1)}, u32[]{:S(2)}, u32[]{:S(2)}) %collective-permute-start.10) | collective-permute-done | bytes 1048608 | tf_op jit(solution)/shard_map/ppermute | solution.py:373
  54.1 7.9 %all-to-all-start.4 = ((f32[16,32,512]{2,1,0:T(8,128)}), f32[16,32,512]{2,1,0:T(8,128)S(1)}, u32[]{:S(2)}, u32[]{:S(2)}) async-start(f32[16,32,512]{2,1,0:T(8,128)} %bitcast.17), calls=%async_computation.4 | async-start | bytes 2097152 | tf_op jit(solution)/shard_map/all_to_all | solution.py:376
  62.7 4.9 %first_sums.3 = (f32[16,2,16,256]{3,2,1,0:T(8,128)}, f32[16,2,16,256]{3,2,1,0:T(8,128)}, f32[16,2,16,256]{3,2,1,0:T(8,128)}, f32[16,2,16,256]{3,2,1,0:T(8,128)}) custom-call(s32[3]{0:T(128)} %pad_add_fusion.1.info_ref, f32[2,16,64,256]{3,2,1,0:T(8,128)} %bitcast.29, f32[2,16,64,256]{3,2,1,0:T(8,128)} %bitcast.12.recv_ref), custom_call_target="tpu_custom_call" | custom-call | flops 524288 | bytes 6291456 | tf_op jit(solution)/shard_map/first_sums/pallas_call | solution.py:172
  70.6 7.4 %all-to-all-done.4 = f32[16,32,512]{2,1,0:T(8,128)S(1)} async-done(((f32[16,32,512]{2,1,0:T(8,128)}), f32[16,32,512]{2,1,0:T(8,128)S(1)}, u32[]{:S(2)}, u32[]{:S(2)}) %all-to-all-start.4) | async-done | bytes 1048608 | tf_op jit(solution)/shard_map/all_to_all | solution.py:376
  79.4 3.0 %collective-permute-done.11 = f32[32,512]{1,0:T(8,128)S(1)} collective-permute-done((f32[32,512]{1,0:T(8,128)S(1)}, f32[32,512]{1,0:T(8,128)S(1)}, u32[]{:S(2)}, u32[]{:S(2)}) %collective-permute-start.11) | collective-permute-done | bytes 65568 | tf_op jit(solution)/shard_map/ppermute | solution.py:380
  82.4 2.7 %collective-permute-start.12 = (f32[32,512]{1,0:T(8,128)S(1)}, f32[32,512]{1,0:T(8,128)S(1)}, u32[]{:S(2)}, u32[]{:S(2)}) collective-permute-start(f32[32,512]{1,0:T(8,128)S(1)} %add.100), channel_id=1, source_target_pairs={{0,6},{1,7},{2,4},{3,5},{4,2},{5,3},{6,0},{7,1},{8,14},{9,15},{10,... | collective-permute-start | bytes 196616 | tf_op jit(solution)/shard_map/ppermute | solution.py:381
  85.2 4.8 %first_sums.2 = (f32[16,2,16,256]{3,2,1,0:T(8,128)}, f32[16,2,16,256]{3,2,1,0:T(8,128)}, f32[16,2,16,256]{3,2,1,0:T(8,128)}, f32[16,2,16,256]{3,2,1,0:T(8,128)}) custom-call(s32[3]{0:T(128)} %pad_add_fusion.1.info_ref, f32[2,16,64,256]{3,2,1,0:T(8,128)} %bitcast.28, f32[2,16,64,256]{3,2,1,0:T(8,128)} %bitcast.8.recv_ref), custom_call_target="tpu_custom_call" | custom-call | flops 524288 | bytes 6291456 | tf_op jit(solution)/shard_map/first_sums/pallas_call | solution.py:172
  90.8 3.1 %second_sums.3 = (f32[2,16,16,256]{3,2,1,0:T(8,128)}, f32[16,16,256]{2,1,0:T(8,128)}, f32[16,16,256]{2,1,0:T(8,128)}) custom-call(s32[3]{0:T(128)} %pad_add_fusion.1.info_ref, f32[16,2,16,256]{3,2,1,0:T(8,128)} %get-tuple-element.38.keep_a, f32[16,2,16,256]{3,2,1,0:T(8,128)} %collective-permute-done.6.recv_a, f32[16,2,16,256]{3,2,1,0:T(8,128)} %get-tuple-element.40.keep_b, ...), custom_call_target="tpu_custom_call" | custom-call | flops 131072 | bytes 3145728 | tf_op jit(solution)/shard_map/second_sums/pallas_call | solution.py:203
  93.9 2.0 collective-permute-start.8
  96.7 10.8 %collective-permute-done.8.recv_a = f32[16,16,256]{2,1,0:T(8,128)S(1)} collective-permute-done((f32[16,16,256]{2,1,0:T(8,128)}, f32[16,16,256]{2,1,0:T(8,128)S(1)}, u32[]{:S(2)}, u32[]{:S(2)}) %collective-permute-start.8) | collective-permute-done | bytes 262176 | tf_op jit(solution)/shard_map/ppermute | solution.py:357
  108.4 2.1 third_sums.3
  110.4 7.5 %all-to-all-start.2 = ((f32[32,16,256]{2,1,0:T(8,128)}), f32[32,16,256]{2,1,0:T(8,128)S(1)}, u32[]{:S(2)}, u32[]{:S(2)}) async-start(f32[32,16,256]{2,1,0:T(8,128)} %bitcast.33), calls=%async_computation.2 | async-start | bytes 1048576 | tf_op jit(solution)/shard_map/all_to_all | solution.py:360
  118.7 3.2 %second_sums.2 = (f32[2,16,16,256]{3,2,1,0:T(8,128)}, f32[16,16,256]{2,1,0:T(8,128)}, f32[16,16,256]{2,1,0:T(8,128)}) custom-call(s32[3]{0:T(128)} %pad_add_fusion.1.info_ref, f32[16,2,16,256]{3,2,1,0:T(8,128)} %get-tuple-element.29.keep_a, f32[16,2,16,256]{3,2,1,0:T(8,128)} %copy-done.20, f32[16,2,16,256]{3,2,1,0:T(8,128)} %get-tuple-element.31.keep_b, ...), custom_call_target="tpu_custom_call" | custom-call | flops 131072 | bytes 3145728 | tf_op jit(solution)/shard_map/second_sums/pallas_call | solution.py:203
  122.5 6.4 %collective-permute-done.3.recv_a = f32[16,16,256]{2,1,0:T(8,128)S(1)} collective-permute-done((f32[16,16,256]{2,1,0:T(8,128)}, f32[16,16,256]{2,1,0:T(8,128)S(1)}, u32[]{:S(2)}, u32[]{:S(2)}) %collective-permute-start.3) | collective-permute-done | bytes 262176 | tf_op jit(solution)/shard_map/ppermute | solution.py:357
  129.7 2.1 third_sums.2
  131.8 6.3 %all-to-all-start = ((f32[32,16,256]{2,1,0:T(8,128)}), f32[32,16,256]{2,1,0:T(8,128)S(1)}, u32[]{:S(2)}, u32[]{:S(2)}) async-start(f32[32,16,256]{2,1,0:T(8,128)} %bitcast.32), calls=%async_computation | async-start | bytes 1048576 | tf_op jit(solution)/shard_map/all_to_all | solution.py:360
  140.1 3.2 %place.3 = f32[64,16,256]{2,1,0:T(8,128)} custom-call(s32[32]{0:T(128)} %compare_select_fusion.2.target_ref, f32[32,16,256]{2,1,0:T(8,128)} %copy-done.18), custom_call_target="tpu_custom_call" | custom-call | flops 131072 | bytes 1572864 | tf_op jit(solution)/shard_map/place/pallas_call | solution.py:253
  143.3 4.2 %all-to-all-done.arrived_ref = f32[32,16,256]{2,1,0:T(8,128)S(1)} async-done(((f32[32,16,256]{2,1,0:T(8,128)}), f32[32,16,256]{2,1,0:T(8,128)S(1)}, u32[]{:S(2)}, u32[]{:S(2)}) %all-to-all-start) | async-done | bytes 524320 | tf_op jit(solution)/shard_map/all_to_all | solution.py:360
  147.5 9.6 %all-to-all-start.3 = ((f32[64,16,256]{2,1,0:T(8,128)}), f32[64,16,256]{2,1,0:T(8,128)}, u32[]{:S(2)}, u32[]{:S(2)}) async-start(f32[64,16,256]{2,1,0:T(8,128)} %place.3), calls=%async_computation.3 | async-start | bytes 2097152 | tf_op jit(solution)/shard_map/all_to_all | solution.py:362
  157.1 2.6 %copy.18 = f32[512,512]{0,1:T(8,128)} copy(f32[512,512]{1,0:T(8,128)} %all-gather.2.cloned.1.call-done) | data formatting | bytes 2097152 | tf_op jit(solution)/shard_map/all_gather | solution.py:383
  159.8 3.3 %place.2 = f32[64,16,256]{2,1,0:T(8,128)} custom-call(s32[32]{0:T(128)} %compare_select_fusion.2.target_ref, f32[32,16,256]{2,1,0:T(8,128)} %copy-done.19), custom_call_target="tpu_custom_call" | custom-call | flops 131072 | bytes 1572864 | tf_op jit(solution)/shard_map/place/pallas_call | solution.py:253
  163.2 9.2 %all-to-all-done.3 = f32[64,16,256]{2,1,0:T(8,128)} async-done(((f32[64,16,256]{2,1,0:T(8,128)}), f32[64,16,256]{2,1,0:T(8,128)}, u32[]{:S(2)}, u32[]{:S(2)}) %all-to-all-start.3) | async-done | bytes 1048608 | tf_op jit(solution)/shard_map/all_to_all | solution.py:362
  172.3 5.0 %all-to-all-start.1 = ((f32[64,16,256]{2,1,0:T(8,128)}), f32[64,16,256]{2,1,0:T(8,128)}, u32[]{:S(2)}, u32[]{:S(2)}) async-start(f32[64,16,256]{2,1,0:T(8,128)} %place.2), calls=%async_computation.1 | async-start | bytes 2097152 | tf_op jit(solution)/shard_map/all_to_all | solution.py:362
  177.4 5.4 %maximum_add_fusion.base_ref = f32[1024,512]{1,0:T(8,128)} fusion(f32[1024,256]{1,0:T(8,128)S(1)} %bitcast.30, f32[1024,256]{1,0:T(8,128)} %bitcast.31, f32[1024,512]{1,0:T(8,128)} %copy-done.1, f32[512,512]{1,0:T(8,128)} %param.14), kind=kOutput, calls=%fused_computation.2 | convolution fusion | flops 1611661312 | bytes 7340032 | tf_op jit(solution)/shard_map/dot_general | solution.py:388
  182.7 9.9 %all-to-all-done.1 = f32[64,16,256]{2,1,0:T(8,128)} async-done(((f32[64,16,256]{2,1,0:T(8,128)}), f32[64,16,256]{2,1,0:T(8,128)}, u32[]{:S(2)}, u32[]{:S(2)}) %all-to-all-start.1) | async-done | bytes 1048608 | tf_op jit(solution)/shard_map/all_to_all | solution.py:362
  192.6 6.1 %finish.1 = f32[1024,512]{1,0:T(8,128)} custom-call(f32[1024,512]{1,0:T(8,128)} %maximum_add_fusion.base_ref, f32[8,8,16,256]{3,2,1,0:T(8,128)} %bitcast.10.rest_0_, f32[8,8,16,256]{3,2,1,0:T(8,128)} %bitcast.14.rest_1_), custom_call_target="tpu_custom_call" | custom-call | flops 524288 | bytes 6291456 | tf_op jit(solution)/shard_map/finish/pallas_call | solution.py:287
  198.7 2.8 %broadcast_select_fusion = (f32[512,512]{0,1:T(8,128)}, f32[512,512]{0,1:T(8,128)}) fusion(f32[512,512]{0,1:T(8,128)} %collective-permute-done.13, f32[512,512]{0,1:T(8,128)S(1)} %copy-done.15, pred[]{:T(512)S(6)} %eq.8), kind=kLoop, calls=%fused_computation.5 | loop fusion | flops 524288 | bytes 4194305 | tf_op jit(solution)/shard_map/jit(_where)/select_n | solution.py:386
  201.5 2.6 %copy.21 = f32[512,512]{1,0:T(8,128)} copy(f32[512,512]{0,1:T(8,128)} %get-tuple-element.54) | data formatting | bytes 2097152
  (89 shorter events, 28.7 us)
Async XLA Ops:
  7.2 37.0 %copy-start = (f32[1024,512]{1,0:T(8,128)S(1)}, f32[1024,512]{1,0:T(8,128)}, u32[]{:S(2)}) copy-start(f32[1024,512]{1,0:T(8,128)} %param.11) | copy-start | bytes 6291460
  12.5 16.1 %copy-start.7 = (f32[512,512]{1,0:T(8,128)S(1)}, f32[512,512]{1,0:T(8,128)}, u32[]{:S(2)}) copy-start(f32[512,512]{1,0:T(8,128)} %weight_ref.3) | copy-start | bytes 3145732
  27.1 35.6 %collective-permute-start.5 = (f32[32,64,256]{2,1,0:T(8,128)}, f32[32,64,256]{2,1,0:T(8,128)}, u32[]{:S(2)}, u32[]{:S(2)}) collective-permute-start(f32[32,64,256]{2,1,0:T(8,128)} %get-tuple-element.37), channel_id=1, source_target_pairs={{0,1},{1,0},{2,3},{3,2},{4,5},{5,4},{6,7},{7,6},{8,9},{9,8},{10,11... | collective-permute-start | bytes 6291464 | tf_op jit(solution)/shard_map/ppermute | solution.py:352
  44.2 2.1 copy-start.8
  44.2 2.5 %copy-start.12 = (f32[8,128,256]{2,1,0:T(8,128)}, f32[8,128,256]{2,1,0:T(8,128)S(1)}, u32[]{:S(2)}) copy-start(f32[8,128,256]{2,1,0:T(8,128)S(1)} %get-tuple-element.25) | copy-start | bytes 3145732
  44.2 3.2 %copy-start.17 = (f32[1024,512]{1,0:T(8,128)S(1)}, f32[1024,512]{1,0:T(8,128)}, u32[]{:S(2)}) copy-start(f32[1024,512]{1,0:T(8,128)} %param.10) | copy-start | bytes 6291460
  49.5 3.3 %collective-permute-start.10 = (f32[512,512]{1,0:T(8,128)S(1)}, f32[512,512]{1,0:T(8,128)S(1)}, u32[]{:S(2)}, u32[]{:S(2)}) collective-permute-start(f32[512,512]{1,0:T(8,128)S(1)} %select_bitcast_fusion), channel_id=1, source_target_pairs={{0,1},{1,0},{2,3},{3,2},{4,5},{5,4},{6,7},{7,6},{8,9},{9,8},{10,11... | collective-permute-start | bytes 3145736 | tf_op jit(solution)/shard_map/ppermute | solution.py:373
  49.6 35.6 %collective-permute-start = (f32[32,64,256]{2,1,0:T(8,128)}, f32[32,64,256]{2,1,0:T(8,128)}, u32[]{:S(2)}, u32[]{:S(2)}) collective-permute-start(f32[32,64,256]{2,1,0:T(8,128)} %get-tuple-element.28), channel_id=1, source_target_pairs={{0,1},{1,0},{2,3},{3,2},{4,5},{5,4},{6,7},{7,6},{8,9},{9,8},{10,11... | collective-permute-start | bytes 6291464 | tf_op jit(solution)/shard_map/ppermute | solution.py:352
  54.1 23.9 %all-to-all-start.4 = ((f32[16,32,512]{2,1,0:T(8,128)}), f32[16,32,512]{2,1,0:T(8,128)S(1)}, u32[]{:S(2)}, u32[]{:S(2)}) async-start(f32[16,32,512]{2,1,0:T(8,128)} %bitcast.17), calls=%async_computation.4 | async-start | bytes 2097152 | tf_op jit(solution)/shard_map/all_to_all | solution.py:376
  62.0 95.1 %all-gather.2.cloned.1.call-start = ((), (), s32[]{:S(2)}) async-start(), calls=%async_computation.5 | async-start | bytes 1114112 | tf_op jit(solution)/shard_map/all_gather | solution.py:383
  67.6 23.2 %collective-permute-start.6 = (f32[16,2,16,256]{3,2,1,0:T(8,128)}, f32[16,2,16,256]{3,2,1,0:T(8,128)}, u32[]{:S(2)}, u32[]{:S(2)}) collective-permute-start(f32[16,2,16,256]{3,2,1,0:T(8,128)} %get-tuple-element.39), channel_id=1, source_target_pairs={{0,2},{1,3},{2,0},{3,1},{4,6},{5,7},{6,4},{7,5},{8,10},{9,11},{10,... | collective-permute-start | bytes 1572872 | tf_op jit(solution)/shard_map/ppermute | solution.py:354
  68.9 22.0 %collective-permute-start.7 = (f32[16,2,16,256]{3,2,1,0:T(8,128)}, f32[16,2,16,256]{3,2,1,0:T(8,128)}, u32[]{:S(2)}, u32[]{:S(2)}) collective-permute-start(f32[16,2,16,256]{3,2,1,0:T(8,128)} %get-tuple-element.41), channel_id=1, source_target_pairs={{0,6},{1,7},{2,4},{3,5},{4,2},{5,3},{6,0},{7,1},{8,14},{9,15},{10,... | collective-permute-start | bytes 1572872 | tf_op jit(solution)/shard_map/ppermute | solution.py:355
  78.1 4.3 %collective-permute-start.11 = (f32[32,512]{1,0:T(8,128)S(1)}, f32[32,512]{1,0:T(8,128)S(1)}, u32[]{:S(2)}, u32[]{:S(2)}) collective-permute-start(f32[32,512]{1,0:T(8,128)S(1)} %reduce_sum.9), channel_id=1, source_target_pairs={{0,2},{1,3},{2,0},{3,1},{4,6},{5,7},{6,4},{7,5},{8,10},{9,11},{10,... | collective-permute-start | bytes 196616 | tf_op jit(solution)/shard_map/ppermute | solution.py:380
  82.4 13.6 %collective-permute-start.12 = (f32[32,512]{1,0:T(8,128)S(1)}, f32[32,512]{1,0:T(8,128)S(1)}, u32[]{:S(2)}, u32[]{:S(2)}) collective-permute-start(f32[32,512]{1,0:T(8,128)S(1)} %add.100), channel_id=1, source_target_pairs={{0,6},{1,7},{2,4},{3,5},{4,2},{5,3},{6,0},{7,1},{8,14},{9,15},{10,... | collective-permute-start | bytes 196616 | tf_op jit(solution)/shard_map/ppermute | solution.py:381
  90.0 27.9 %collective-permute-start.1 = (f32[16,2,16,256]{3,2,1,0:T(8,128)}, f32[16,2,16,256]{3,2,1,0:T(8,128)S(1)}, u32[]{:S(2)}, u32[]{:S(2)}) collective-permute-start(f32[16,2,16,256]{3,2,1,0:T(8,128)} %get-tuple-element.30), channel_id=1, source_target_pairs={{0,2},{1,3},{2,0},{3,1},{4,6},{5,7},{6,4},{7,5},{8,10},{9,11},{10,... | collective-permute-start | bytes 1572872 | tf_op jit(solution)/shard_map/ppermute | solution.py:354
  90.0 27.9 %collective-permute-start.2 = (f32[16,2,16,256]{3,2,1,0:T(8,128)}, f32[16,2,16,256]{3,2,1,0:T(8,128)}, u32[]{:S(2)}, u32[]{:S(2)}) collective-permute-start(f32[16,2,16,256]{3,2,1,0:T(8,128)} %get-tuple-element.32), channel_id=1, source_target_pairs={{0,6},{1,7},{2,4},{3,5},{4,2},{5,3},{6,0},{7,1},{8,14},{9,15},{10,... | collective-permute-start | bytes 1572872 | tf_op jit(solution)/shard_map/ppermute | solution.py:355
  93.9 13.6 %collective-permute-start.8 = (f32[16,16,256]{2,1,0:T(8,128)}, f32[16,16,256]{2,1,0:T(8,128)S(1)}, u32[]{:S(2)}, u32[]{:S(2)}) collective-permute-start(f32[16,16,256]{2,1,0:T(8,128)} %get-tuple-element.43), channel_id=1, source_target_pairs={{0,6},{1,7},{2,4},{3,5},{4,2},{5,3},{6,0},{7,1},{8,14},{9,15},{10,... | collective-permute-start | bytes 786440 | tf_op jit(solution)/shard_map/ppermute | solution.py:357
  95.9 11.7 %collective-permute-start.9 = (f32[16,16,256]{2,1,0:T(8,128)}, f32[16,16,256]{2,1,0:T(8,128)S(1)}, u32[]{:S(2)}, u32[]{:S(2)}) collective-permute-start(f32[16,16,256]{2,1,0:T(8,128)} %get-tuple-element.44), channel_id=1, source_target_pairs={{0,2},{1,3},{2,0},{3,1},{4,6},{5,7},{6,4},{7,5},{8,10},{9,11},{10,... | collective-permute-start | bytes 786440 | tf_op jit(solution)/shard_map/ppermute | solution.py:358
  110.4 21.4 %all-to-all-start.2 = ((f32[32,16,256]{2,1,0:T(8,128)}), f32[32,16,256]{2,1,0:T(8,128)S(1)}, u32[]{:S(2)}, u32[]{:S(2)}) async-start(f32[32,16,256]{2,1,0:T(8,128)} %bitcast.33), calls=%async_computation.2 | async-start | bytes 1048576 | tf_op jit(solution)/shard_map/all_to_all | solution.py:360
  118.7 19.4 %copy-start.13 = (s32[16,32]{1,0:T(8,128)S(1)}, s32[16,32]{1,0:T(8,128)}, u32[]{:S(2)}) copy-start(s32[16,32]{1,0:T(8,128)} %param.19) | copy-start | bytes 6148
  121.9 16.9 %copy-start.14 = (s32[16,16]{1,0:T(8,128)S(1)}, s32[16,16]{1,0:T(8,128)}, u32[]{:S(2)}) copy-start(s32[16,16]{1,0:T(8,128)} %param.18) | copy-start | bytes 3076
  121.9 7.0 %collective-permute-start.3 = (f32[16,16,256]{2,1,0:T(8,128)}, f32[16,16,256]{2,1,0:T(8,128)S(1)}, u32[]{:S(2)}, u32[]{:S(2)}) collective-permute-start(f32[16,16,256]{2,1,0:T(8,128)} %get-tuple-element.34), channel_id=1, source_target_pairs={{0,6},{1,7},{2,4},{3,5},{4,2},{5,3},{6,0},{7,1},{8,14},{9,15},{10,... | collective-permute-start | bytes 786440 | tf_op jit(solution)/shard_map/ppermute | solution.py:357
  122.5 6.4 %collective-permute-start.4 = (f32[16,16,256]{2,1,0:T(8,128)}, f32[16,16,256]{2,1,0:T(8,128)S(1)}, u32[]{:S(2)}, u32[]{:S(2)}) collective-permute-start(f32[16,16,256]{2,1,0:T(8,128)} %get-tuple-element.35), channel_id=1, source_target_pairs={{0,2},{1,3},{2,0},{3,1},{4,6},{5,7},{6,4},{7,5},{8,10},{9,11},{10,... | collective-permute-start | bytes 786440 | tf_op jit(solution)/shard_map/ppermute | solution.py:358
  131.8 8.3 %copy-start.18 = (f32[32,16,256]{2,1,0:T(8,128)}, f32[32,16,256]{2,1,0:T(8,128)S(1)}, u32[]{:S(2)}) copy-start(f32[32,16,256]{2,1,0:T(8,128)S(1)} %all-to-all-done.2.arrived_ref) | copy-start | bytes 1572868
  131.8 15.8 %all-to-all-start = ((f32[32,16,256]{2,1,0:T(8,128)}), f32[32,16,256]{2,1,0:T(8,128)S(1)}, u32[]{:S(2)}, u32[]{:S(2)}) async-start(f32[32,16,256]{2,1,0:T(8,128)} %bitcast.32), calls=%async_computation | async-start | bytes 1048576 | tf_op jit(solution)/shard_map/all_to_all | solution.py:360
  147.5 9.6 %copy-start.19 = (f32[32,16,256]{2,1,0:T(8,128)}, f32[32,16,256]{2,1,0:T(8,128)S(1)}, u32[]{:S(2)}) copy-start(f32[32,16,256]{2,1,0:T(8,128)S(1)} %all-to-all-done.arrived_ref) | copy-start | bytes 1572868
  147.5 24.8 %all-to-all-start.3 = ((f32[64,16,256]{2,1,0:T(8,128)}), f32[64,16,256]{2,1,0:T(8,128)}, u32[]{:S(2)}, u32[]{:S(2)}) async-start(f32[64,16,256]{2,1,0:T(8,128)} %place.3), calls=%async_computation.3 | async-start | bytes 2097152 | tf_op jit(solution)/shard_map/all_to_all | solution.py:362
  159.7 17.7 %copy-start.11 = (f32[8,128,256]{2,1,0:T(8,128)S(1)}, f32[8,128,256]{2,1,0:T(8,128)}, u32[]{:S(2)}) copy-start(f32[8,128,256]{2,1,0:T(8,128)} %copy-done.10) | copy-start | bytes 3145732
  159.7 39.1 %collective-permute-start.13 = (f32[512,512]{0,1:T(8,128)}, f32[512,512]{0,1:T(8,128)}, u32[]{:S(2)}, u32[]{:S(2)}) collective-permute-start(f32[512,512]{0,1:T(8,128)} %copy.18), channel_id=1, source_target_pairs={{0,1},{1,0},{2,3},{3,2},{4,5},{5,4},{6,7},{7,6},{8,9},{9,8},{10,11... | collective-permute-start | bytes 3145736 | tf_op jit(solution)/shard_map/ppermute | solution.py:384
  172.3 20.3 %all-to-all-start.1 = ((f32[64,16,256]{2,1,0:T(8,128)}), f32[64,16,256]{2,1,0:T(8,128)}, u32[]{:S(2)}, u32[]{:S(2)}) async-start(f32[64,16,256]{2,1,0:T(8,128)} %place.2), calls=%async_computation.1 | async-start | bytes 2097152 | tf_op jit(solution)/shard_map/all_to_all | solution.py:362
  192.6 6.1 %copy-start.15 = (f32[512,512]{0,1:T(8,128)S(1)}, f32[512,512]{0,1:T(8,128)}, u32[]{:S(2)}) copy-start(f32[512,512]{0,1:T(8,128)} %copy.18) | copy-start | bytes 3145732
  201.5 2.6 %copy-start.16 = (f32[512,512]{0,1:T(8,128)S(1)}, f32[512,512]{0,1:T(8,128)}, u32[]{:S(2)}) copy-start(f32[512,512]{0,1:T(8,128)} %get-tuple-element.55) | copy-start | bytes 3145732
  (13 other events, 15.6 us)
Sparse Core Ops, SparseCore 0:
  96.8 45.1 all-gather.1

commit v3 on v0

v3 whole, which is shorter than its diff:
```python
import functools

import jax
import jax.numpy as jnp
from jax import lax
from jax.experimental import pallas as pl
from jax.experimental.pallas import tpu as pltpu
from jax.sharding import PartitionSpec as P

F32 = jnp.float32
BF16 = jnp.bfloat16
BLOCK = 128
CHUNKS = 2
MAIN = 26
QUARTER = (0, 1, 3, 2)
LIMIT = 24


def split(x):
    high = x.astype(BF16)
    low = (x - high.astype(F32)).astype(BF16)
    return high, low


def whereabouts():
    member = lax.axis_index("local")
    chip = member // 2
    side = chip // 2
    return member % 2, side, (chip + side) % 2


def slot_places(count_ref, places):
    slots = places.shape[0]
    owners = count_ref.shape[1]
    capacity = slots // owners
    group = lax.axis_index("group")

    def owner(o, carry):
        live, dead = carry
        count = count_ref[group, o]
        for j in range(capacity):
            is_live = j < count
            places[o * capacity + j] = jnp.where(is_live, live, slots - 1 - dead)
            live = live + is_live.astype(jnp.int32)
            dead = dead + 1 - is_live.astype(jnp.int32)
        return live, dead

    zero = jnp.int32(0)
    lax.fori_loop(0, owners, owner, (zero, zero))


def tile_kernel(own, blocks, main, over, col_ref, count_ref, *rest):
    if own:
        pre_hbm, weight_hbm, tiles_hbm, recv_ref, local_ref, over_ref, *rest = rest
        keep_a, send_a, keep_b, send_b, pre, weight, tiles, sums, places, column, sems = rest
    else:
        pre_hbm, grad_hbm, weight_hbm, tiles_hbm, pre_ref, local_ref, over_ref, *rest = rest
        send_ref, pre, grad, weight, tiles, sums, places, column, sems = rest
    width = weight.shape[0]
    rows = pre.shape[0] // CHUNKS
    count = tiles.shape[0] // CHUNKS
    core, p, q = whereabouts()
    half = core if own else 1 - core
    some = pl.ds(pl.multiple_of(half * width, width), width)
    weight_copy = pltpu.make_async_copy(weight_hbm.at[some], weight, sems.at[0])
    weight_copy.start()
    if own:
        main_sums = sums.at[pl.ds(blocks, main)]
        recv_copy = pltpu.make_async_copy(recv_ref, main_sums, sems.at[1])
        recv_copy.start()
    chunks = []
    for i in range(CHUNKS):
        at = pl.ds(i * rows, rows)
        copies = [pltpu.make_async_copy(pre_hbm.at[at], pre.at[at], sems.at[2 + 3 * i])]
        if not own:
            copies.append(pltpu.make_async_copy(grad_hbm.at[at], grad.at[at], sems.at[3 + 3 * i]))
        some_tiles = pl.ds(i * count, count)
        copies.append(
            pltpu.make_async_copy(tiles_hbm.at[some_tiles], tiles.at[some_tiles], sems.at[4 + 3 * i])
        )
        for copy in copies:
            copy.start()
        chunks.append(copies)
    sums[0:blocks] = jnp.zeros((blocks,) + sums.shape[1:], F32)
    sums[blocks + main :] = jnp.zeros((over,) + sums.shape[1:], F32)
    if not own:
        sums[blocks : blocks + main] = jnp.zeros((main,) + sums.shape[1:], F32)
    slot_places(count_ref, places)

    def place_tile(t, _):
        col = col_ref[t]
        slot = jnp.maximum(col - blocks, 0)
        column[t] = jnp.where(col < blocks, col, blocks + places[slot])
        return 0

    lax.fori_loop(0, tiles.shape[0], place_tile, 0)
    weight_copy.wait()
    weight_high, weight_low = split(weight[...])
    contract = (((1,), (1,)), ((), ()))
    for i in range(CHUNKS):
        at = pl.ds(i * rows, rows)
        *copies, tiles_copy = chunks[i]
        for copy in copies:
            copy.wait()
        if own:
            pre_grad = pre[at]
        else:
            pre_grad = jnp.where(pre[at] > 0, grad[at], 0.0)
            grad[at] = pre_grad
        pre_high, pre_low = split(pre_grad)
        part = lax.dot_general(weight_high, pre_high, contract, preferred_element_type=F32)
        part += lax.dot_general(weight_high, pre_low, contract, preferred_element_type=F32)
        part += lax.dot_general(weight_low, pre_high, contract, preferred_element_type=F32)
        row_high, row_low = split(part)
        tiles_copy.wait()
        if own and i == 0:
            recv_copy.wait()
        for r in range(rows // BLOCK):
            mine = slice(r * BLOCK, (r + 1) * BLOCK)
            high = row_high[:, mine]
            left = jnp.concatenate([high, high, row_low[:, mine]], axis=1)
            each = count * BLOCK // rows
            for k in range(0, each, 2):
                t = i * count + r * each + k
                first_high, first_low = split(tiles[t])
                next_high, next_low = split(tiles[t + 1])
                high = jnp.concatenate([first_high, next_high], axis=1)
                low = jnp.concatenate([first_low, next_low], axis=1)
                right = jnp.concatenate([high, low, high], axis=0)
                product = jnp.dot(left, right, preferred_element_type=F32)
                sums[column[t]] += product[:, :BLOCK]
                sums[column[t + 1]] += product[:, BLOCK:]

    copies = []

    def out(source, target):
        copy = pltpu.make_async_copy(source, target, sems.at[2 + len(copies)])
        copy.start()
        copies.append(copy)

    if own:
        some = main // 2
        share = width // 4

        def piece(first, p_at, q_at, target):
            share_rows = pl.ds(pl.multiple_of((p_at * 2 + q_at) * share, share), share)
            out(sums.at[pl.ds(blocks + first, some), share_rows], target)

        for k in range(2):
            piece(0, k, 1 - q, send_a.at[k])
            piece(some, 1 - p, k, send_b.at[k])
        for k in range(2):
            piece(0, k, q, keep_a.at[k])
            piece(some, p, k, keep_b.at[k])
    else:
        out(sums.at[pl.ds(blocks, main)], send_ref)
        out(grad, pre_ref)
    out(sums.at[pl.ds(0, blocks)], local_ref)
    out(sums.at[pl.ds(blocks + main, over)], over_ref)
    for copy in copies:
        copy.wait()


def tile_sums(
    tile_col, halo_count, weight, tile_vals, main, over, preact=None, grad_out=None,
    pre_grad=None, recv=None,
):
    own = recv is not None
    node_rows, feat = (pre_grad if own else preact).shape
    width = weight.shape[0] // 2
    blocks = node_rows // BLOCK
    some = main // 2
    anywhere = pl.BlockSpec(memory_space=pl.ANY)
    local = jax.ShapeDtypeStruct((blocks, width, BLOCK), F32)
    over_shape = jax.ShapeDtypeStruct((over, width, BLOCK), F32)
    piece = jax.ShapeDtypeStruct((2, some, width // 4, BLOCK), F32)
    if own:
        args = [pre_grad, weight, tile_vals, recv]
        out_shape = [local, over_shape] + [piece] * 4
    else:
        args = [preact, grad_out, weight, tile_vals]
        out_shape = [
            jax.ShapeDtypeStruct((node_rows, feat), F32),
            local,
            over_shape,
            jax.ShapeDtypeStruct((main, width, BLOCK), F32),
        ]
    scratch = [pltpu.VMEM((node_rows, feat), F32)]
    if not own:
        scratch.append(pltpu.VMEM((node_rows, feat), F32))
    scratch += [
        pltpu.VMEM((width, feat), F32),
        pltpu.VMEM(tile_vals.shape, F32),
        pltpu.VMEM((blocks + main + over, width, BLOCK), F32),
        pltpu.SMEM((main + over,), jnp.int32),
        pltpu.SMEM((tile_vals.shape[0],), jnp.int32),
        pltpu.SemaphoreType.DMA((12,)),
    ]
    return pl.pallas_call(
        functools.partial(tile_kernel, own, blocks, main, over),
        out_shape=out_shape,
        in_specs=[pl.BlockSpec(memory_space=pltpu.SMEM)] * 2 + [anywhere] * len(args),
        out_specs=[anywhere] * len(out_shape),
        scratch_shapes=scratch,
        compiler_params=pltpu.CompilerParams(vmem_limit_bytes=LIMIT * 1024 * 1024),
        cost_estimate=pl.CostEstimate(
            flops=6 * (tile_vals.size + node_rows * feat) * width,
            bytes_accessed=14 * 1024 * 1024,
            transcendentals=0,
        ),
        name="own_tile_sums" if own else "other_tile_sums",
    )(tile_col, halo_count, *args)


IN_VMEM = pl.BlockSpec(memory_space=pltpu.VMEM)
IN_SMEM = pl.BlockSpec(memory_space=pltpu.SMEM)


def second_kernel(keep_a, recv_a, keep_b, recv_b, keep, send_a, send_b):
    _, p, q = whereabouts()
    send_a[...] = keep_a[1 - p] + recv_a[1 - p]
    send_b[...] = keep_b[1 - q] + recv_b[1 - q]
    keep[0] = keep_a[p] + recv_a[p]
    keep[1] = keep_b[q] + recv_b[q]


def second_sums(keep_a, recv_a, keep_b, recv_b):
    send = jax.ShapeDtypeStruct(keep_a.shape[1:], F32)
    return pl.pallas_call(
        second_kernel,
        out_shape=[jax.ShapeDtypeStruct(keep_a.shape, F32), send, send],
        in_specs=[IN_VMEM] * 4,
        out_specs=[IN_VMEM] * 3,
        cost_estimate=pl.CostEstimate(
            flops=2 * keep_a.size, bytes_accessed=24 * keep_a.size, transcendentals=0
        ),
        name="second_sums",
    )(keep_a, recv_a, keep_b, recv_b)


def third_kernel(count_ref, keep, recv_a, recv_b, over, out, total, places):
    half = recv_a.shape[0]
    main = 2 * half
    total[0:half] = keep[0] + recv_a[...]
    total[half:main] = keep[1] + recv_b[...]
    total[main:] = over[...]
    slot_places(count_ref, places)

    @pl.loop(0, out.shape[0])
    def _(slot):
        out[slot] = total[places[slot]]


def third_sums(halo_count, keep, recv_a, recv_b, over):
    slots = 2 * recv_a.shape[0] + over.shape[0]
    shape = (slots,) + recv_a.shape[1:]
    return pl.pallas_call(
        third_kernel,
        out_shape=jax.ShapeDtypeStruct(shape, F32),
        in_specs=[IN_SMEM] + [IN_VMEM] * 4,
        out_specs=IN_VMEM,
        scratch_shapes=[pltpu.VMEM(shape, F32), pltpu.SMEM((slots,), jnp.int32)],
        cost_estimate=pl.CostEstimate(
            flops=keep.size, bytes_accessed=16 * keep.size, transcendentals=0
        ),
        name="third_sums",
    )(halo_count, keep, recv_a, recv_b, over)


def place_kernel(count_ref, target_ref, arrived, out):
    group = lax.axis_index("group")
    sources = count_ref.shape[0]
    capacity = arrived.shape[0] // sources
    out[...] = jnp.zeros_like(out)

    @pl.loop(0, sources)
    def _(source):
        for j in range(capacity):

            @pl.when(j < count_ref[source, group])
            def _():
                out[target_ref[source, group * capacity + j]] += arrived[source * capacity + j]


def place(halo_count, halo_target, arrived, group_blocks):
    return pl.pallas_call(
        place_kernel,
        out_shape=jax.ShapeDtypeStruct((group_blocks,) + arrived.shape[1:], F32),
        in_specs=[IN_SMEM] * 2 + [IN_VMEM],
        out_specs=IN_VMEM,
        cost_estimate=pl.CostEstimate(
            flops=arrived.size, bytes_accessed=12 * arrived.size, transcendentals=0
        ),
        name="place",
    )(halo_count, halo_target, arrived)


def finish_kernel(base, other_local, own_local, received, out, total):
    core, _, _ = whereabouts()
    width = other_local.shape[1]
    share = received.shape[2]
    total[pl.ds(pl.multiple_of(core * width, width), width)] = own_local[0]
    total[pl.ds(pl.multiple_of((1 - core) * width, width), width)] = other_local[0]
    for member in range(received.shape[0]):
        start = (member % 2) * width + QUARTER[member // 2] * share
        total[start : start + share] += received[member, 0]
    out[...] = base[...] + total[...].T


def finish(base, other_local, own_local, received):
    node_rows, feat = base.shape
    blocks, width, _ = other_local.shape
    row_spec = pl.BlockSpec((BLOCK, feat), lambda i: (i, 0))
    local_spec = pl.BlockSpec((1, width, BLOCK), lambda i: (i, 0, 0))
    shape = (received.shape[0], 1) + received.shape[2:]
    return pl.pallas_call(
        finish_kernel,
        out_shape=jax.ShapeDtypeStruct(base.shape, F32),
        grid=(blocks,),
        in_specs=[row_spec, local_spec, local_spec, pl.BlockSpec(shape, lambda i: (0, i, 0, 0))],
        out_specs=row_spec,
        scratch_shapes=[pltpu.VMEM((feat, BLOCK), F32)],
        cost_estimate=pl.CostEstimate(
            flops=2 * base.size, bytes_accessed=16 * base.size, transcendentals=0
        ),
        name="finish",
    )(base, other_local, own_local, received)


def on_device(
    features,
    aggregated,
    preact,
    grad_out,
    w_self,
    w_neigh,
    tile_vals,
    tile_col,
    halo_count,
    halo_target,
):
    high = lax.Precision.HIGH
    node_rows, width = features.shape
    blocks = node_rows // BLOCK
    groups = lax.axis_size("group")
    members = lax.axis_size("local")
    slot_count = halo_target.shape[1]
    over = slot_count - MAIN
    member = lax.axis_index("local")
    swap = [(i, i ^ 1) for i in range(members)]
    pairs = [(i, i ^ 2) for i in range(members)]
    across = [(i, members - 2 - (i - i % 2) + i % 2) for i in range(members)]

    pre_grad, other_local, other_over, send = tile_sums(
        tile_col, halo_count, w_neigh, tile_vals, MAIN, over, preact=preact, grad_out=grad_out
    )
    recv = lax.ppermute(send, "local", swap)
    own_local, own_over, keep_a, send_a, keep_b, send_b = tile_sums(
        tile_col, halo_count, w_neigh, tile_vals, MAIN, over, pre_grad=pre_grad, recv=recv
    )
    recv_a = lax.ppermute(send_a, "local", pairs)
    recv_b = lax.ppermute(send_b, "local", across)
    keep, send_a, send_b = second_sums(keep_a, recv_a, keep_b, recv_b)
    recv_a = lax.ppermute(send_a, "local", across)
    recv_b = lax.ppermute(send_b, "local", pairs)

    def more():
        sums = own_over + lax.ppermute(other_over, "local", swap)
        shares = sums.reshape(over, 4, -1, BLOCK)
        quarters = jnp.array(QUARTER, dtype=jnp.int32)
        chip = member // 2
        total = lax.dynamic_index_in_dim(shares, quarters[chip], 1, keepdims=False)
        for away in range(1, 4):
            theirs = lax.dynamic_index_in_dim(
                shares, quarters[(chip + away) % 4], 1, keepdims=False
            )
            steps = [(i, (i + 2 * away) % members) for i in range(members)]
            total = total + lax.ppermute(theirs, "local", steps)
        return total

    def none():
        return jnp.zeros((over,) + recv_a.shape[1:], F32)

    most = jnp.max(jnp.sum(halo_count, axis=1))
    over_share = lax.cond(most > MAIN, more, none)
    shares = third_sums(halo_count, keep, recv_a, recv_b, over_share)
    arrived = lax.all_to_all(shares, "group", split_axis=0, concat_axis=0, tiled=True)
    placed = place(halo_count, halo_target, arrived, blocks * members)
    received = lax.all_to_all(placed, "local", split_axis=0, concat_axis=0, tiled=True)
    received = received.reshape((members, blocks) + received.shape[1:])

    contract = (((0,), (0,)), ((), ()))
    self_term = lax.dot_general(
        features, pre_grad, contract, precision=high, preferred_element_type=F32
    )
    neigh_term = lax.dot_general(
        aggregated, pre_grad, contract, precision=high, preferred_element_type=F32
    )
    first = member % 2 == 0
    mine = jnp.where(first, self_term, neigh_term) + lax.ppermute(
        jnp.where(first, neigh_term, self_term), "local", swap
    )
    parts = lax.all_to_all(
        mine.reshape(groups, -1, width), "group", split_axis=0, concat_axis=0, tiled=True
    )
    total = jnp.sum(parts, axis=0)
    total = total + lax.ppermute(total, "local", pairs)
    total = total + lax.ppermute(total, "local", across)
    scale = float(node_rows * groups * members) ** (-0.5)
    whole = lax.all_gather(total * scale, "group", tiled=True)
    other = lax.ppermute(whole, "local", swap)
    self_grad = jnp.where(first, whole, other)
    neigh_grad = jnp.where(first, other, whole)

    base = jnp.dot(pre_grad, w_self.T, precision=high, preferred_element_type=F32)
    node_grad = finish(base, other_local, own_local, received)
    return (node_grad, self_grad, neigh_grad)


def solution(mesh):
    in_specs = (
        P(("group", "local"), None),
        P(("group", "local"), None),
        P(("group", "local"), None),
        P(("group", "local"), None),
        P(),
        P(),
        P(("group", "local"), None, None),
        P(("group", "local")),
        P(),
        P(),
    )
    out_specs = (P(("group", "local"), None), P(), P())
    return jax.shard_map(
        on_device, mesh=mesh, in_specs=in_specs, out_specs=out_specs, check_vma=False
    )
```

time: 338 us -> 180 us (0.53)
  waiting for transfers between devices: 206 us -> 43.3 us
  matrix products: 61.3 us -> 10.5 us
  Pallas kernels: 0 us -> 32.9 us
  blocking collectives: 0 us -> 17.9 us
  starting transfers between devices: 14.3 us -> 30.2 us
  local copies, waits for them, and re-layouts: 34.2 us -> 23.5 us
    psum x1 -> x0, waiting for transfers between devices: 137 us -> none  [on_device(): lax.psum((self_term, neigh_term), ('group', 'local'))]
    reduce_scatter x1 -> x0, waiting for transfers between devices: 55.2 us -> none  [on_device(): lax.psum_scatter(halo_terms, 'local', scatter_dimension=1, tiled=True)]
    dot_general x8 -> x3, matrix products: 61.3 us -> 10.5 us  [the longest x1 5.06 us: on_device(): jnp.dot(pre_grad, w_self.T, precision=high, preferred_element_type=F32)]
    pallas_call x0 -> x6, Pallas kernels: none -> 32.9 us  [the longest x2 16.5 us: tile_sums(): pl.pallas_call(functools.partial(tile_kernel, own, blocks, main, over), o...]
    ppermute x0 -> x9, waiting for transfers between devices: none -> 29.2 us  [the longest x1 17.1 us: on_device(): total = total + lax.ppermute(total, 'local', pairs)]
    all_to_all x0 -> x1, blocking collectives: none -> 17.9 us  [on_device(): lax.all_to_all(shares, 'group', split_axis=0, concat_axis=0, tiled=True)]
    reshape x1 -> x0, local copies, waits for them, and re-layouts: 17.5 us -> none  [on_device(): contrib = jnp.einsum('rkab,raf->rkbf', tile_blocks, neigh_rows.reshape(bl...]
    unnamed x24 -> x46, local copies, waits for them, and re-layouts: 4.82 us -> 21.9 us
  transfers between devices with their start and end apart: 4 -> 12, of which waited for: 3 -> 6; matrix products, arithmetic and copies ran while one was open for 9% -> 12% of each run, Pallas kernels for 0% -> 9%
where the time goes in v3:
time: 180 us; the launch traced here: 179 us
  waiting for transfers between devices  43.3 us (24%)
  Pallas kernels  32.9 us (18%)
  starting transfers between devices  30.2 us (17%)
  local copies, waits for them, and re-layouts  23.5 us (13%)
  blocking collectives  17.9 us (10%)
  between operations  14.9 us (8%)
  matrix products  10.5 us (6%)
  other arithmetic  5.79 us (3%)
    unnamed x46, local copies, waits for them, and re-layouts  21.9 us
    all_to_all x1, blocking collectives, on_device(): lax.all_to_all(shares, 'group', split_axis=0, concat_axis=0, tiled=True)  17.9 us
    ppermute x1, waiting for transfers between devices, on_device(): total = total + lax.ppermute(total, 'local', pairs)  17.1 us
    pallas_call x2, Pallas kernels, tile_sums(): pl.pallas_call(functools.partial(tile_kernel, own, blocks, main, over), o...  16.5 us
    all_to_all x1, waiting for transfers between devices, on_device(): lax.all_to_all(placed, 'local', split_axis=0, concat_axis=0, tiled=True)  14.1 us
    all_to_all x1, starting transfers between devices, on_device(): lax.all_to_all(placed, 'local', split_axis=0, concat_axis=0, tiled=True)  11.7 us
    all_to_all x1, starting transfers between devices, on_device(): lax.all_to_all(mine.reshape(groups, -1, width), 'group', split_axis=0, co...  8.04 us
    pallas_call x1, Pallas kernels, finish(): pl.pallas_call(finish_kernel, out_shape=jax.ShapeDtypeStruct(base.shape,...  7.03 us
  transfers between devices with their start and end apart: 12, of which 6 were waited for; matrix products, arithmetic and copies ran while one was open for 12% of the time, Pallas kernels for 9%

profile of v3, /device:TPU:1, one launch (start us, length us, event | category | flops | bytes accessed | tf_op | source)
XLA Modules:
  0.0 179.0 jit_solution(9888141728407359236)
XLA Ops:
  7.2 2.3 %copy-done.4 = f32[64,128,128]{2,1,0:T(8,128)S(1)} copy-done((f32[64,128,128]{2,1,0:T(8,128)S(1)}, f32[64,128,128]{2,1,0:T(8,128)}, u32[]{:S(2)}) %copy-start.4) | copy-done | bytes 4194328
  10.7 1.6 copy-done.8
  12.3 1.6 copy-done.9
  15.3 8.8 %other_tile_sums.1 = (f32[1024,512]{1,0:T(8,128)S(1)}, f32[8,256,128]{2,1,0:T(8,128)S(1)}, f32[6,256,128]{2,1,0:T(8,128)}, f32[26,256,128]{2,1,0:T(8,128)}) custom-call(s32[64]{0:T(128)S(1)} %copy-done.16, s32[16,16]{1,0:T(8,128)S(1)} %copy-done.14, f32[1024,512]{1,0:T(8,128)S(1)} %copy-done.8, f32[1024,512]{1,0:T(8,128)S(1)} %copy-done.9, ...), custom_call_target="tpu_custom_call" | custom-call | flops 2415919104 | bytes 14680064 | tf_op jit(solution)/shard_map/other_tile_sums/pallas_call | solution.py:199
  24.1 1.3 copy-done.1
  26.5 1.4 collective-permute-start.4
  27.9 3.6 %fusion.5 = f32[512,512]{0,1:T(8,128)S(1)} fusion(f32[1024,512]{1,0:T(8,128)} %copy-done.1, f32[1024,512]{1,0:T(8,128)S(1)} %copy-done), kind=kOutput, calls=%fused_computation.14 | convolution fusion | flops 1610612736 | bytes 5242880 | tf_op jit(solution)/shard_map/dot_general | solution.py:396
  31.5 1.9 %fusion.4 = f32[512,512]{0,1:T(8,128)S(1)} fusion(f32[1024,512]{1,0:T(8,128)S(1)} %copy-done.2, f32[1024,512]{1,0:T(8,128)S(1)} %copy-done.19), kind=kOutput, calls=%fused_computation.13 | convolution fusion | flops 1610612736 | bytes 5242880 | tf_op jit(solution)/shard_map/dot_general | solution.py:393
  33.7 2.6 %collective-permute-done.9 = f32[512,512]{1,0:T(8,128)S(1)} collective-permute-done((f32[512,512]{1,0:T(8,128)S(1)}, f32[512,512]{1,0:T(8,128)S(1)}, u32[]{:S(2)}, u32[]{:S(2)}) %collective-permute-start.9) | collective-permute-done | bytes 1048608 | tf_op jit(solution)/shard_map/ppermute | solution.py:400
  36.3 1.3 bitcast_add_fusion.1
  37.7 8.0 %all-to-all-start.2 = ((f32[16,32,512]{2,1,0:T(8,128)}), f32[16,32,512]{2,1,0:T(8,128)}, u32[]{:S(2)}, u32[]{:S(2)}) async-start(f32[16,32,512]{2,1,0:T(8,128)} %bitcast.37), calls=%async_computation.2 | async-start | bytes 2097152 | tf_op jit(solution)/shard_map/all_to_all | solution.py:403
  46.0 1.6 copy-done.3
  47.6 2.2 %copy-done.5 = f32[64,128,128]{2,1,0:T(8,128)S(1)} copy-done((f32[64,128,128]{2,1,0:T(8,128)S(1)}, f32[64,128,128]{2,1,0:T(8,128)}, u32[]{:S(2)}) %copy-start.5) | copy-done | bytes 4194328
  49.8 7.6 %own_tile_sums.1 = (f32[8,256,128]{2,1,0:T(8,128)S(1)}, f32[6,256,128]{2,1,0:T(8,128)}, f32[2,13,64,128]{3,2,1,0:T(8,128)S(1)}, f32[2,13,64,128]{3,2,1,0:T(8,128...) custom-call(s32[64]{0:T(128)S(1)} %copy-done.17, s32[16,16]{1,0:T(8,128)S(1)} %copy-done.15, ...), custom_call_target="tpu_custom_call" | custom-call | flops 2415919104 | bytes 14680064 | tf_op jit(solution)/shard_map/own_tile_sums/pallas_call | solution.py:199
  61.5 1.8 %collective-permute-start.6 = (f32[2,13,64,128]{3,2,1,0:T(8,128)}, f32[2,13,64,128]{3,2,1,0:T(8,128)}, u32[]{:S(2)}, u32[]{:S(2)}) collective-permute-start(f32[2,13,64,128]{3,2,1,0:T(8,128)} %get-tuple-element.38), channel_id=1, source_target_pairs={{0,6},{1,7},{2,4},{3,5},{4,2},{5,3},{6,0},{7,1},{8,14},{9,15},{10,... | collective-permute-start | bytes 2555912 | tf_op jit(solution)/shard_map/ppermute | solution.py:362
  65.0 17.1 %collective-permute-done.10 = f32[32,512]{1,0:T(8,128)S(1)} collective-permute-done((f32[32,512]{1,0:T(8,128)S(1)}, f32[32,512]{1,0:T(8,128)S(1)}, u32[]{:S(2)}, u32[]{:S(2)}) %collective-permute-start.10) | collective-permute-done | bytes 65568 | tf_op jit(solution)/shard_map/ppermute | solution.py:407
  82.1 2.6 %collective-permute-start.11 = (f32[32,512]{1,0:T(8,128)S(1)}, f32[32,512]{1,0:T(8,128)S(1)}, u32[]{:S(2)}, u32[]{:S(2)}) collective-permute-start(f32[32,512]{1,0:T(8,128)S(1)} %add.71), channel_id=1, source_target_pairs={{0,6},{1,7},{2,4},{3,5},{4,2},{5,3},{6,0},{7,1},{8,14},{9,15},{10,... | collective-permute-start | bytes 196616 | tf_op jit(solution)/shard_map/ppermute | solution.py:408
  84.7 1.8 %collective-permute-done.11 = f32[32,512]{1,0:T(8,128)S(1)} collective-permute-done((f32[32,512]{1,0:T(8,128)S(1)}, f32[32,512]{1,0:T(8,128)S(1)}, u32[]{:S(2)}, u32[]{:S(2)}) %collective-permute-start.11) | collective-permute-done | bytes 65568 | tf_op jit(solution)/shard_map/ppermute | solution.py:408
  88.1 3.3 %second_sums.1 = (f32[2,13,64,128]{3,2,1,0:T(8,128)}, f32[13,64,128]{2,1,0:T(8,128)}, f32[13,64,128]{2,1,0:T(8,128)}) custom-call(f32[2,13,64,128]{3,2,1,0:T(8,128)} %copy-done.12, f32[2,13,64,128]{3,2,1,0:T(8,128)} %copy-done.20, f32[2,13,64,128]{3,2,1,0:T(8,128)} %copy-done.13, f32[2,13,64,128]{3,2,1,0:T(8,128)} %collective-permute-done.6.recv_b), custom_call_target="tpu_custom_call" | custom-call | flops 425984 | bytes 5111808 | tf_op jit(solution)/shard_map/second_sums/pallas_call | solution.py:229
  91.4 2.5 %collective-permute-start.7 = (f32[13,64,128]{2,1,0:T(8,128)}, f32[13,64,128]{2,1,0:T(8,128)S(1)}, u32[]{:S(2)}, u32[]{:S(2)}) collective-permute-start(f32[13,64,128]{2,1,0:T(8,128)} %get-tuple-element.40), channel_id=1, source_target_pairs={{0,6},{1,7},{2,4},{3,5},{4,2},{5,3},{6,0},{7,1},{8,14},{9,15},{10,... | collective-permute-start | bytes 1277960 | tf_op jit(solution)/shard_map/ppermute | solution.py:364
  95.3 6.5 %collective-permute-done.7.recv_a = f32[13,64,128]{2,1,0:T(8,128)S(1)} collective-permute-done((f32[13,64,128]{2,1,0:T(8,128)}, f32[13,64,128]{2,1,0:T(8,128)S(1)}, u32[]{:S(2)}, u32[]{:S(2)}) %collective-permute-start.7) | collective-permute-done | bytes 426016 | tf_op jit(solution)/shard_map/ppermute | solution.py:364
  102.9 2.9 %third_sums.1 = f32[32,64,128]{2,1,0:T(8,128)} custom-call(s32[16,16]{1,0:T(8,128)} %count_ref.7, f32[2,13,64,128]{3,2,1,0:T(8,128)} %get-tuple-element.39.keep, f32[13,64,128]{2,1,0:T(8,128)} %copy-done.22, f32[13,64,128]{2,1,0:T(8,128)} %collective-permute-done.8.recv_b, f32[6,64,128]{2,1,0:T(8,128)S(1)} %get-tuple-element.61.over), custom_call_target="tpu_custom_call" | custom-call | flops 212992 | bytes 3407872 | tf_op jit(solution)/shard_map/third_sums/pallas_call | solution.py:257
  105.8 17.9 %all_to_all.15.arrived = f32[32,64,128]{2,1,0:T(8,128)} all-to-all(f32[32,64,128]{2,1,0:T(8,128)} %third_sums.1), channel_id=1, replica_groups=mesh['group'=16,'local'=8] {'group'}, dimensions={0} | all-to-all | bytes 2097152 | tf_op jit(solution)/shard_map/all_to_all | solution.py:387
  123.7 3.2 %place.1 = f32[64,64,128]{2,1,0:T(8,128)} custom-call(s32[16,16]{1,0:T(8,128)} %count_ref.7, s32[16,32]{1,0:T(8,128)} %target_ref.1, f32[32,64,128]{2,1,0:T(8,128)} %all_to_all.15.arrived), custom_call_target="tpu_custom_call" | custom-call | flops 262144 | bytes 3145728 | tf_op jit(solution)/shard_map/place/pallas_call | solution.py:286
  126.9 11.7 %all-to-all-start.1 = ((f32[64,64,128]{2,1,0:T(8,128)}), f32[64,64,128]{2,1,0:T(8,128)}, u32[]{:S(2)}, u32[]{:S(2)}) async-start(f32[64,64,128]{2,1,0:T(8,128)} %place.1), calls=%async_computation.1 | async-start | bytes 4194304 | tf_op jit(solution)/shard_map/all_to_all | solution.py:389
  138.6 1.6 copy.26
  140.4 5.1 %fusion.3.base = f32[1024,512]{1,0:T(8,128)} fusion(f32[1024,512]{1,0:T(8,128)} %copy-done.1, f32[512,512]{1,0:T(8,128)} %param.17), kind=kOutput, calls=%fused_computation.12 | convolution fusion | flops 1610612736 | bytes 5242880 | tf_op jit(solution)/shard_map/dot_general | solution.py:415
  145.5 1.6 broadcast_select_fusion
  147.0 2.6 %copy.28 = f32[512,512]{1,0:T(8,128)} copy(f32[512,512]{0,1:T(8,128)} %get-tuple-element.60) | data formatting | bytes 2097152
  149.7 1.3 copy.29
  151.0 14.1 %all-to-all-done.1 = f32[64,64,128]{2,1,0:T(8,128)} async-done(((f32[64,64,128]{2,1,0:T(8,128)}), f32[64,64,128]{2,1,0:T(8,128)}, u32[]{:S(2)}, u32[]{:S(2)}) %all-to-all-start.1) | async-done | bytes 2097184 | tf_op jit(solution)/shard_map/all_to_all | solution.py:389
  165.1 7.0 %finish.1 = f32[1024,512]{1,0:T(8,128)} custom-call(f32[1024,512]{1,0:T(8,128)} %fusion.3.base, f32[8,256,128]{2,1,0:T(8,128)} %copy-done.10, f32[8,256,128]{2,1,0:T(8,128)} %copy-done.11, f32[8,8,64,128]{3,2,1,0:T(8,128)} %bitcast.9.received), custom_call_target="tpu_custom_call" | custom-call | flops 1048576 | bytes 8388608 | tf_op jit(solution)/shard_map/finish/pallas_call | solution.py:316
  (60 shorter events, 13.7 us)
Async XLA Ops:
  7.2 20.7 %copy-start = (f32[1024,512]{1,0:T(8,128)S(1)}, f32[1024,512]{1,0:T(8,128)}, u32[]{:S(2)}) copy-start(f32[1024,512]{1,0:T(8,128)} %param.14) | copy-start | bytes 6291460
  7.2 2.3 %copy-start.4 = (f32[64,128,128]{2,1,0:T(8,128)S(1)}, f32[64,128,128]{2,1,0:T(8,128)}, u32[]{:S(2)}) copy-start(f32[64,128,128]{2,1,0:T(8,128)} %rest_2_.3) | copy-start | bytes 12582916
  9.5 1.2 copy-start.6
  10.7 1.6 copy-start.8
  12.3 1.6 copy-start.9
  24.1 1.3 copy-start.1
  25.4 1.0 copy-start.10
  26.5 19.5 %collective-permute-start.4 = (f32[26,256,128]{2,1,0:T(8,128)}, f32[26,256,128]{2,1,0:T(8,128)}, u32[]{:S(2)}, u32[]{:S(2)}) collective-permute-start(f32[26,256,128]{2,1,0:T(8,128)} %get-tuple-element.33), channel_id=1, source_target_pairs={{0,1},{1,0},{2,3},{3,2},{4,5},{5,4},{6,7},{7,6},{8,9},{9,8},{10,11... | collective-permute-start | bytes 10223624 | tf_op jit(solution)/shard_map/ppermute | solution.py:357
  27.9 3.6 %copy-start.2 = (f32[1024,512]{1,0:T(8,128)S(1)}, f32[1024,512]{1,0:T(8,128)}, u32[]{:S(2)}) copy-start(f32[1024,512]{1,0:T(8,128)} %copy-done.1) | copy-start | bytes 6291460
  27.9 3.6 %copy-start.19 = (f32[1024,512]{1,0:T(8,128)S(1)}, f32[1024,512]{1,0:T(8,128)}, u32[]{:S(2)}) copy-start(f32[1024,512]{1,0:T(8,128)} %param.13) | copy-start | bytes 6291460
  33.6 2.7 %collective-permute-start.9 = (f32[512,512]{1,0:T(8,128)S(1)}, f32[512,512]{1,0:T(8,128)S(1)}, u32[]{:S(2)}, u32[]{:S(2)}) collective-permute-start(f32[512,512]{1,0:T(8,128)S(1)} %select_bitcast_fusion), channel_id=1, source_target_pairs={{0,1},{1,0},{2,3},{3,2},{4,5},{5,4},{6,7},{7,6},{8,9},{9,8},{10,11... | collective-permute-start | bytes 3145736 | tf_op jit(solution)/shard_map/ppermute | solution.py:400
  37.7 8.3 %copy-start.7 = (f32[512,512]{1,0:T(8,128)S(1)}, f32[512,512]{1,0:T(8,128)}, u32[]{:S(2)}) copy-start(f32[512,512]{1,0:T(8,128)} %rest_1_.3) | copy-start | bytes 3145732
  37.7 8.3 %copy-start.15 = (s32[16,16]{1,0:T(8,128)S(1)}, s32[16,16]{1,0:T(8,128)}, u32[]{:S(2)}) copy-start(s32[16,16]{1,0:T(8,128)} %count_ref.7) | copy-start | bytes 3076
  37.7 8.3 %copy-start.17 = (s32[64]{0:T(128)S(1)}, s32[64]{0:T(128)}, u32[]{:S(2)}) copy-start(s32[64]{0:T(128)} %col_ref.3) | copy-start | bytes 772
  37.7 25.7 %all-to-all-start.2 = ((f32[16,32,512]{2,1,0:T(8,128)}), f32[16,32,512]{2,1,0:T(8,128)}, u32[]{:S(2)}, u32[]{:S(2)}) async-start(f32[16,32,512]{2,1,0:T(8,128)} %bitcast.37), calls=%async_computation.2 | async-start | bytes 2097152 | tf_op jit(solution)/shard_map/all_to_all | solution.py:403
  45.7 92.9 %all-gather.2.cloned.1.call-start = ((), (), s32[]{:S(2)}) async-start(), calls=%async_computation.3 | async-start | bytes 1114112 | tf_op jit(solution)/shard_map/all_gather | solution.py:410
  46.0 1.6 copy-start.3
  47.6 2.2 %copy-start.5 = (f32[64,128,128]{2,1,0:T(8,128)S(1)}, f32[64,128,128]{2,1,0:T(8,128)}, u32[]{:S(2)}) copy-start(f32[64,128,128]{2,1,0:T(8,128)} %rest_2_.3) | copy-start | bytes 12582916
  57.4 1.1 copy-start.11
  58.5 0.9 copy-start.12
  59.4 0.9 copy-start.13
  60.3 26.9 %collective-permute-start.5 = (f32[2,13,64,128]{3,2,1,0:T(8,128)}, f32[2,13,64,128]{3,2,1,0:T(8,128)S(1)}, u32[]{:S(2)}, u32[]{:S(2)}) collective-permute-start(f32[2,13,64,128]{3,2,1,0:T(8,128)} %get-tuple-element.36), channel_id=1, source_target_pairs={{0,2},{1,3},{2,0},{3,1},{4,6},{5,7},{6,4},{7,5},{8,10},{9,11},{10,... | collective-permute-start | bytes 2555912 | tf_op jit(solution)/shard_map/ppermute | solution.py:361
  61.5 25.7 %collective-permute-start.6 = (f32[2,13,64,128]{3,2,1,0:T(8,128)}, f32[2,13,64,128]{3,2,1,0:T(8,128)}, u32[]{:S(2)}, u32[]{:S(2)}) collective-permute-start(f32[2,13,64,128]{3,2,1,0:T(8,128)} %get-tuple-element.38), channel_id=1, source_target_pairs={{0,6},{1,7},{2,4},{3,5},{4,2},{5,3},{6,0},{7,1},{8,14},{9,15},{10,... | collective-permute-start | bytes 2555912 | tf_op jit(solution)/shard_map/ppermute | solution.py:362
  64.6 17.5 %collective-permute-start.10 = (f32[32,512]{1,0:T(8,128)S(1)}, f32[32,512]{1,0:T(8,128)S(1)}, u32[]{:S(2)}, u32[]{:S(2)}) collective-permute-start(f32[32,512]{1,0:T(8,128)S(1)} %reduce_sum.19), channel_id=1, source_target_pairs={{0,2},{1,3},{2,0},{3,1},{4,6},{5,7},{6,4},{7,5},{8,10},{9,11},{10,... | collective-permute-start | bytes 196616 | tf_op jit(solution)/shard_map/ppermute | solution.py:407
  82.1 4.4 %collective-permute-start.11 = (f32[32,512]{1,0:T(8,128)S(1)}, f32[32,512]{1,0:T(8,128)S(1)}, u32[]{:S(2)}, u32[]{:S(2)}) collective-permute-start(f32[32,512]{1,0:T(8,128)S(1)} %add.71), channel_id=1, source_target_pairs={{0,6},{1,7},{2,4},{3,5},{4,2},{5,3},{6,0},{7,1},{8,14},{9,15},{10,... | collective-permute-start | bytes 196616 | tf_op jit(solution)/shard_map/ppermute | solution.py:408
  87.2 0.9 copy-start.20
  91.4 10.4 %collective-permute-start.7 = (f32[13,64,128]{2,1,0:T(8,128)}, f32[13,64,128]{2,1,0:T(8,128)S(1)}, u32[]{:S(2)}, u32[]{:S(2)}) collective-permute-start(f32[13,64,128]{2,1,0:T(8,128)} %get-tuple-element.40), channel_id=1, source_target_pairs={{0,6},{1,7},{2,4},{3,5},{4,2},{5,3},{6,0},{7,1},{8,14},{9,15},{10,... | collective-permute-start | bytes 1277960 | tf_op jit(solution)/shard_map/ppermute | solution.py:364
  93.9 9.0 %collective-permute-start.8 = (f32[13,64,128]{2,1,0:T(8,128)}, f32[13,64,128]{2,1,0:T(8,128)}, u32[]{:S(2)}, u32[]{:S(2)}) collective-permute-start(f32[13,64,128]{2,1,0:T(8,128)} %get-tuple-element.41), channel_id=1, source_target_pairs={{0,2},{1,3},{2,0},{3,1},{4,6},{5,7},{6,4},{7,5},{8,10},{9,11},{10,... | collective-permute-start | bytes 1277960 | tf_op jit(solution)/shard_map/ppermute | solution.py:365
  101.8 1.1 copy-start.22
  126.9 38.2 %all-to-all-start.1 = ((f32[64,64,128]{2,1,0:T(8,128)}), f32[64,64,128]{2,1,0:T(8,128)}, u32[]{:S(2)}, u32[]{:S(2)}) async-start(f32[64,64,128]{2,1,0:T(8,128)} %place.1), calls=%async_computation.1 | async-start | bytes 4194304 | tf_op jit(solution)/shard_map/all_to_all | solution.py:389
  140.2 5.3 %collective-permute-start.12 = (f32[512,512]{0,1:T(8,128)S(1)}, f32[512,512]{0,1:T(8,128)S(1)}, u32[]{:S(2)}, u32[]{:S(2)}) collective-permute-start(f32[512,512]{0,1:T(8,128)S(1)} %copy.26), channel_id=1, source_target_pairs={{0,1},{1,0},{2,3},{3,2},{4,5},{5,4},{6,7},{7,6},{8,9},{9,8},{10,11... | collective-permute-start | bytes 3145736 | tf_op jit(solution)/shard_map/ppermute | solution.py:411
  147.0 2.6 %copy-start.18 = (f32[512,512]{0,1:T(8,128)S(1)}, f32[512,512]{0,1:T(8,128)}, u32[]{:S(2)}) copy-start(f32[512,512]{0,1:T(8,128)} %get-tuple-element.59) | copy-start | bytes 3145732
  (2 other events, 1.4 us)
Sparse Core Ops, SparseCore 0:
  87.3 47.0 all-gather.1

commit v4 on v3

--- a/solution.py
+++ b/solution.py
@@ -13,13 +13,19 @@
 CHUNKS = 2
 MAIN = 26
 QUARTER = (0, 1, 3, 2)
-LIMIT = 24
+LIMIT_OTHER = 55
+LIMIT_OWN = 20
+LIMIT_SMALL = 6
 
 
 def split(x):
     high = x.astype(BF16)
     low = (x - high.astype(F32)).astype(BF16)
     return high, low
+
+
+def limit(mebibytes):
+    return pltpu.CompilerParams(vmem_limit_bytes=mebibytes * 1024 * 1024)
 
 
 def whereabouts():
@@ -51,7 +57,7 @@
 
 def tile_kernel(own, blocks, main, over, col_ref, count_ref, *rest):
     if own:
-        pre_hbm, weight_hbm, tiles_hbm, recv_ref, local_ref, over_ref, *rest = rest
+        pre_hbm, weight_hbm, tiles_hbm, recv_ref, local_ref, over_ref, flag_ref, *rest = rest
         keep_a, send_a, keep_b, send_b, pre, weight, tiles, sums, places, column, sems = rest
     else:
         pre_hbm, grad_hbm, weight_hbm, tiles_hbm, pre_ref, local_ref, over_ref, *rest = rest
@@ -65,6 +71,7 @@
     weight_copy = pltpu.make_async_copy(weight_hbm.at[some], weight, sems.at[0])
     weight_copy.start()
     if own:
+        flag_ref[0] = core
         main_sums = sums.at[pl.ds(blocks, main)]
         recv_copy = pltpu.make_async_copy(recv_ref, main_sums, sems.at[1])
         recv_copy.start()
@@ -97,6 +104,7 @@
     weight_copy.wait()
     weight_high, weight_low = split(weight[...])
     contract = (((1,), (1,)), ((), ()))
+    pre_copies = []
     for i in range(CHUNKS):
         at = pl.ds(i * rows, rows)
         *copies, tiles_copy = chunks[i]
@@ -107,6 +115,9 @@
         else:
             pre_grad = jnp.where(pre[at] > 0, grad[at], 0.0)
             grad[at] = pre_grad
+            pre_copy = pltpu.make_async_copy(grad.at[at], pre_ref.at[at], sems.at[2 + 3 * i])
+            pre_copy.start()
+            pre_copies.append(pre_copy)
         pre_high, pre_low = split(pre_grad)
         part = lax.dot_general(weight_high, pre_high, contract, preferred_element_type=F32)
         part += lax.dot_general(weight_high, pre_low, contract, preferred_element_type=F32)
@@ -134,7 +145,7 @@
     copies = []
 
     def out(source, target):
-        copy = pltpu.make_async_copy(source, target, sems.at[2 + len(copies)])
+        copy = pltpu.make_async_copy(source, target, sems.at[2 + 3 * CHUNKS + len(copies)])
         copy.start()
         copies.append(copy)
 
@@ -154,10 +165,9 @@
             piece(some, p, k, keep_b.at[k])
     else:
         out(sums.at[pl.ds(blocks, main)], send_ref)
-        out(grad, pre_ref)
     out(sums.at[pl.ds(0, blocks)], local_ref)
     out(sums.at[pl.ds(blocks + main, over)], over_ref)
-    for copy in copies:
+    for copy in pre_copies + copies:
         copy.wait()
 
 
@@ -176,7 +186,8 @@
     piece = jax.ShapeDtypeStruct((2, some, width // 4, BLOCK), F32)
     if own:
         args = [pre_grad, weight, tile_vals, recv]
-        out_shape = [local, over_shape] + [piece] * 4
+        flag = jax.ShapeDtypeStruct((1,), jnp.int32)
+        out_shape = [local, over_shape, flag] + [piece] * 4
     else:
         args = [preact, grad_out, weight, tile_vals]
         out_shape = [
@@ -194,15 +205,18 @@
         pltpu.VMEM((blocks + main + over, width, BLOCK), F32),
         pltpu.SMEM((main + over,), jnp.int32),
         pltpu.SMEM((tile_vals.shape[0],), jnp.int32),
-        pltpu.SemaphoreType.DMA((12,)),
+        pltpu.SemaphoreType.DMA((2 + 3 * CHUNKS + 10,)),
     ]
     return pl.pallas_call(
         functools.partial(tile_kernel, own, blocks, main, over),
         out_shape=out_shape,
         in_specs=[pl.BlockSpec(memory_space=pltpu.SMEM)] * 2 + [anywhere] * len(args),
-        out_specs=[anywhere] * len(out_shape),
+        out_specs=[
+            pl.BlockSpec(memory_space=pltpu.SMEM) if x.dtype == jnp.int32 else anywhere
+            for x in out_shape
+        ],
         scratch_shapes=scratch,
-        compiler_params=pltpu.CompilerParams(vmem_limit_bytes=LIMIT * 1024 * 1024),
+        compiler_params=limit(LIMIT_OWN if own else LIMIT_OTHER),
         cost_estimate=pl.CostEstimate(
             flops=6 * (tile_vals.size + node_rows * feat) * width,
             bytes_accessed=14 * 1024 * 1024,
@@ -234,6 +248,7 @@
         cost_estimate=pl.CostEstimate(
             flops=2 * keep_a.size, bytes_accessed=24 * keep_a.size, transcendentals=0
         ),
+        compiler_params=limit(LIMIT_SMALL),
         name="second_sums",
     )(keep_a, recv_a, keep_b, recv_b)
 
@@ -263,8 +278,31 @@
         cost_estimate=pl.CostEstimate(
             flops=keep.size, bytes_accessed=16 * keep.size, transcendentals=0
         ),
+        compiler_params=limit(LIMIT_SMALL),
         name="third_sums",
     )(halo_count, keep, recv_a, recv_b, over)
+
+
+def part_kernel(parts, after, out):
+    del after
+    total = parts[0]
+    for k in range(1, parts.shape[0]):
+        total += parts[k]
+    out[...] = total
+
+
+def part_sum(parts, after):
+    return pl.pallas_call(
+        part_kernel,
+        out_shape=jax.ShapeDtypeStruct(parts.shape[1:], F32),
+        in_specs=[IN_VMEM, pl.BlockSpec(memory_space=pl.ANY)],
+        out_specs=IN_VMEM,
+        cost_estimate=pl.CostEstimate(
+            flops=parts.size, bytes_accessed=4 * parts.size, transcendentals=0
+        ),
+        compiler_params=limit(LIMIT_SMALL),
+        name="part_sum",
+    )(parts, after)
 
 
 def place_kernel(count_ref, target_ref, arrived, out):
@@ -291,6 +329,7 @@
         cost_estimate=pl.CostEstimate(
             flops=arrived.size, bytes_accessed=12 * arrived.size, transcendentals=0
         ),
+        compiler_params=limit(LIMIT_SMALL),
         name="place",
     )(halo_count, halo_target, arrived)
 
@@ -323,6 +362,7 @@
         cost_estimate=pl.CostEstimate(
             flops=2 * base.size, bytes_accessed=16 * base.size, transcendentals=0
         ),
+        compiler_params=limit(LIMIT_SMALL),
         name="finish",
     )(base, other_local, own_local, received)
 
@@ -355,7 +395,7 @@
         tile_col, halo_count, w_neigh, tile_vals, MAIN, over, preact=preact, grad_out=grad_out
     )
     recv = lax.ppermute(send, "local", swap)
-    own_local, own_over, keep_a, send_a, keep_b, send_b = tile_sums(
+    own_local, own_over, flag, keep_a, send_a, keep_b, send_b = tile_sums(
         tile_col, halo_count, w_neigh, tile_vals, MAIN, over, pre_grad=pre_grad, recv=recv
     )
     recv_a = lax.ppermute(send_a, "local", pairs)
@@ -396,14 +436,14 @@
     neigh_term = lax.dot_general(
         aggregated, pre_grad, contract, precision=high, preferred_element_type=F32
     )
-    first = member % 2 == 0
+    first = flag[0] == 0
     mine = jnp.where(first, self_term, neigh_term) + lax.ppermute(
         jnp.where(first, neigh_term, self_term), "local", swap
     )
     parts = lax.all_to_all(
         mine.reshape(groups, -1, width), "group", split_axis=0, concat_axis=0, tiled=True
     )
-    total = jnp.sum(parts, axis=0)
+    total = part_sum(parts, send_a)
     total = total + lax.ppermute(total, "local", pairs)
     total = total + lax.ppermute(total, "local", across)
     scale = float(node_rows * groups * members) ** (-0.5)

time: 180 us -> 174 us (0.967)
  waiting for transfers between devices: 43.3 us -> 52.2 us
  local copies, waits for them, and re-layouts: 23.5 us -> 16.8 us
  Pallas kernels: 32.9 us -> 27.3 us
  starting transfers between devices: 30.2 us -> 26.6 us
  blocking collectives: 17.9 us -> 19.8 us
    ppermute x1, waiting for transfers between devices: 0.01 us -> 17.2 us  [on_device(): recv_a = lax.ppermute(send_a, 'local', pairs)]
    ppermute x1, waiting for transfers between devices: 17.1 us -> 3.1 us  [on_device(): total = total + lax.ppermute(total, 'local', pairs)]
    all_gather x1, waiting for transfers between devices: 0.01 us -> 8.91 us  [on_device(): whole = lax.all_gather(total * scale, 'group', tiled=True)]
    unnamed x46 -> x50, local copies, waits for them, and re-layouts: 21.9 us -> 14.8 us
    all_to_all x1, waiting for transfers between devices: 14.1 us -> 10.7 us  [on_device(): lax.all_to_all(placed, 'local', split_axis=0, concat_axis=0, tiled=True)]
    pallas_call x1, Pallas kernels: 3.28 us -> 0.17 us  [second_sums(): pl.pallas_call(second_kernel, out_shape=[jax.ShapeDtypeStruct(keep_a.shap...]
    all_to_all x1, starting transfers between devices: 11.7 us -> 9.05 us  [on_device(): lax.all_to_all(placed, 'local', split_axis=0, concat_axis=0, tiled=True)]
    ppermute x1, waiting for transfers between devices: 0.01 us -> 2.1 us  [on_device(): recv_b = lax.ppermute(send_b, 'local', across)]
  transfers between devices with their start and end apart: 12 -> 12, of which waited for: 6 -> 9; matrix products, arithmetic and copies ran while one was open for 12% -> 7% of each run, Pallas kernels for 9% -> 5%
where the time goes in v4:
time: 174 us
  waiting for transfers between devices  52.2 us (30%)
  Pallas kernels  27.3 us (16%)
  starting transfers between devices  26.6 us (15%)
  blocking collectives  19.8 us (11%)
  local copies, waits for them, and re-layouts  16.8 us (10%)
  between operations  15.5 us (9%)
  matrix products  10.5 us (6%)
  other arithmetic  4.87 us (3%)
    all_to_all x1, blocking collectives, on_device(): lax.all_to_all(shares, 'group', split_axis=0, concat_axis=0, tiled=True)  19.8 us
    pallas_call x2, Pallas kernels, tile_sums(): pl.pallas_call(functools.partial(tile_kernel, own, blocks, main, over), o...  17.8 us
    ppermute x1, waiting for transfers between devices, on_device(): recv_a = lax.ppermute(send_a, 'local', pairs)  17.2 us
    unnamed x50, local copies, waits for them, and re-layouts  14.8 us
    all_to_all x1, waiting for transfers between devices, on_device(): lax.all_to_all(placed, 'local', split_axis=0, concat_axis=0, tiled=True)  10.7 us
    all_to_all x1, starting transfers between devices, on_device(): lax.all_to_all(placed, 'local', split_axis=0, concat_axis=0, tiled=True)  9.05 us
    all_gather x1, waiting for transfers between devices, on_device(): whole = lax.all_gather(total * scale, 'group', tiled=True)  8.91 us
    all_to_all x1, starting transfers between devices, on_device(): lax.all_to_all(mine.reshape(groups, -1, width), 'group', split_axis=0, co...  7.84 us
  transfers between devices with their start and end apart: 12, of which 9 were waited for; matrix products, arithmetic and copies ran while one was open for 7% of the time, Pallas kernels for 5%

profile of v4, /device:TPU:1, one launch (start us, length us, event | category | flops | bytes accessed | tf_op | source)
XLA Modules:
  0.0 173.7 jit_solution(4232362090849942922)
XLA Ops:
  7.2 9.5 %other_tile_sums.1 = (f32[1024,512]{1,0:T(8,128)}, f32[8,256,128]{2,1,0:T(8,128)}, f32[6,256,128]{2,1,0:T(8,128)}, f32[26,256,128]{2,1,0:T(8,128)}) custom-call(s32[64]{0:T(128)} %col_ref.3, s32[16,16]{1,0:T(8,128)} %count_ref.7, f32[1024,512]{1,0:T(8,128)} %rest_0_.1, f32[1024,512]{1,0:T(8,128)} %rest_1_.2, f32[512,512]{1,0:T(8,128)} %rest_1_.3, ...), custom_call_target="tpu_custom_call" | custom-call | flops 2415919104 | bytes 14680064 | tf_op jit(solution)/shard_map/other_tile_sums/pallas_call | solution.py:210
  16.7 1.7 collective-permute-start.4
  18.4 3.6 %fusion.4 = f32[512,512]{1,0:T(8,128)S(1)} fusion(f32[1024,512]{1,0:T(8,128)} %get-tuple-element.32.rest_0_, f32[1024,512]{1,0:T(8,128)S(1)} %copy-done), kind=kOutput, calls=%fused_computation.13 | convolution fusion | flops 1610612736 | bytes 5242880 | tf_op jit(solution)/shard_map/dot_general | solution.py:433
  22.0 1.9 %fusion.5 = f32[512,512]{1,0:T(8,128)S(1)} fusion(f32[1024,512]{1,0:T(8,128)S(1)} %copy-done.1, f32[1024,512]{1,0:T(8,128)S(1)} %copy-done.24), kind=kOutput, calls=%fused_computation.14 | convolution fusion | flops 1610612736 | bytes 5242880 | tf_op jit(solution)/shard_map/dot_general | solution.py:436
  24.5 8.3 %own_tile_sums.1 = (f32[8,256,128]{2,1,0:T(8,128)S(1)}, f32[6,256,128]{2,1,0:T(8,128)}, s32[1]{0:T(128)}, f32[2,13,64,128]{3,2,1,0:T(8,128)S(1)}, f32[2,13,64,12...) custom-call(s32[64]{0:T(128)S(1)} %copy-done.19, s32[16,16]{1,0:T(8,128)S(1)} %copy-done.17, ...), custom_call_target="tpu_custom_call" | custom-call | flops 2415919104 | bytes 14680064 | tf_op jit(solution)/shard_map/own_tile_sums/pallas_call | solution.py:210
  38.5 2.5 %collective-permute-done.9 = f32[512,512]{0,1:T(8,128)S(1)} collective-permute-done((f32[512,512]{0,1:T(8,128)S(1)}, f32[512,512]{0,1:T(8,128)S(1)}, u32[]{:S(2)}, u32[]{:S(2)}) %collective-permute-start.9) | collective-permute-done | bytes 1048608 | tf_op jit(solution)/shard_map/ppermute | solution.py:440
  41.4 1.3 copy.23
  42.7 7.8 %all-to-all-start.2 = ((f32[16,32,512]{2,1,0:T(8,128)}), f32[16,32,512]{2,1,0:T(8,128)S(1)}, u32[]{:S(2)}, u32[]{:S(2)}) async-start(f32[16,32,512]{2,1,0:T(8,128)} %bitcast.38), calls=%async_computation.2 | async-start | bytes 2097152 | tf_op jit(solution)/shard_map/all_to_all | solution.py:443
  50.6 1.3 collective-permute-start.5
  51.9 1.8 %collective-permute-start.6 = (f32[2,13,64,128]{3,2,1,0:T(8,128)}, f32[2,13,64,128]{3,2,1,0:T(8,128)S(1)}, u32[]{:S(2)}, u32[]{:S(2)}) collective-permute-start(f32[2,13,64,128]{3,2,1,0:T(8,128)} %copy-done.20), channel_id=1, source_target_pairs={{0,6},{1,7},{2,4},{3,5},{4,2},{5,3},{6,0},{7,1},{8,14},{9,15},{10,... | collective-permute-start | bytes 2555912 | tf_op jit(solution)/shard_map/ppermute | solution.py:402
  53.7 17.2 %collective-permute-done.5.recv_a = f32[2,13,64,128]{3,2,1,0:T(8,128)S(1)} collective-permute-done((f32[2,13,64,128]{3,2,1,0:T(8,128)}, f32[2,13,64,128]{3,2,1,0:T(8,128)S(1)}, u32[]{:S(2)}, u32[]{:S(2)}) %collective-permute-start.5) | collective-permute-done | bytes 852000 | tf_op jit(solution)/shard_map/ppermute | solution.py:401
  71.0 2.1 %collective-permute-done.6.recv_b = f32[2,13,64,128]{3,2,1,0:T(8,128)S(1)} collective-permute-done((f32[2,13,64,128]{3,2,1,0:T(8,128)}, f32[2,13,64,128]{3,2,1,0:T(8,128)S(1)}, u32[]{:S(2)}, u32[]{:S(2)}) %collective-permute-start.6) | collective-permute-done | bytes 852000 | tf_op jit(solution)/shard_map/ppermute | solution.py:402
  73.1 1.2 copy-done.12
  74.2 1.2 copy-done.14
  78.0 1.0 copy-done.16
  79.2 3.1 %collective-permute-done.10 = f32[32,512]{1,0:T(8,128)S(1)} collective-permute-done((f32[32,512]{1,0:T(8,128)S(1)}, f32[32,512]{1,0:T(8,128)S(1)}, u32[]{:S(2)}, u32[]{:S(2)}) %collective-permute-start.10) | collective-permute-done | bytes 65568 | tf_op jit(solution)/shard_map/ppermute | solution.py:447
  82.3 1.9 %collective-permute-start.11 = (f32[32,512]{1,0:T(8,128)S(1)}, f32[32,512]{1,0:T(8,128)S(1)}, u32[]{:S(2)}, u32[]{:S(2)}) collective-permute-start(f32[32,512]{1,0:T(8,128)S(1)} %add.67), channel_id=1, source_target_pairs={{0,6},{1,7},{2,4},{3,5},{4,2},{5,3},{6,0},{7,1},{8,14},{9,15},{10,... | collective-permute-start | bytes 196616 | tf_op jit(solution)/shard_map/ppermute | solution.py:448
  85.0 1.6 collective-permute-done.11
  89.6 5.7 %collective-permute-done.7.recv_a = f32[13,64,128]{2,1,0:T(8,128)S(1)} collective-permute-done((f32[13,64,128]{2,1,0:T(8,128)}, f32[13,64,128]{2,1,0:T(8,128)S(1)}, u32[]{:S(2)}, u32[]{:S(2)}) %collective-permute-start.7) | collective-permute-done | bytes 426016 | tf_op jit(solution)/shard_map/ppermute | solution.py:404
  95.3 1.6 third_sums.1
  96.9 19.8 %all_to_all.15.arrived = f32[32,64,128]{2,1,0:T(8,128)S(1)} all-to-all(f32[32,64,128]{2,1,0:T(8,128)S(1)} %third_sums.1), channel_id=1, replica_groups=mesh['group'=16,'local'=8] {'group'}, dimensions={0} | all-to-all | bytes 2097152 | tf_op jit(solution)/shard_map/all_to_all | solution.py:427
  116.7 1.4 place.1
  118.1 1.3 copy-done.3
  119.4 9.1 %all-to-all-start.1 = ((f32[64,64,128]{2,1,0:T(8,128)}), f32[64,64,128]{2,1,0:T(8,128)}, u32[]{:S(2)}, u32[]{:S(2)}) async-start(f32[64,64,128]{2,1,0:T(8,128)} %copy-done.3), calls=%async_computation.1 | async-start | bytes 4194304 | tf_op jit(solution)/shard_map/all_to_all | solution.py:429
  128.5 8.9 %all-gather.2.cloned.1.call-done = f32[512,512]{1,0:T(8,128)} async-done(((f32[32,512]{1,0:T(8,128)}), f32[512,512]{1,0:T(8,128)}) %all-gather.2.cloned.1.call-update) | async-done | bytes 1048592 | tf_op jit(solution)/shard_map/all_gather | solution.py:450
  137.4 1.8 %collective-permute-start.12 = (f32[512,512]{1,0:T(8,128)}, f32[512,512]{1,0:T(8,128)}, u32[]{:S(2)}, u32[]{:S(2)}) collective-permute-start(f32[512,512]{1,0:T(8,128)} %all-gather.2.cloned.1.call-done), channel_id=1, source_target_pairs={{0,1},{1,0},{2,3},{3,2},{4,5},{5,4},{6,7},{7,6},{8,9},{9,8},{10,11... | collective-permute-start | bytes 3145736 | tf_op jit(solution)/shard_map/ppermute | solution.py:451
  139.2 5.1 %fusion.3.base = f32[1024,512]{1,0:T(8,128)} fusion(f32[1024,512]{1,0:T(8,128)} %get-tuple-element.32.rest_0_, f32[512,512]{1,0:T(8,128)} %param.17), kind=kOutput, calls=%fused_computation.12 | convolution fusion | flops 1610612736 | bytes 5242880 | tf_op jit(solution)/shard_map/dot_general | solution.py:455
  144.2 10.7 %all-to-all-done.1 = f32[64,64,128]{2,1,0:T(8,128)} async-done(((f32[64,64,128]{2,1,0:T(8,128)}), f32[64,64,128]{2,1,0:T(8,128)}, u32[]{:S(2)}, u32[]{:S(2)}) %all-to-all-start.1) | async-done | bytes 2097184 | tf_op jit(solution)/shard_map/all_to_all | solution.py:429
  154.9 1.6 copy-done.4
  156.5 1.2 copy-done.8
  157.8 6.2 %finish.1 = f32[1024,512]{1,0:T(8,128)} custom-call(f32[1024,512]{1,0:T(8,128)S(1)} %copy-done.4, f32[8,256,128]{2,1,0:T(8,128)S(1)} %copy-done.6, f32[8,256,128]{2,1,0:T(8,128)S(1)} %copy-done.8, f32[8,8,64,128]{3,2,1,0:T(8,128)} %bitcast.9.received), custom_call_target="tpu_custom_call" | custom-call | flops 1048576 | bytes 8388608 | tf_op jit(solution)/shard_map/finish/pallas_call | solution.py:355
  164.0 2.8 %broadcast_select_fusion = (f32[512,512]{1,0:T(8,128)}, f32[512,512]{1,0:T(8,128)}) fusion(f32[512,512]{1,0:T(8,128)} %collective-permute-done.12, f32[512,512]{1,0:T(8,128)S(1)} %copy-done.25, pred[]{:T(512)} %bitcast.10), kind=kLoop, calls=%fused_computation.8 | loop fusion | flops 524288 | bytes 4194305 | tf_op jit(solution)/shard_map/jit(_where)/select_n | solution.py:453
  (64 shorter events, 12.6 us)
Async XLA Ops:
  7.2 11.2 %copy-start = (f32[1024,512]{1,0:T(8,128)S(1)}, f32[1024,512]{1,0:T(8,128)}, u32[]{:S(2)}) copy-start(f32[1024,512]{1,0:T(8,128)} %param.13) | copy-start | bytes 6291460
  16.7 7.6 %collective-permute-start.4 = (f32[26,256,128]{2,1,0:T(8,128)}, f32[26,256,128]{2,1,0:T(8,128)S(1)}, u32[]{:S(2)}, u32[]{:S(2)}) collective-permute-start(f32[26,256,128]{2,1,0:T(8,128)} %get-tuple-element.34), channel_id=1, source_target_pairs={{0,1},{1,0},{2,3},{3,2},{4,5},{5,4},{6,7},{7,6},{8,9},{9,8},{10,11... | collective-permute-start | bytes 10223624 | tf_op jit(solution)/shard_map/ppermute | solution.py:397
  18.4 3.6 %copy-start.1 = (f32[1024,512]{1,0:T(8,128)S(1)}, f32[1024,512]{1,0:T(8,128)}, u32[]{:S(2)}) copy-start(f32[1024,512]{1,0:T(8,128)} %get-tuple-element.32.rest_0_) | copy-start | bytes 6291460
  18.4 3.6 %copy-start.24 = (f32[1024,512]{1,0:T(8,128)S(1)}, f32[1024,512]{1,0:T(8,128)}, u32[]{:S(2)}) copy-start(f32[1024,512]{1,0:T(8,128)} %param.14) | copy-start | bytes 6291460
  18.4 5.9 %copy-start.17 = (s32[16,16]{1,0:T(8,128)S(1)}, s32[16,16]{1,0:T(8,128)}, u32[]{:S(2)}) copy-start(s32[16,16]{1,0:T(8,128)} %count_ref.7) | copy-start | bytes 3076
  18.4 5.9 %copy-start.19 = (s32[64]{0:T(128)S(1)}, s32[64]{0:T(128)}, u32[]{:S(2)}) copy-start(s32[64]{0:T(128)} %col_ref.3) | copy-start | bytes 772
  22.0 2.3 %copy-start.2 = (f32[64,128,128]{2,1,0:T(8,128)S(1)}, f32[64,128,128]{2,1,0:T(8,128)}, u32[]{:S(2)}) copy-start(f32[64,128,128]{2,1,0:T(8,128)} %rest_2_.3) | copy-start | bytes 12582916
  22.0 2.5 %copy-start.5 = (f32[512,512]{1,0:T(8,128)S(1)}, f32[512,512]{1,0:T(8,128)}, u32[]{:S(2)}) copy-start(f32[512,512]{1,0:T(8,128)} %rest_1_.3) | copy-start | bytes 3145732
  32.8 1.0 copy-start.7
  34.7 0.9 copy-start.13
  35.6 0.9 copy-start.20
  38.2 2.7 %collective-permute-start.9 = (f32[512,512]{0,1:T(8,128)S(1)}, f32[512,512]{0,1:T(8,128)S(1)}, u32[]{:S(2)}, u32[]{:S(2)}) collective-permute-start(f32[512,512]{0,1:T(8,128)S(1)} %select_bitcast_fusion), channel_id=1, source_target_pairs={{0,1},{1,0},{2,3},{3,2},{4,5},{5,4},{6,7},{7,6},{8,9},{9,8},{10,11... | collective-permute-start | bytes 3145736 | tf_op jit(solution)/shard_map/ppermute | solution.py:440
  42.7 35.3 %all-to-all-start.2 = ((f32[16,32,512]{2,1,0:T(8,128)}), f32[16,32,512]{2,1,0:T(8,128)S(1)}, u32[]{:S(2)}, u32[]{:S(2)}) async-start(f32[16,32,512]{2,1,0:T(8,128)} %bitcast.38), calls=%async_computation.2 | async-start | bytes 2097152 | tf_op jit(solution)/shard_map/all_to_all | solution.py:443
  50.5 86.8 %all-gather.2.cloned.1.call-start = ((), (), s32[]{:S(2)}) async-start(), calls=%async_computation.3 | async-start | bytes 1114112 | tf_op jit(solution)/shard_map/all_gather | solution.py:450
  50.6 20.4 %collective-permute-start.5 = (f32[2,13,64,128]{3,2,1,0:T(8,128)}, f32[2,13,64,128]{3,2,1,0:T(8,128)S(1)}, u32[]{:S(2)}, u32[]{:S(2)}) collective-permute-start(f32[2,13,64,128]{3,2,1,0:T(8,128)} %copy-done.21), channel_id=1, source_target_pairs={{0,2},{1,3},{2,0},{3,1},{4,6},{5,7},{6,4},{7,5},{8,10},{9,11},{10,... | collective-permute-start | bytes 2555912 | tf_op jit(solution)/shard_map/ppermute | solution.py:401
  51.9 21.2 %collective-permute-start.6 = (f32[2,13,64,128]{3,2,1,0:T(8,128)}, f32[2,13,64,128]{3,2,1,0:T(8,128)S(1)}, u32[]{:S(2)}, u32[]{:S(2)}) collective-permute-start(f32[2,13,64,128]{3,2,1,0:T(8,128)} %copy-done.20), channel_id=1, source_target_pairs={{0,6},{1,7},{2,4},{3,5},{4,2},{5,3},{6,0},{7,1},{8,14},{9,15},{10,... | collective-permute-start | bytes 2555912 | tf_op jit(solution)/shard_map/ppermute | solution.py:402
  73.1 1.2 copy-start.12
  74.2 1.2 copy-start.14
  78.0 1.0 copy-start.16
  79.1 3.2 %collective-permute-start.10 = (f32[32,512]{1,0:T(8,128)S(1)}, f32[32,512]{1,0:T(8,128)S(1)}, u32[]{:S(2)}, u32[]{:S(2)}) collective-permute-start(f32[32,512]{1,0:T(8,128)S(1)} %part_sum.1), channel_id=1, source_target_pairs={{0,2},{1,3},{2,0},{3,1},{4,6},{5,7},{6,4},{7,5},{8,10},{9,11},{10,... | collective-permute-start | bytes 196616 | tf_op jit(solution)/shard_map/ppermute | solution.py:447
  82.3 4.4 %collective-permute-start.11 = (f32[32,512]{1,0:T(8,128)S(1)}, f32[32,512]{1,0:T(8,128)S(1)}, u32[]{:S(2)}, u32[]{:S(2)}) collective-permute-start(f32[32,512]{1,0:T(8,128)S(1)} %add.67), channel_id=1, source_target_pairs={{0,6},{1,7},{2,4},{3,5},{4,2},{5,3},{6,0},{7,1},{8,14},{9,15},{10,... | collective-permute-start | bytes 196616 | tf_op jit(solution)/shard_map/ppermute | solution.py:448
  84.2 11.1 %collective-permute-start.7 = (f32[13,64,128]{2,1,0:T(8,128)}, f32[13,64,128]{2,1,0:T(8,128)S(1)}, u32[]{:S(2)}, u32[]{:S(2)}) collective-permute-start(f32[13,64,128]{2,1,0:T(8,128)} %copy-done.15), channel_id=1, source_target_pairs={{0,6},{1,7},{2,4},{3,5},{4,2},{5,3},{6,0},{7,1},{8,14},{9,15},{10,... | collective-permute-start | bytes 1277960 | tf_op jit(solution)/shard_map/ppermute | solution.py:404
  85.0 10.3 %collective-permute-start.8 = (f32[13,64,128]{2,1,0:T(8,128)}, f32[13,64,128]{2,1,0:T(8,128)}, u32[]{:S(2)}, u32[]{:S(2)}) collective-permute-start(f32[13,64,128]{2,1,0:T(8,128)} %copy-done.22), channel_id=1, source_target_pairs={{0,2},{1,3},{2,0},{3,1},{4,6},{5,7},{6,4},{7,5},{8,10},{9,11},{10,... | collective-permute-start | bytes 1277960 | tf_op jit(solution)/shard_map/ppermute | solution.py:405
  88.9 6.4 %copy-start.10 = (f32[2,13,64,128]{3,2,1,0:T(8,128)S(1)}, f32[2,13,64,128]{3,2,1,0:T(8,128)}, u32[]{:S(2)}) copy-start(f32[2,13,64,128]{3,2,1,0:T(8,128)} %copy-done.9) | copy-start | bytes 2555908
  95.3 21.4 %copy-start.18 = (s32[16,32]{1,0:T(8,128)S(1)}, s32[16,32]{1,0:T(8,128)}, u32[]{:S(2)}) copy-start(s32[16,32]{1,0:T(8,128)} %target_ref.1) | copy-start | bytes 6148
  118.1 1.3 copy-start.3
  119.4 35.5 %all-to-all-start.1 = ((f32[64,64,128]{2,1,0:T(8,128)}), f32[64,64,128]{2,1,0:T(8,128)}, u32[]{:S(2)}, u32[]{:S(2)}) async-start(f32[64,64,128]{2,1,0:T(8,128)} %copy-done.3), calls=%async_computation.1 | async-start | bytes 4194304 | tf_op jit(solution)/shard_map/all_to_all | solution.py:429
  128.5 26.5 %copy-start.6 = (f32[8,256,128]{2,1,0:T(8,128)S(1)}, f32[8,256,128]{2,1,0:T(8,128)}, u32[]{:S(2)}) copy-start(f32[8,256,128]{2,1,0:T(8,128)} %get-tuple-element.33.other_local) | copy-start | bytes 3145732
  137.4 26.6 %collective-permute-start.12 = (f32[512,512]{1,0:T(8,128)}, f32[512,512]{1,0:T(8,128)}, u32[]{:S(2)}, u32[]{:S(2)}) collective-permute-start(f32[512,512]{1,0:T(8,128)} %all-gather.2.cloned.1.call-done), channel_id=1, source_target_pairs={{0,1},{1,0},{2,3},{3,2},{4,5},{5,4},{6,7},{7,6},{8,9},{9,8},{10,11... | collective-permute-start | bytes 3145736 | tf_op jit(solution)/shard_map/ppermute | solution.py:451
  154.9 1.6 copy-start.4
  156.5 1.2 copy-start.8
  157.8 6.2 %copy-start.25 = (f32[512,512]{1,0:T(8,128)S(1)}, f32[512,512]{1,0:T(8,128)}, u32[]{:S(2)}) copy-start(f32[512,512]{1,0:T(8,128)} %all-gather.2.cloned.1.call-done) | copy-start | bytes 3145732
  (5 other events, 4.2 us)
Sparse Core Ops, SparseCore 0:
  87.5 49.8 all-gather.1

commit v5 on v4

--- a/solution.py
+++ b/solution.py
@@ -16,6 +16,7 @@
 LIMIT_OTHER = 55
 LIMIT_OWN = 20
 LIMIT_SMALL = 6
+PARTS = 2
 
 
 def split(x):
@@ -230,79 +231,139 @@
 IN_SMEM = pl.BlockSpec(memory_space=pltpu.SMEM)
 
 
-def second_kernel(keep_a, recv_a, keep_b, recv_b, keep, send_a, send_b):
+def second_kernel(keep_a, recv_a, keep_b, recv_b, parts, keep, send_a, send_b, share):
     _, p, q = whereabouts()
-    send_a[...] = keep_a[1 - p] + recv_a[1 - p]
-    send_b[...] = keep_b[1 - q] + recv_b[1 - q]
+    half = keep_a.shape[1]
+    total = parts[0]
+    for k in range(1, parts.shape[0]):
+        total += parts[k]
+    rows = total.shape[1]
+    for k in range(total.shape[0]):
+        at = (k * rows // share.shape[1], pl.ds(k * rows % share.shape[1], rows))
+        share[at] = total[k]
+    send_a[0:half] = keep_a[1 - p] + recv_a[1 - p]
+    send_b[0:half] = keep_b[1 - q] + recv_b[1 - q]
+    send_a[half:] = share[...]
+    send_b[half:] = share[...]
     keep[0] = keep_a[p] + recv_a[p]
     keep[1] = keep_b[q] + recv_b[q]
 
 
-def second_sums(keep_a, recv_a, keep_b, recv_b):
-    send = jax.ShapeDtypeStruct(keep_a.shape[1:], F32)
+def second_sums(keep_a, recv_a, keep_b, recv_b, parts):
+    _, half, share, _ = keep_a.shape
+    extra = parts[0].size // (share * BLOCK)
+    send = jax.ShapeDtypeStruct((half + extra, share, BLOCK), F32)
     return pl.pallas_call(
         second_kernel,
-        out_shape=[jax.ShapeDtypeStruct(keep_a.shape, F32), send, send],
-        in_specs=[IN_VMEM] * 4,
-        out_specs=[IN_VMEM] * 3,
+        out_shape=[
+            jax.ShapeDtypeStruct(keep_a.shape, F32),
+            send,
+            send,
+            jax.ShapeDtypeStruct((extra, share, BLOCK), F32),
+        ],
+        in_specs=[IN_VMEM] * 5,
+        out_specs=[IN_VMEM] * 4,
         cost_estimate=pl.CostEstimate(
             flops=2 * keep_a.size, bytes_accessed=24 * keep_a.size, transcendentals=0
         ),
         compiler_params=limit(LIMIT_SMALL),
         name="second_sums",
-    )(keep_a, recv_a, keep_b, recv_b)
-
-
-def third_kernel(count_ref, keep, recv_a, recv_b, over, out, total, places):
-    half = recv_a.shape[0]
+    )(keep_a, recv_a, keep_b, recv_b, parts)
+
+
+def third_kernel(scale, count_ref, keep, recv_a, recv_b, over, share, recv_share, *rest):
+    *outs, weight, total, places = rest
+    half = keep.shape[1]
     main = 2 * half
-    total[0:half] = keep[0] + recv_a[...]
-    total[half:main] = keep[1] + recv_b[...]
+    total[0:half] = keep[0] + recv_a[0:half]
+    total[half:main] = keep[1] + recv_b[0:half]
     total[main:] = over[...]
+    weight[...] = ((share[...] + recv_b[half:]) + (recv_a[half:] + recv_share[...])) * scale
     slot_places(count_ref, places)
-
-    @pl.loop(0, out.shape[0])
+    rows = outs[0].shape[1]
+
+    @pl.loop(0, total.shape[0])
     def _(slot):
-        out[slot] = total[places[slot]]
-
-
-def third_sums(halo_count, keep, recv_a, recv_b, over):
-    slots = 2 * recv_a.shape[0] + over.shape[0]
-    shape = (slots,) + recv_a.shape[1:]
+        for h, out in enumerate(outs):
+            out[slot] = total[places[slot], h * rows : (h + 1) * rows]
+
+
+def third_sums(halo_count, keep, recv_a, recv_b, over, share, recv_share, scale):
+    _, half, rows, _ = keep.shape
+    slots = 2 * half + over.shape[0]
     return pl.pallas_call(
-        third_kernel,
-        out_shape=jax.ShapeDtypeStruct(shape, F32),
-        in_specs=[IN_SMEM] + [IN_VMEM] * 4,
-        out_specs=IN_VMEM,
-        scratch_shapes=[pltpu.VMEM(shape, F32), pltpu.SMEM((slots,), jnp.int32)],
+        functools.partial(third_kernel, scale),
+        out_shape=[jax.ShapeDtypeStruct((slots, rows // PARTS, BLOCK), F32)] * PARTS
+        + [jax.ShapeDtypeStruct(share.shape, F32)],
+        in_specs=[IN_SMEM] + [IN_VMEM] * 6,
+        out_specs=[IN_VMEM] * (PARTS + 1),
+        scratch_shapes=[pltpu.VMEM((slots, rows, BLOCK), F32), pltpu.SMEM((slots,), jnp.int32)],
         cost_estimate=pl.CostEstimate(
             flops=keep.size, bytes_accessed=16 * keep.size, transcendentals=0
         ),
         compiler_params=limit(LIMIT_SMALL),
         name="third_sums",
-    )(halo_count, keep, recv_a, recv_b, over)
-
-
-def part_kernel(parts, after, out):
+    )(halo_count, keep, recv_a, recv_b, over, share, recv_share)
+
+
+def small(kernel, out_shape, args, name, specs=None, out_specs=None):
+    size = max(x.size for x in args)
+    return pl.pallas_call(
+        kernel,
+        out_shape=out_shape,
+        in_specs=specs or [IN_VMEM] * len(args),
+        out_specs=out_specs or jax.tree.map(lambda _: IN_VMEM, out_shape),
+        cost_estimate=pl.CostEstimate(flops=size, bytes_accessed=12 * size, transcendentals=0),
+        compiler_params=limit(LIMIT_SMALL),
+        name=name,
+    )(*args)
+
+
+def sort_kernel(self_term, neigh_term, keep, send):
+    core, _, _ = whereabouts()
+    pieces, columns, rows, _ = keep.shape
+
+    def copy(source, target):
+        for g in range(pieces):
+            for c in range(columns):
+                some = (slice(g * rows, (g + 1) * rows), slice(c * BLOCK, (c + 1) * BLOCK))
+                target[g, c] = source[some]
+
+    @pl.when(core == 0)
+    def _():
+        copy(self_term, keep)
+        copy(neigh_term, send)
+
+    @pl.when(core != 0)
+    def _():
+        copy(neigh_term, keep)
+        copy(self_term, send)
+
+
+def grads_kernel(whole, other, self_grad, neigh_grad):
+    core, _, _ = whereabouts()
+    pieces, columns, rows, _ = whole.shape
+
+    def copy(source, target):
+        for g in range(pieces):
+            for c in range(columns):
+                some = (slice(g * rows, (g + 1) * rows), slice(c * BLOCK, (c + 1) * BLOCK))
+                target[some] = source[g, c]
+
+    @pl.when(core == 0)
+    def _():
+        copy(whole, self_grad)
+        copy(other, neigh_grad)
+
+    @pl.when(core != 0)
+    def _():
+        copy(other, self_grad)
+        copy(whole, neigh_grad)
+
+
+def add_kernel(one, two, after, out):
     del after
-    total = parts[0]
-    for k in range(1, parts.shape[0]):
-        total += parts[k]
-    out[...] = total
-
-
-def part_sum(parts, after):
-    return pl.pallas_call(
-        part_kernel,
-        out_shape=jax.ShapeDtypeStruct(parts.shape[1:], F32),
-        in_specs=[IN_VMEM, pl.BlockSpec(memory_space=pl.ANY)],
-        out_specs=IN_VMEM,
-        cost_estimate=pl.CostEstimate(
-            flops=parts.size, bytes_accessed=4 * parts.size, transcendentals=0
-        ),
-        compiler_params=limit(LIMIT_SMALL),
-        name="part_sum",
-    )(parts, after)
+    out[...] = one[...] + two[...]
 
 
 def place_kernel(count_ref, target_ref, arrived, out):
@@ -334,37 +395,50 @@
     )(halo_count, halo_target, arrived)
 
 
-def finish_kernel(base, other_local, own_local, received, out, total):
+def finish_kernel(base, other_local, own_local, *rest):
+    *received, out, total, rows, sems = rest
     core, _, _ = whereabouts()
-    width = other_local.shape[1]
-    share = received.shape[2]
-    total[pl.ds(pl.multiple_of(core * width, width), width)] = own_local[0]
-    total[pl.ds(pl.multiple_of((1 - core) * width, width), width)] = other_local[0]
-    for member in range(received.shape[0]):
-        start = (member % 2) * width + QUARTER[member // 2] * share
-        total[start : start + share] += received[member, 0]
-    out[...] = base[...] + total[...].T
+    blocks, width, _ = other_local.shape
+    members, _, part, _ = received[0].shape
+    share = part * len(received)
+    own = pl.ds(pl.multiple_of(core * width, width), width)
+    other = pl.ds(pl.multiple_of((1 - core) * width, width), width)
+    copies = []
+    for b in range(blocks):
+        total[b, own] = own_local[b]
+        total[b, other] = other_local[b]
+        for member in range(members):
+            start = (member % 2) * width + QUARTER[member // 2] * share
+            for h, some in enumerate(received):
+                total[b, start + h * part : start + (h + 1) * part] += some[member, b]
+        at = slice(b * BLOCK, (b + 1) * BLOCK)
+        rows[at] = base[at] + total[b].T
+        copy = pltpu.make_async_copy(rows.at[at], out.at[at], sems.at[b])
+        copy.start()
+        copies.append(copy)
+    for copy in copies:
+        copy.wait()
 
 
 def finish(base, other_local, own_local, received):
     node_rows, feat = base.shape
-    blocks, width, _ = other_local.shape
-    row_spec = pl.BlockSpec((BLOCK, feat), lambda i: (i, 0))
-    local_spec = pl.BlockSpec((1, width, BLOCK), lambda i: (i, 0, 0))
-    shape = (received.shape[0], 1) + received.shape[2:]
+    blocks = other_local.shape[0]
     return pl.pallas_call(
         finish_kernel,
         out_shape=jax.ShapeDtypeStruct(base.shape, F32),
-        grid=(blocks,),
-        in_specs=[row_spec, local_spec, local_spec, pl.BlockSpec(shape, lambda i: (0, i, 0, 0))],
-        out_specs=row_spec,
-        scratch_shapes=[pltpu.VMEM((feat, BLOCK), F32)],
+        in_specs=[IN_VMEM] * (3 + len(received)),
+        out_specs=pl.BlockSpec(memory_space=pl.ANY),
+        scratch_shapes=[
+            pltpu.VMEM((blocks, feat, BLOCK), F32),
+            pltpu.VMEM((node_rows, feat), F32),
+            pltpu.SemaphoreType.DMA((blocks,)),
+        ],
         cost_estimate=pl.CostEstimate(
             flops=2 * base.size, bytes_accessed=16 * base.size, transcendentals=0
         ),
-        compiler_params=limit(LIMIT_SMALL),
+        compiler_params=limit(8),
         name="finish",
-    )(base, other_local, own_local, received)
+    )(base, other_local, own_local, *received)
 
 
 def on_device(
@@ -400,9 +474,31 @@
     )
     recv_a = lax.ppermute(send_a, "local", pairs)
     recv_b = lax.ppermute(send_b, "local", across)
-    keep, send_a, send_b = second_sums(keep_a, recv_a, keep_b, recv_b)
+
+    contract = (((0,), (0,)), ((), ()))
+    self_term = lax.dot_general(
+        features, pre_grad, contract, precision=high, preferred_element_type=F32
+    )
+    neigh_term = lax.dot_general(
+        aggregated, pre_grad, contract, precision=high, preferred_element_type=F32
+    )
+    pieces = jax.ShapeDtypeStruct(
+        (groups, width // BLOCK, width // groups, BLOCK), F32
+    )
+    stay, leave = small(sort_kernel, [pieces] * 2, [self_term, neigh_term], "sort_terms")
+    mine = small(
+        add_kernel,
+        pieces,
+        [stay, lax.ppermute(leave, "local", swap), flag],
+        "add_terms",
+        [IN_VMEM, IN_VMEM, IN_SMEM],
+    )
+    parts = lax.all_to_all(mine, "group", split_axis=0, concat_axis=0, tiled=True)
+
+    keep, send_a, send_b, share = second_sums(keep_a, recv_a, keep_b, recv_b, parts)
     recv_a = lax.ppermute(send_a, "local", across)
     recv_b = lax.ppermute(send_b, "local", pairs)
+    recv_share = lax.ppermute(share, "local", [(i, i ^ 4) for i in range(members)])
 
     def more():
         sums = own_over + lax.ppermute(other_over, "local", swap)
@@ -419,38 +515,26 @@
         return total
 
     def none():
-        return jnp.zeros((over,) + recv_a.shape[1:], F32)
+        return jnp.zeros((over,) + share.shape[1:], F32)
 
     most = jnp.max(jnp.sum(halo_count, axis=1))
     over_share = lax.cond(most > MAIN, more, none)
-    shares = third_sums(halo_count, keep, recv_a, recv_b, over_share)
-    arrived = lax.all_to_all(shares, "group", split_axis=0, concat_axis=0, tiled=True)
-    placed = place(halo_count, halo_target, arrived, blocks * members)
-    received = lax.all_to_all(placed, "local", split_axis=0, concat_axis=0, tiled=True)
-    received = received.reshape((members, blocks) + received.shape[1:])
-
-    contract = (((0,), (0,)), ((), ()))
-    self_term = lax.dot_general(
-        features, pre_grad, contract, precision=high, preferred_element_type=F32
-    )
-    neigh_term = lax.dot_general(
-        aggregated, pre_grad, contract, precision=high, preferred_element_type=F32
-    )
-    first = flag[0] == 0
-    mine = jnp.where(first, self_term, neigh_term) + lax.ppermute(
-        jnp.where(first, neigh_term, self_term), "local", swap
-    )
-    parts = lax.all_to_all(
-        mine.reshape(groups, -1, width), "group", split_axis=0, concat_axis=0, tiled=True
-    )
-    total = part_sum(parts, send_a)
-    total = total + lax.ppermute(total, "local", pairs)
-    total = total + lax.ppermute(total, "local", across)
     scale = float(node_rows * groups * members) ** (-0.5)
-    whole = lax.all_gather(total * scale, "group", tiled=True)
+    *shares, weight_share = third_sums(
+        halo_count, keep, recv_a, recv_b, over_share, share, recv_share, scale
+    )
+    arrived = [
+        lax.all_to_all(some, "group", split_axis=0, concat_axis=0, tiled=True) for some in shares
+    ]
+    received = []
+    for some in arrived:
+        placed = place(halo_count, halo_target, some, blocks * members)
+        some = lax.all_to_all(placed, "local", split_axis=0, concat_axis=0, tiled=True)
+        received.append(some.reshape((members, blocks) + some.shape[1:]))
+    whole = lax.all_gather(weight_share, "group", tiled=True).reshape(pieces.shape)
     other = lax.ppermute(whole, "local", swap)
-    self_grad = jnp.where(first, whole, other)
-    neigh_grad = jnp.where(first, other, whole)
+    square = jax.ShapeDtypeStruct(self_term.shape, F32)
+    self_grad, neigh_grad = small(grads_kernel, [square] * 2, [whole, other], "sort_grads")
 
     base = jnp.dot(pre_grad, w_self.T, precision=high, preferred_element_type=F32)
     node_grad = finish(base, other_local, own_local, received)

time: 174 us -> 188 us (1.080)
  starting transfers between devices: 26.6 us -> 36.5 us
  local copies, waits for them, and re-layouts: 16.8 us -> 23.6 us
  blocking collectives: 19.8 us -> 14.8 us
  Pallas kernels: 27.3 us -> 31.9 us
  other arithmetic: 4.87 us -> 0.78 us
    unnamed x50 -> x64, local copies, waits for them, and re-layouts: 14.8 us -> 22.9 us
    all_to_all x1 -> x2, waiting for transfers between devices: 0.01 us -> 6.75 us  [the longest x1 6.75 us: on_device(): lax.all_to_all(some, 'group', split_axis=0, concat_axis=0, tiled=True)]
    ppermute x1, waiting for transfers between devices: 5.68 us -> 0.01 us  [on_device(): recv_a = lax.ppermute(send_a, 'local', across)]
    all_to_all x1 -> x2, starting transfers between devices: 9.05 us -> 14.1 us  [on_device(): lax.all_to_all(placed, 'local', split_axis=0, concat_axis=0, tiled=True)]
    all_to_all x1, blocking collectives: 19.8 us -> 14.8 us  [on_device(): lax.all_to_all(some, 'group', split_axis=0, concat_axis=0, tiled=True)]
    all_to_all x1 -> x2, starting transfers between devices: 7.84 us -> 11.4 us  [the longest x1 7.85 us: on_device(): lax.all_to_all(mine, 'group', split_axis=0, concat_axis=0, tiled=True)]
    pallas_call x2 -> x4, Pallas kernels: 1.65 us -> 5.09 us  [the longest x3 3.49 us: small(): pl.pallas_call(kernel, out_shape=out_shape, in_specs=specs or [IN_VMEM] *...]
    pallas_call x1 -> x2, Pallas kernels: 1.42 us -> 4.68 us  [place(): pl.pallas_call(place_kernel, out_shape=jax.ShapeDtypeStruct((group_blocks...]
  transfers between devices with their start and end apart: 12 -> 13, of which waited for: 9 -> 7; matrix products, arithmetic and copies ran while one was open for 7% -> 6% of each run, Pallas kernels for 5% -> 9%
where the time goes in v5:
time: 188 us; the launch traced here: 187 us
  waiting for transfers between devices  53.9 us (29%)
  starting transfers between devices  36.5 us (19%)
  Pallas kernels  31.9 us (17%)
  local copies, waits for them, and re-layouts  23.6 us (13%)
  between operations  14.9 us (8%)
  blocking collectives  14.8 us (8%)
  matrix products  10.5 us (6%)
    unnamed x64, local copies, waits for them, and re-layouts  22.9 us
    pallas_call x2, Pallas kernels, tile_sums(): pl.pallas_call(functools.partial(tile_kernel, own, blocks, main, over), o...  17.6 us
    ppermute x1, waiting for transfers between devices, on_device(): recv_a = lax.ppermute(send_a, 'local', pairs)  17.4 us
    all_to_all x1, blocking collectives, on_device(): lax.all_to_all(some, 'group', split_axis=0, concat_axis=0, tiled=True)  14.8 us
    all_to_all x2, starting transfers between devices, on_device(): lax.all_to_all(placed, 'local', split_axis=0, concat_axis=0, tiled=True)  14.1 us
    all_to_all x2, waiting for transfers between devices, on_device(): lax.all_to_all(placed, 'local', split_axis=0, concat_axis=0, tiled=True)  11.9 us
    ppermute x1, waiting for transfers between devices, on_device(): lax.ppermute(share, 'local', [(i, i ^ 4) for i in range(members)])  8.74 us
    all_gather x1, waiting for transfers between devices, on_device(): lax.all_gather(weight_share, 'group', tiled=True).reshape(pieces.shape)  7.92 us
  transfers between devices with their start and end apart: 13, of which 7 were waited for; matrix products, arithmetic and copies ran while one was open for 6% of the time, Pallas kernels for 9%

profile of v5, /device:TPU:1, one launch (start us, length us, event | category | flops | bytes accessed | tf_op | source)
XLA Modules:
  0.0 186.9 jit_solution(5528600848237994928)
XLA Ops:
  7.2 9.4 %other_tile_sums.1 = (f32[1024,512]{1,0:T(8,128)}, f32[8,256,128]{2,1,0:T(8,128)}, f32[6,256,128]{2,1,0:T(8,128)}, f32[26,256,128]{2,1,0:T(8,128)}) custom-call(s32[64]{0:T(128)} %col_ref.3, s32[16,16]{1,0:T(8,128)} %count_ref.9, f32[1024,512]{1,0:T(8,128)} %rest_0_.1, f32[1024,512]{1,0:T(8,128)} %rest_1_.2, f32[512,512]{1,0:T(8,128)} %rest_1_.3, ...), custom_call_target="tpu_custom_call" | custom-call | flops 2415919104 | bytes 14680064 | tf_op jit(solution)/shard_map/other_tile_sums/pallas_call | solution.py:211
  16.6 1.5 collective-permute-start.4
  18.1 3.6 %convolution_bitcast_fusion.neigh_term = f32[512,512]{1,0:T(8,128)S(1)} fusion(f32[1024,512]{1,0:T(8,128)} %get-tuple-element.40.rest_0_, f32[1024,512]{1,0:T(8,128)S(1)} %copy-done), kind=kOutput, calls=%fused_computation.6 | convolution fusion | flops 1610612736 | bytes 5242880 | tf_op jit(solution)/shard_map/dot_general | solution.py:482
  21.7 1.8 convolution_bitcast_fusion.1.self_term
  24.9 8.2 %own_tile_sums.1 = (f32[8,256,128]{2,1,0:T(8,128)S(1)}, f32[6,256,128]{2,1,0:T(8,128)}, s32[1]{0:T(128)}, f32[2,13,64,128]{3,2,1,0:T(8,128)S(1)}, f32[2,13,64,12...) custom-call(s32[64]{0:T(128)S(1)} %copy-done.28, s32[16,16]{1,0:T(8,128)S(1)} %copy-done.25, ...), custom_call_target="tpu_custom_call" | custom-call | flops 2415919104 | bytes 14680064 | tf_op jit(solution)/shard_map/own_tile_sums/pallas_call | solution.py:211
  39.4 7.9 %all-to-all-start = ((f32[16,4,32,128]{3,2,1,0:T(8,128)}), f32[16,4,32,128]{3,2,1,0:T(8,128)S(1)}, u32[]{:S(2)}, u32[]{:S(2)}) async-start(f32[16,4,32,128]{3,2,1,0:T(8,128)} %copy-done.4), calls=%async_computation | async-start | bytes 2097152 | tf_op jit(solution)/shard_map/all_to_all | solution.py:496
  47.3 1.3 collective-permute-start.5
  48.6 1.8 collective-permute-start.6
  50.4 17.4 %collective-permute-done.5.recv_a = f32[2,13,64,128]{3,2,1,0:T(8,128)S(1)} collective-permute-done((f32[2,13,64,128]{3,2,1,0:T(8,128)}, f32[2,13,64,128]{3,2,1,0:T(8,128)S(1)}, u32[]{:S(2)}, u32[]{:S(2)}) %collective-permute-start.5) | collective-permute-done | bytes 852000 | tf_op jit(solution)/shard_map/ppermute | solution.py:475
  68.7 1.2 collective-permute-done.6.recv_b
  75.5 1.2 second_sums.1
  77.6 1.8 collective-permute-start.8
  81.5 2.1 %collective-permute-start.10 = (f32[2,64,128]{2,1,0:T(8,128)S(1)}, f32[2,64,128]{2,1,0:T(8,128)S(1)}, u32[]{:S(2)}, u32[]{:S(2)}) collective-permute-start(f32[2,64,128]{2,1,0:T(8,128)S(1)} %get-tuple-element.56.share), channel_id=1, source_target_pairs={{0,4},{1,5},{2,6},{3,7},{4,0},{5,1},{6,2},{7,3},{8,12},{9,13},{10,... | collective-permute-start | bytes 196616 | tf_op jit(solution)/shard_map/ppermute | solution.py:501
  83.6 8.7 %collective-permute-done.10.recv_share = f32[2,64,128]{2,1,0:T(8,128)S(1)} collective-permute-done((f32[2,64,128]{2,1,0:T(8,128)S(1)}, f32[2,64,128]{2,1,0:T(8,128)S(1)}, u32[]{:S(2)}, u32[]{:S(2)}) %collective-permute-start.10) | collective-permute-done | bytes 65568 | tf_op jit(solution)/shard_map/ppermute | solution.py:501
  94.1 1.6 third_sums.1
  97.2 14.8 %all_to_all.25.arrived = f32[32,32,128]{2,1,0:T(8,128)S(1)} all-to-all(f32[32,32,128]{2,1,0:T(8,128)S(1)} %get-tuple-element.57), channel_id=1, replica_groups=mesh['group'=16,'local'=8] {'group'}, dimensions={0} | all-to-all | bytes 1048576 | tf_op jit(solution)/shard_map/all_to_all | solution.py:527
  112.0 3.6 %all-to-all-start.3 = ((f32[32,32,128]{2,1,0:T(8,128)}), f32[32,32,128]{2,1,0:T(8,128)S(1)}, u32[]{:S(2)}, u32[]{:S(2)}) async-start(f32[32,32,128]{2,1,0:T(8,128)} %copy-done.22), calls=%async_computation.3 | async-start | bytes 1048576 | tf_op jit(solution)/shard_map/all_to_all | solution.py:527
  115.6 2.3 %place.2 = f32[64,32,128]{2,1,0:T(8,128)} custom-call(s32[16,16]{1,0:T(8,128)S(1)} %copy-done.25, s32[16,32]{1,0:T(8,128)S(1)} %copy-done.27, f32[32,32,128]{2,1,0:T(8,128)S(1)} %all_to_all.25.arrived), custom_call_target="tpu_custom_call" | custom-call | flops 131072 | bytes 1572864 | tf_op jit(solution)/shard_map/place/pallas_call | solution.py:385
  117.9 6.7 %all-to-all-done.3.arrived = f32[32,32,128]{2,1,0:T(8,128)S(1)} async-done(((f32[32,32,128]{2,1,0:T(8,128)}), f32[32,32,128]{2,1,0:T(8,128)S(1)}, u32[]{:S(2)}, u32[]{:S(2)}) %all-to-all-start.3) | async-done | bytes 524320 | tf_op jit(solution)/shard_map/all_to_all | solution.py:527
  125.4 9.1 %all-to-all-start.2 = ((f32[64,32,128]{2,1,0:T(8,128)}), f32[64,32,128]{2,1,0:T(8,128)S(1)}, u32[]{:S(2)}, u32[]{:S(2)}) async-start(f32[64,32,128]{2,1,0:T(8,128)} %place.2), calls=%async_computation.2 | async-start | bytes 2097152 | tf_op jit(solution)/shard_map/all_to_all | solution.py:532
  134.6 7.9 %all-gather.2.cloned.1.call-done = f32[32,64,128]{2,1,0:T(8,128)} async-done(((f32[2,64,128]{2,1,0:T(8,128)}), f32[32,64,128]{2,1,0:T(8,128)}) %all-gather.2.cloned.1.call-update) | async-done | bytes 1048592 | tf_op jit(solution)/shard_map/all_gather | solution.py:534
  142.5 2.1 %collective-permute-start.11 = (f32[16,4,32,128]{3,2,1,0:T(8,128)}, f32[16,4,32,128]{3,2,1,0:T(8,128)}, u32[]{:S(2)}, u32[]{:S(2)}) collective-permute-start(f32[16,4,32,128]{3,2,1,0:T(8,128)} %bitcast.39), channel_id=1, source_target_pairs={{0,1},{1,0},{2,3},{3,2},{4,5},{5,4},{6,7},{7,6},{8,9},{9,8},{10,11... | collective-permute-start | bytes 3145736 | tf_op jit(solution)/shard_map/ppermute | solution.py:535
  145.7 2.3 %place.3 = f32[64,32,128]{2,1,0:T(8,128)} custom-call(s32[16,16]{1,0:T(8,128)S(1)} %copy-done.25, s32[16,32]{1,0:T(8,128)S(1)} %copy-done.27, f32[32,32,128]{2,1,0:T(8,128)S(1)} %copy-done.7), custom_call_target="tpu_custom_call" | custom-call | flops 131072 | bytes 1572864 | tf_op jit(solution)/shard_map/place/pallas_call | solution.py:385
  148.0 1.7 all-to-all-done.2
  149.7 5.0 %all-to-all-start.4 = ((f32[64,32,128]{2,1,0:T(8,128)}), f32[64,32,128]{2,1,0:T(8,128)}, u32[]{:S(2)}, u32[]{:S(2)}) async-start(f32[64,32,128]{2,1,0:T(8,128)} %place.3), calls=%async_computation.4 | async-start | bytes 2097152 | tf_op jit(solution)/shard_map/all_to_all | solution.py:532
  154.7 5.0 %fusion.3.base = f32[1024,512]{1,0:T(8,128)} fusion(f32[1024,512]{1,0:T(8,128)} %get-tuple-element.40.rest_0_, f32[512,512]{1,0:T(8,128)} %param.17), kind=kOutput, calls=%fused_computation.9 | convolution fusion | flops 1610612736 | bytes 5242880 | tf_op jit(solution)/shard_map/dot_general | solution.py:539
  159.7 10.2 %all-to-all-done.4 = f32[64,32,128]{2,1,0:T(8,128)} async-done(((f32[64,32,128]{2,1,0:T(8,128)}), f32[64,32,128]{2,1,0:T(8,128)}, u32[]{:S(2)}, u32[]{:S(2)}) %all-to-all-start.4) | async-done | bytes 1048608 | tf_op jit(solution)/shard_map/all_to_all | solution.py:532
  169.9 1.6 copy-done.3
  171.5 1.2 copy-done.9
  172.7 1.2 copy-done.11
  174.0 3.4 %finish.1 = f32[1024,512]{1,0:T(8,128)} custom-call(f32[1024,512]{1,0:T(8,128)S(1)} %copy-done.3, f32[8,256,128]{2,1,0:T(8,128)S(1)} %copy-done.9, f32[8,256,128]{2,1,0:T(8,128)S(1)} %copy-done.11, f32[8,8,32,128]{3,2,1,0:T(8,128)S(1)} %bitcast.38, f32[8,8,32,128]{3,2,1,0:T(8,128)} %bitcast.12.rest_1_), custom_call_target="tpu_custom_call" | custom-call | flops 1048576 | bytes 8388608 | tf_op jit(solution)/shard_map/finish/pallas_call | solution.py:426
  177.4 2.7 %sort_grads.1 = (f32[512,512]{1,0:T(8,128)}, f32[512,512]{1,0:T(8,128)}) custom-call(f32[16,4,32,128]{3,2,1,0:T(8,128)S(1)} %bitcast.40, f32[16,4,32,128]{3,2,1,0:T(8,128)} %collective-permute-done.11.other), custom_call_target="tpu_custom_call" | custom-call | flops 262144 | bytes 3145728 | tf_op jit(solution)/shard_map/sort_grads/pallas_call | solution.py:311
  (77 shorter events, 22.3 us)
Async XLA Ops:
  7.2 10.9 %copy-start = (f32[1024,512]{1,0:T(8,128)S(1)}, f32[1024,512]{1,0:T(8,128)}, u32[]{:S(2)}) copy-start(f32[1024,512]{1,0:T(8,128)} %param.14) | copy-start | bytes 6291460
  16.6 7.5 %collective-permute-start.4 = (f32[26,256,128]{2,1,0:T(8,128)}, f32[26,256,128]{2,1,0:T(8,128)S(1)}, u32[]{:S(2)}, u32[]{:S(2)}) collective-permute-start(f32[26,256,128]{2,1,0:T(8,128)} %get-tuple-element.42), channel_id=1, source_target_pairs={{0,1},{1,0},{2,3},{3,2},{4,5},{5,4},{6,7},{7,6},{8,9},{9,8},{10,11... | collective-permute-start | bytes 10223624 | tf_op jit(solution)/shard_map/ppermute | solution.py:471
  18.1 3.6 %copy-start.1 = (f32[1024,512]{1,0:T(8,128)S(1)}, f32[1024,512]{1,0:T(8,128)}, u32[]{:S(2)}) copy-start(f32[1024,512]{1,0:T(8,128)} %get-tuple-element.40.rest_0_) | copy-start | bytes 6291460
  18.1 3.6 %copy-start.32 = (f32[1024,512]{1,0:T(8,128)S(1)}, f32[1024,512]{1,0:T(8,128)}, u32[]{:S(2)}) copy-start(f32[1024,512]{1,0:T(8,128)} %param.13) | copy-start | bytes 6291460
  21.7 2.4 %copy-start.2 = (f32[64,128,128]{2,1,0:T(8,128)S(1)}, f32[64,128,128]{2,1,0:T(8,128)}, u32[]{:S(2)}) copy-start(f32[64,128,128]{2,1,0:T(8,128)} %rest_2_.3) | copy-start | bytes 12582916
  23.6 1.3 copy-start.5
  23.6 1.3 copy-start.25
  23.6 1.3 copy-start.28
  23.8 13.9 %collective-permute-start.7 = (f32[16,4,32,128]{3,2,1,0:T(8,128)S(1)}, f32[16,4,32,128]{3,2,1,0:T(8,128)S(1)}, u32[]{:S(2)}, u32[]{:S(2)}) collective-permute-start(f32[16,4,32,128]{3,2,1,0:T(8,128)S(1)} %get-tuple-element.49), channel_id=1, source_target_pairs={{0,1},{1,0},{2,3},{3,2},{4,5},{5,4},{6,7},{7,6},{8,9},{9,8},{10,11... | collective-permute-start | bytes 3145736 | tf_op jit(solution)/shard_map/ppermute | solution.py:492
  39.4 31.5 %all-to-all-start = ((f32[16,4,32,128]{3,2,1,0:T(8,128)}), f32[16,4,32,128]{3,2,1,0:T(8,128)S(1)}, u32[]{:S(2)}, u32[]{:S(2)}) async-start(f32[16,4,32,128]{3,2,1,0:T(8,128)} %copy-done.4), calls=%async_computation | async-start | bytes 2097152 | tf_op jit(solution)/shard_map/all_to_all | solution.py:496
  47.2 95.2 %all-gather.2.cloned.1.call-start = ((), (), s32[]{:S(2)}) async-start(), calls=%async_computation.5 | async-start | bytes 1114112 | tf_op jit(solution)/shard_map/all_gather | solution.py:534
  47.3 20.5 %collective-permute-start.5 = (f32[2,13,64,128]{3,2,1,0:T(8,128)}, f32[2,13,64,128]{3,2,1,0:T(8,128)S(1)}, u32[]{:S(2)}, u32[]{:S(2)}) collective-permute-start(f32[2,13,64,128]{3,2,1,0:T(8,128)} %copy-done.30), channel_id=1, source_target_pairs={{0,2},{1,3},{2,0},{3,1},{4,6},{5,7},{6,4},{7,5},{8,10},{9,11},{10,... | collective-permute-start | bytes 2555912 | tf_op jit(solution)/shard_map/ppermute | solution.py:475
  48.6 21.3 %collective-permute-start.6 = (f32[2,13,64,128]{3,2,1,0:T(8,128)}, f32[2,13,64,128]{3,2,1,0:T(8,128)S(1)}, u32[]{:S(2)}, u32[]{:S(2)}) collective-permute-start(f32[2,13,64,128]{3,2,1,0:T(8,128)} %copy-done.29), channel_id=1, source_target_pairs={{0,6},{1,7},{2,4},{3,5},{4,2},{5,3},{6,0},{7,1},{8,14},{9,15},{10,... | collective-permute-start | bytes 2555912 | tf_op jit(solution)/shard_map/ppermute | solution.py:476
  70.9 1.2 copy-start.15
  72.0 1.2 copy-start.17
  73.2 1.2 copy-start.19
  74.3 1.2 copy-start.21
  77.6 14.7 %collective-permute-start.8 = (f32[15,64,128]{2,1,0:T(8,128)}, f32[15,64,128]{2,1,0:T(8,128)S(1)}, u32[]{:S(2)}, u32[]{:S(2)}) collective-permute-start(f32[15,64,128]{2,1,0:T(8,128)} %get-tuple-element.52), channel_id=1, source_target_pairs={{0,6},{1,7},{2,4},{3,5},{4,2},{5,3},{6,0},{7,1},{8,14},{9,15},{10,... | collective-permute-start | bytes 1474568 | tf_op jit(solution)/shard_map/ppermute | solution.py:499
  79.4 13.7 %collective-permute-start.9 = (f32[15,64,128]{2,1,0:T(8,128)}, f32[15,64,128]{2,1,0:T(8,128)}, u32[]{:S(2)}, u32[]{:S(2)}) collective-permute-start(f32[15,64,128]{2,1,0:T(8,128)} %get-tuple-element.53), channel_id=1, source_target_pairs={{0,2},{1,3},{2,0},{3,1},{4,6},{5,7},{6,4},{7,5},{8,10},{9,11},{10,... | collective-permute-start | bytes 1474568 | tf_op jit(solution)/shard_map/ppermute | solution.py:500
  80.8 12.3 %copy-start.13 = (f32[2,13,64,128]{3,2,1,0:T(8,128)S(1)}, f32[2,13,64,128]{3,2,1,0:T(8,128)}, u32[]{:S(2)}) copy-start(f32[2,13,64,128]{3,2,1,0:T(8,128)} %copy-done.12) | copy-start | bytes 2555908
  81.5 10.8 %collective-permute-start.10 = (f32[2,64,128]{2,1,0:T(8,128)S(1)}, f32[2,64,128]{2,1,0:T(8,128)S(1)}, u32[]{:S(2)}, u32[]{:S(2)}) collective-permute-start(f32[2,64,128]{2,1,0:T(8,128)S(1)} %get-tuple-element.56.share), channel_id=1, source_target_pairs={{0,4},{1,5},{2,6},{3,7},{4,0},{5,1},{6,2},{7,3},{8,12},{9,13},{10,... | collective-permute-start | bytes 196616 | tf_op jit(solution)/shard_map/ppermute | solution.py:501
  93.1 1.0 copy-start.24
  94.1 21.4 %copy-start.27 = (s32[16,32]{1,0:T(8,128)S(1)}, s32[16,32]{1,0:T(8,128)}, u32[]{:S(2)}) copy-start(s32[16,32]{1,0:T(8,128)} %target_ref.3) | copy-start | bytes 6148
  112.0 12.7 %all-to-all-start.3 = ((f32[32,32,128]{2,1,0:T(8,128)}), f32[32,32,128]{2,1,0:T(8,128)S(1)}, u32[]{:S(2)}, u32[]{:S(2)}) async-start(f32[32,32,128]{2,1,0:T(8,128)} %copy-done.22), calls=%async_computation.3 | async-start | bytes 1048576 | tf_op jit(solution)/shard_map/all_to_all | solution.py:527
  125.4 24.2 %all-to-all-start.2 = ((f32[64,32,128]{2,1,0:T(8,128)}), f32[64,32,128]{2,1,0:T(8,128)S(1)}, u32[]{:S(2)}, u32[]{:S(2)}) async-start(f32[64,32,128]{2,1,0:T(8,128)} %place.2), calls=%async_computation.2 | async-start | bytes 2097152 | tf_op jit(solution)/shard_map/all_to_all | solution.py:532
  142.5 34.9 %collective-permute-start.11 = (f32[16,4,32,128]{3,2,1,0:T(8,128)}, f32[16,4,32,128]{3,2,1,0:T(8,128)}, u32[]{:S(2)}, u32[]{:S(2)}) collective-permute-start(f32[16,4,32,128]{3,2,1,0:T(8,128)} %bitcast.39), channel_id=1, source_target_pairs={{0,1},{1,0},{2,3},{3,2},{4,5},{5,4},{6,7},{7,6},{8,9},{9,8},{10,11... | collective-permute-start | bytes 3145736 | tf_op jit(solution)/shard_map/ppermute | solution.py:535
  144.6 1.0 copy-start.7
  149.7 20.2 %all-to-all-start.4 = ((f32[64,32,128]{2,1,0:T(8,128)}), f32[64,32,128]{2,1,0:T(8,128)}, u32[]{:S(2)}, u32[]{:S(2)}) async-start(f32[64,32,128]{2,1,0:T(8,128)} %place.3), calls=%async_computation.4 | async-start | bytes 2097152 | tf_op jit(solution)/shard_map/all_to_all | solution.py:532
  169.9 1.6 copy-start.3
  171.5 1.2 copy-start.9
  172.7 1.2 copy-start.11
  174.0 3.4 %copy-start.8 = (f32[32,64,128]{2,1,0:T(8,128)S(1)}, f32[32,64,128]{2,1,0:T(8,128)}, u32[]{:S(2)}) copy-start(f32[32,64,128]{2,1,0:T(8,128)} %all-gather.2.cloned.1.call-done) | copy-start | bytes 3145732
  (13 other events, 11.4 us)
Sparse Core Ops, SparseCore 0:
  97.3 45.1 all-gather.1

commit v6 on v5

--- a/solution.py
+++ b/solution.py
@@ -11,12 +11,10 @@
 BF16 = jnp.bfloat16
 BLOCK = 128
 CHUNKS = 2
-MAIN = 26
-QUARTER = (0, 1, 3, 2)
+MAIN = 30
 LIMIT_OTHER = 55
 LIMIT_OWN = 20
 LIMIT_SMALL = 6
-PARTS = 2
 
 
 def split(x):
@@ -58,10 +56,10 @@
 
 def tile_kernel(own, blocks, main, over, col_ref, count_ref, *rest):
     if own:
-        pre_hbm, weight_hbm, tiles_hbm, recv_ref, local_ref, over_ref, flag_ref, *rest = rest
+        pre_hbm, weight_hbm, tiles_hbm, recv_ref, local_ref, flag_ref, *rest = rest
         keep_a, send_a, keep_b, send_b, pre, weight, tiles, sums, places, column, sems = rest
     else:
-        pre_hbm, grad_hbm, weight_hbm, tiles_hbm, pre_ref, local_ref, over_ref, *rest = rest
+        pre_hbm, grad_hbm, weight_hbm, tiles_hbm, pre_ref, local_ref, *rest = rest
         send_ref, pre, grad, weight, tiles, sums, places, column, sems = rest
     width = weight.shape[0]
     rows = pre.shape[0] // CHUNKS
@@ -167,7 +165,6 @@
     else:
         out(sums.at[pl.ds(blocks, main)], send_ref)
     out(sums.at[pl.ds(0, blocks)], local_ref)
-    out(sums.at[pl.ds(blocks + main, over)], over_ref)
     for copy in pre_copies + copies:
         copy.wait()
 
@@ -183,18 +180,16 @@
     some = main // 2
     anywhere = pl.BlockSpec(memory_space=pl.ANY)
     local = jax.ShapeDtypeStruct((blocks, width, BLOCK), F32)
-    over_shape = jax.ShapeDtypeStruct((over, width, BLOCK), F32)
     piece = jax.ShapeDtypeStruct((2, some, width // 4, BLOCK), F32)
     if own:
         args = [pre_grad, weight, tile_vals, recv]
         flag = jax.ShapeDtypeStruct((1,), jnp.int32)
-        out_shape = [local, over_shape, flag] + [piece] * 4
+        out_shape = [local, flag] + [piece] * 4
     else:
         args = [preact, grad_out, weight, tile_vals]
         out_shape = [
             jax.ShapeDtypeStruct((node_rows, feat), F32),
             local,
-            over_shape,
             jax.ShapeDtypeStruct((main, width, BLOCK), F32),
         ]
     scratch = [pltpu.VMEM((node_rows, feat), F32)]
@@ -231,16 +226,17 @@
 IN_SMEM = pl.BlockSpec(memory_space=pltpu.SMEM)
 
 
-def second_kernel(keep_a, recv_a, keep_b, recv_b, parts, keep, send_a, send_b, share):
+def second_kernel(keep_a, recv_a, keep_b, recv_b, *rest):
+    *parts, keep, send_a, send_b, share = rest
     _, p, q = whereabouts()
     half = keep_a.shape[1]
-    total = parts[0]
-    for k in range(1, parts.shape[0]):
-        total += parts[k]
-    rows = total.shape[1]
-    for k in range(total.shape[0]):
+    rows = parts[0].shape[1]
+    for k in range(parts[0].shape[0]):
         at = (k * rows // share.shape[1], pl.ds(k * rows % share.shape[1], rows))
-        share[at] = total[k]
+        total = parts[0][k]
+        for part in parts[1:]:
+            total += part[k]
+        share[at] = total
     send_a[0:half] = keep_a[1 - p] + recv_a[1 - p]
     send_b[0:half] = keep_b[1 - q] + recv_b[1 - q]
     send_a[half:] = share[...]
@@ -253,66 +249,55 @@
     _, half, share, _ = keep_a.shape
     extra = parts[0].size // (share * BLOCK)
     send = jax.ShapeDtypeStruct((half + extra, share, BLOCK), F32)
-    return pl.pallas_call(
-        second_kernel,
-        out_shape=[
-            jax.ShapeDtypeStruct(keep_a.shape, F32),
-            send,
-            send,
-            jax.ShapeDtypeStruct((extra, share, BLOCK), F32),
-        ],
-        in_specs=[IN_VMEM] * 5,
-        out_specs=[IN_VMEM] * 4,
-        cost_estimate=pl.CostEstimate(
-            flops=2 * keep_a.size, bytes_accessed=24 * keep_a.size, transcendentals=0
-        ),
-        compiler_params=limit(LIMIT_SMALL),
-        name="second_sums",
-    )(keep_a, recv_a, keep_b, recv_b, parts)
-
-
-def third_kernel(scale, count_ref, keep, recv_a, recv_b, over, share, recv_share, *rest):
-    *outs, weight, total, places = rest
+    weight_share = jax.ShapeDtypeStruct((extra, share, BLOCK), F32)
+    out_shape = [jax.ShapeDtypeStruct(keep_a.shape, F32), send, send, weight_share]
+    return small(second_kernel, out_shape, [keep_a, recv_a, keep_b, recv_b, *parts], "second_sums")
+
+
+def third_kernel(scale, count_ref, keep, recv_a, recv_b, share, recv_share, out, weight, places):
     half = keep.shape[1]
-    main = 2 * half
-    total[0:half] = keep[0] + recv_a[0:half]
-    total[half:main] = keep[1] + recv_b[0:half]
-    total[main:] = over[...]
     weight[...] = ((share[...] + recv_b[half:]) + (recv_a[half:] + recv_share[...])) * scale
     slot_places(count_ref, places)
-    rows = outs[0].shape[1]
-
-    @pl.loop(0, total.shape[0])
+
+    @pl.loop(0, out.shape[0])
     def _(slot):
-        for h, out in enumerate(outs):
-            out[slot] = total[places[slot], h * rows : (h + 1) * rows]
-
-
-def third_sums(halo_count, keep, recv_a, recv_b, over, share, recv_share, scale):
-    _, half, rows, _ = keep.shape
-    slots = 2 * half + over.shape[0]
-    return pl.pallas_call(
+        place = places[slot]
+
+        @pl.when(place < half)
+        def _():
+            out[slot] = keep[0, place] + recv_a[place]
+
+        @pl.when((place >= half) & (place < 2 * half))
+        def _():
+            out[slot] = keep[1, place - half] + recv_b[place - half]
+
+        @pl.when(place >= 2 * half)
+        def _():
+            out[slot] = jnp.zeros_like(out[slot])
+
+
+def third_sums(halo_count, keep, recv_a, recv_b, share, recv_share, slots, scale):
+    return small(
         functools.partial(third_kernel, scale),
-        out_shape=[jax.ShapeDtypeStruct((slots, rows // PARTS, BLOCK), F32)] * PARTS
-        + [jax.ShapeDtypeStruct(share.shape, F32)],
-        in_specs=[IN_SMEM] + [IN_VMEM] * 6,
-        out_specs=[IN_VMEM] * (PARTS + 1),
-        scratch_shapes=[pltpu.VMEM((slots, rows, BLOCK), F32), pltpu.SMEM((slots,), jnp.int32)],
-        cost_estimate=pl.CostEstimate(
-            flops=keep.size, bytes_accessed=16 * keep.size, transcendentals=0
-        ),
-        compiler_params=limit(LIMIT_SMALL),
-        name="third_sums",
-    )(halo_count, keep, recv_a, recv_b, over, share, recv_share)
-
-
-def small(kernel, out_shape, args, name, specs=None, out_specs=None):
+        [
+            jax.ShapeDtypeStruct((slots,) + keep.shape[2:], F32),
+            jax.ShapeDtypeStruct(share.shape, F32),
+        ],
+        [halo_count, keep, recv_a, recv_b, share, recv_share],
+        "third_sums",
+        [IN_SMEM] + [IN_VMEM] * 5,
+        scratch=[pltpu.SMEM((slots,), jnp.int32)],
+    )
+
+
+def small(kernel, out_shape, args, name, specs=None, scratch=()):
     size = max(x.size for x in args)
     return pl.pallas_call(
         kernel,
         out_shape=out_shape,
         in_specs=specs or [IN_VMEM] * len(args),
-        out_specs=out_specs or jax.tree.map(lambda _: IN_VMEM, out_shape),
+        out_specs=jax.tree.map(lambda _: IN_VMEM, out_shape),
+        scratch_shapes=scratch,
         cost_estimate=pl.CostEstimate(flops=size, bytes_accessed=12 * size, transcendentals=0),
         compiler_params=limit(LIMIT_SMALL),
         name=name,
@@ -361,56 +346,88 @@
         copy(whole, neigh_grad)
 
 
-def add_kernel(one, two, after, out):
-    del after
-    out[...] = one[...] + two[...]
-
-
-def place_kernel(count_ref, target_ref, arrived, out):
+def scatter_kernel(axis_of, count, *rest):
+    terms = rest[:count]
+    outs = rest[-4:]
+    me = axis_of(lax.axis_index("group"))
+    for away, out in enumerate(outs):
+        at = lax.rem(me + away, 4)
+        total = terms[0][at]
+        for term in terms[1:]:
+            total += term[at]
+        out[...] = total
+
+
+def scatter(axis_of, terms, name, after=()):
+    piece = jax.ShapeDtypeStruct(terms[0].shape[1:], F32)
+    return small(
+        functools.partial(scatter_kernel, axis_of, len(terms)),
+        [piece] * 4,
+        [*terms, *after],
+        name,
+        [IN_VMEM] * len(terms) + [IN_SMEM] * len(after),
+    )
+
+
+def place_kernel(count_ref, target_ref, arrived, send, *keeps):
+    core, _, _ = whereabouts()
+    chip = lax.axis_index("local") // 2
     group = lax.axis_index("group")
     sources = count_ref.shape[0]
     capacity = arrived.shape[0] // sources
-    out[...] = jnp.zeros_like(out)
+    blocks = send.shape[1]
+    for out in (send, *keeps):
+        out[...] = jnp.zeros_like(out)
 
     @pl.loop(0, sources)
     def _(source):
         for j in range(capacity):
-
-            @pl.when(j < count_ref[source, group])
+            target = target_ref[source, group * capacity + j]
+            live = j < count_ref[source, group]
+            member = target // blocks
+            block = target - member * blocks
+            away = (member // 2 - chip + 4) % 4
+            mine = member % 2 == core
+
+            @pl.when(live & jnp.logical_not(mine))
             def _():
-                out[target_ref[source, group * capacity + j]] += arrived[source * capacity + j]
-
-
-def place(halo_count, halo_target, arrived, group_blocks):
-    return pl.pallas_call(
-        place_kernel,
-        out_shape=jax.ShapeDtypeStruct((group_blocks,) + arrived.shape[1:], F32),
-        in_specs=[IN_SMEM] * 2 + [IN_VMEM],
-        out_specs=IN_VMEM,
-        cost_estimate=pl.CostEstimate(
-            flops=arrived.size, bytes_accessed=12 * arrived.size, transcendentals=0
-        ),
-        compiler_params=limit(LIMIT_SMALL),
-        name="place",
-    )(halo_count, halo_target, arrived)
+                send[away, block] += arrived[source * capacity + j]
+
+            for k, keep in enumerate(keeps):
+
+                @pl.when(live & mine & (away == k))
+                def _():
+                    keep[block] += arrived[source * capacity + j]
+
+
+def place(halo_count, halo_target, arrived, blocks):
+    keep = jax.ShapeDtypeStruct((blocks,) + arrived.shape[1:], F32)
+    send = jax.ShapeDtypeStruct((4,) + keep.shape, F32)
+    specs = [IN_SMEM, IN_SMEM, IN_VMEM]
+    return small(
+        place_kernel, [send] + [keep] * 4, [halo_count, halo_target, arrived], "place", specs
+    )
 
 
 def finish_kernel(base, other_local, own_local, *rest):
     *received, out, total, rows, sems = rest
     core, _, _ = whereabouts()
+    chip = lax.axis_index("local") // 2
     blocks, width, _ = other_local.shape
-    members, _, part, _ = received[0].shape
-    share = part * len(received)
+    share = received[0].shape[1]
     own = pl.ds(pl.multiple_of(core * width, width), width)
     other = pl.ds(pl.multiple_of((1 - core) * width, width), width)
     copies = []
     for b in range(blocks):
         total[b, own] = own_local[b]
         total[b, other] = other_local[b]
-        for member in range(members):
-            start = (member % 2) * width + QUARTER[member // 2] * share
-            for h, some in enumerate(received):
-                total[b, start + h * part : start + (h + 1) * part] += some[member, b]
+        for k, some in enumerate(received):
+            source = lax.rem(chip - k // 2 + 4, 4)
+            side = source // 2
+            quarter = side * 2 + lax.rem(source + side, 2)
+            first = core if k % 2 == 0 else 1 - core
+            start = pl.multiple_of(first * width + quarter * share, share)
+            total[b, pl.ds(start, share)] += some[b]
         at = slice(b * BLOCK, (b + 1) * BLOCK)
         rows[at] = base[at] + total[b].T
         copy = pltpu.make_async_copy(rows.at[at], out.at[at], sems.at[b])
@@ -459,18 +476,20 @@
     groups = lax.axis_size("group")
     members = lax.axis_size("local")
     slot_count = halo_target.shape[1]
-    over = slot_count - MAIN
-    member = lax.axis_index("local")
+    dead = slot_count - MAIN
     swap = [(i, i ^ 1) for i in range(members)]
     pairs = [(i, i ^ 2) for i in range(members)]
     across = [(i, members - 2 - (i - i % 2) + i % 2) for i in range(members)]
-
-    pre_grad, other_local, other_over, send = tile_sums(
-        tile_col, halo_count, w_neigh, tile_vals, MAIN, over, preact=preact, grad_out=grad_out
+    along_x = [[(i, (i + 2 * k) % members) for i in range(members)] for k in range(4)]
+    along_y = [[(i, (i + 4 * k) % groups) for i in range(groups)] for k in range(4)]
+    along_z = [[(i, i // 4 * 4 + (i + k) % 4) for i in range(groups)] for k in range(4)]
+
+    pre_grad, other_local, send = tile_sums(
+        tile_col, halo_count, w_neigh, tile_vals, MAIN, dead, preact=preact, grad_out=grad_out
     )
     recv = lax.ppermute(send, "local", swap)
-    own_local, own_over, flag, keep_a, send_a, keep_b, send_b = tile_sums(
-        tile_col, halo_count, w_neigh, tile_vals, MAIN, over, pre_grad=pre_grad, recv=recv
+    own_local, flag, keep_a, send_a, keep_b, send_b = tile_sums(
+        tile_col, halo_count, w_neigh, tile_vals, MAIN, dead, pre_grad=pre_grad, recv=recv
     )
     recv_a = lax.ppermute(send_a, "local", pairs)
     recv_b = lax.ppermute(send_b, "local", across)
@@ -482,55 +501,37 @@
     neigh_term = lax.dot_general(
         aggregated, pre_grad, contract, precision=high, preferred_element_type=F32
     )
-    pieces = jax.ShapeDtypeStruct(
-        (groups, width // BLOCK, width // groups, BLOCK), F32
-    )
+    pieces = jax.ShapeDtypeStruct((groups, width // BLOCK, width // groups, BLOCK), F32)
     stay, leave = small(sort_kernel, [pieces] * 2, [self_term, neigh_term], "sort_terms")
-    mine = small(
-        add_kernel,
-        pieces,
-        [stay, lax.ppermute(leave, "local", swap), flag],
-        "add_terms",
-        [IN_VMEM, IN_VMEM, IN_SMEM],
-    )
-    parts = lax.all_to_all(mine, "group", split_axis=0, concat_axis=0, tiled=True)
-
-    keep, send_a, send_b, share = second_sums(keep_a, recv_a, keep_b, recv_b, parts)
+    by_y = (4, groups // 4) + pieces.shape[1:]
+    stay, leave = stay.reshape(by_y), lax.ppermute(leave, "local", swap).reshape(by_y)
+    mine, *sends = scatter(lambda g: g // 4, [stay, leave], "sum_cores", [flag])
+    terms = [mine] + [
+        lax.ppermute(some, "group", along_y[k + 1]) for k, some in enumerate(sends)
+    ]
+    mine, *sends = scatter(lambda g: lax.rem(g, 4), terms, "sum_y")
+    terms = [mine] + [
+        lax.ppermute(some, "group", along_z[k + 1]) for k, some in enumerate(sends)
+    ]
+
+    keep, send_a, send_b, share = second_sums(keep_a, recv_a, keep_b, recv_b, terms)
     recv_a = lax.ppermute(send_a, "local", across)
     recv_b = lax.ppermute(send_b, "local", pairs)
-    recv_share = lax.ppermute(share, "local", [(i, i ^ 4) for i in range(members)])
-
-    def more():
-        sums = own_over + lax.ppermute(other_over, "local", swap)
-        shares = sums.reshape(over, 4, -1, BLOCK)
-        quarters = jnp.array(QUARTER, dtype=jnp.int32)
-        chip = member // 2
-        total = lax.dynamic_index_in_dim(shares, quarters[chip], 1, keepdims=False)
-        for away in range(1, 4):
-            theirs = lax.dynamic_index_in_dim(
-                shares, quarters[(chip + away) % 4], 1, keepdims=False
-            )
-            steps = [(i, (i + 2 * away) % members) for i in range(members)]
-            total = total + lax.ppermute(theirs, "local", steps)
-        return total
-
-    def none():
-        return jnp.zeros((over,) + share.shape[1:], F32)
-
-    most = jnp.max(jnp.sum(halo_count, axis=1))
-    over_share = lax.cond(most > MAIN, more, none)
+    recv_share = lax.ppermute(share, "local", along_x[2])
     scale = float(node_rows * groups * members) ** (-0.5)
-    *shares, weight_share = third_sums(
-        halo_count, keep, recv_a, recv_b, over_share, share, recv_share, scale
-    )
-    arrived = [
-        lax.all_to_all(some, "group", split_axis=0, concat_axis=0, tiled=True) for some in shares
-    ]
+    shares, weight_share = third_sums(
+        halo_count, keep, recv_a, recv_b, share, recv_share, slot_count, scale
+    )
+    arrived = lax.all_to_all(shares, "group", split_axis=0, concat_axis=0, tiled=True)
+    send, *keeps = place(halo_count, halo_target, arrived, blocks)
+    swapped = lax.ppermute(send, "local", swap)
     received = []
-    for some in arrived:
-        placed = place(halo_count, halo_target, some, blocks * members)
-        some = lax.all_to_all(placed, "local", split_axis=0, concat_axis=0, tiled=True)
-        received.append(some.reshape((members, blocks) + some.shape[1:]))
+    for k in range(4):
+        pair = [keeps[k], swapped[k]]
+        if k > 0:
+            pair = [lax.ppermute(some, "local", along_x[k]) for some in pair]
+        received += pair
+
     whole = lax.all_gather(weight_share, "group", tiled=True).reshape(pieces.shape)
     other = lax.ppermute(whole, "local", swap)
     square = jax.ShapeDtypeStruct(self_term.shape, F32)

time: 188 us -> 162 us (0.86)
  local copies, waits for them, and re-layouts: 23.6 us -> 1.51 us
  Pallas kernels: 31.9 us -> 27 us
  blocking collectives: 14.8 us -> 19.5 us
  waiting for transfers between devices: 53.9 us -> 56.9 us
  starting transfers between devices: 36.5 us -> 33.9 us
    ppermute x2 -> x15, waiting for transfers between devices: 8.74 us -> 40.3 us  [the longest x6 15.8 us: on_device(): pair = [lax.ppermute(some, 'local', along_x[k]) for some in pair]]
    all_to_all x4 -> x0, starting transfers between devices: 25.6 us -> none  [the longest x2 14.1 us: on_device(): lax.all_to_all(placed, 'local', split_axis=0, concat_axis=0, tiled=True)]
    ppermute x2 -> x15, starting transfers between devices: 2.35 us -> 26.1 us  [the longest x6 6.62 us: on_device(): pair = [lax.ppermute(some, 'local', along_x[k]) for some in pair]]
    unnamed x64 -> x26, local copies, waits for them, and re-layouts: 22.9 us -> 0.26 us
    all_to_all x4 -> x0, waiting for transfers between devices: 18.6 us -> none  [the longest x2 11.9 us: on_device(): lax.all_to_all(placed, 'local', split_axis=0, concat_axis=0, tiled=True)]
    ppermute x1, waiting for transfers between devices: 17.4 us -> 0.01 us  [on_device(): recv_a = lax.ppermute(send_a, 'local', pairs)]
    all_gather x1, waiting for transfers between devices: 7.92 us -> 16 us  [on_device(): lax.all_gather(weight_share, 'group', tiled=True).reshape(pieces.shape)]
    pallas_call x4 -> x0, Pallas kernels: 7.47 us -> none  [the longest x2 4.68 us: place(): pl.pallas_call(place_kernel, out_shape=jax.ShapeDtypeStruct((group_blocks...]
  transfers between devices with their start and end apart: 13 -> 22, of which waited for: 7 -> 11; matrix products, arithmetic and copies ran while one was open for 6% -> 6% of each run, Pallas kernels for 9% -> 8%
where the time goes in v6:
time: 162 us
  waiting for transfers between devices  56.9 us (35%)
  starting transfers between devices  33.9 us (21%)
  Pallas kernels  27 us (17%)
  blocking collectives  19.5 us (12%)
  between operations  14.3 us (9%)
  matrix products  8.69 us (5%)
    all_to_all x1, blocking collectives, on_device(): lax.all_to_all(shares, 'group', split_axis=0, concat_axis=0, tiled=True)  19.5 us
    pallas_call x2, Pallas kernels, tile_sums(): pl.pallas_call(functools.partial(tile_kernel, own, blocks, main, over), o...  16.6 us
    all_gather x1, waiting for transfers between devices, on_device(): lax.all_gather(weight_share, 'group', tiled=True).reshape(pieces.shape)  16 us
    ppermute x6, waiting for transfers between devices, on_device(): pair = [lax.ppermute(some, 'local', along_x[k]) for some in pair]  15.8 us
    ppermute x1, waiting for transfers between devices, on_device(): recv_share = lax.ppermute(share, 'local', along_x[2])  11 us
    ppermute x3, waiting for transfers between devices, on_device(): lax.ppermute(some, 'group', along_y[k + 1])  10.2 us
    pallas_call x7, Pallas kernels, small(): pl.pallas_call(kernel, out_shape=out_shape, in_specs=specs or [IN_VMEM] *...  8.45 us
    ppermute x6, starting transfers between devices, on_device(): pair = [lax.ppermute(some, 'local', along_x[k]) for some in pair]  6.62 us
  transfers between devices with their start and end apart: 22, of which 11 were waited for; matrix products, arithmetic and copies ran while one was open for 6% of the time, Pallas kernels for 8%

profile of v6, /device:TPU:1, one launch (start us, length us, event | category | flops | bytes accessed | tf_op | source)
XLA Modules:
  0.0 161.8 jit_solution(17689238800098834227)
XLA Ops:
  7.2 9.3 %other_tile_sums.1 = (f32[1024,512]{1,0:T(8,128)}, f32[8,256,128]{2,1,0:T(8,128)}, f32[30,256,128]{2,1,0:T(8,128)}) custom-call(s32[64]{0:T(128)} %col_ref.3, s32[16,16]{1,0:T(8,128)} %count_ref.7, f32[1024,512]{1,0:T(8,128)} %rest_0_.1, f32[1024,512]{1,0:T(8,128)} %rest_1_.2, f32[512,512]{1,0:T(8,128)} %rest_1_.3, f32[64,128,128]{2,1,0:T(8,128)} %rest_2_.3), custom_call_target="tpu_custom_call" | custom-call | flops 2415919104 | bytes 14680064 | tf_op jit(solution)/shard_map/other_tile_sums/pallas_call | solution.py:206
  16.5 1.5 collective-permute-start
  18.0 3.6 %convolution_bitcast_fusion.neigh_term = f32[512,512]{1,0:T(8,128)S(1)} fusion(f32[1024,512]{1,0:T(8,128)} %get-tuple-element.35.rest_0_, f32[1024,512]{1,0:T(8,128)S(1)} %copy-done), kind=kOutput, calls=%fused_computation | convolution fusion | flops 1610612736 | bytes 5242880 | tf_op jit(solution)/shard_map/dot_general | solution.py:501
  21.6 1.9 %convolution_bitcast_fusion.1.self_term = f32[512,512]{1,0:T(8,128)S(1)} fusion(f32[1024,512]{1,0:T(8,128)S(1)} %copy-done.1, f32[1024,512]{1,0:T(8,128)S(1)} %copy-done.12), kind=kOutput, calls=%fused_computation.1 | convolution fusion | flops 1610612736 | bytes 5242880 | tf_op jit(solution)/shard_map/dot_general | solution.py:498
  24.8 7.4 %own_tile_sums.1 = (f32[8,256,128]{2,1,0:T(8,128)S(1)}, s32[1]{0:T(128)}, f32[2,15,64,128]{3,2,1,0:T(8,128)S(1)}, f32[2,15,64,128]{3,2,1,0:T(8,128)S(1)}, f32[2,...) custom-call(s32[64]{0:T(128)S(1)} %copy-done.11, s32[16,16]{1,0:T(8,128)S(1)} %copy-done.9, ...), custom_call_target="tpu_custom_call" | custom-call | flops 2415919104 | bytes 14680064 | tf_op jit(solution)/shard_map/own_tile_sums/pallas_call | solution.py:206
  32.2 1.4 collective-permute-start.1
  33.6 1.8 %collective-permute-start.2 = (f32[2,15,64,128]{3,2,1,0:T(8,128)S(1)}, f32[2,15,64,128]{3,2,1,0:T(8,128)S(1)}, u32[]{:S(2)}, u32[]{:S(2)}) collective-permute-start(f32[2,15,64,128]{3,2,1,0:T(8,128)S(1)} %get-tuple-element.42), channel_id=1, source_target_pairs={{0,6},{1,7},{2,4},{3,5},{4,2},{5,3},{6,0},{7,1},{8,14},{9,15},{10,... | collective-permute-start | bytes 2949128 | tf_op jit(solution)/shard_map/ppermute | solution.py:495
  36.1 1.4 collective-permute-start.4
  37.4 2.6 %collective-permute-start.5 = (f32[4,4,32,128]{3,2,1,0:T(8,128)S(1)}, f32[4,4,32,128]{3,2,1,0:T(8,128)S(1)}, u32[]{:S(2)}, u32[]{:S(2)}) collective-permute-start(f32[4,4,32,128]{3,2,1,0:T(8,128)S(1)} %get-tuple-element.48), channel_id=1, source_target_pairs={{0,64},{8,72},{16,80},{24,88},{32,96},{40,104},{48,112},{56,120},{... | collective-permute-start | bytes 786440 | tf_op jit(solution)/shard_map/ppermute | solution.py:510
  41.1 3.4 %collective-permute-done.4.rest_1_ = f32[4,4,32,128]{3,2,1,0:T(8,128)S(1)} collective-permute-done((f32[4,4,32,128]{3,2,1,0:T(8,128)S(1)}, f32[4,4,32,128]{3,2,1,0:T(8,128)S(1)}, u32[]{:S(2)}, u32[]{:S(2)}) %collective-permute-start.4) | collective-permute-done | bytes 262176 | tf_op jit(solution)/shard_map/ppermute | solution.py:510
  44.6 6.7 %collective-permute-done.5.rest_2_ = f32[4,4,32,128]{3,2,1,0:T(8,128)S(1)} collective-permute-done((f32[4,4,32,128]{3,2,1,0:T(8,128)S(1)}, f32[4,4,32,128]{3,2,1,0:T(8,128)S(1)}, u32[]{:S(2)}, u32[]{:S(2)}) %collective-permute-start.5) | collective-permute-done | bytes 262176 | tf_op jit(solution)/shard_map/ppermute | solution.py:510
  51.4 1.7 %collective-permute-start.7 = (f32[4,32,128]{2,1,0:T(8,128)S(1)}, f32[4,32,128]{2,1,0:T(8,128)S(1)}, u32[]{:S(2)}, u32[]{:S(2)}) collective-permute-start(f32[4,32,128]{2,1,0:T(8,128)S(1)} %get-tuple-element.51), channel_id=1, source_target_pairs={{0,8},{8,16},{16,24},{24,0},{32,40},{40,48},{48,56},{56,32},{64,72... | collective-permute-start | bytes 196616 | tf_op jit(solution)/shard_map/ppermute | solution.py:514
  53.1 3.3 %collective-permute-start.8 = (f32[4,32,128]{2,1,0:T(8,128)S(1)}, f32[4,32,128]{2,1,0:T(8,128)S(1)}, u32[]{:S(2)}, u32[]{:S(2)}) collective-permute-start(f32[4,32,128]{2,1,0:T(8,128)S(1)} %get-tuple-element.52), channel_id=1, source_target_pairs={{0,16},{8,24},{16,0},{24,8},{32,48},{40,56},{48,32},{56,40},{64,80... | collective-permute-start | bytes 196616 | tf_op jit(solution)/shard_map/ppermute | solution.py:514
  57.1 1.7 %collective-permute-done.8.rest_2_ = f32[4,32,128]{2,1,0:T(8,128)S(1)} collective-permute-done((f32[4,32,128]{2,1,0:T(8,128)S(1)}, f32[4,32,128]{2,1,0:T(8,128)S(1)}, u32[]{:S(2)}, u32[]{:S(2)}) %collective-permute-start.8) | collective-permute-done | bytes 65568 | tf_op jit(solution)/shard_map/ppermute | solution.py:514
  58.8 1.5 collective-permute-done.9.rest_3_
  61.6 3.0 %collective-permute-start.12 = (f32[2,64,128]{2,1,0:T(8,128)S(1)}, f32[2,64,128]{2,1,0:T(8,128)S(1)}, u32[]{:S(2)}, u32[]{:S(2)}) collective-permute-start(f32[2,64,128]{2,1,0:T(8,128)S(1)} %get-tuple-element.57.share), channel_id=1, source_target_pairs={{0,4},{1,5},{2,6},{3,7},{4,0},{5,1},{6,2},{7,3},{8,12},{9,13},{10,... | collective-permute-start | bytes 196616 | tf_op jit(solution)/shard_map/ppermute | solution.py:520
  64.6 11.0 %collective-permute-done.12.recv_share = f32[2,64,128]{2,1,0:T(8,128)S(1)} collective-permute-done((f32[2,64,128]{2,1,0:T(8,128)S(1)}, f32[2,64,128]{2,1,0:T(8,128)S(1)}, u32[]{:S(2)}, u32[]{:S(2)}) %collective-permute-start.12) | collective-permute-done | bytes 65568 | tf_op jit(solution)/shard_map/ppermute | solution.py:520
  75.6 2.3 %third_sums.1 = (f32[32,64,128]{2,1,0:T(8,128)S(1)}, f32[2,64,128]{2,1,0:T(8,128)}) custom-call(s32[16,16]{1,0:T(8,128)S(1)} %copy-done.9, f32[2,15,64,128]{3,2,1,0:T(8,128)S(1)} %get-tuple-element.54.keep, f32[17,64,128]{2,1,0:T(8,128)S(1)} %collective-permute-done.10.recv_a, f32[17,64,128]{2,1,0:T(8,128)S(1)} %collective-permute-done.11.recv_b, ...), custom_call_target="tpu_custom_call" | custom-call | flops 245760 | bytes 2949120 | tf_op jit(solution)/shard_map/third_sums/pallas_call | solution.py:295
  77.9 19.5 %all_to_all.5.arrived = f32[32,64,128]{2,1,0:T(8,128)S(1)} all-to-all(f32[32,64,128]{2,1,0:T(8,128)S(1)} %get-tuple-element.58), channel_id=1, replica_groups=mesh['group'=16,'local'=8] {'group'}, dimensions={0} | all-to-all | bytes 2097152 | tf_op jit(solution)/shard_map/all_to_all | solution.py:525
  97.4 3.6 %place.1 = (f32[4,8,64,128]{3,2,1,0:T(8,128)}, f32[8,64,128]{2,1,0:T(8,128)S(1)}, f32[8,64,128]{2,1,0:T(8,128)S(1)}, f32[8,64,128]{2,1,0:T(8,128)S(1)}, f32[8,64,128]{2,1,0:T(8,128)S(1)}) custom-call(s32[16,16]{1,0:T(8,128)S(1)} %copy-done.9, s32[16,32]{1,0:T(8,128)S(1)} %copy-done.10, f32[32,64,128]{2,1,0:T(8,128)S(1)} %all_to_all.5.arrived), custom_call_target="tpu_custom_call" | custom-call | flops 262144 | bytes 3145728 | tf_op jit(solution)/shard_map/place/pallas_call | solution.py:295
  101.0 5.4 %collective-permute-start.13 = (f32[4,8,64,128]{3,2,1,0:T(8,128)}, f32[4,8,64,128]{3,2,1,0:T(8,128)}, u32[]{:S(2)}, u32[]{:S(2)}) collective-permute-start(f32[4,8,64,128]{3,2,1,0:T(8,128)} %get-tuple-element.60), channel_id=1, source_target_pairs={{0,1},{1,0},{2,3},{3,2},{4,5},{5,4},{6,7},{7,6},{8,9},{9,8},{10,11... | collective-permute-start | bytes 3145736 | tf_op jit(solution)/shard_map/ppermute | solution.py:527
  106.4 16.0 %all-gather.2.cloned.1.call-done = f32[32,64,128]{2,1,0:T(8,128)} async-done(((f32[2,64,128]{2,1,0:T(8,128)}), f32[32,64,128]{2,1,0:T(8,128)}) %all-gather.2.cloned.1.call-update) | async-done | bytes 1048592 | tf_op jit(solution)/shard_map/all_gather | solution.py:535
  122.4 2.1 %collective-permute-start.20 = (f32[16,4,32,128]{3,2,1,0:T(8,128)}, f32[16,4,32,128]{3,2,1,0:T(8,128)S(1)}, u32[]{:S(2)}, u32[]{:S(2)}) collective-permute-start(f32[16,4,32,128]{3,2,1,0:T(8,128)} %bitcast.23), channel_id=1, source_target_pairs={{0,1},{1,0},{2,3},{3,2},{4,5},{5,4},{6,7},{7,6},{8,9},{9,8},{10,11... | collective-permute-start | bytes 3145736 | tf_op jit(solution)/shard_map/ppermute | solution.py:536
  125.8 2.4 %collective-permute-start.16 = (f32[8,64,128]{2,1,0:T(8,128)S(1)}, f32[8,64,128]{2,1,0:T(8,128)S(1)}, u32[]{:S(2)}, u32[]{:S(2)}) collective-permute-start(f32[8,64,128]{2,1,0:T(8,128)S(1)} %get-tuple-element.62), channel_id=1, source_target_pairs={{0,4},{1,5},{2,6},{3,7},{4,0},{5,1},{6,2},{7,3},{8,12},{9,13},{10,... | collective-permute-start | bytes 786440 | tf_op jit(solution)/shard_map/ppermute | solution.py:532
  131.0 2.8 %collective-permute-done.14.rest_2_ = f32[8,64,128]{2,1,0:T(8,128)S(1)} collective-permute-done((f32[8,64,128]{2,1,0:T(8,128)S(1)}, f32[8,64,128]{2,1,0:T(8,128)S(1)}, u32[]{:S(2)}, u32[]{:S(2)}) %collective-permute-start.14) | collective-permute-done | bytes 262176 | tf_op jit(solution)/shard_map/ppermute | solution.py:532
  133.7 1.5 collective-permute-start.17
  135.2 5.1 %collective-permute-done.16.rest_4_ = f32[8,64,128]{2,1,0:T(8,128)S(1)} collective-permute-done((f32[8,64,128]{2,1,0:T(8,128)S(1)}, f32[8,64,128]{2,1,0:T(8,128)S(1)}, u32[]{:S(2)}, u32[]{:S(2)}) %collective-permute-start.16) | collective-permute-done | bytes 262176 | tf_op jit(solution)/shard_map/ppermute | solution.py:532
  140.3 3.2 %fusion.base = f32[1024,512]{1,0:T(8,128)S(1)} fusion(f32[1024,512]{1,0:T(8,128)S(1)} %copy-done.2, f32[512,512]{1,0:T(8,128)} %param.14), kind=kOutput, calls=%fused_computation.6 | convolution fusion | flops 1610612736 | bytes 5242880 | tf_op jit(solution)/shard_map/dot_general | solution.py:540
  143.6 1.7 %collective-permute-done.15.rest_3_ = f32[8,64,128]{2,1,0:T(8,128)S(1)} collective-permute-done((f32[8,64,128]{2,1,0:T(8,128)S(1)}, f32[8,64,128]{2,1,0:T(8,128)S(1)}, u32[]{:S(2)}, u32[]{:S(2)}) %collective-permute-start.15) | collective-permute-done | bytes 262176 | tf_op jit(solution)/shard_map/ppermute | solution.py:532
  145.3 6.3 %collective-permute-done.17.rest_5_ = f32[8,64,128]{2,1,0:T(8,128)S(1)} collective-permute-done((f32[8,64,128]{2,1,0:T(8,128)S(1)}, f32[8,64,128]{2,1,0:T(8,128)S(1)}, u32[]{:S(2)}, u32[]{:S(2)}) %collective-permute-start.17) | collective-permute-done | bytes 262176 | tf_op jit(solution)/shard_map/ppermute | solution.py:532
  151.6 1.9 %finish.1 = f32[1024,512]{1,0:T(8,128)} custom-call(f32[1024,512]{1,0:T(8,128)S(1)} %fusion.base, f32[8,256,128]{2,1,0:T(8,128)S(1)} %copy-done.6, f32[8,256,128]{2,1,0:T(8,128)S(1)} %copy-done.8, f32[8,64,128]{2,1,0:T(8,128)S(1)} %get-tuple-element.59.rest_0_, f32[8,64,128]{2,1,0:T(8,128)S(1)} %get-tuple-element.70.rest_1_, ...), custom_call_target="tpu_custom_call" | custom-call | flops 1048576 | bytes 8388608 | tf_op jit(solution)/shard_map/finish/pallas_call | solution.py:443
  153.5 1.5 sort_grads.1
  (54 shorter events, 9.1 us)
Async XLA Ops:
  7.2 10.9 %copy-start = (f32[1024,512]{1,0:T(8,128)S(1)}, f32[1024,512]{1,0:T(8,128)}, u32[]{:S(2)}) copy-start(f32[1024,512]{1,0:T(8,128)} %param.11) | copy-start | bytes 6291460
  7.2 115.3 %all-gather.2.cloned.1.call-start = ((), (), s32[]{:S(2)}) async-start(), calls=%async_computation.1 | async-start | bytes 1114112 | tf_op jit(solution)/shard_map/all_gather | solution.py:535
  16.5 8.1 %collective-permute-start = (f32[30,256,128]{2,1,0:T(8,128)}, f32[30,256,128]{2,1,0:T(8,128)S(1)}, u32[]{:S(2)}, u32[]{:S(2)}) collective-permute-start(f32[30,256,128]{2,1,0:T(8,128)} %get-tuple-element.37), channel_id=1, source_target_pairs={{0,1},{1,0},{2,3},{3,2},{4,5},{5,4},{6,7},{7,6},{8,9},{9,8},{10,11... | collective-permute-start | bytes 11796488 | tf_op jit(solution)/shard_map/ppermute | solution.py:490
  18.0 3.6 %copy-start.1 = (f32[1024,512]{1,0:T(8,128)S(1)}, f32[1024,512]{1,0:T(8,128)}, u32[]{:S(2)}) copy-start(f32[1024,512]{1,0:T(8,128)} %get-tuple-element.35.rest_0_) | copy-start | bytes 6291460
  18.0 3.6 %copy-start.12 = (f32[1024,512]{1,0:T(8,128)S(1)}, f32[1024,512]{1,0:T(8,128)}, u32[]{:S(2)}) copy-start(f32[1024,512]{1,0:T(8,128)} %param.10) | copy-start | bytes 6291460
  21.6 3.0 %copy-start.3 = (f32[64,128,128]{2,1,0:T(8,128)S(1)}, f32[64,128,128]{2,1,0:T(8,128)}, u32[]{:S(2)}) copy-start(f32[64,128,128]{2,1,0:T(8,128)} %rest_2_.3) | copy-start | bytes 12582916
  23.7 11.7 %collective-permute-start.3 = (f32[16,4,32,128]{3,2,1,0:T(8,128)S(1)}, f32[16,4,32,128]{3,2,1,0:T(8,128)S(1)}, u32[]{:S(2)}, u32[]{:S(2)}) collective-permute-start(f32[16,4,32,128]{3,2,1,0:T(8,128)S(1)} %get-tuple-element.44), channel_id=1, source_target_pairs={{0,1},{1,0},{2,3},{3,2},{4,5},{5,4},{6,7},{7,6},{8,9},{9,8},{10,11... | collective-permute-start | bytes 3145736 | tf_op jit(solution)/shard_map/ppermute | solution.py:507
  32.2 28.4 %copy-start.7 = (f32[8,256,128]{2,1,0:T(8,128)}, f32[8,256,128]{2,1,0:T(8,128)S(1)}, u32[]{:S(2)}) copy-start(f32[8,256,128]{2,1,0:T(8,128)S(1)} %get-tuple-element.38.own_local) | copy-start | bytes 3145732
  32.2 28.2 %collective-permute-start.1 = (f32[2,15,64,128]{3,2,1,0:T(8,128)S(1)}, f32[2,15,64,128]{3,2,1,0:T(8,128)S(1)}, u32[]{:S(2)}, u32[]{:S(2)}) collective-permute-start(f32[2,15,64,128]{3,2,1,0:T(8,128)S(1)} %get-tuple-element.40), channel_id=1, source_target_pairs={{0,2},{1,3},{2,0},{3,1},{4,6},{5,7},{6,4},{7,5},{8,10},{9,11},{10,... | collective-permute-start | bytes 2949128 | tf_op jit(solution)/shard_map/ppermute | solution.py:494
  33.6 26.8 %collective-permute-start.2 = (f32[2,15,64,128]{3,2,1,0:T(8,128)S(1)}, f32[2,15,64,128]{3,2,1,0:T(8,128)S(1)}, u32[]{:S(2)}, u32[]{:S(2)}) collective-permute-start(f32[2,15,64,128]{3,2,1,0:T(8,128)S(1)} %get-tuple-element.42), channel_id=1, source_target_pairs={{0,6},{1,7},{2,4},{3,5},{4,2},{5,3},{6,0},{7,1},{8,14},{9,15},{10,... | collective-permute-start | bytes 2949128 | tf_op jit(solution)/shard_map/ppermute | solution.py:495
  36.1 8.5 %collective-permute-start.4 = (f32[4,4,32,128]{3,2,1,0:T(8,128)S(1)}, f32[4,4,32,128]{3,2,1,0:T(8,128)S(1)}, u32[]{:S(2)}, u32[]{:S(2)}) collective-permute-start(f32[4,4,32,128]{3,2,1,0:T(8,128)S(1)} %get-tuple-element.47), channel_id=1, source_target_pairs={{0,32},{8,40},{16,48},{24,56},{32,64},{40,72},{48,80},{56,88},{64,... | collective-permute-start | bytes 786440 | tf_op jit(solution)/shard_map/ppermute | solution.py:510
  37.4 13.9 %collective-permute-start.5 = (f32[4,4,32,128]{3,2,1,0:T(8,128)S(1)}, f32[4,4,32,128]{3,2,1,0:T(8,128)S(1)}, u32[]{:S(2)}, u32[]{:S(2)}) collective-permute-start(f32[4,4,32,128]{3,2,1,0:T(8,128)S(1)} %get-tuple-element.48), channel_id=1, source_target_pairs={{0,64},{8,72},{16,80},{24,88},{32,96},{40,104},{48,112},{56,120},{... | collective-permute-start | bytes 786440 | tf_op jit(solution)/shard_map/ppermute | solution.py:510
  40.1 11.2 %collective-permute-start.6 = (f32[4,4,32,128]{3,2,1,0:T(8,128)S(1)}, f32[4,4,32,128]{3,2,1,0:T(8,128)S(1)}, u32[]{:S(2)}, u32[]{:S(2)}) collective-permute-start(f32[4,4,32,128]{3,2,1,0:T(8,128)S(1)} %get-tuple-element.49), channel_id=1, source_target_pairs={{0,96},{8,104},{16,112},{24,120},{32,0},{40,8},{48,16},{56,24},{64... | collective-permute-start | bytes 786440 | tf_op jit(solution)/shard_map/ppermute | solution.py:510
  51.4 5.8 %collective-permute-start.7 = (f32[4,32,128]{2,1,0:T(8,128)S(1)}, f32[4,32,128]{2,1,0:T(8,128)S(1)}, u32[]{:S(2)}, u32[]{:S(2)}) collective-permute-start(f32[4,32,128]{2,1,0:T(8,128)S(1)} %get-tuple-element.51), channel_id=1, source_target_pairs={{0,8},{8,16},{16,24},{24,0},{32,40},{40,48},{48,56},{56,32},{64,72... | collective-permute-start | bytes 196616 | tf_op jit(solution)/shard_map/ppermute | solution.py:514
  53.1 5.8 %collective-permute-start.8 = (f32[4,32,128]{2,1,0:T(8,128)S(1)}, f32[4,32,128]{2,1,0:T(8,128)S(1)}, u32[]{:S(2)}, u32[]{:S(2)}) collective-permute-start(f32[4,32,128]{2,1,0:T(8,128)S(1)} %get-tuple-element.52), channel_id=1, source_target_pairs={{0,16},{8,24},{16,0},{24,8},{32,48},{40,56},{48,32},{56,40},{64,80... | collective-permute-start | bytes 196616 | tf_op jit(solution)/shard_map/ppermute | solution.py:514
  56.4 4.0 %collective-permute-start.9 = (f32[4,32,128]{2,1,0:T(8,128)S(1)}, f32[4,32,128]{2,1,0:T(8,128)S(1)}, u32[]{:S(2)}, u32[]{:S(2)}) collective-permute-start(f32[4,32,128]{2,1,0:T(8,128)S(1)} %get-tuple-element.53), channel_id=1, source_target_pairs={{0,24},{8,0},{16,8},{24,16},{32,56},{40,32},{48,40},{56,48},{64,88... | collective-permute-start | bytes 196616 | tf_op jit(solution)/shard_map/ppermute | solution.py:514
  60.6 14.9 %collective-permute-start.10 = (f32[17,64,128]{2,1,0:T(8,128)S(1)}, f32[17,64,128]{2,1,0:T(8,128)S(1)}, u32[]{:S(2)}, u32[]{:S(2)}) collective-permute-start(f32[17,64,128]{2,1,0:T(8,128)S(1)} %get-tuple-element.55), channel_id=1, source_target_pairs={{0,6},{1,7},{2,4},{3,5},{4,2},{5,3},{6,0},{7,1},{8,14},{9,15},{10,... | collective-permute-start | bytes 1671176 | tf_op jit(solution)/shard_map/ppermute | solution.py:518
  61.5 14.0 %collective-permute-start.11 = (f32[17,64,128]{2,1,0:T(8,128)S(1)}, f32[17,64,128]{2,1,0:T(8,128)S(1)}, u32[]{:S(2)}, u32[]{:S(2)}) collective-permute-start(f32[17,64,128]{2,1,0:T(8,128)S(1)} %get-tuple-element.56), channel_id=1, source_target_pairs={{0,2},{1,3},{2,0},{3,1},{4,6},{5,7},{6,4},{7,5},{8,10},{9,11},{10,... | collective-permute-start | bytes 1671176 | tf_op jit(solution)/shard_map/ppermute | solution.py:519
  61.6 14.0 %collective-permute-start.12 = (f32[2,64,128]{2,1,0:T(8,128)S(1)}, f32[2,64,128]{2,1,0:T(8,128)S(1)}, u32[]{:S(2)}, u32[]{:S(2)}) collective-permute-start(f32[2,64,128]{2,1,0:T(8,128)S(1)} %get-tuple-element.57.share), channel_id=1, source_target_pairs={{0,4},{1,5},{2,6},{3,7},{4,0},{5,1},{6,2},{7,3},{8,12},{9,13},{10,... | collective-permute-start | bytes 196616 | tf_op jit(solution)/shard_map/ppermute | solution.py:520
  75.6 21.9 %copy-start.10 = (s32[16,32]{1,0:T(8,128)S(1)}, s32[16,32]{1,0:T(8,128)}, u32[]{:S(2)}) copy-start(s32[16,32]{1,0:T(8,128)} %target_ref.1) | copy-start | bytes 6148
  101.0 28.3 %collective-permute-start.13 = (f32[4,8,64,128]{3,2,1,0:T(8,128)}, f32[4,8,64,128]{3,2,1,0:T(8,128)}, u32[]{:S(2)}, u32[]{:S(2)}) collective-permute-start(f32[4,8,64,128]{3,2,1,0:T(8,128)} %get-tuple-element.60), channel_id=1, source_target_pairs={{0,1},{1,0},{2,3},{3,2},{4,5},{5,4},{6,7},{7,6},{8,9},{9,8},{10,11... | collective-permute-start | bytes 3145736 | tf_op jit(solution)/shard_map/ppermute | solution.py:527
  122.4 17.9 %copy-start.2 = (f32[1024,512]{1,0:T(8,128)S(1)}, f32[1024,512]{1,0:T(8,128)}, u32[]{:S(2)}) copy-start(f32[1024,512]{1,0:T(8,128)} %get-tuple-element.35.rest_0_) | copy-start | bytes 6291460
  122.4 31.1 %collective-permute-start.20 = (f32[16,4,32,128]{3,2,1,0:T(8,128)}, f32[16,4,32,128]{3,2,1,0:T(8,128)S(1)}, u32[]{:S(2)}, u32[]{:S(2)}) collective-permute-start(f32[16,4,32,128]{3,2,1,0:T(8,128)} %bitcast.23), channel_id=1, source_target_pairs={{0,1},{1,0},{2,3},{3,2},{4,5},{5,4},{6,7},{7,6},{8,9},{9,8},{10,11... | collective-permute-start | bytes 3145736 | tf_op jit(solution)/shard_map/ppermute | solution.py:536
  124.6 9.1 %collective-permute-start.14 = (f32[8,64,128]{2,1,0:T(8,128)S(1)}, f32[8,64,128]{2,1,0:T(8,128)S(1)}, u32[]{:S(2)}, u32[]{:S(2)}) collective-permute-start(f32[8,64,128]{2,1,0:T(8,128)S(1)} %get-tuple-element.61), channel_id=1, source_target_pairs={{0,2},{1,3},{2,4},{3,5},{4,6},{5,7},{6,0},{7,1},{8,10},{9,11},{10,... | collective-permute-start | bytes 786440 | tf_op jit(solution)/shard_map/ppermute | solution.py:532
  125.8 14.5 %collective-permute-start.16 = (f32[8,64,128]{2,1,0:T(8,128)S(1)}, f32[8,64,128]{2,1,0:T(8,128)S(1)}, u32[]{:S(2)}, u32[]{:S(2)}) collective-permute-start(f32[8,64,128]{2,1,0:T(8,128)S(1)} %get-tuple-element.62), channel_id=1, source_target_pairs={{0,4},{1,5},{2,6},{3,7},{4,0},{5,1},{6,2},{7,3},{8,12},{9,13},{10,... | collective-permute-start | bytes 786440 | tf_op jit(solution)/shard_map/ppermute | solution.py:532
  128.2 15.4 %collective-permute-start.18 = (f32[8,64,128]{2,1,0:T(8,128)S(1)}, f32[8,64,128]{2,1,0:T(8,128)S(1)}, u32[]{:S(2)}, u32[]{:S(2)}) collective-permute-start(f32[8,64,128]{2,1,0:T(8,128)S(1)} %get-tuple-element.63), channel_id=1, source_target_pairs={{0,6},{1,7},{2,0},{3,1},{4,2},{5,3},{6,4},{7,5},{8,14},{9,15},{10,... | collective-permute-start | bytes 786440 | tf_op jit(solution)/shard_map/ppermute | solution.py:532
  130.6 14.7 %collective-permute-start.15 = (f32[8,64,128]{2,1,0:T(8,128)S(1)}, f32[8,64,128]{2,1,0:T(8,128)S(1)}, u32[]{:S(2)}, u32[]{:S(2)}) collective-permute-start(f32[8,64,128]{2,1,0:T(8,128)S(1)} %get-tuple-element.69), channel_id=1, source_target_pairs={{0,2},{1,3},{2,4},{3,5},{4,6},{5,7},{6,0},{7,1},{8,10},{9,11},{10,... | collective-permute-start | bytes 786440 | tf_op jit(solution)/shard_map/ppermute | solution.py:532
  133.7 17.8 %collective-permute-start.17 = (f32[8,64,128]{2,1,0:T(8,128)S(1)}, f32[8,64,128]{2,1,0:T(8,128)S(1)}, u32[]{:S(2)}, u32[]{:S(2)}) collective-permute-start(f32[8,64,128]{2,1,0:T(8,128)S(1)} %get-tuple-element.68), channel_id=1, source_target_pairs={{0,4},{1,5},{2,6},{3,7},{4,0},{5,1},{6,2},{7,3},{8,12},{9,13},{10,... | collective-permute-start | bytes 786440 | tf_op jit(solution)/shard_map/ppermute | solution.py:532
  140.3 11.2 %copy-start.6 = (f32[8,256,128]{2,1,0:T(8,128)S(1)}, f32[8,256,128]{2,1,0:T(8,128)}, u32[]{:S(2)}) copy-start(f32[8,256,128]{2,1,0:T(8,128)} %get-tuple-element.36.other_local) | copy-start | bytes 3145732
  140.3 11.2 %copy-start.8 = (f32[8,256,128]{2,1,0:T(8,128)S(1)}, f32[8,256,128]{2,1,0:T(8,128)}, u32[]{:S(2)}) copy-start(f32[8,256,128]{2,1,0:T(8,128)} %copy-done.7) | copy-start | bytes 3145732
  140.3 11.2 %collective-permute-start.19 = (f32[8,64,128]{2,1,0:T(8,128)S(1)}, f32[8,64,128]{2,1,0:T(8,128)S(1)}, u32[]{:S(2)}, u32[]{:S(2)}) collective-permute-start(f32[8,64,128]{2,1,0:T(8,128)S(1)} %get-tuple-element.67), channel_id=1, source_target_pairs={{0,6},{1,7},{2,0},{3,1},{4,2},{5,3},{6,4},{7,5},{8,14},{9,15},{10,... | collective-permute-start | bytes 786440 | tf_op jit(solution)/shard_map/ppermute | solution.py:532
  151.6 1.9 %copy-start.5 = (f32[32,64,128]{2,1,0:T(8,128)S(1)}, f32[32,64,128]{2,1,0:T(8,128)}, u32[]{:S(2)}) copy-start(f32[32,64,128]{2,1,0:T(8,128)} %all-gather.2.cloned.1.call-done) | copy-start | bytes 3145732
  (3 other events, 3.9 us)
Sparse Core Ops, SparseCore 0:
  78.0 44.3 all-gather.1

commit v7 on v6

--- a/solution.py
+++ b/solution.py
@@ -29,9 +29,9 @@
 
 def whereabouts():
     member = lax.axis_index("local")
-    chip = member // 2
-    side = chip // 2
-    return member % 2, side, (chip + side) % 2
+    chip = member >> 1
+    side = chip >> 1
+    return member & 1, side, (chip + side) & 1
 
 
 def slot_places(count_ref, places):
@@ -224,73 +224,57 @@
 
 IN_VMEM = pl.BlockSpec(memory_space=pltpu.VMEM)
 IN_SMEM = pl.BlockSpec(memory_space=pltpu.SMEM)
-
-
-def second_kernel(keep_a, recv_a, keep_b, recv_b, *rest):
-    *parts, keep, send_a, send_b, share = rest
+ANYWHERE = pl.BlockSpec(memory_space=pl.ANY)
+
+
+def second_kernel(keep_a, recv_a, keep_b, recv_b, after, keep, send_a, send_b):
+    del after
     _, p, q = whereabouts()
-    half = keep_a.shape[1]
-    rows = parts[0].shape[1]
-    for k in range(parts[0].shape[0]):
-        at = (k * rows // share.shape[1], pl.ds(k * rows % share.shape[1], rows))
-        total = parts[0][k]
-        for part in parts[1:]:
-            total += part[k]
-        share[at] = total
-    send_a[0:half] = keep_a[1 - p] + recv_a[1 - p]
-    send_b[0:half] = keep_b[1 - q] + recv_b[1 - q]
-    send_a[half:] = share[...]
-    send_b[half:] = share[...]
+    send_a[...] = keep_a[1 - p] + recv_a[1 - p]
+    send_b[...] = keep_b[1 - q] + recv_b[1 - q]
     keep[0] = keep_a[p] + recv_a[p]
     keep[1] = keep_b[q] + recv_b[q]
 
 
-def second_sums(keep_a, recv_a, keep_b, recv_b, parts):
-    _, half, share, _ = keep_a.shape
-    extra = parts[0].size // (share * BLOCK)
-    send = jax.ShapeDtypeStruct((half + extra, share, BLOCK), F32)
-    weight_share = jax.ShapeDtypeStruct((extra, share, BLOCK), F32)
-    out_shape = [jax.ShapeDtypeStruct(keep_a.shape, F32), send, send, weight_share]
-    return small(second_kernel, out_shape, [keep_a, recv_a, keep_b, recv_b, *parts], "second_sums")
-
-
-def third_kernel(scale, count_ref, keep, recv_a, recv_b, share, recv_share, out, weight, places):
-    half = keep.shape[1]
-    weight[...] = ((share[...] + recv_b[half:]) + (recv_a[half:] + recv_share[...])) * scale
+def second_sums(keep_a, recv_a, keep_b, recv_b, after):
+    send = jax.ShapeDtypeStruct(keep_a.shape[1:], F32)
+    out_shape = [jax.ShapeDtypeStruct(keep_a.shape, F32), send, send]
+    return small(
+        second_kernel,
+        out_shape,
+        [keep_a, recv_a, keep_b, recv_b, after],
+        "second_sums",
+        [IN_VMEM] * 4 + [ANYWHERE],
+    )
+
+
+def third_kernel(count_ref, keep, recv_a, recv_b, after, out, total, places):
+    del after
+    half = recv_a.shape[0]
+    main = 2 * half
+    total[0:half] = keep[0] + recv_a[...]
+    total[half:main] = keep[1] + recv_b[...]
+    total[main:] = jnp.zeros_like(total[main:])
     slot_places(count_ref, places)
-
-    @pl.loop(0, out.shape[0])
-    def _(slot):
-        place = places[slot]
-
-        @pl.when(place < half)
-        def _():
-            out[slot] = keep[0, place] + recv_a[place]
-
-        @pl.when((place >= half) & (place < 2 * half))
-        def _():
-            out[slot] = keep[1, place - half] + recv_b[place - half]
-
-        @pl.when(place >= 2 * half)
-        def _():
-            out[slot] = jnp.zeros_like(out[slot])
-
-
-def third_sums(halo_count, keep, recv_a, recv_b, share, recv_share, slots, scale):
+    for slot in range(out.shape[0]):
+        out[slot] = total[places[slot]]
+
+
+def third_sums(halo_count, keep, recv_a, recv_b, after, slots):
+    shape = (slots,) + keep.shape[2:]
     return small(
-        functools.partial(third_kernel, scale),
-        [
-            jax.ShapeDtypeStruct((slots,) + keep.shape[2:], F32),
-            jax.ShapeDtypeStruct(share.shape, F32),
-        ],
-        [halo_count, keep, recv_a, recv_b, share, recv_share],
+        third_kernel,
+        jax.ShapeDtypeStruct(shape, F32),
+        [halo_count, keep, recv_a, recv_b, after],
         "third_sums",
-        [IN_SMEM] + [IN_VMEM] * 5,
-        scratch=[pltpu.SMEM((slots,), jnp.int32)],
-    )
-
-
-def small(kernel, out_shape, args, name, specs=None, scratch=()):
+        [IN_SMEM] + [IN_VMEM] * 3 + [ANYWHERE],
+        scratch=[pltpu.VMEM(shape, F32), pltpu.SMEM((slots,), jnp.int32)],
+    )
+
+
+def small(
+    kernel, out_shape, args, name, specs=None, scratch=(), mebibytes=LIMIT_SMALL, flops=None
+):
     size = max(x.size for x in args)
     return pl.pallas_call(
         kernel,
@@ -298,8 +282,10 @@
         in_specs=specs or [IN_VMEM] * len(args),
         out_specs=jax.tree.map(lambda _: IN_VMEM, out_shape),
         scratch_shapes=scratch,
-        cost_estimate=pl.CostEstimate(flops=size, bytes_accessed=12 * size, transcendentals=0),
-        compiler_params=limit(LIMIT_SMALL),
+        cost_estimate=pl.CostEstimate(
+            flops=flops or size, bytes_accessed=12 * size, transcendentals=0
+        ),
+        compiler_params=limit(mebibytes),
         name=name,
     )(*args)
 
@@ -351,7 +337,7 @@
     outs = rest[-4:]
     me = axis_of(lax.axis_index("group"))
     for away, out in enumerate(outs):
-        at = lax.rem(me + away, 4)
+        at = (me + away) & 3
         total = terms[0][at]
         for term in terms[1:]:
             total += term[at]
@@ -369,50 +355,85 @@
     )
 
 
-def place_kernel(count_ref, target_ref, arrived, send, *keeps):
+def sum_kernel(*rest):
+    *terms, _, out = rest
+    total = terms[0][...]
+    for term in terms[1:]:
+        total += term[...]
+    out[...] = total
+
+
+def chips_kernel(scale, mine, pair, far_one, far_two, out):
+    out[...] = ((mine[...] + pair[...]) + (far_one[...] + far_two[...])) * scale
+
+
+def late_kernel(whole, *rest):
+    rest[-1][...] = whole[...]
+
+
+def place_kernel(count_ref, target_ref, arrived, after, send, *keeps):
+    del after
     core, _, _ = whereabouts()
-    chip = lax.axis_index("local") // 2
+    chip = lax.axis_index("local") >> 1
     group = lax.axis_index("group")
     sources = count_ref.shape[0]
     capacity = arrived.shape[0] // sources
     blocks = send.shape[1]
+    shift = blocks.bit_length() - 1
     for out in (send, *keeps):
         out[...] = jnp.zeros_like(out)
 
     @pl.loop(0, sources)
     def _(source):
+        count = count_ref[source, group]
         for j in range(capacity):
             target = target_ref[source, group * capacity + j]
-            live = j < count_ref[source, group]
-            member = target // blocks
-            block = target - member * blocks
-            away = (member // 2 - chip + 4) % 4
-            mine = member % 2 == core
-
-            @pl.when(live & jnp.logical_not(mine))
+            member = lax.shift_right_logical(target, shift)
+            block = target & (blocks - 1)
+            away = (lax.shift_right_logical(member, 1) - chip) & 3
+            mine = (member & 1) == core
+
+            @pl.when(j < count)
             def _():
-                send[away, block] += arrived[source * capacity + j]
-
-            for k, keep in enumerate(keeps):
-
-                @pl.when(live & mine & (away == k))
+                @pl.when(jnp.logical_not(mine))
                 def _():
-                    keep[block] += arrived[source * capacity + j]
-
-
-def place(halo_count, halo_target, arrived, blocks):
+                    send[away, block] += arrived[source * capacity + j]
+
+                @pl.when(mine)
+                def _():
+                    for k, keep in enumerate(keeps):
+
+                        @pl.when(away == k)
+                        def _():
+                            keep[block] += arrived[source * capacity + j]
+
+
+def place(halo_count, halo_target, arrived, after, blocks):
     keep = jax.ShapeDtypeStruct((blocks,) + arrived.shape[1:], F32)
     send = jax.ShapeDtypeStruct((4,) + keep.shape, F32)
-    specs = [IN_SMEM, IN_SMEM, IN_VMEM]
-    return small(
-        place_kernel, [send] + [keep] * 4, [halo_count, halo_target, arrived], "place", specs
-    )
+    specs = [IN_SMEM, IN_SMEM, IN_VMEM, ANYWHERE]
+    args = [halo_count, halo_target, arrived, after]
+    return small(place_kernel, [send] + [keep] * 4, args, "place", specs)
+
+
+def self_kernel(pre_grad, weight, after, out):
+    del after
+    contract = (((1,), (1,)), ((), ()))
+    weight_high, weight_low = split(weight[...])
+    rows = out.shape[0] // 4
+    for i in range(4):
+        at = slice(i * rows, (i + 1) * rows)
+        high, low = split(pre_grad[at])
+        total = lax.dot_general(high, weight_high, contract, preferred_element_type=F32)
+        total += lax.dot_general(high, weight_low, contract, preferred_element_type=F32)
+        total += lax.dot_general(low, weight_high, contract, preferred_element_type=F32)
+        out[at] = total
 
 
 def finish_kernel(base, other_local, own_local, *rest):
     *received, out, total, rows, sems = rest
     core, _, _ = whereabouts()
-    chip = lax.axis_index("local") // 2
+    chip = lax.axis_index("local") >> 1
     blocks, width, _ = other_local.shape
     share = received[0].shape[1]
     own = pl.ds(pl.multiple_of(core * width, width), width)
@@ -422,9 +443,9 @@
         total[b, own] = own_local[b]
         total[b, other] = other_local[b]
         for k, some in enumerate(received):
-            source = lax.rem(chip - k // 2 + 4, 4)
-            side = source // 2
-            quarter = side * 2 + lax.rem(source + side, 2)
+            source = (chip - k // 2) & 3
+            side = source >> 1
+            quarter = side * 2 + ((source + side) & 1)
             first = core if k % 2 == 0 else 1 - core
             start = pl.multiple_of(first * width + quarter * share, share)
             total[b, pl.ds(start, share)] += some[b]
@@ -505,25 +526,36 @@
     stay, leave = small(sort_kernel, [pieces] * 2, [self_term, neigh_term], "sort_terms")
     by_y = (4, groups // 4) + pieces.shape[1:]
     stay, leave = stay.reshape(by_y), lax.ppermute(leave, "local", swap).reshape(by_y)
-    mine, *sends = scatter(lambda g: g // 4, [stay, leave], "sum_cores", [flag])
+    mine, *sends = scatter(lambda g: g >> 2, [stay, leave], "sum_cores", [flag])
     terms = [mine] + [
         lax.ppermute(some, "group", along_y[k + 1]) for k, some in enumerate(sends)
     ]
-    mine, *sends = scatter(lambda g: lax.rem(g, 4), terms, "sum_y")
+    mine, *sends = scatter(lambda g: g & 3, terms, "sum_y")
     terms = [mine] + [
         lax.ppermute(some, "group", along_z[k + 1]) for k, some in enumerate(sends)
     ]
 
-    keep, send_a, send_b, share = second_sums(keep_a, recv_a, keep_b, recv_b, terms)
+    keep, send_a, send_b = second_sums(keep_a, recv_a, keep_b, recv_b, mine)
+    share_shape = jax.ShapeDtypeStruct(mine.shape, F32)
+    share = small(sum_kernel, share_shape, [*terms, keep], "sum_z", [IN_VMEM] * 4 + [ANYWHERE])
     recv_a = lax.ppermute(send_a, "local", across)
     recv_b = lax.ppermute(send_b, "local", pairs)
-    recv_share = lax.ppermute(share, "local", along_x[2])
+    terms = [share] + [lax.ppermute(share, "local", p) for p in (pairs, across, along_x[2])]
     scale = float(node_rows * groups * members) ** (-0.5)
-    shares, weight_share = third_sums(
-        halo_count, keep, recv_a, recv_b, share, recv_share, slot_count, scale
+    share = small(functools.partial(chips_kernel, scale), share_shape, terms, "sum_chips")
+    whole = lax.all_gather(share, "group", tiled=True)
+    shares = third_sums(halo_count, keep, recv_a, recv_b, share, slot_count)
+    base = small(
+        self_kernel,
+        jax.ShapeDtypeStruct(pre_grad.shape, F32),
+        [pre_grad, w_self, shares],
+        "self_rows",
+        [IN_VMEM, IN_VMEM, ANYWHERE],
+        mebibytes=16,
+        flops=6 * pre_grad.size * width,
     )
     arrived = lax.all_to_all(shares, "group", split_axis=0, concat_axis=0, tiled=True)
-    send, *keeps = place(halo_count, halo_target, arrived, blocks)
+    send, *keeps = place(halo_count, halo_target, arrived, base, blocks)
     swapped = lax.ppermute(send, "local", swap)
     received = []
     for k in range(4):
@@ -532,12 +564,17 @@
             pair = [lax.ppermute(some, "local", along_x[k]) for some in pair]
         received += pair
 
-    whole = lax.all_gather(weight_share, "group", tiled=True).reshape(pieces.shape)
+    whole = small(
+        late_kernel,
+        pieces,
+        [whole.reshape(pieces.shape), *received[2:]],
+        "late",
+        [IN_VMEM] + [ANYWHERE] * 6,
+    )
     other = lax.ppermute(whole, "local", swap)
     square = jax.ShapeDtypeStruct(self_term.shape, F32)
     self_grad, neigh_grad = small(grads_kernel, [square] * 2, [whole, other], "sort_grads")
 
-    base = jnp.dot(pre_grad, w_self.T, precision=high, preferred_element_type=F32)
     node_grad = finish(base, other_local, own_local, received)
     return (node_grad, self_grad, neigh_grad)
 

time: 162 us -> 151 us (0.932)
  blocking collectives: 19.5 us -> 0 us
  local copies, waits for them, and re-layouts: 1.51 us -> 10.2 us
  waiting for transfers between devices: 56.9 us -> 49.7 us
  starting transfers between devices: 33.9 us -> 40.5 us
  matrix products: 8.69 us -> 5.46 us
  Pallas kernels: 27 us -> 30.1 us
    all_to_all x1 -> x0, blocking collectives: 19.5 us -> none  [on_device(): lax.all_to_all(shares, 'group', split_axis=0, concat_axis=0, tiled=True)]
    unnamed x26 -> x40, local copies, waits for them, and re-layouts: 0.26 us -> 9.24 us
    ppermute x1 -> x3, waiting for transfers between devices: 11 us -> 3.51 us  [on_device(): lax.ppermute(share, 'local', p)]
    ppermute x6, waiting for transfers between devices: 15.8 us -> 8.5 us  [on_device(): pair = [lax.ppermute(some, 'local', along_x[k]) for some in pair]]
    all_to_all x0 -> x1, starting transfers between devices: none -> 6.56 us  [on_device(): lax.all_to_all(shares, 'group', split_axis=0, concat_axis=0, tiled=True)]
    all_to_all x0 -> x1, waiting for transfers between devices: none -> 5.34 us  [on_device(): lax.all_to_all(shares, 'group', split_axis=0, concat_axis=0, tiled=True)]
    all_gather x1, waiting for transfers between devices: 16 us -> 11 us  [on_device(): whole = lax.all_gather(share, 'group', tiled=True)]
    ppermute x1, waiting for transfers between devices: 0.01 us -> 4.01 us  [on_device(): recv_a = lax.ppermute(send_a, 'local', pairs)]
  transfers between devices with their start and end apart: 22 -> 25, of which waited for: 11 -> 17; matrix products, arithmetic and copies ran while one was open for 6% -> 4% of each run, Pallas kernels for 8% -> 10%
where the time goes in v7:
time: 151 us; the launch traced here: 150 us
  waiting for transfers between devices  49.7 us (33%)
  starting transfers between devices  40.5 us (27%)
  Pallas kernels  30.1 us (20%)
  between operations  14.3 us (9%)
  local copies, waits for them, and re-layouts  10.2 us (7%)
  matrix products  5.46 us (4%)
    pallas_call x2, Pallas kernels, tile_sums(): pl.pallas_call(functools.partial(tile_kernel, own, blocks, main, over), o...  16.6 us
    all_gather x1, waiting for transfers between devices, on_device(): whole = lax.all_gather(share, 'group', tiled=True)  11 us
    pallas_call x11, Pallas kernels, small(): pl.pallas_call(kernel, out_shape=out_shape, in_specs=specs or [IN_VMEM] *...  10.3 us
    ppermute x3, waiting for transfers between devices, on_device(): lax.ppermute(some, 'group', along_y[k + 1])  10.2 us
    unnamed x40, local copies, waits for them, and re-layouts  9.24 us
    ppermute x6, waiting for transfers between devices, on_device(): pair = [lax.ppermute(some, 'local', along_x[k]) for some in pair]  8.5 us
    all_to_all x1, starting transfers between devices, on_device(): lax.all_to_all(shares, 'group', split_axis=0, concat_axis=0, tiled=True)  6.56 us
    ppermute x1, starting transfers between devices, on_device(): swapped = lax.ppermute(send, 'local', swap)  6.02 us
  transfers between devices with their start and end apart: 25, of which 17 were waited for; matrix products, arithmetic and copies ran while one was open for 4% of the time, Pallas kernels for 10%

profile of v7, /device:TPU:1, one launch (start us, length us, event | category | flops | bytes accessed | tf_op | source)
XLA Modules:
  0.0 150.3 jit_solution(17384129288049721872)
XLA Ops:
  7.2 9.3 %other_tile_sums.1 = (f32[1024,512]{1,0:T(8,128)}, f32[8,256,128]{2,1,0:T(8,128)}, f32[30,256,128]{2,1,0:T(8,128)}) custom-call(s32[64]{0:T(128)} %col_ref.3, s32[16,16]{1,0:T(8,128)} %count_ref.7, f32[1024,512]{1,0:T(8,128)} %rest_0_.1, f32[1024,512]{1,0:T(8,128)} %rest_1_.2, f32[512,512]{1,0:T(8,128)} %rest_1_.3, f32[64,128,128]{2,1,0:T(8,128)} %rest_2_.3), custom_call_target="tpu_custom_call" | custom-call | flops 2415919104 | bytes 14680064 | tf_op jit(solution)/shard_map/other_tile_sums/pallas_call | solution.py:206
  16.5 1.5 collective-permute-start
  18.0 3.6 %convolution_bitcast_fusion.neigh_term = f32[512,512]{1,0:T(8,128)S(1)} fusion(f32[1024,512]{1,0:T(8,128)} %get-tuple-element.32.rest_0_.pre_grad, f32[1024,512]{1,0:T(8,128)S(1)} %copy-done), kind=kOutput, calls=%fused_computation | convolution fusion | flops 1610612736 | bytes 5242880 | tf_op jit(solution)/shard_map/dot_general | solution.py:522
  21.6 1.9 %convolution_bitcast_fusion.1.self_term = f32[512,512]{1,0:T(8,128)S(1)} fusion(f32[1024,512]{1,0:T(8,128)S(1)} %copy-done.1, f32[1024,512]{1,0:T(8,128)S(1)} %copy-done.19), kind=kOutput, calls=%fused_computation.1 | convolution fusion | flops 1610612736 | bytes 5242880 | tf_op jit(solution)/shard_map/dot_general | solution.py:519
  24.8 7.3 %own_tile_sums.1 = (f32[8,256,128]{2,1,0:T(8,128)S(1)}, s32[1]{0:T(128)}, f32[2,15,64,128]{3,2,1,0:T(8,128)S(1)}, f32[2,15,64,128]{3,2,1,0:T(8,128)S(1)}, f32[2,...) custom-call(s32[64]{0:T(128)S(1)} %copy-done.18, s32[16,16]{1,0:T(8,128)S(1)} %copy-done.16, ...), custom_call_target="tpu_custom_call" | custom-call | flops 2415919104 | bytes 14680064 | tf_op jit(solution)/shard_map/own_tile_sums/pallas_call | solution.py:206
  32.1 1.4 collective-permute-start.1
  33.5 1.8 %collective-permute-start.2 = (f32[2,15,64,128]{3,2,1,0:T(8,128)S(1)}, f32[2,15,64,128]{3,2,1,0:T(8,128)S(1)}, u32[]{:S(2)}, u32[]{:S(2)}) collective-permute-start(f32[2,15,64,128]{3,2,1,0:T(8,128)S(1)} %get-tuple-element.37), channel_id=1, source_target_pairs={{0,6},{1,7},{2,4},{3,5},{4,2},{5,3},{6,0},{7,1},{8,14},{9,15},{10,... | collective-permute-start | bytes 2949128 | tf_op jit(solution)/shard_map/ppermute | solution.py:516
  37.5 2.6 %collective-permute-start.5 = (f32[4,4,32,128]{3,2,1,0:T(8,128)S(1)}, f32[4,4,32,128]{3,2,1,0:T(8,128)S(1)}, u32[]{:S(2)}, u32[]{:S(2)}) collective-permute-start(f32[4,4,32,128]{3,2,1,0:T(8,128)S(1)} %get-tuple-element.43), channel_id=1, source_target_pairs={{0,64},{8,72},{16,80},{24,88},{32,96},{40,104},{48,112},{56,120},{... | collective-permute-start | bytes 786440 | tf_op jit(solution)/shard_map/ppermute | solution.py:531
  41.2 3.4 %collective-permute-done.4.rest_1_ = f32[4,4,32,128]{3,2,1,0:T(8,128)S(1)} collective-permute-done((f32[4,4,32,128]{3,2,1,0:T(8,128)S(1)}, f32[4,4,32,128]{3,2,1,0:T(8,128)S(1)}, u32[]{:S(2)}, u32[]{:S(2)}) %collective-permute-start.4) | collective-permute-done | bytes 262176 | tf_op jit(solution)/shard_map/ppermute | solution.py:531
  44.6 6.7 %collective-permute-done.5.rest_2_ = f32[4,4,32,128]{3,2,1,0:T(8,128)S(1)} collective-permute-done((f32[4,4,32,128]{3,2,1,0:T(8,128)S(1)}, f32[4,4,32,128]{3,2,1,0:T(8,128)S(1)}, u32[]{:S(2)}, u32[]{:S(2)}) %collective-permute-start.5) | collective-permute-done | bytes 262176 | tf_op jit(solution)/shard_map/ppermute | solution.py:531
  51.4 4.0 %collective-permute-done.1.recv_a = f32[2,15,64,128]{3,2,1,0:T(8,128)S(1)} collective-permute-done((f32[2,15,64,128]{3,2,1,0:T(8,128)S(1)}, f32[2,15,64,128]{3,2,1,0:T(8,128)S(1)}, u32[]{:S(2)}, u32[]{:S(2)}) %collective-permute-start.1) | collective-permute-done | bytes 983072 | tf_op jit(solution)/shard_map/ppermute | solution.py:515
  55.4 2.2 %collective-permute-done.2.recv_b = f32[2,15,64,128]{3,2,1,0:T(8,128)S(1)} collective-permute-done((f32[2,15,64,128]{3,2,1,0:T(8,128)S(1)}, f32[2,15,64,128]{3,2,1,0:T(8,128)S(1)}, u32[]{:S(2)}, u32[]{:S(2)}) %collective-permute-start.2) | collective-permute-done | bytes 983072 | tf_op jit(solution)/shard_map/ppermute | solution.py:516
  58.7 1.8 %collective-permute-start.7 = (f32[15,64,128]{2,1,0:T(8,128)}, f32[15,64,128]{2,1,0:T(8,128)}, u32[]{:S(2)}, u32[]{:S(2)}) collective-permute-start(f32[15,64,128]{2,1,0:T(8,128)} %get-tuple-element.47), channel_id=1, source_target_pairs={{0,6},{1,7},{2,4},{3,5},{4,2},{5,3},{6,0},{7,1},{8,14},{9,15},{10,... | collective-permute-start | bytes 1474568 | tf_op jit(solution)/shard_map/ppermute | solution.py:541
  60.6 3.6 %collective-permute-start.10 = (f32[4,32,128]{2,1,0:T(8,128)S(1)}, f32[4,32,128]{2,1,0:T(8,128)S(1)}, u32[]{:S(2)}, u32[]{:S(2)}) collective-permute-start(f32[4,32,128]{2,1,0:T(8,128)S(1)} %get-tuple-element.50), channel_id=1, source_target_pairs={{0,16},{8,24},{16,0},{24,8},{32,48},{40,56},{48,32},{56,40},{64,80... | collective-permute-start | bytes 196616 | tf_op jit(solution)/shard_map/ppermute | solution.py:535
  65.8 1.9 %collective-permute-done.11.rest_3_ = f32[4,32,128]{2,1,0:T(8,128)S(1)} collective-permute-done((f32[4,32,128]{2,1,0:T(8,128)S(1)}, f32[4,32,128]{2,1,0:T(8,128)S(1)}, u32[]{:S(2)}, u32[]{:S(2)}) %collective-permute-start.11) | collective-permute-done | bytes 65568 | tf_op jit(solution)/shard_map/ppermute | solution.py:535
  67.7 1.6 %collective-permute-done.9.rest_1_ = f32[4,32,128]{2,1,0:T(8,128)S(1)} collective-permute-done((f32[4,32,128]{2,1,0:T(8,128)S(1)}, f32[4,32,128]{2,1,0:T(8,128)S(1)}, u32[]{:S(2)}, u32[]{:S(2)}) %collective-permute-start.9) | collective-permute-done | bytes 65568 | tf_op jit(solution)/shard_map/ppermute | solution.py:535
  74.8 1.4 collective-permute-done.14.far_two
  76.8 2.5 %third_sums.1.after = f32[32,64,128]{2,1,0:T(8,128)} custom-call(s32[16,16]{1,0:T(8,128)S(1)} %copy-done.16, f32[2,15,64,128]{3,2,1,0:T(8,128)S(1)} %get-tuple-element.46.rest_4_.keep, f32[15,64,128]{2,1,0:T(8,128)} %collective-permute-done.7.recv_a, f32[15,64,128]{2,1,0:T(8,128)} %collective-permute-done.8.recv_b, f32[4,32,128]{2,1,0:T(8,128)} %sum_chips.1.after), custom_call_target="tpu_custom_call" | custom-call | flops 245760 | bytes 2949120 | tf_op jit(solution)/shard_map/third_sums/pallas_call | solution.py:279
  79.3 6.6 %all-to-all-start = ((f32[32,64,128]{2,1,0:T(8,128)}), f32[32,64,128]{2,1,0:T(8,128)S(1)}, u32[]{:S(2)}, u32[]{:S(2)}) async-start(f32[32,64,128]{2,1,0:T(8,128)} %third_sums.1.after), calls=%async_computation | async-start | bytes 2097152 | tf_op jit(solution)/shard_map/all_to_all | solution.py:557
  86.7 1.6 %copy-done.2 = f32[1024,512]{1,0:T(8,128)S(1)} copy-done((f32[1024,512]{1,0:T(8,128)S(1)}, f32[1024,512]{1,0:T(8,128)}, u32[]{:S(2)}) %copy-start.2) | copy-done | bytes 2097176
  89.5 1.8 %self_rows.1.after.base = f32[1024,512]{1,0:T(8,128)S(1)} custom-call(f32[1024,512]{1,0:T(8,128)S(1)} %copy-done.2, f32[512,512]{1,0:T(8,128)S(1)} %copy-done.9, f32[32,64,128]{2,1,0:T(8,128)} %third_sums.1.after), custom_call_target="tpu_custom_call" | custom-call | flops 1610612736 | bytes 6291456 | tf_op jit(solution)/shard_map/self_rows/pallas_call | solution.py:279
  92.6 5.3 %all-to-all-done.arrived = f32[32,64,128]{2,1,0:T(8,128)S(1)} async-done(((f32[32,64,128]{2,1,0:T(8,128)}), f32[32,64,128]{2,1,0:T(8,128)S(1)}, u32[]{:S(2)}, u32[]{:S(2)}) %all-to-all-start) | async-done | bytes 1048608 | tf_op jit(solution)/shard_map/all_to_all | solution.py:557
  98.0 1.6 %copy-done.4 = f32[1024,512]{1,0:T(8,128)S(1)} copy-done((f32[1024,512]{1,0:T(8,128)S(1)}, f32[1024,512]{1,0:T(8,128)}, u32[]{:S(2)}) %copy-start.4) | copy-done | bytes 2097176
  99.6 1.7 %place.1 = (f32[4,8,64,128]{3,2,1,0:T(8,128)S(1)}, f32[8,64,128]{2,1,0:T(8,128)S(1)}, f32[8,64,128]{2,1,0:T(8,128)S(1)}, f32[8,64,128]{2,1,0:T(8,128)S(1)}, f32[8,64,128]{2,1,0:T(8,128)S(1)}) custom-call(s32[16,16]{1,0:T(8,128)S(1)} %copy-done.16, s32[16,32]{1,0:T(8,128)S(1)} %copy-done.17, f32[32,64,128]{2,1,0:T(8,128)S(1)} %all-to-all-done.arrived, ...), custom_call_target="tpu_custom_call" | custom-call | flops 524288 | bytes 6291456 | tf_op jit(solution)/shard_map/place/pallas_call | solution.py:279
  102.0 6.0 %collective-permute-start.15 = (f32[4,8,64,128]{3,2,1,0:T(8,128)S(1)}, f32[4,8,64,128]{3,2,1,0:T(8,128)S(1)}, u32[]{:S(2)}, u32[]{:S(2)}) collective-permute-start(f32[4,8,64,128]{3,2,1,0:T(8,128)S(1)} %get-tuple-element.55), channel_id=1, source_target_pairs={{0,1},{1,0},{2,3},{3,2},{4,5},{5,4},{6,7},{7,6},{8,9},{9,8},{10,11... | collective-permute-start | bytes 3145736 | tf_op jit(solution)/shard_map/ppermute | solution.py:559
  108.0 3.0 %collective-permute-start.18 = (f32[8,64,128]{2,1,0:T(8,128)S(1)}, f32[8,64,128]{2,1,0:T(8,128)S(1)}, u32[]{:S(2)}, u32[]{:S(2)}) collective-permute-start(f32[8,64,128]{2,1,0:T(8,128)S(1)} %get-tuple-element.57), channel_id=1, source_target_pairs={{0,4},{1,5},{2,6},{3,7},{4,0},{5,1},{6,2},{7,3},{8,12},{9,13},{10,... | collective-permute-start | bytes 786440 | tf_op jit(solution)/shard_map/ppermute | solution.py:564
  114.3 2.9 %collective-permute-done.16.rest_2_.rest_0_ = f32[8,64,128]{2,1,0:T(8,128)S(1)} collective-permute-done((f32[8,64,128]{2,1,0:T(8,128)S(1)}, f32[8,64,128]{2,1,0:T(8,128)S(1)}, u32[]{:S(2)}, u32[]{:S(2)}) %collective-permute-start.16) | collective-permute-done | bytes 262176 | tf_op jit(solution)/shard_map/ppermute | solution.py:564
  117.7 5.4 %collective-permute-done.18.rest_4_.rest_2_ = f32[8,64,128]{2,1,0:T(8,128)S(1)} collective-permute-done((f32[8,64,128]{2,1,0:T(8,128)S(1)}, f32[8,64,128]{2,1,0:T(8,128)S(1)}, u32[]{:S(2)}, u32[]{:S(2)}) %collective-permute-start.18) | collective-permute-done | bytes 262176 | tf_op jit(solution)/shard_map/ppermute | solution.py:564
  123.1 11.0 %all-gather.2.cloned.1.call-done = f32[64,32,128]{2,1,0:T(8,128)} async-done(((f32[4,32,128]{2,1,0:T(8,128)}), f32[64,32,128]{2,1,0:T(8,128)}) %all-gather.2.cloned.1.call-update) | async-done | bytes 1048592 | tf_op jit(solution)/shard_map/all_gather | solution.py:546
  135.9 1.7 %collective-permute-start.22 = (f32[16,4,32,128]{3,2,1,0:T(8,128)S(1)}, f32[16,4,32,128]{3,2,1,0:T(8,128)S(1)}, u32[]{:S(2)}, u32[]{:S(2)}) collective-permute-start(f32[16,4,32,128]{3,2,1,0:T(8,128)S(1)} %late.1.whole), channel_id=1, source_target_pairs={{0,1},{1,0},{2,3},{3,2},{4,5},{5,4},{6,7},{7,6},{8,9},{9,8},{10,11... | collective-permute-start | bytes 3145736 | tf_op jit(solution)/shard_map/ppermute | solution.py:574
  138.8 3.1 %finish.1 = f32[1024,512]{1,0:T(8,128)} custom-call(f32[1024,512]{1,0:T(8,128)S(1)} %copy-done.5, f32[8,256,128]{2,1,0:T(8,128)S(1)} %copy-done.11, f32[8,256,128]{2,1,0:T(8,128)S(1)} %copy-done.13, f32[8,64,128]{2,1,0:T(8,128)S(1)} %copy-done.15, f32[8,64,128]{2,1,0:T(8,128)S(1)} %copy-done.10, f32[8,64,128]{2,1,0:T(8,128)S(1)} %collective-permute-done.16.rest_2_.rest_0_, ...), custom_call_target="tpu_custom_call" | custom-call | flops 1048576 | bytes 8388608 | tf_op jit(solution)/shard_map/finish/pallas_call | solution.py:464
  142.0 1.5 sort_grads.1
  (76 shorter events, 24.3 us)
Async XLA Ops:
  7.2 10.8 %copy-start = (f32[1024,512]{1,0:T(8,128)S(1)}, f32[1024,512]{1,0:T(8,128)}, u32[]{:S(2)}) copy-start(f32[1024,512]{1,0:T(8,128)} %param.11) | copy-start | bytes 6291460
  16.5 8.1 %collective-permute-start = (f32[30,256,128]{2,1,0:T(8,128)}, f32[30,256,128]{2,1,0:T(8,128)S(1)}, u32[]{:S(2)}, u32[]{:S(2)}) collective-permute-start(f32[30,256,128]{2,1,0:T(8,128)} %get-tuple-element.33), channel_id=1, source_target_pairs={{0,1},{1,0},{2,3},{3,2},{4,5},{5,4},{6,7},{7,6},{8,9},{9,8},{10,11... | collective-permute-start | bytes 11796488 | tf_op jit(solution)/shard_map/ppermute | solution.py:511
  18.0 3.6 %copy-start.1 = (f32[1024,512]{1,0:T(8,128)S(1)}, f32[1024,512]{1,0:T(8,128)}, u32[]{:S(2)}) copy-start(f32[1024,512]{1,0:T(8,128)} %get-tuple-element.32.rest_0_.pre_grad) | copy-start | bytes 6291460
  18.0 3.6 %copy-start.19 = (f32[1024,512]{1,0:T(8,128)S(1)}, f32[1024,512]{1,0:T(8,128)}, u32[]{:S(2)}) copy-start(f32[1024,512]{1,0:T(8,128)} %param.10) | copy-start | bytes 6291460
  21.6 3.0 %copy-start.6 = (f32[64,128,128]{2,1,0:T(8,128)S(1)}, f32[64,128,128]{2,1,0:T(8,128)}, u32[]{:S(2)}) copy-start(f32[64,128,128]{2,1,0:T(8,128)} %rest_2_.3) | copy-start | bytes 12582916
  23.7 11.7 %collective-permute-start.3 = (f32[16,4,32,128]{3,2,1,0:T(8,128)S(1)}, f32[16,4,32,128]{3,2,1,0:T(8,128)S(1)}, u32[]{:S(2)}, u32[]{:S(2)}) collective-permute-start(f32[16,4,32,128]{3,2,1,0:T(8,128)S(1)} %get-tuple-element.39), channel_id=1, source_target_pairs={{0,1},{1,0},{2,3},{3,2},{4,5},{5,4},{6,7},{7,6},{8,9},{9,8},{10,11... | collective-permute-start | bytes 3145736 | tf_op jit(solution)/shard_map/ppermute | solution.py:528
  32.1 26.6 %copy-start.12 = (f32[8,256,128]{2,1,0:T(8,128)}, f32[8,256,128]{2,1,0:T(8,128)S(1)}, u32[]{:S(2)}) copy-start(f32[8,256,128]{2,1,0:T(8,128)S(1)} %get-tuple-element.53.own_local) | copy-start | bytes 3145732
  32.1 23.2 %collective-permute-start.1 = (f32[2,15,64,128]{3,2,1,0:T(8,128)S(1)}, f32[2,15,64,128]{3,2,1,0:T(8,128)S(1)}, u32[]{:S(2)}, u32[]{:S(2)}) collective-permute-start(f32[2,15,64,128]{3,2,1,0:T(8,128)S(1)} %get-tuple-element.35), channel_id=1, source_target_pairs={{0,2},{1,3},{2,0},{3,1},{4,6},{5,7},{6,4},{7,5},{8,10},{9,11},{10,... | collective-permute-start | bytes 2949128 | tf_op jit(solution)/shard_map/ppermute | solution.py:515
  33.5 24.1 %collective-permute-start.2 = (f32[2,15,64,128]{3,2,1,0:T(8,128)S(1)}, f32[2,15,64,128]{3,2,1,0:T(8,128)S(1)}, u32[]{:S(2)}, u32[]{:S(2)}) collective-permute-start(f32[2,15,64,128]{3,2,1,0:T(8,128)S(1)} %get-tuple-element.37), channel_id=1, source_target_pairs={{0,6},{1,7},{2,4},{3,5},{4,2},{5,3},{6,0},{7,1},{8,14},{9,15},{10,... | collective-permute-start | bytes 2949128 | tf_op jit(solution)/shard_map/ppermute | solution.py:516
  36.1 8.5 %collective-permute-start.4 = (f32[4,4,32,128]{3,2,1,0:T(8,128)S(1)}, f32[4,4,32,128]{3,2,1,0:T(8,128)S(1)}, u32[]{:S(2)}, u32[]{:S(2)}) collective-permute-start(f32[4,4,32,128]{3,2,1,0:T(8,128)S(1)} %get-tuple-element.42), channel_id=1, source_target_pairs={{0,32},{8,40},{16,48},{24,56},{32,64},{40,72},{48,80},{56,88},{64,... | collective-permute-start | bytes 786440 | tf_op jit(solution)/shard_map/ppermute | solution.py:531
  37.5 13.9 %collective-permute-start.5 = (f32[4,4,32,128]{3,2,1,0:T(8,128)S(1)}, f32[4,4,32,128]{3,2,1,0:T(8,128)S(1)}, u32[]{:S(2)}, u32[]{:S(2)}) collective-permute-start(f32[4,4,32,128]{3,2,1,0:T(8,128)S(1)} %get-tuple-element.43), channel_id=1, source_target_pairs={{0,64},{8,72},{16,80},{24,88},{32,96},{40,104},{48,112},{56,120},{... | collective-permute-start | bytes 786440 | tf_op jit(solution)/shard_map/ppermute | solution.py:531
  40.1 11.2 %collective-permute-start.6 = (f32[4,4,32,128]{3,2,1,0:T(8,128)S(1)}, f32[4,4,32,128]{3,2,1,0:T(8,128)S(1)}, u32[]{:S(2)}, u32[]{:S(2)}) collective-permute-start(f32[4,4,32,128]{3,2,1,0:T(8,128)S(1)} %get-tuple-element.44), channel_id=1, source_target_pairs={{0,96},{8,104},{16,112},{24,120},{32,0},{40,8},{48,16},{56,24},{64... | collective-permute-start | bytes 786440 | tf_op jit(solution)/shard_map/ppermute | solution.py:531
  58.7 18.1 %collective-permute-start.7 = (f32[15,64,128]{2,1,0:T(8,128)}, f32[15,64,128]{2,1,0:T(8,128)}, u32[]{:S(2)}, u32[]{:S(2)}) collective-permute-start(f32[15,64,128]{2,1,0:T(8,128)} %get-tuple-element.47), channel_id=1, source_target_pairs={{0,6},{1,7},{2,4},{3,5},{4,2},{5,3},{6,0},{7,1},{8,14},{9,15},{10,... | collective-permute-start | bytes 1474568 | tf_op jit(solution)/shard_map/ppermute | solution.py:541
  60.6 16.3 %collective-permute-start.8 = (f32[15,64,128]{2,1,0:T(8,128)}, f32[15,64,128]{2,1,0:T(8,128)}, u32[]{:S(2)}, u32[]{:S(2)}) collective-permute-start(f32[15,64,128]{2,1,0:T(8,128)} %get-tuple-element.48), channel_id=1, source_target_pairs={{0,2},{1,3},{2,0},{3,1},{4,6},{5,7},{6,4},{7,5},{8,10},{9,11},{10,... | collective-permute-start | bytes 1474568 | tf_op jit(solution)/shard_map/ppermute | solution.py:542
  60.6 5.3 %collective-permute-start.10 = (f32[4,32,128]{2,1,0:T(8,128)S(1)}, f32[4,32,128]{2,1,0:T(8,128)S(1)}, u32[]{:S(2)}, u32[]{:S(2)}) collective-permute-start(f32[4,32,128]{2,1,0:T(8,128)S(1)} %get-tuple-element.50), channel_id=1, source_target_pairs={{0,16},{8,24},{16,0},{24,8},{32,48},{40,56},{48,32},{56,40},{64,80... | collective-permute-start | bytes 196616 | tf_op jit(solution)/shard_map/ppermute | solution.py:535
  64.2 3.5 %collective-permute-start.11 = (f32[4,32,128]{2,1,0:T(8,128)S(1)}, f32[4,32,128]{2,1,0:T(8,128)S(1)}, u32[]{:S(2)}, u32[]{:S(2)}) collective-permute-start(f32[4,32,128]{2,1,0:T(8,128)S(1)} %get-tuple-element.51), channel_id=1, source_target_pairs={{0,24},{8,0},{16,8},{24,16},{32,56},{40,32},{48,40},{56,48},{64,88... | collective-permute-start | bytes 196616 | tf_op jit(solution)/shard_map/ppermute | solution.py:535
  64.6 4.7 %collective-permute-start.9 = (f32[4,32,128]{2,1,0:T(8,128)S(1)}, f32[4,32,128]{2,1,0:T(8,128)S(1)}, u32[]{:S(2)}, u32[]{:S(2)}) collective-permute-start(f32[4,32,128]{2,1,0:T(8,128)S(1)} %get-tuple-element.49), channel_id=1, source_target_pairs={{0,8},{8,16},{16,24},{24,0},{32,40},{40,48},{48,56},{56,32},{64,72... | collective-permute-start | bytes 196616 | tf_op jit(solution)/shard_map/ppermute | solution.py:535
  69.3 4.4 %collective-permute-start.12 = (f32[4,32,128]{2,1,0:T(8,128)S(1)}, f32[4,32,128]{2,1,0:T(8,128)S(1)}, u32[]{:S(2)}, u32[]{:S(2)}) collective-permute-start(f32[4,32,128]{2,1,0:T(8,128)S(1)} %sum_z.1.mine), channel_id=1, source_target_pairs={{0,2},{1,3},{2,0},{3,1},{4,6},{5,7},{6,4},{7,5},{8,10},{9,11},{10,... | collective-permute-start | bytes 196616 | tf_op jit(solution)/shard_map/ppermute | solution.py:543
  70.5 4.3 %collective-permute-start.13 = (f32[4,32,128]{2,1,0:T(8,128)S(1)}, f32[4,32,128]{2,1,0:T(8,128)S(1)}, u32[]{:S(2)}, u32[]{:S(2)}) collective-permute-start(f32[4,32,128]{2,1,0:T(8,128)S(1)} %sum_z.1.mine), channel_id=1, source_target_pairs={{0,6},{1,7},{2,4},{3,5},{4,2},{5,3},{6,0},{7,1},{8,14},{9,15},{10,... | collective-permute-start | bytes 196616 | tf_op jit(solution)/shard_map/ppermute | solution.py:543
  71.3 4.9 %collective-permute-start.14 = (f32[4,32,128]{2,1,0:T(8,128)S(1)}, f32[4,32,128]{2,1,0:T(8,128)S(1)}, u32[]{:S(2)}, u32[]{:S(2)}) collective-permute-start(f32[4,32,128]{2,1,0:T(8,128)S(1)} %sum_z.1.mine), channel_id=1, source_target_pairs={{0,4},{1,5},{2,6},{3,7},{4,0},{5,1},{6,2},{7,3},{8,12},{9,13},{10,... | collective-permute-start | bytes 196616 | tf_op jit(solution)/shard_map/ppermute | solution.py:543
  79.3 18.6 %all-to-all-start = ((f32[32,64,128]{2,1,0:T(8,128)}), f32[32,64,128]{2,1,0:T(8,128)S(1)}, u32[]{:S(2)}, u32[]{:S(2)}) async-start(f32[32,64,128]{2,1,0:T(8,128)} %third_sums.1.after), calls=%async_computation | async-start | bytes 2097152 | tf_op jit(solution)/shard_map/all_to_all | solution.py:557
  85.9 48.3 %all-gather.2.cloned.1.call-start = ((), (), s32[]{:S(2)}) async-start(), calls=%async_computation.1 | async-start | bytes 1114112 | tf_op jit(solution)/shard_map/all_gather | solution.py:546
  89.5 8.5 %copy-start.17 = (s32[16,32]{1,0:T(8,128)S(1)}, s32[16,32]{1,0:T(8,128)}, u32[]{:S(2)}) copy-start(s32[16,32]{1,0:T(8,128)} %target_ref.1) | copy-start | bytes 6148
  102.0 9.5 %collective-permute-start.15 = (f32[4,8,64,128]{3,2,1,0:T(8,128)S(1)}, f32[4,8,64,128]{3,2,1,0:T(8,128)S(1)}, u32[]{:S(2)}, u32[]{:S(2)}) collective-permute-start(f32[4,8,64,128]{3,2,1,0:T(8,128)S(1)} %get-tuple-element.55), channel_id=1, source_target_pairs={{0,1},{1,0},{2,3},{3,2},{4,5},{5,4},{6,7},{7,6},{8,9},{9,8},{10,11... | collective-permute-start | bytes 3145736 | tf_op jit(solution)/shard_map/ppermute | solution.py:559
  108.0 9.1 %collective-permute-start.16 = (f32[8,64,128]{2,1,0:T(8,128)S(1)}, f32[8,64,128]{2,1,0:T(8,128)S(1)}, u32[]{:S(2)}, u32[]{:S(2)}) collective-permute-start(f32[8,64,128]{2,1,0:T(8,128)S(1)} %get-tuple-element.56), channel_id=1, source_target_pairs={{0,2},{1,3},{2,4},{3,5},{4,6},{5,7},{6,0},{7,1},{8,10},{9,11},{10,... | collective-permute-start | bytes 786440 | tf_op jit(solution)/shard_map/ppermute | solution.py:564
  108.0 15.1 %collective-permute-start.18 = (f32[8,64,128]{2,1,0:T(8,128)S(1)}, f32[8,64,128]{2,1,0:T(8,128)S(1)}, u32[]{:S(2)}, u32[]{:S(2)}) collective-permute-start(f32[8,64,128]{2,1,0:T(8,128)S(1)} %get-tuple-element.57), channel_id=1, source_target_pairs={{0,4},{1,5},{2,6},{3,7},{4,0},{5,1},{6,2},{7,3},{8,12},{9,13},{10,... | collective-permute-start | bytes 786440 | tf_op jit(solution)/shard_map/ppermute | solution.py:564
  111.0 12.1 %collective-permute-start.20 = (f32[8,64,128]{2,1,0:T(8,128)S(1)}, f32[8,64,128]{2,1,0:T(8,128)S(1)}, u32[]{:S(2)}, u32[]{:S(2)}) collective-permute-start(f32[8,64,128]{2,1,0:T(8,128)S(1)} %get-tuple-element.58), channel_id=1, source_target_pairs={{0,6},{1,7},{2,0},{3,1},{4,2},{5,3},{6,4},{7,5},{8,14},{9,15},{10,... | collective-permute-start | bytes 786440 | tf_op jit(solution)/shard_map/ppermute | solution.py:564
  112.4 21.8 %collective-permute-start.17 = (f32[8,64,128]{2,1,0:T(8,128)}, f32[8,64,128]{2,1,0:T(8,128)S(1)}, u32[]{:S(2)}, u32[]{:S(2)}) collective-permute-start(f32[8,64,128]{2,1,0:T(8,128)} %get-tuple-element.63), channel_id=1, source_target_pairs={{0,2},{1,3},{2,4},{3,5},{4,6},{5,7},{6,0},{7,1},{8,10},{9,11},{10,... | collective-permute-start | bytes 786440 | tf_op jit(solution)/shard_map/ppermute | solution.py:564
  113.5 20.9 %collective-permute-start.19 = (f32[8,64,128]{2,1,0:T(8,128)}, f32[8,64,128]{2,1,0:T(8,128)S(1)}, u32[]{:S(2)}, u32[]{:S(2)}) collective-permute-start(f32[8,64,128]{2,1,0:T(8,128)} %get-tuple-element.62), channel_id=1, source_target_pairs={{0,4},{1,5},{2,6},{3,7},{4,0},{5,1},{6,2},{7,3},{8,12},{9,13},{10,... | collective-permute-start | bytes 786440 | tf_op jit(solution)/shard_map/ppermute | solution.py:564
  117.1 17.3 %collective-permute-start.21 = (f32[8,64,128]{2,1,0:T(8,128)}, f32[8,64,128]{2,1,0:T(8,128)}, u32[]{:S(2)}, u32[]{:S(2)}) collective-permute-start(f32[8,64,128]{2,1,0:T(8,128)} %get-tuple-element.61), channel_id=1, source_target_pairs={{0,6},{1,7},{2,0},{3,1},{4,2},{5,3},{6,4},{7,5},{8,14},{9,15},{10,... | collective-permute-start | bytes 786440 | tf_op jit(solution)/shard_map/ppermute | solution.py:564
  134.2 3.4 %copy-start.5 = (f32[1024,512]{1,0:T(8,128)S(1)}, f32[1024,512]{1,0:T(8,128)}, u32[]{:S(2)}) copy-start(f32[1024,512]{1,0:T(8,128)} %copy-done.3) | copy-start | bytes 6291460
  135.9 6.1 %collective-permute-start.22 = (f32[16,4,32,128]{3,2,1,0:T(8,128)S(1)}, f32[16,4,32,128]{3,2,1,0:T(8,128)S(1)}, u32[]{:S(2)}, u32[]{:S(2)}) collective-permute-start(f32[16,4,32,128]{3,2,1,0:T(8,128)S(1)} %late.1.whole), channel_id=1, source_target_pairs={{0,1},{1,0},{2,3},{3,2},{4,5},{5,4},{6,7},{7,6},{8,9},{9,8},{10,11... | collective-permute-start | bytes 3145736 | tf_op jit(solution)/shard_map/ppermute | solution.py:574
  (13 other events, 18.3 us)
Sparse Core Ops, SparseCore 0:
  88.9 45.2 all-gather.1

commit v8 on v7

--- a/solution.py
+++ b/solution.py
@@ -57,10 +57,11 @@
 def tile_kernel(own, blocks, main, over, col_ref, count_ref, *rest):
     if own:
         pre_hbm, weight_hbm, tiles_hbm, recv_ref, local_ref, flag_ref, *rest = rest
-        keep_a, send_a, keep_b, send_b, pre, weight, tiles, sums, places, column, sems = rest
+        keep_a, send_a, keep_b, send_b, pre, weight, tiles, sums, sems = rest
+        column = col_ref
     else:
-        pre_hbm, grad_hbm, weight_hbm, tiles_hbm, pre_ref, local_ref, *rest = rest
-        send_ref, pre, grad, weight, tiles, sums, places, column, sems = rest
+        pre_hbm, grad_hbm, weight_hbm, tiles_hbm, pre_ref, local_ref, send_ref, places, column, *rest = rest
+        pre, grad, weight, tiles, sums, sems = rest
     width = weight.shape[0]
     rows = pre.shape[0] // CHUNKS
     count = tiles.shape[0] // CHUNKS
@@ -91,15 +92,16 @@
     sums[blocks + main :] = jnp.zeros((over,) + sums.shape[1:], F32)
     if not own:
         sums[blocks : blocks + main] = jnp.zeros((main,) + sums.shape[1:], F32)
-    slot_places(count_ref, places)
-
-    def place_tile(t, _):
-        col = col_ref[t]
-        slot = jnp.maximum(col - blocks, 0)
-        column[t] = jnp.where(col < blocks, col, blocks + places[slot])
-        return 0
-
-    lax.fori_loop(0, tiles.shape[0], place_tile, 0)
+    if not own:
+        slot_places(count_ref, places)
+
+        def place_tile(t, _):
+            col = col_ref[t]
+            slot = jnp.maximum(col - blocks, 0)
+            column[t] = jnp.where(col < blocks, col, blocks + places[slot])
+            return 0
+
+        lax.fori_loop(0, tiles.shape[0], place_tile, 0)
     weight_copy.wait()
     weight_high, weight_low = split(weight[...])
     contract = (((1,), (1,)), ((), ()))
@@ -191,6 +193,8 @@
             jax.ShapeDtypeStruct((node_rows, feat), F32),
             local,
             jax.ShapeDtypeStruct((main, width, BLOCK), F32),
+            jax.ShapeDtypeStruct((main + over,), jnp.int32),
+            jax.ShapeDtypeStruct(tile_col.shape, jnp.int32),
         ]
     scratch = [pltpu.VMEM((node_rows, feat), F32)]
     if not own:
@@ -199,8 +203,6 @@
         pltpu.VMEM((width, feat), F32),
         pltpu.VMEM(tile_vals.shape, F32),
         pltpu.VMEM((blocks + main + over, width, BLOCK), F32),
-        pltpu.SMEM((main + over,), jnp.int32),
-        pltpu.SMEM((tile_vals.shape[0],), jnp.int32),
         pltpu.SemaphoreType.DMA((2 + 3 * CHUNKS + 10,)),
     ]
     return pl.pallas_call(
@@ -248,27 +250,26 @@
     )
 
 
-def third_kernel(count_ref, keep, recv_a, recv_b, after, out, total, places):
+def third_kernel(places, keep, recv_a, recv_b, after, out, total):
     del after
     half = recv_a.shape[0]
     main = 2 * half
     total[0:half] = keep[0] + recv_a[...]
     total[half:main] = keep[1] + recv_b[...]
     total[main:] = jnp.zeros_like(total[main:])
-    slot_places(count_ref, places)
     for slot in range(out.shape[0]):
         out[slot] = total[places[slot]]
 
 
-def third_sums(halo_count, keep, recv_a, recv_b, after, slots):
-    shape = (slots,) + keep.shape[2:]
+def third_sums(places, keep, recv_a, recv_b, after):
+    shape = (places.shape[0],) + keep.shape[2:]
     return small(
         third_kernel,
         jax.ShapeDtypeStruct(shape, F32),
-        [halo_count, keep, recv_a, recv_b, after],
+        [places, keep, recv_a, recv_b, after],
         "third_sums",
         [IN_SMEM] + [IN_VMEM] * 3 + [ANYWHERE],
-        scratch=[pltpu.VMEM(shape, F32), pltpu.SMEM((slots,), jnp.int32)],
+        scratch=[pltpu.VMEM(shape, F32)],
     )
 
 
@@ -367,8 +368,21 @@
     out[...] = ((mine[...] + pair[...]) + (far_one[...] + far_two[...])) * scale
 
 
-def late_kernel(whole, *rest):
-    rest[-1][...] = whole[...]
+def pass_kernel(value, *rest):
+    rest[-1][...] = value[...]
+
+
+def gather_kernel(axis_of, *rest):
+    pieces = rest[:4]
+    out = rest[-1]
+    me = axis_of(lax.axis_index("group"))
+    for away, piece in enumerate(pieces):
+        out[(me - away) & 3] = piece[...]
+
+
+def gather(axis_of, pieces, name):
+    whole = jax.ShapeDtypeStruct((4,) + pieces[0].shape, F32)
+    return small(functools.partial(gather_kernel, axis_of), whole, pieces, name)
 
 
 def place_kernel(count_ref, target_ref, arrived, after, send, *keeps):
@@ -505,12 +519,12 @@
     along_y = [[(i, (i + 4 * k) % groups) for i in range(groups)] for k in range(4)]
     along_z = [[(i, i // 4 * 4 + (i + k) % 4) for i in range(groups)] for k in range(4)]
 
-    pre_grad, other_local, send = tile_sums(
+    pre_grad, other_local, send, places, column = tile_sums(
         tile_col, halo_count, w_neigh, tile_vals, MAIN, dead, preact=preact, grad_out=grad_out
     )
     recv = lax.ppermute(send, "local", swap)
     own_local, flag, keep_a, send_a, keep_b, send_b = tile_sums(
-        tile_col, halo_count, w_neigh, tile_vals, MAIN, dead, pre_grad=pre_grad, recv=recv
+        column, halo_count, w_neigh, tile_vals, MAIN, dead, pre_grad=pre_grad, recv=recv
     )
     recv_a = lax.ppermute(send_a, "local", pairs)
     recv_b = lax.ppermute(send_b, "local", across)
@@ -535,27 +549,34 @@
         lax.ppermute(some, "group", along_z[k + 1]) for k, some in enumerate(sends)
     ]
 
-    keep, send_a, send_b = second_sums(keep_a, recv_a, keep_b, recv_b, mine)
-    share_shape = jax.ShapeDtypeStruct(mine.shape, F32)
-    share = small(sum_kernel, share_shape, [*terms, keep], "sum_z", [IN_VMEM] * 4 + [ANYWHERE])
-    recv_a = lax.ppermute(send_a, "local", across)
-    recv_b = lax.ppermute(send_b, "local", pairs)
-    terms = [share] + [lax.ppermute(share, "local", p) for p in (pairs, across, along_x[2])]
-    scale = float(node_rows * groups * members) ** (-0.5)
-    share = small(functools.partial(chips_kernel, scale), share_shape, terms, "sum_chips")
-    whole = lax.all_gather(share, "group", tiled=True)
-    shares = third_sums(halo_count, keep, recv_a, recv_b, share, slot_count)
     base = small(
         self_kernel,
         jax.ShapeDtypeStruct(pre_grad.shape, F32),
-        [pre_grad, w_self, shares],
+        [pre_grad, w_self, mine],
         "self_rows",
         [IN_VMEM, IN_VMEM, ANYWHERE],
         mebibytes=16,
         flops=6 * pre_grad.size * width,
     )
+    keep, send_a, send_b = second_sums(keep_a, recv_a, keep_b, recv_b, base)
+    recv_a = lax.ppermute(send_a, "local", across)
+    recv_b = lax.ppermute(send_b, "local", pairs)
+    share_shape = jax.ShapeDtypeStruct(mine.shape, F32)
+    share = small(sum_kernel, share_shape, [*terms, keep], "sum_z", [IN_VMEM] * 4 + [ANYWHERE])
+    shares = third_sums(places, keep, recv_a, recv_b, share)
     arrived = lax.all_to_all(shares, "group", split_axis=0, concat_axis=0, tiled=True)
-    send, *keeps = place(halo_count, halo_target, arrived, base, blocks)
+
+    share = small(pass_kernel, share_shape, [share, shares], "pass", [IN_VMEM, ANYWHERE])
+    terms = [share] + [lax.ppermute(share, "local", p) for p in (pairs, across, along_x[2])]
+    scale = float(node_rows * groups * members) ** (-0.5)
+    share = small(functools.partial(chips_kernel, scale), share_shape, terms, "sum_chips")
+    terms = [share] + [lax.ppermute(share, "group", along_z[k]) for k in range(1, 4)]
+
+    row = gather(lambda g: g & 3, terms, "gather_z")
+    rows_of_y = [[z + 4 * y for y in range(4)] for z in range(4)]
+    whole = lax.all_gather(row, "group", axis_index_groups=rows_of_y)
+
+    send, *keeps = place(halo_count, halo_target, arrived, row, blocks)
     swapped = lax.ppermute(send, "local", swap)
     received = []
     for k in range(4):
@@ -565,10 +586,10 @@
         received += pair
 
     whole = small(
-        late_kernel,
+        pass_kernel,
         pieces,
         [whole.reshape(pieces.shape), *received[2:]],
-        "late",
+        "pass",
         [IN_VMEM] + [ANYWHERE] * 6,
     )
     other = lax.ppermute(whole, "local", swap)

time: 151 us -> 146 us (0.967)
  local copies, waits for them, and re-layouts: 10.2 us -> 4.49 us
  waiting for transfers between devices: 49.7 us -> 52.7 us
  Pallas kernels: 30.1 us -> 28 us
    ppermute x0 -> x3, waiting for transfers between devices: none -> 8.28 us  [on_device(): lax.ppermute(share, 'group', along_z[k])]
    ppermute x6, waiting for transfers between devices: 8.5 us -> 16.3 us  [on_device(): pair = [lax.ppermute(some, 'local', along_x[k]) for some in pair]]
    all_gather x1, waiting for transfers between devices: 11 us -> 4.12 us  [on_device(): whole = lax.all_gather(row, 'group', axis_index_groups=rows_of_y)]
    unnamed x40 -> x38, local copies, waits for them, and re-layouts: 9.24 us -> 3.5 us
    all_to_all x1, waiting for transfers between devices: 5.34 us -> 0.01 us  [on_device(): lax.all_to_all(shares, 'group', split_axis=0, concat_axis=0, tiled=True)]
    ppermute x1, starting transfers between devices: 6.02 us -> 0.88 us  [on_device(): swapped = lax.ppermute(send, 'local', swap)]
    ppermute x0 -> x3, starting transfers between devices: none -> 5.01 us  [on_device(): lax.ppermute(share, 'group', along_z[k])]
    ppermute x1, waiting for transfers between devices: 0.01 us -> 2.06 us  [on_device(): recv_a = lax.ppermute(send_a, 'local', across)]
  transfers between devices with their start and end apart: 25 -> 28, of which waited for: 17 -> 21; matrix products, arithmetic and copies ran while one was open for 4% -> 4% of each run, Pallas kernels for 10% -> 10%
where the time goes in v8:
time: 146 us; the launch traced here: 145 us
  waiting for transfers between devices  52.7 us (36%)
  starting transfers between devices  40.4 us (28%)
  Pallas kernels  28 us (19%)
  between operations  14.3 us (10%)
  matrix products  5.45 us (4%)
  local copies, waits for them, and re-layouts  4.49 us (3%)
    pallas_call x2, Pallas kernels, tile_sums(): pl.pallas_call(functools.partial(tile_kernel, own, blocks, main, over), o...  16.3 us
    ppermute x6, waiting for transfers between devices, on_device(): pair = [lax.ppermute(some, 'local', along_x[k]) for some in pair]  16.3 us
    ppermute x3, waiting for transfers between devices, on_device(): lax.ppermute(some, 'group', along_y[k + 1])  10.1 us
    pallas_call x13, Pallas kernels, small(): pl.pallas_call(kernel, out_shape=out_shape, in_specs=specs or [IN_VMEM] *...  8.51 us
    ppermute x3, waiting for transfers between devices, on_device(): lax.ppermute(share, 'group', along_z[k])  8.28 us
    all_to_all x1, starting transfers between devices, on_device(): lax.all_to_all(shares, 'group', split_axis=0, concat_axis=0, tiled=True)  7.9 us
    ppermute x6, starting transfers between devices, on_device(): pair = [lax.ppermute(some, 'local', along_x[k]) for some in pair]  5.07 us
    ppermute x3, starting transfers between devices, on_device(): lax.ppermute(some, 'group', along_z[k + 1])  5.06 us
  transfers between devices with their start and end apart: 28, of which 21 were waited for; matrix products, arithmetic and copies ran while one was open for 4% of the time, Pallas kernels for 10%

profile of v8, /device:TPU:1, one launch (start us, length us, event | category | flops | bytes accessed | tf_op | source)
XLA Modules:
  0.0 145.4 jit_solution(15284074461089949412)
XLA Ops:
  7.2 9.8 %other_tile_sums.1 = (f32[1024,512]{1,0:T(8,128)}, f32[8,256,128]{2,1,0:T(8,128)}, f32[30,256,128]{2,1,0:T(8,128)}, s32[32]{0:T(128)}, s32[64]{0:T(128)}) custom-call(s32[64]{0:T(128)} %col_ref.1, s32[16,16]{1,0:T(8,128)} %count_ref.5, f32[1024,512]{1,0:T(8,128)} %rest_0_.1, f32[1024,512]{1,0:T(8,128)} %rest_1_.2, f32[512,512]{1,0:T(8,128)} %rest_1_.3, ...), custom_call_target="tpu_custom_call" | custom-call | flops 2415919104 | bytes 14680064 | tf_op jit(solution)/shard_map/other_tile_sums/pallas_call | solution.py:208
  17.0 1.5 %collective-permute-start.1 = (f32[30,256,128]{2,1,0:T(8,128)}, f32[30,256,128]{2,1,0:T(8,128)S(1)}, u32[]{:S(2)}, u32[]{:S(2)}) collective-permute-start(f32[30,256,128]{2,1,0:T(8,128)} %get-tuple-element.38), channel_id=1, source_target_pairs={{0,1},{1,0},{2,3},{3,2},{4,5},{5,4},{6,7},{7,6},{8,9},{9,8},{10,11... | collective-permute-start | bytes 11796488 | tf_op jit(solution)/shard_map/ppermute | solution.py:525
  18.5 3.6 %convolution_bitcast_fusion.neigh_term = f32[512,512]{1,0:T(8,128)S(1)} fusion(f32[1024,512]{1,0:T(8,128)} %get-tuple-element.34.rest_0_.pre_grad, f32[1024,512]{1,0:T(8,128)S(1)} %copy-done), kind=kOutput, calls=%fused_computation | convolution fusion | flops 1610612736 | bytes 5242880 | tf_op jit(solution)/shard_map/dot_general | solution.py:536
  22.1 1.9 %convolution_bitcast_fusion.1.self_term = f32[512,512]{1,0:T(8,128)S(1)} fusion(f32[1024,512]{1,0:T(8,128)S(1)} %copy-done.1, f32[1024,512]{1,0:T(8,128)S(1)} %copy-done.18), kind=kOutput, calls=%fused_computation.1 | convolution fusion | flops 1610612736 | bytes 5242880 | tf_op jit(solution)/shard_map/dot_general | solution.py:533
  25.3 6.5 %own_tile_sums.1 = (f32[8,256,128]{2,1,0:T(8,128)S(1)}, s32[1]{0:T(128)}, f32[2,15,64,128]{3,2,1,0:T(8,128)S(1)}, f32[2,15,64,128]{3,2,1,0:T(8,128)S(1)}, f32[2,...) custom-call(s32[64]{0:T(128)S(1)} %copy-done.16, s32[16,16]{1,0:T(8,128)S(1)} %copy-done.13, ...), custom_call_target="tpu_custom_call" | custom-call | flops 2415919104 | bytes 14680064 | tf_op jit(solution)/shard_map/own_tile_sums/pallas_call | solution.py:208
  33.2 1.8 %collective-permute-start.6 = (f32[2,15,64,128]{3,2,1,0:T(8,128)S(1)}, f32[2,15,64,128]{3,2,1,0:T(8,128)S(1)}, u32[]{:S(2)}, u32[]{:S(2)}) collective-permute-start(f32[2,15,64,128]{3,2,1,0:T(8,128)S(1)} %get-tuple-element.51), channel_id=1, source_target_pairs={{0,6},{1,7},{2,4},{3,5},{4,2},{5,3},{6,0},{7,1},{8,14},{9,15},{10,... | collective-permute-start | bytes 2949128 | tf_op jit(solution)/shard_map/ppermute | solution.py:530
  37.2 2.6 %collective-permute-start.3 = (f32[4,4,32,128]{3,2,1,0:T(8,128)S(1)}, f32[4,4,32,128]{3,2,1,0:T(8,128)S(1)}, u32[]{:S(2)}, u32[]{:S(2)}) collective-permute-start(f32[4,4,32,128]{3,2,1,0:T(8,128)S(1)} %get-tuple-element.42), channel_id=1, source_target_pairs={{0,64},{8,72},{16,80},{24,88},{32,96},{40,104},{48,112},{56,120},{... | collective-permute-start | bytes 786440 | tf_op jit(solution)/shard_map/ppermute | solution.py:545
  40.9 3.4 %collective-permute-done.2.rest_1_ = f32[4,4,32,128]{3,2,1,0:T(8,128)S(1)} collective-permute-done((f32[4,4,32,128]{3,2,1,0:T(8,128)S(1)}, f32[4,4,32,128]{3,2,1,0:T(8,128)S(1)}, u32[]{:S(2)}, u32[]{:S(2)}) %collective-permute-start.2) | collective-permute-done | bytes 262176 | tf_op jit(solution)/shard_map/ppermute | solution.py:545
  44.3 6.7 %collective-permute-done.3.rest_2_ = f32[4,4,32,128]{3,2,1,0:T(8,128)S(1)} collective-permute-done((f32[4,4,32,128]{3,2,1,0:T(8,128)S(1)}, f32[4,4,32,128]{3,2,1,0:T(8,128)S(1)}, u32[]{:S(2)}, u32[]{:S(2)}) %collective-permute-start.3) | collective-permute-done | bytes 262176 | tf_op jit(solution)/shard_map/ppermute | solution.py:545
  51.1 1.8 %self_rows.1.after.base = f32[1024,512]{1,0:T(8,128)S(1)} custom-call(f32[1024,512]{1,0:T(8,128)S(1)} %copy-done.1, f32[512,512]{1,0:T(8,128)S(1)} %copy-done.17, f32[4,32,128]{2,1,0:T(8,128)S(1)} %get-tuple-element.44.after.rest_0_), custom_call_target="tpu_custom_call" | custom-call | flops 1610612736 | bytes 6291456 | tf_op jit(solution)/shard_map/self_rows/pallas_call | solution.py:280
  53.0 2.1 %collective-permute-done.5.recv_a = f32[2,15,64,128]{3,2,1,0:T(8,128)S(1)} collective-permute-done((f32[2,15,64,128]{3,2,1,0:T(8,128)S(1)}, f32[2,15,64,128]{3,2,1,0:T(8,128)S(1)}, u32[]{:S(2)}, u32[]{:S(2)}) %collective-permute-start.5) | collective-permute-done | bytes 983072 | tf_op jit(solution)/shard_map/ppermute | solution.py:529
  55.1 2.2 %collective-permute-done.6.recv_b = f32[2,15,64,128]{3,2,1,0:T(8,128)S(1)} collective-permute-done((f32[2,15,64,128]{3,2,1,0:T(8,128)S(1)}, f32[2,15,64,128]{3,2,1,0:T(8,128)S(1)}, u32[]{:S(2)}, u32[]{:S(2)}) %collective-permute-start.6) | collective-permute-done | bytes 983072 | tf_op jit(solution)/shard_map/ppermute | solution.py:530
  57.5 1.9 %collective-permute-start.7 = (f32[15,64,128]{2,1,0:T(8,128)S(1)}, f32[15,64,128]{2,1,0:T(8,128)S(1)}, u32[]{:S(2)}, u32[]{:S(2)}) collective-permute-start(f32[15,64,128]{2,1,0:T(8,128)S(1)} %get-tuple-element.53), channel_id=1, source_target_pairs={{0,6},{1,7},{2,4},{3,5},{4,2},{5,3},{6,0},{7,1},{8,14},{9,15},{10,... | collective-permute-start | bytes 1474568 | tf_op jit(solution)/shard_map/ppermute | solution.py:562
  59.4 3.6 %collective-permute-start.10 = (f32[4,32,128]{2,1,0:T(8,128)S(1)}, f32[4,32,128]{2,1,0:T(8,128)S(1)}, u32[]{:S(2)}, u32[]{:S(2)}) collective-permute-start(f32[4,32,128]{2,1,0:T(8,128)S(1)} %get-tuple-element.56), channel_id=1, source_target_pairs={{0,16},{8,24},{16,0},{24,8},{32,48},{40,56},{48,32},{56,40},{64,80... | collective-permute-start | bytes 196616 | tf_op jit(solution)/shard_map/ppermute | solution.py:549
  64.7 1.8 %collective-permute-done.11.rest_3_ = f32[4,32,128]{2,1,0:T(8,128)S(1)} collective-permute-done((f32[4,32,128]{2,1,0:T(8,128)S(1)}, f32[4,32,128]{2,1,0:T(8,128)S(1)}, u32[]{:S(2)}, u32[]{:S(2)}) %collective-permute-start.11) | collective-permute-done | bytes 65568 | tf_op jit(solution)/shard_map/ppermute | solution.py:549
  66.4 1.6 %collective-permute-done.9.rest_1_ = f32[4,32,128]{2,1,0:T(8,128)S(1)} collective-permute-done((f32[4,32,128]{2,1,0:T(8,128)S(1)}, f32[4,32,128]{2,1,0:T(8,128)S(1)}, u32[]{:S(2)}, u32[]{:S(2)}) %collective-permute-start.9) | collective-permute-done | bytes 65568 | tf_op jit(solution)/shard_map/ppermute | solution.py:549
  68.1 2.1 %collective-permute-done.7.recv_a = f32[15,64,128]{2,1,0:T(8,128)S(1)} collective-permute-done((f32[15,64,128]{2,1,0:T(8,128)S(1)}, f32[15,64,128]{2,1,0:T(8,128)S(1)}, u32[]{:S(2)}, u32[]{:S(2)}) %collective-permute-start.7) | collective-permute-done | bytes 491552 | tf_op jit(solution)/shard_map/ppermute | solution.py:562
  70.5 1.7 %third_sums.1.rest_0_ = f32[32,64,128]{2,1,0:T(8,128)} custom-call(s32[32]{0:T(128)S(1)} %copy-done.15, f32[2,15,64,128]{3,2,1,0:T(8,128)S(1)} %get-tuple-element.52.rest_4_.keep, f32[15,64,128]{2,1,0:T(8,128)S(1)} %collective-permute-done.7.recv_a, f32[15,64,128]{2,1,0:T(8,128)S(1)} %collective-permute-done.8.recv_b, f32[4,32,128]{2,1,0:T(8,128)S(1)} %sum_z.1.after.value), custom_call_target="tpu_custom_call" | custom-call | flops 245760 | bytes 2949120 | tf_op jit(solution)/shard_map/third_sums/pallas_call | solution.py:280
  72.2 7.9 %all-to-all-start = ((f32[32,64,128]{2,1,0:T(8,128)}), f32[32,64,128]{2,1,0:T(8,128)S(1)}, u32[]{:S(2)}, u32[]{:S(2)}) async-start(f32[32,64,128]{2,1,0:T(8,128)} %third_sums.1.rest_0_), calls=%async_computation | async-start | bytes 2097152 | tf_op jit(solution)/shard_map/all_to_all | solution.py:567
  81.8 1.7 %collective-permute-start.14 = (f32[4,32,128]{2,1,0:T(8,128)S(1)}, f32[4,32,128]{2,1,0:T(8,128)S(1)}, u32[]{:S(2)}, u32[]{:S(2)}) collective-permute-start(f32[4,32,128]{2,1,0:T(8,128)S(1)} %pass.2.mine), channel_id=1, source_target_pairs={{0,4},{1,5},{2,6},{3,7},{4,0},{5,1},{6,2},{7,3},{8,12},{9,13},{10,... | collective-permute-start | bytes 196616 | tf_op jit(solution)/shard_map/ppermute | solution.py:570
  84.9 1.6 %collective-permute-done.14.far_two = f32[4,32,128]{2,1,0:T(8,128)S(1)} collective-permute-done((f32[4,32,128]{2,1,0:T(8,128)S(1)}, f32[4,32,128]{2,1,0:T(8,128)S(1)}, u32[]{:S(2)}, u32[]{:S(2)}) %collective-permute-start.14) | collective-permute-done | bytes 65568 | tf_op jit(solution)/shard_map/ppermute | solution.py:570
  87.9 2.4 %collective-permute-start.16 = (f32[4,32,128]{2,1,0:T(8,128)S(1)}, f32[4,32,128]{2,1,0:T(8,128)S(1)}, u32[]{:S(2)}, u32[]{:S(2)}) collective-permute-start(f32[4,32,128]{2,1,0:T(8,128)S(1)} %sum_chips.1.rest_0_), channel_id=1, source_target_pairs={{0,16},{8,24},{16,0},{24,8},{32,48},{40,56},{48,32},{56,40},{64,80... | collective-permute-start | bytes 196616 | tf_op jit(solution)/shard_map/ppermute | solution.py:573
  91.5 5.8 %collective-permute-done.15.rest_1_ = f32[4,32,128]{2,1,0:T(8,128)S(1)} collective-permute-done((f32[4,32,128]{2,1,0:T(8,128)S(1)}, f32[4,32,128]{2,1,0:T(8,128)S(1)}, u32[]{:S(2)}, u32[]{:S(2)}) %collective-permute-start.15) | collective-permute-done | bytes 65568 | tf_op jit(solution)/shard_map/ppermute | solution.py:573
  97.3 2.5 %collective-permute-done.16.rest_2_ = f32[4,32,128]{2,1,0:T(8,128)S(1)} collective-permute-done((f32[4,32,128]{2,1,0:T(8,128)S(1)}, f32[4,32,128]{2,1,0:T(8,128)S(1)}, u32[]{:S(2)}, u32[]{:S(2)}) %collective-permute-start.16) | collective-permute-done | bytes 65568 | tf_op jit(solution)/shard_map/ppermute | solution.py:573
  100.5 1.5 %place.1 = (f32[4,8,64,128]{3,2,1,0:T(8,128)S(1)}, f32[8,64,128]{2,1,0:T(8,128)S(1)}, f32[8,64,128]{2,1,0:T(8,128)S(1)}, f32[8,64,128]{2,1,0:T(8,128)S(1)}, f32[8,64,128]{2,1,0:T(8,128)S(1)}) custom-call(s32[16,16]{1,0:T(8,128)S(1)} %copy-done.13, s32[16,32]{1,0:T(8,128)S(1)} %copy-done.14, f32[32,64,128]{2,1,0:T(8,128)S(1)} %all-to-all-done.arrived, ...), custom_call_target="tpu_custom_call" | custom-call | flops 262144 | bytes 3145728 | tf_op jit(solution)/shard_map/place/pallas_call | solution.py:280
  104.2 2.0 %collective-permute-start.21 = (f32[8,64,128]{2,1,0:T(8,128)S(1)}, f32[8,64,128]{2,1,0:T(8,128)S(1)}, u32[]{:S(2)}, u32[]{:S(2)}) collective-permute-start(f32[8,64,128]{2,1,0:T(8,128)S(1)} %get-tuple-element.61), channel_id=1, source_target_pairs={{0,4},{1,5},{2,6},{3,7},{4,0},{5,1},{6,2},{7,3},{8,12},{9,13},{10,... | collective-permute-start | bytes 786440 | tf_op jit(solution)/shard_map/ppermute | solution.py:585
  109.7 3.2 %collective-permute-done.19.rest_2_.rest_0_ = f32[8,64,128]{2,1,0:T(8,128)S(1)} collective-permute-done((f32[8,64,128]{2,1,0:T(8,128)S(1)}, f32[8,64,128]{2,1,0:T(8,128)S(1)}, u32[]{:S(2)}, u32[]{:S(2)}) %collective-permute-start.19) | collective-permute-done | bytes 262176 | tf_op jit(solution)/shard_map/ppermute | solution.py:585
  113.0 5.4 %collective-permute-done.21.rest_4_.rest_2_ = f32[8,64,128]{2,1,0:T(8,128)S(1)} collective-permute-done((f32[8,64,128]{2,1,0:T(8,128)S(1)}, f32[8,64,128]{2,1,0:T(8,128)S(1)}, u32[]{:S(2)}, u32[]{:S(2)}) %collective-permute-start.21) | collective-permute-done | bytes 262176 | tf_op jit(solution)/shard_map/ppermute | solution.py:585
  118.8 4.1 %all-gather.3.cloned.1.call-done.value = f32[16,4,32,128]{3,2,1,0:T(8,128)} async-done(((f32[4,4,32,128]{3,2,1,0:T(8,128)}), f32[16,4,32,128]{3,2,1,0:T(8,128)}) %all-gather.3.cloned.1.call-update) | async-done | bytes 1048592 | tf_op jit(solution)/shard_map/all_gather | solution.py:577
  124.1 5.5 %collective-permute-done.22.rest_5_.rest_3_ = f32[8,64,128]{2,1,0:T(8,128)S(1)} collective-permute-done((f32[8,64,128]{2,1,0:T(8,128)}, f32[8,64,128]{2,1,0:T(8,128)S(1)}, u32[]{:S(2)}, u32[]{:S(2)}) %collective-permute-start.22) | collective-permute-done | bytes 262176 | tf_op jit(solution)/shard_map/ppermute | solution.py:585
  133.9 3.1 %finish.1 = f32[1024,512]{1,0:T(8,128)} custom-call(f32[1024,512]{1,0:T(8,128)S(1)} %copy-done.4, f32[8,256,128]{2,1,0:T(8,128)S(1)} %copy-done.8, f32[8,256,128]{2,1,0:T(8,128)S(1)} %copy-done.10, f32[8,64,128]{2,1,0:T(8,128)S(1)} %copy-done.12, f32[8,64,128]{2,1,0:T(8,128)S(1)} %copy-done.7, f32[8,64,128]{2,1,0:T(8,128)S(1)} %collective-permute-done.19.rest_2_.rest_0_, ...), custom_call_target="tpu_custom_call" | custom-call | flops 1048576 | bytes 8388608 | tf_op jit(solution)/shard_map/finish/pallas_call | solution.py:478
  137.1 1.5 %sort_grads.1 = (f32[512,512]{1,0:T(8,128)}, f32[512,512]{1,0:T(8,128)}) custom-call(f32[16,4,32,128]{3,2,1,0:T(8,128)S(1)} %pass.3.whole, f32[16,4,32,128]{3,2,1,0:T(8,128)S(1)} %collective-permute-done.25.other), custom_call_target="tpu_custom_call" | custom-call | flops 262144 | bytes 3145728 | tf_op jit(solution)/shard_map/sort_grads/pallas_call | solution.py:280
  (82 shorter events, 26.2 us)
Async XLA Ops:
  17.0 8.1 %collective-permute-start.1 = (f32[30,256,128]{2,1,0:T(8,128)}, f32[30,256,128]{2,1,0:T(8,128)S(1)}, u32[]{:S(2)}, u32[]{:S(2)}) collective-permute-start(f32[30,256,128]{2,1,0:T(8,128)} %get-tuple-element.38), channel_id=1, source_target_pairs={{0,1},{1,0},{2,3},{3,2},{4,5},{5,4},{6,7},{7,6},{8,9},{9,8},{10,11... | collective-permute-start | bytes 11796488 | tf_op jit(solution)/shard_map/ppermute | solution.py:525
  24.2 10.9 %collective-permute-start = (f32[16,4,32,128]{3,2,1,0:T(8,128)S(1)}, f32[16,4,32,128]{3,2,1,0:T(8,128)S(1)}, u32[]{:S(2)}, u32[]{:S(2)}) collective-permute-start(f32[16,4,32,128]{3,2,1,0:T(8,128)S(1)} %get-tuple-element.36), channel_id=1, source_target_pairs={{0,1},{1,0},{2,3},{3,2},{4,5},{5,4},{6,7},{7,6},{8,9},{9,8},{10,11... | collective-permute-start | bytes 3145736 | tf_op jit(solution)/shard_map/ppermute | solution.py:542
  31.8 21.1 %copy-start.9 = (f32[8,256,128]{2,1,0:T(8,128)}, f32[8,256,128]{2,1,0:T(8,128)S(1)}, u32[]{:S(2)}) copy-start(f32[8,256,128]{2,1,0:T(8,128)S(1)} %get-tuple-element.46.own_local) | copy-start | bytes 3145732
  31.8 19.3 %copy-start.17 = (f32[512,512]{1,0:T(8,128)S(1)}, f32[512,512]{1,0:T(8,128)}, u32[]{:S(2)}) copy-start(f32[512,512]{1,0:T(8,128)} %weight.1) | copy-start | bytes 3145732
  31.8 23.2 %collective-permute-start.5 = (f32[2,15,64,128]{3,2,1,0:T(8,128)S(1)}, f32[2,15,64,128]{3,2,1,0:T(8,128)S(1)}, u32[]{:S(2)}, u32[]{:S(2)}) collective-permute-start(f32[2,15,64,128]{3,2,1,0:T(8,128)S(1)} %get-tuple-element.49), channel_id=1, source_target_pairs={{0,2},{1,3},{2,0},{3,1},{4,6},{5,7},{6,4},{7,5},{8,10},{9,11},{10,... | collective-permute-start | bytes 2949128 | tf_op jit(solution)/shard_map/ppermute | solution.py:529
  33.2 24.0 %collective-permute-start.6 = (f32[2,15,64,128]{3,2,1,0:T(8,128)S(1)}, f32[2,15,64,128]{3,2,1,0:T(8,128)S(1)}, u32[]{:S(2)}, u32[]{:S(2)}) collective-permute-start(f32[2,15,64,128]{3,2,1,0:T(8,128)S(1)} %get-tuple-element.51), channel_id=1, source_target_pairs={{0,6},{1,7},{2,4},{3,5},{4,2},{5,3},{6,0},{7,1},{8,14},{9,15},{10,... | collective-permute-start | bytes 2949128 | tf_op jit(solution)/shard_map/ppermute | solution.py:530
  35.8 8.5 %collective-permute-start.2 = (f32[4,4,32,128]{3,2,1,0:T(8,128)S(1)}, f32[4,4,32,128]{3,2,1,0:T(8,128)S(1)}, u32[]{:S(2)}, u32[]{:S(2)}) collective-permute-start(f32[4,4,32,128]{3,2,1,0:T(8,128)S(1)} %get-tuple-element.41), channel_id=1, source_target_pairs={{0,32},{8,40},{16,48},{24,56},{32,64},{40,72},{48,80},{56,88},{64,... | collective-permute-start | bytes 786440 | tf_op jit(solution)/shard_map/ppermute | solution.py:545
  37.2 13.8 %collective-permute-start.3 = (f32[4,4,32,128]{3,2,1,0:T(8,128)S(1)}, f32[4,4,32,128]{3,2,1,0:T(8,128)S(1)}, u32[]{:S(2)}, u32[]{:S(2)}) collective-permute-start(f32[4,4,32,128]{3,2,1,0:T(8,128)S(1)} %get-tuple-element.42), channel_id=1, source_target_pairs={{0,64},{8,72},{16,80},{24,88},{32,96},{40,104},{48,112},{56,120},{... | collective-permute-start | bytes 786440 | tf_op jit(solution)/shard_map/ppermute | solution.py:545
  39.8 11.2 %collective-permute-start.4 = (f32[4,4,32,128]{3,2,1,0:T(8,128)S(1)}, f32[4,4,32,128]{3,2,1,0:T(8,128)S(1)}, u32[]{:S(2)}, u32[]{:S(2)}) collective-permute-start(f32[4,4,32,128]{3,2,1,0:T(8,128)S(1)} %get-tuple-element.43), channel_id=1, source_target_pairs={{0,96},{8,104},{16,112},{24,120},{32,0},{40,8},{48,16},{56,24},{64... | collective-permute-start | bytes 786440 | tf_op jit(solution)/shard_map/ppermute | solution.py:545
  57.3 13.2 %copy-start.15 = (s32[32]{0:T(128)S(1)}, s32[32]{0:T(128)}, u32[]{:S(2)}) copy-start(s32[32]{0:T(128)} %get-tuple-element.47.places) | copy-start | bytes 388
  57.5 12.7 %collective-permute-start.7 = (f32[15,64,128]{2,1,0:T(8,128)S(1)}, f32[15,64,128]{2,1,0:T(8,128)S(1)}, u32[]{:S(2)}, u32[]{:S(2)}) collective-permute-start(f32[15,64,128]{2,1,0:T(8,128)S(1)} %get-tuple-element.53), channel_id=1, source_target_pairs={{0,6},{1,7},{2,4},{3,5},{4,2},{5,3},{6,0},{7,1},{8,14},{9,15},{10,... | collective-permute-start | bytes 1474568 | tf_op jit(solution)/shard_map/ppermute | solution.py:562
  59.4 11.1 %collective-permute-start.8 = (f32[15,64,128]{2,1,0:T(8,128)S(1)}, f32[15,64,128]{2,1,0:T(8,128)S(1)}, u32[]{:S(2)}, u32[]{:S(2)}) collective-permute-start(f32[15,64,128]{2,1,0:T(8,128)S(1)} %get-tuple-element.54), channel_id=1, source_target_pairs={{0,2},{1,3},{2,0},{3,1},{4,6},{5,7},{6,4},{7,5},{8,10},{9,11},{10,... | collective-permute-start | bytes 1474568 | tf_op jit(solution)/shard_map/ppermute | solution.py:563
  59.4 5.3 %collective-permute-start.10 = (f32[4,32,128]{2,1,0:T(8,128)S(1)}, f32[4,32,128]{2,1,0:T(8,128)S(1)}, u32[]{:S(2)}, u32[]{:S(2)}) collective-permute-start(f32[4,32,128]{2,1,0:T(8,128)S(1)} %get-tuple-element.56), channel_id=1, source_target_pairs={{0,16},{8,24},{16,0},{24,8},{32,48},{40,56},{48,32},{56,40},{64,80... | collective-permute-start | bytes 196616 | tf_op jit(solution)/shard_map/ppermute | solution.py:549
  63.0 3.4 %collective-permute-start.11 = (f32[4,32,128]{2,1,0:T(8,128)S(1)}, f32[4,32,128]{2,1,0:T(8,128)S(1)}, u32[]{:S(2)}, u32[]{:S(2)}) collective-permute-start(f32[4,32,128]{2,1,0:T(8,128)S(1)} %get-tuple-element.57), channel_id=1, source_target_pairs={{0,24},{8,0},{16,8},{24,16},{32,56},{40,32},{48,40},{56,48},{64,88... | collective-permute-start | bytes 196616 | tf_op jit(solution)/shard_map/ppermute | solution.py:549
  63.4 4.6 %collective-permute-start.9 = (f32[4,32,128]{2,1,0:T(8,128)S(1)}, f32[4,32,128]{2,1,0:T(8,128)S(1)}, u32[]{:S(2)}, u32[]{:S(2)}) collective-permute-start(f32[4,32,128]{2,1,0:T(8,128)S(1)} %get-tuple-element.55), channel_id=1, source_target_pairs={{0,8},{8,16},{16,24},{24,0},{32,40},{40,48},{48,56},{56,32},{64,72... | collective-permute-start | bytes 196616 | tf_op jit(solution)/shard_map/ppermute | solution.py:549
  72.2 28.3 %copy-start.14 = (s32[16,32]{1,0:T(8,128)S(1)}, s32[16,32]{1,0:T(8,128)}, u32[]{:S(2)}) copy-start(s32[16,32]{1,0:T(8,128)} %target_ref.1) | copy-start | bytes 6148
  72.2 28.3 %all-to-all-start = ((f32[32,64,128]{2,1,0:T(8,128)}), f32[32,64,128]{2,1,0:T(8,128)S(1)}, u32[]{:S(2)}, u32[]{:S(2)}) async-start(f32[32,64,128]{2,1,0:T(8,128)} %third_sums.1.rest_0_), calls=%async_computation | async-start | bytes 2097152 | tf_op jit(solution)/shard_map/all_to_all | solution.py:567
  80.1 42.9 %all-gather.3.cloned.1.call-start = ((), (), s32[]{:S(2)}) async-start(), calls=%async_computation.1 | async-start | bytes 1310720 | tf_op jit(solution)/shard_map/all_gather | solution.py:577
  80.2 3.3 %collective-permute-start.12 = (f32[4,32,128]{2,1,0:T(8,128)S(1)}, f32[4,32,128]{2,1,0:T(8,128)S(1)}, u32[]{:S(2)}, u32[]{:S(2)}) collective-permute-start(f32[4,32,128]{2,1,0:T(8,128)S(1)} %pass.2.mine), channel_id=1, source_target_pairs={{0,2},{1,3},{2,0},{3,1},{4,6},{5,7},{6,4},{7,5},{8,10},{9,11},{10,... | collective-permute-start | bytes 196616 | tf_op jit(solution)/shard_map/ppermute | solution.py:570
  80.5 4.3 %collective-permute-start.13 = (f32[4,32,128]{2,1,0:T(8,128)S(1)}, f32[4,32,128]{2,1,0:T(8,128)S(1)}, u32[]{:S(2)}, u32[]{:S(2)}) collective-permute-start(f32[4,32,128]{2,1,0:T(8,128)S(1)} %pass.2.mine), channel_id=1, source_target_pairs={{0,6},{1,7},{2,4},{3,5},{4,2},{5,3},{6,0},{7,1},{8,14},{9,15},{10,... | collective-permute-start | bytes 196616 | tf_op jit(solution)/shard_map/ppermute | solution.py:570
  81.8 4.6 %collective-permute-start.14 = (f32[4,32,128]{2,1,0:T(8,128)S(1)}, f32[4,32,128]{2,1,0:T(8,128)S(1)}, u32[]{:S(2)}, u32[]{:S(2)}) collective-permute-start(f32[4,32,128]{2,1,0:T(8,128)S(1)} %pass.2.mine), channel_id=1, source_target_pairs={{0,4},{1,5},{2,6},{3,7},{4,0},{5,1},{6,2},{7,3},{8,12},{9,13},{10,... | collective-permute-start | bytes 196616 | tf_op jit(solution)/shard_map/ppermute | solution.py:570
  86.5 10.8 %collective-permute-start.15 = (f32[4,32,128]{2,1,0:T(8,128)S(1)}, f32[4,32,128]{2,1,0:T(8,128)S(1)}, u32[]{:S(2)}, u32[]{:S(2)}) collective-permute-start(f32[4,32,128]{2,1,0:T(8,128)S(1)} %sum_chips.1.rest_0_), channel_id=1, source_target_pairs={{0,8},{8,16},{16,24},{24,0},{32,40},{40,48},{48,56},{56,32},{64,72... | collective-permute-start | bytes 196616 | tf_op jit(solution)/shard_map/ppermute | solution.py:573
  87.9 11.9 %collective-permute-start.16 = (f32[4,32,128]{2,1,0:T(8,128)S(1)}, f32[4,32,128]{2,1,0:T(8,128)S(1)}, u32[]{:S(2)}, u32[]{:S(2)}) collective-permute-start(f32[4,32,128]{2,1,0:T(8,128)S(1)} %sum_chips.1.rest_0_), channel_id=1, source_target_pairs={{0,16},{8,24},{16,0},{24,8},{32,48},{40,56},{48,32},{56,40},{64,80... | collective-permute-start | bytes 196616 | tf_op jit(solution)/shard_map/ppermute | solution.py:573
  90.3 9.5 %collective-permute-start.17 = (f32[4,32,128]{2,1,0:T(8,128)S(1)}, f32[4,32,128]{2,1,0:T(8,128)S(1)}, u32[]{:S(2)}, u32[]{:S(2)}) collective-permute-start(f32[4,32,128]{2,1,0:T(8,128)S(1)} %sum_chips.1.rest_0_), channel_id=1, source_target_pairs={{0,24},{8,0},{16,8},{24,16},{32,56},{40,32},{48,40},{56,48},{64,88... | collective-permute-start | bytes 196616 | tf_op jit(solution)/shard_map/ppermute | solution.py:573
  102.8 4.0 %collective-permute-start.18 = (f32[4,8,64,128]{3,2,1,0:T(8,128)S(1)}, f32[4,8,64,128]{3,2,1,0:T(8,128)S(1)}, u32[]{:S(2)}, u32[]{:S(2)}) collective-permute-start(f32[4,8,64,128]{3,2,1,0:T(8,128)S(1)} %get-tuple-element.59), channel_id=1, source_target_pairs={{0,1},{1,0},{2,3},{3,2},{4,5},{5,4},{6,7},{7,6},{8,9},{9,8},{10,11... | collective-permute-start | bytes 3145736 | tf_op jit(solution)/shard_map/ppermute | solution.py:580
  103.7 9.3 %collective-permute-start.19 = (f32[8,64,128]{2,1,0:T(8,128)S(1)}, f32[8,64,128]{2,1,0:T(8,128)S(1)}, u32[]{:S(2)}, u32[]{:S(2)}) collective-permute-start(f32[8,64,128]{2,1,0:T(8,128)S(1)} %get-tuple-element.60), channel_id=1, source_target_pairs={{0,2},{1,3},{2,4},{3,5},{4,6},{5,7},{6,0},{7,1},{8,10},{9,11},{10,... | collective-permute-start | bytes 786440 | tf_op jit(solution)/shard_map/ppermute | solution.py:585
  104.2 14.2 %collective-permute-start.21 = (f32[8,64,128]{2,1,0:T(8,128)S(1)}, f32[8,64,128]{2,1,0:T(8,128)S(1)}, u32[]{:S(2)}, u32[]{:S(2)}) collective-permute-start(f32[8,64,128]{2,1,0:T(8,128)S(1)} %get-tuple-element.61), channel_id=1, source_target_pairs={{0,4},{1,5},{2,6},{3,7},{4,0},{5,1},{6,2},{7,3},{8,12},{9,13},{10,... | collective-permute-start | bytes 786440 | tf_op jit(solution)/shard_map/ppermute | solution.py:585
  106.2 12.6 %collective-permute-start.23 = (f32[8,64,128]{2,1,0:T(8,128)S(1)}, f32[8,64,128]{2,1,0:T(8,128)S(1)}, u32[]{:S(2)}, u32[]{:S(2)}) collective-permute-start(f32[8,64,128]{2,1,0:T(8,128)S(1)} %get-tuple-element.62), channel_id=1, source_target_pairs={{0,6},{1,7},{2,0},{3,1},{4,2},{5,3},{6,4},{7,5},{8,14},{9,15},{10,... | collective-permute-start | bytes 786440 | tf_op jit(solution)/shard_map/ppermute | solution.py:585
  107.8 16.4 %collective-permute-start.20 = (f32[8,64,128]{2,1,0:T(8,128)}, f32[8,64,128]{2,1,0:T(8,128)S(1)}, u32[]{:S(2)}, u32[]{:S(2)}) collective-permute-start(f32[8,64,128]{2,1,0:T(8,128)} %get-tuple-element.67), channel_id=1, source_target_pairs={{0,2},{1,3},{2,4},{3,5},{4,6},{5,7},{6,0},{7,1},{8,10},{9,11},{10,... | collective-permute-start | bytes 786440 | tf_op jit(solution)/shard_map/ppermute | solution.py:585
  108.7 20.9 %collective-permute-start.22 = (f32[8,64,128]{2,1,0:T(8,128)}, f32[8,64,128]{2,1,0:T(8,128)S(1)}, u32[]{:S(2)}, u32[]{:S(2)}) collective-permute-start(f32[8,64,128]{2,1,0:T(8,128)} %get-tuple-element.66), channel_id=1, source_target_pairs={{0,4},{1,5},{2,6},{3,7},{4,0},{5,1},{6,2},{7,3},{8,12},{9,13},{10,... | collective-permute-start | bytes 786440 | tf_op jit(solution)/shard_map/ppermute | solution.py:585
  112.9 17.2 %collective-permute-start.24 = (f32[8,64,128]{2,1,0:T(8,128)}, f32[8,64,128]{2,1,0:T(8,128)}, u32[]{:S(2)}, u32[]{:S(2)}) collective-permute-start(f32[8,64,128]{2,1,0:T(8,128)} %get-tuple-element.65), channel_id=1, source_target_pairs={{0,6},{1,7},{2,0},{3,1},{4,2},{5,3},{6,4},{7,5},{8,14},{9,15},{10,... | collective-permute-start | bytes 786440 | tf_op jit(solution)/shard_map/ppermute | solution.py:585
  131.4 5.6 %collective-permute-start.25 = (f32[16,4,32,128]{3,2,1,0:T(8,128)S(1)}, f32[16,4,32,128]{3,2,1,0:T(8,128)S(1)}, u32[]{:S(2)}, u32[]{:S(2)}) collective-permute-start(f32[16,4,32,128]{3,2,1,0:T(8,128)S(1)} %pass.3.whole), channel_id=1, source_target_pairs={{0,1},{1,0},{2,3},{3,2},{4,5},{5,4},{6,7},{7,6},{8,9},{9,8},{10,11... | collective-permute-start | bytes 3145736 | tf_op jit(solution)/shard_map/ppermute | solution.py:595
  (15 other events, 46.7 us)
Sparse Core Ops, SparseCore 0:
  100.6 22.2 all-gather.2

commit v9 on v8

--- a/solution.py
+++ b/solution.py
@@ -229,8 +229,8 @@
 ANYWHERE = pl.BlockSpec(memory_space=pl.ANY)
 
 
-def second_kernel(keep_a, recv_a, keep_b, recv_b, after, keep, send_a, send_b):
-    del after
+def second_kernel(keep_a, recv_a, keep_b, recv_b, *rest):
+    keep, send_a, send_b = rest[-3:]
     _, p, q = whereabouts()
     send_a[...] = keep_a[1 - p] + recv_a[1 - p]
     send_b[...] = keep_b[1 - q] + recv_b[1 - q]
@@ -244,9 +244,9 @@
     return small(
         second_kernel,
         out_shape,
-        [keep_a, recv_a, keep_b, recv_b, after],
+        [keep_a, recv_a, keep_b, recv_b, *after],
         "second_sums",
-        [IN_VMEM] * 4 + [ANYWHERE],
+        [IN_VMEM] * 4 + [ANYWHERE] * len(after),
     )
 
 
@@ -357,7 +357,7 @@
 
 
 def sum_kernel(*rest):
-    *terms, _, out = rest
+    *terms, out = rest
     total = terms[0][...]
     for term in terms[1:]:
         total += term[...]
@@ -380,9 +380,10 @@
         out[(me - away) & 3] = piece[...]
 
 
-def gather(axis_of, pieces, name):
+def gather(axis_of, pieces, name, after=()):
     whole = jax.ShapeDtypeStruct((4,) + pieces[0].shape, F32)
-    return small(functools.partial(gather_kernel, axis_of), whole, pieces, name)
+    specs = [IN_VMEM] * 4 + [ANYWHERE] * len(after)
+    return small(functools.partial(gather_kernel, axis_of), whole, [*pieces, *after], name, specs)
 
 
 def place_kernel(count_ref, target_ref, arrived, after, send, *keeps):
@@ -430,39 +431,50 @@
     return small(place_kernel, [send] + [keep] * 4, args, "place", specs)
 
 
-def self_kernel(pre_grad, weight, after, out):
+def join_kernel(*rest):
+    *keeps, swapped = rest[: len(rest) // 2 + 1]
+    for k, out in enumerate(rest[len(rest) // 2 + 1 :]):
+        out[0] = keeps[k][...]
+        out[1] = swapped[k + 1]
+
+
+def self_kernel(pre_grad, weight, other_local, own_local, after, out, total):
     del after
+    core, _, _ = whereabouts()
+    width = own_local.shape[1]
+    own = pl.ds(pl.multiple_of(core * width, width), width)
+    other = pl.ds(pl.multiple_of((1 - core) * width, width), width)
     contract = (((1,), (1,)), ((), ()))
     weight_high, weight_low = split(weight[...])
     rows = out.shape[0] // 4
     for i in range(4):
         at = slice(i * rows, (i + 1) * rows)
         high, low = split(pre_grad[at])
-        total = lax.dot_general(high, weight_high, contract, preferred_element_type=F32)
-        total += lax.dot_general(high, weight_low, contract, preferred_element_type=F32)
-        total += lax.dot_general(low, weight_high, contract, preferred_element_type=F32)
-        out[at] = total
-
-
-def finish_kernel(base, other_local, own_local, *rest):
+        rows_of = lax.dot_general(high, weight_high, contract, preferred_element_type=F32)
+        rows_of += lax.dot_general(high, weight_low, contract, preferred_element_type=F32)
+        rows_of += lax.dot_general(low, weight_high, contract, preferred_element_type=F32)
+        out[at] = rows_of
+    for b in range(own_local.shape[0]):
+        total[b, own] = own_local[b]
+        total[b, other] = other_local[b]
+        out[b * BLOCK : (b + 1) * BLOCK] += total[b].T
+
+
+def finish_kernel(base, keep, swapped, *rest):
     *received, out, total, rows, sems = rest
     core, _, _ = whereabouts()
     chip = lax.axis_index("local") >> 1
-    blocks, width, _ = other_local.shape
-    share = received[0].shape[1]
-    own = pl.ds(pl.multiple_of(core * width, width), width)
-    other = pl.ds(pl.multiple_of((1 - core) * width, width), width)
+    blocks, share, _ = keep.shape
+    pieces = [keep, swapped.at[0]] + [some.at[k] for some in received for k in range(2)]
     copies = []
     for b in range(blocks):
-        total[b, own] = own_local[b]
-        total[b, other] = other_local[b]
-        for k, some in enumerate(received):
+        for k, some in enumerate(pieces):
             source = (chip - k // 2) & 3
             side = source >> 1
             quarter = side * 2 + ((source + side) & 1)
             first = core if k % 2 == 0 else 1 - core
-            start = pl.multiple_of(first * width + quarter * share, share)
-            total[b, pl.ds(start, share)] += some[b]
+            start = pl.multiple_of((first * 4 + quarter) * share, share)
+            total[b, pl.ds(start, share)] = some[b]
         at = slice(b * BLOCK, (b + 1) * BLOCK)
         rows[at] = base[at] + total[b].T
         copy = pltpu.make_async_copy(rows.at[at], out.at[at], sems.at[b])
@@ -472,14 +484,14 @@
         copy.wait()
 
 
-def finish(base, other_local, own_local, received):
+def finish(base, keep, swapped, received):
     node_rows, feat = base.shape
-    blocks = other_local.shape[0]
+    blocks = keep.shape[0]
     return pl.pallas_call(
         finish_kernel,
         out_shape=jax.ShapeDtypeStruct(base.shape, F32),
         in_specs=[IN_VMEM] * (3 + len(received)),
-        out_specs=pl.BlockSpec(memory_space=pl.ANY),
+        out_specs=ANYWHERE,
         scratch_shapes=[
             pltpu.VMEM((blocks, feat, BLOCK), F32),
             pltpu.VMEM((node_rows, feat), F32),
@@ -490,7 +502,7 @@
         ),
         compiler_params=limit(8),
         name="finish",
-    )(base, other_local, own_local, *received)
+    )(base, keep, swapped, *received)
 
 
 def on_device(
@@ -552,51 +564,46 @@
     base = small(
         self_kernel,
         jax.ShapeDtypeStruct(pre_grad.shape, F32),
-        [pre_grad, w_self, mine],
+        [pre_grad, w_self, other_local, own_local, mine],
         "self_rows",
-        [IN_VMEM, IN_VMEM, ANYWHERE],
+        [IN_VMEM] * 4 + [ANYWHERE],
+        scratch=[pltpu.VMEM((blocks, width, BLOCK), F32)],
         mebibytes=16,
         flops=6 * pre_grad.size * width,
     )
-    keep, send_a, send_b = second_sums(keep_a, recv_a, keep_b, recv_b, base)
+    keep, send_a, send_b = second_sums(keep_a, recv_a, keep_b, recv_b, [base, terms[1]])
     recv_a = lax.ppermute(send_a, "local", across)
     recv_b = lax.ppermute(send_b, "local", pairs)
     share_shape = jax.ShapeDtypeStruct(mine.shape, F32)
-    share = small(sum_kernel, share_shape, [*terms, keep], "sum_z", [IN_VMEM] * 4 + [ANYWHERE])
-    shares = third_sums(places, keep, recv_a, recv_b, share)
-    arrived = lax.all_to_all(shares, "group", split_axis=0, concat_axis=0, tiled=True)
-
-    share = small(pass_kernel, share_shape, [share, shares], "pass", [IN_VMEM, ANYWHERE])
+    share = small(sum_kernel, share_shape, terms, "sum_z")
     terms = [share] + [lax.ppermute(share, "local", p) for p in (pairs, across, along_x[2])]
     scale = float(node_rows * groups * members) ** (-0.5)
     share = small(functools.partial(chips_kernel, scale), share_shape, terms, "sum_chips")
+    shares = third_sums(places, keep, recv_a, recv_b, share)
+    arrived = lax.all_to_all(shares, "group", split_axis=0, concat_axis=0, tiled=True)
     terms = [share] + [lax.ppermute(share, "group", along_z[k]) for k in range(1, 4)]
-
     row = gather(lambda g: g & 3, terms, "gather_z")
-    rows_of_y = [[z + 4 * y for y in range(4)] for z in range(4)]
-    whole = lax.all_gather(row, "group", axis_index_groups=rows_of_y)
 
     send, *keeps = place(halo_count, halo_target, arrived, row, blocks)
     swapped = lax.ppermute(send, "local", swap)
-    received = []
-    for k in range(4):
-        pair = [keeps[k], swapped[k]]
-        if k > 0:
-            pair = [lax.ppermute(some, "local", along_x[k]) for some in pair]
-        received += pair
-
-    whole = small(
+    joined = jax.ShapeDtypeStruct((2,) + keeps[0].shape, F32)
+    joined = small(join_kernel, [joined] * 3, [*keeps[1:], swapped], "join")
+    received = [lax.ppermute(joined[k - 1], "local", along_x[k]) for k in range(1, 4)]
+
+    row = small(
         pass_kernel,
-        pieces,
-        [whole.reshape(pieces.shape), *received[2:]],
+        jax.ShapeDtypeStruct(row.shape, F32),
+        [row, joined[0]],
         "pass",
-        [IN_VMEM] + [ANYWHERE] * 6,
-    )
+        [IN_VMEM, ANYWHERE],
+    )
+    rows = [row] + [lax.ppermute(row, "group", along_y[k]) for k in range(1, 4)]
+    whole = gather(lambda g: g >> 2, rows, "gather_y", received).reshape(pieces.shape)
     other = lax.ppermute(whole, "local", swap)
     square = jax.ShapeDtypeStruct(self_term.shape, F32)
     self_grad, neigh_grad = small(grads_kernel, [square] * 2, [whole, other], "sort_grads")
 
-    node_grad = finish(base, other_local, own_local, received)
+    node_grad = finish(base, keeps[0], swapped, received)
     return (node_grad, self_grad, neigh_grad)
 
 

time: 146 us -> 132 us (0.904)
  between operations: 14.3 us -> 0.9 us
  starting transfers between devices: 40.4 us -> 47.4 us
  local copies, waits for them, and re-layouts: 4.49 us -> 0.25 us
  Pallas kernels: 28 us -> 26.4 us
    ppermute x1, starting transfers between devices: 0.88 us -> 5.17 us  [on_device(): swapped = lax.ppermute(send, 'local', swap)]
    all_gather x1 -> x0, waiting for transfers between devices: 4.12 us -> none  [on_device(): whole = lax.all_gather(row, 'group', axis_index_groups=rows_of_y)]
    unnamed x38 -> x26, local copies, waits for them, and re-layouts: 3.5 us -> 0.25 us
    ppermute x6, waiting for transfers between devices: 16.3 us -> 19.3 us  [the longest x3 9.76 us: on_device(): rows = [row] + [lax.ppermute(row, 'group', along_y[k]) for k in range(1, 4)]]
    ppermute x6, starting transfers between devices: 5.07 us -> 7.43 us  [the longest x3 4.16 us: on_device(): rows = [row] + [lax.ppermute(row, 'group', along_y[k]) for k in range(1, 4)]]
    ppermute x1, waiting for transfers between devices: 0.01 us -> 2.29 us  [on_device(): swapped = lax.ppermute(send, 'local', swap)]
    ppermute x1, waiting for transfers between devices: 2.12 us -> 0.01 us  [on_device(): recv_a = lax.ppermute(send_a, 'local', pairs)]
    ppermute x1, waiting for transfers between devices: 2.06 us -> 0.01 us  [on_device(): recv_a = lax.ppermute(send_a, 'local', across)]
  transfers between devices with their start and end apart: 28 -> 27, of which waited for: 21 -> 21; matrix products, arithmetic and copies ran while one was open for 4% -> 4% of each run, Pallas kernels for 10% -> 9%
where the time goes in v9:
time: 132 us
  waiting for transfers between devices  51.7 us (39%)
  starting transfers between devices  47.4 us (36%)
  Pallas kernels  26.4 us (20%)
  matrix products  5.45 us (4%)
    pallas_call x2, Pallas kernels, tile_sums(): pl.pallas_call(functools.partial(tile_kernel, own, blocks, main, over), o...  16.3 us
    ppermute x3, waiting for transfers between devices, on_device(): lax.ppermute(some, 'group', along_y[k + 1])  10.2 us
    ppermute x3, waiting for transfers between devices, on_device(): rows = [row] + [lax.ppermute(row, 'group', along_y[k]) for k in range(1, 4)]  9.76 us
    ppermute x3, waiting for transfers between devices, on_device(): lax.ppermute(joined[k - 1], 'local', along_x[k])  9.5 us
    pallas_call x14, Pallas kernels, small(): pl.pallas_call(kernel, out_shape=out_shape, in_specs=specs or [IN_VMEM] *...  8.45 us
    ppermute x3, waiting for transfers between devices, on_device(): lax.ppermute(share, 'group', along_z[k])  8.15 us
    all_to_all x1, starting transfers between devices, on_device(): lax.all_to_all(shares, 'group', split_axis=0, concat_axis=0, tiled=True)  7.15 us
    ppermute x3, starting transfers between devices, on_device(): lax.ppermute(some, 'group', along_z[k + 1])  5.71 us
  transfers between devices with their start and end apart: 27, of which 21 were waited for; matrix products, arithmetic and copies ran while one was open for 4% of the time, Pallas kernels for 9%

profile of v9, /device:TPU:1, one launch (start us, length us, event | category | flops | bytes accessed | tf_op | source)
XLA Modules:
  0.0 132.1 jit_solution(3992388213890533858)
XLA Ops:
  0.6 9.8 %other_tile_sums.1 = (f32[1024,512]{1,0:T(8,128)}, f32[8,256,128]{2,1,0:T(8,128)}, f32[30,256,128]{2,1,0:T(8,128)}, s32[32]{0:T(128)}, s32[64]{0:T(128)}) custom-call(s32[64]{0:T(128)} %col_ref.1, s32[16,16]{1,0:T(8,128)} %count_ref.5, f32[1024,512]{1,0:T(8,128)} %rest_0_.1, f32[1024,512]{1,0:T(8,128)} %rest_1_.2, f32[512,512]{1,0:T(8,128)} %rest_1_.3, ...), custom_call_target="tpu_custom_call" | custom-call | flops 2415919104 | bytes 14680064 | tf_op jit(solution)/shard_map/other_tile_sums/pallas_call | solution.py:208
  12.0 3.6 %convolution_bitcast_fusion.neigh_term = f32[512,512]{1,0:T(8,128)S(1)} fusion(f32[1024,512]{1,0:T(8,128)} %get-tuple-element.37.rest_0_.pre_grad, f32[1024,512]{1,0:T(8,128)S(1)} %copy-done), kind=kOutput, calls=%fused_computation | convolution fusion | flops 1610612736 | bytes 5242880 | tf_op jit(solution)/shard_map/dot_general | solution.py:548
  15.6 1.9 %convolution_bitcast_fusion.1.self_term = f32[512,512]{1,0:T(8,128)S(1)} fusion(f32[1024,512]{1,0:T(8,128)S(1)} %copy-done.1, f32[1024,512]{1,0:T(8,128)S(1)} %copy-done.12), kind=kOutput, calls=%fused_computation.1 | convolution fusion | flops 1610612736 | bytes 5242880 | tf_op jit(solution)/shard_map/dot_general | solution.py:545
  18.8 6.5 %own_tile_sums.1 = (f32[8,256,128]{2,1,0:T(8,128)S(1)}, s32[1]{0:T(128)}, f32[2,15,64,128]{3,2,1,0:T(8,128)S(1)}, f32[2,15,64,128]{3,2,1,0:T(8,128)S(1)}, f32[2,...) custom-call(s32[64]{0:T(128)S(1)} %copy-done.11, s32[16,16]{1,0:T(8,128)S(1)} %copy-done.8, ...), custom_call_target="tpu_custom_call" | custom-call | flops 2415919104 | bytes 14680064 | tf_op jit(solution)/shard_map/own_tile_sums/pallas_call | solution.py:208
  26.7 1.8 %collective-permute-start.6 = (f32[2,15,64,128]{3,2,1,0:T(8,128)S(1)}, f32[2,15,64,128]{3,2,1,0:T(8,128)S(1)}, u32[]{:S(2)}, u32[]{:S(2)}) collective-permute-start(f32[2,15,64,128]{3,2,1,0:T(8,128)S(1)} %get-tuple-element.54), channel_id=1, source_target_pairs={{0,6},{1,7},{2,4},{3,5},{4,2},{5,3},{6,0},{7,1},{8,14},{9,15},{10,... | collective-permute-start | bytes 2949128 | tf_op jit(solution)/shard_map/ppermute | solution.py:542
  30.7 2.6 %collective-permute-start.3 = (f32[4,4,32,128]{3,2,1,0:T(8,128)S(1)}, f32[4,4,32,128]{3,2,1,0:T(8,128)S(1)}, u32[]{:S(2)}, u32[]{:S(2)}) collective-permute-start(f32[4,4,32,128]{3,2,1,0:T(8,128)S(1)} %get-tuple-element.47), channel_id=1, source_target_pairs={{0,64},{8,72},{16,80},{24,88},{32,96},{40,104},{48,112},{56,120},{... | collective-permute-start | bytes 786440 | tf_op jit(solution)/shard_map/ppermute | solution.py:557
  34.4 3.4 %collective-permute-done.2.rest_1_ = f32[4,4,32,128]{3,2,1,0:T(8,128)S(1)} collective-permute-done((f32[4,4,32,128]{3,2,1,0:T(8,128)S(1)}, f32[4,4,32,128]{3,2,1,0:T(8,128)S(1)}, u32[]{:S(2)}, u32[]{:S(2)}) %collective-permute-start.2) | collective-permute-done | bytes 262176 | tf_op jit(solution)/shard_map/ppermute | solution.py:557
  37.8 6.7 %collective-permute-done.3.rest_2_ = f32[4,4,32,128]{3,2,1,0:T(8,128)S(1)} collective-permute-done((f32[4,4,32,128]{3,2,1,0:T(8,128)S(1)}, f32[4,4,32,128]{3,2,1,0:T(8,128)S(1)}, u32[]{:S(2)}, u32[]{:S(2)}) %collective-permute-start.3) | collective-permute-done | bytes 262176 | tf_op jit(solution)/shard_map/ppermute | solution.py:557
  44.6 1.7 %collective-permute-start.7 = (f32[4,32,128]{2,1,0:T(8,128)S(1)}, f32[4,32,128]{2,1,0:T(8,128)S(1)}, u32[]{:S(2)}, u32[]{:S(2)}) collective-permute-start(f32[4,32,128]{2,1,0:T(8,128)S(1)} %get-tuple-element.55), channel_id=1, source_target_pairs={{0,8},{8,16},{16,24},{24,0},{32,40},{40,48},{48,56},{56,32},{64,72... | collective-permute-start | bytes 196616 | tf_op jit(solution)/shard_map/ppermute | solution.py:561
  46.3 2.2 %self_rows.1.rest_0_.base = f32[1024,512]{1,0:T(8,128)S(1)} custom-call(f32[1024,512]{1,0:T(8,128)S(1)} %copy-done.1, f32[512,512]{1,0:T(8,128)S(1)} %copy-done.6, f32[8,256,128]{2,1,0:T(8,128)S(1)} %copy-done.7, f32[8,256,128]{2,1,0:T(8,128)S(1)} %get-tuple-element.41.own_local, f32[4,32,128]{2,1,0:T(8,128)S(1)} %get-tuple-element.49.after.rest_0_), custom_call_target="tpu_custom_call" | custom-call | flops 1610612736 | bytes 6291456 | tf_op jit(solution)/shard_map/self_rows/pallas_call | solution.py:280
  48.6 1.8 %collective-permute-done.7.rest_1_ = f32[4,32,128]{2,1,0:T(8,128)S(1)} collective-permute-done((f32[4,32,128]{2,1,0:T(8,128)S(1)}, f32[4,32,128]{2,1,0:T(8,128)S(1)}, u32[]{:S(2)}, u32[]{:S(2)}) %collective-permute-start.7) | collective-permute-done | bytes 65568 | tf_op jit(solution)/shard_map/ppermute | solution.py:561
  51.0 1.9 %collective-permute-start.8 = (f32[15,64,128]{2,1,0:T(8,128)S(1)}, f32[15,64,128]{2,1,0:T(8,128)S(1)}, u32[]{:S(2)}, u32[]{:S(2)}) collective-permute-start(f32[15,64,128]{2,1,0:T(8,128)S(1)} %get-tuple-element.57), channel_id=1, source_target_pairs={{0,6},{1,7},{2,4},{3,5},{4,2},{5,3},{6,0},{7,1},{8,14},{9,15},{10,... | collective-permute-start | bytes 1474568 | tf_op jit(solution)/shard_map/ppermute | solution.py:575
  52.9 3.6 %collective-permute-start.10 = (f32[4,32,128]{2,1,0:T(8,128)S(1)}, f32[4,32,128]{2,1,0:T(8,128)S(1)}, u32[]{:S(2)}, u32[]{:S(2)}) collective-permute-start(f32[4,32,128]{2,1,0:T(8,128)S(1)} %get-tuple-element.59), channel_id=1, source_target_pairs={{0,16},{8,24},{16,0},{24,8},{32,48},{40,56},{48,32},{56,40},{64,80... | collective-permute-start | bytes 196616 | tf_op jit(solution)/shard_map/ppermute | solution.py:561
  58.1 1.8 %collective-permute-done.11.rest_3_ = f32[4,32,128]{2,1,0:T(8,128)S(1)} collective-permute-done((f32[4,32,128]{2,1,0:T(8,128)S(1)}, f32[4,32,128]{2,1,0:T(8,128)S(1)}, u32[]{:S(2)}, u32[]{:S(2)}) %collective-permute-start.11) | collective-permute-done | bytes 65568 | tf_op jit(solution)/shard_map/ppermute | solution.py:561
  63.3 2.1 %collective-permute-done.12.pair = f32[4,32,128]{2,1,0:T(8,128)S(1)} collective-permute-done((f32[4,32,128]{2,1,0:T(8,128)S(1)}, f32[4,32,128]{2,1,0:T(8,128)S(1)}, u32[]{:S(2)}, u32[]{:S(2)}) %collective-permute-start.12) | collective-permute-done | bytes 65568 | tf_op jit(solution)/shard_map/ppermute | solution.py:579
  65.9 1.8 %collective-permute-done.14.far_two = f32[4,32,128]{2,1,0:T(8,128)S(1)} collective-permute-done((f32[4,32,128]{2,1,0:T(8,128)S(1)}, f32[4,32,128]{2,1,0:T(8,128)S(1)}, u32[]{:S(2)}, u32[]{:S(2)}) %collective-permute-start.14) | collective-permute-done | bytes 65568 | tf_op jit(solution)/shard_map/ppermute | solution.py:579
  67.8 1.7 %third_sums.1 = f32[32,64,128]{2,1,0:T(8,128)} custom-call(s32[32]{0:T(128)S(1)} %copy-done.10, f32[2,15,64,128]{3,2,1,0:T(8,128)S(1)} %get-tuple-element.56.keep, f32[15,64,128]{2,1,0:T(8,128)S(1)} %collective-permute-done.8.recv_a, f32[15,64,128]{2,1,0:T(8,128)S(1)} %collective-permute-done.9.recv_b, f32[4,32,128]{2,1,0:T(8,128)S(1)} %sum_chips.1.after.rest_0_), custom_call_target="tpu_custom_call" | custom-call | flops 245760 | bytes 2949120 | tf_op jit(solution)/shard_map/third_sums/pallas_call | solution.py:280
  69.4 7.2 %all-to-all-start = ((f32[32,64,128]{2,1,0:T(8,128)}), f32[32,64,128]{2,1,0:T(8,128)S(1)}, u32[]{:S(2)}, u32[]{:S(2)}) async-start(f32[32,64,128]{2,1,0:T(8,128)} %third_sums.1), calls=%async_computation | async-start | bytes 2097152 | tf_op jit(solution)/shard_map/all_to_all | solution.py:583
  78.0 2.4 %collective-permute-start.16 = (f32[4,32,128]{2,1,0:T(8,128)S(1)}, f32[4,32,128]{2,1,0:T(8,128)S(1)}, u32[]{:S(2)}, u32[]{:S(2)}) collective-permute-start(f32[4,32,128]{2,1,0:T(8,128)S(1)} %sum_chips.1.after.rest_0_), channel_id=1, source_target_pairs={{0,16},{8,24},{16,0},{24,8},{32,48},{40,56},{48,32},{56,40},{64,80... | collective-permute-start | bytes 196616 | tf_op jit(solution)/shard_map/ppermute | solution.py:584
  82.4 5.3 %collective-permute-done.16.rest_2_ = f32[4,32,128]{2,1,0:T(8,128)S(1)} collective-permute-done((f32[4,32,128]{2,1,0:T(8,128)S(1)}, f32[4,32,128]{2,1,0:T(8,128)S(1)}, u32[]{:S(2)}, u32[]{:S(2)}) %collective-permute-start.16) | collective-permute-done | bytes 65568 | tf_op jit(solution)/shard_map/ppermute | solution.py:584
  87.8 1.9 %collective-permute-done.17.rest_3_ = f32[4,32,128]{2,1,0:T(8,128)S(1)} collective-permute-done((f32[4,32,128]{2,1,0:T(8,128)S(1)}, f32[4,32,128]{2,1,0:T(8,128)S(1)}, u32[]{:S(2)}, u32[]{:S(2)}) %collective-permute-start.17) | collective-permute-done | bytes 65568 | tf_op jit(solution)/shard_map/ppermute | solution.py:584
  90.7 1.6 %place.1 = (f32[4,8,64,128]{3,2,1,0:T(8,128)S(1)}, f32[8,64,128]{2,1,0:T(8,128)S(1)}, f32[8,64,128]{2,1,0:T(8,128)S(1)}, f32[8,64,128]{2,1,0:T(8,128)S(1)}, f32[8,64,128]{2,1,0:T(8,128)S(1)}) custom-call(s32[16,16]{1,0:T(8,128)S(1)} %copy-done.8, s32[16,32]{1,0:T(8,128)S(1)} %copy-done.9, f32[32,64,128]{2,1,0:T(8,128)S(1)} %all-to-all-done.arrived, ...), custom_call_target="tpu_custom_call" | custom-call | flops 262144 | bytes 3145728 | tf_op jit(solution)/shard_map/place/pallas_call | solution.py:280
  92.4 5.2 %collective-permute-start.18 = (f32[4,8,64,128]{3,2,1,0:T(8,128)S(1)}, f32[4,8,64,128]{3,2,1,0:T(8,128)S(1)}, u32[]{:S(2)}, u32[]{:S(2)}) collective-permute-start(f32[4,8,64,128]{3,2,1,0:T(8,128)S(1)} %get-tuple-element.62), channel_id=1, source_target_pairs={{0,1},{1,0},{2,3},{3,2},{4,5},{5,4},{6,7},{7,6},{8,9},{9,8},{10,11... | collective-permute-start | bytes 3145736 | tf_op jit(solution)/shard_map/ppermute | solution.py:588
  97.6 2.3 %collective-permute-done.18.rest_3_.swapped = f32[4,8,64,128]{3,2,1,0:T(8,128)S(1)} collective-permute-done((f32[4,8,64,128]{3,2,1,0:T(8,128)S(1)}, f32[4,8,64,128]{3,2,1,0:T(8,128)S(1)}, u32[]{:S(2)}, u32[]{:S(2)}) %collective-permute-start.18) | collective-permute-done | bytes 1048608 | tf_op jit(solution)/shard_map/ppermute | solution.py:588
  100.8 3.0 %collective-permute-start.20 = (f32[2,8,64,128]{3,2,1,0:T(8,128)S(1)}, f32[2,8,64,128]{3,2,1,0:T(8,128)S(1)}, u32[]{:S(2)}, u32[]{:S(2)}) collective-permute-start(f32[2,8,64,128]{3,2,1,0:T(8,128)S(1)} %get-tuple-element.67), channel_id=1, source_target_pairs={{0,4},{1,5},{2,6},{3,7},{4,0},{5,1},{6,2},{7,3},{8,12},{9,13},{10,... | collective-permute-start | bytes 1572872 | tf_op jit(solution)/shard_map/ppermute | solution.py:591
  104.1 2.5 %collective-permute-start.23 = (f32[4,4,32,128]{3,2,1,0:T(8,128)S(1)}, f32[4,4,32,128]{3,2,1,0:T(8,128)S(1)}, u32[]{:S(2)}, u32[]{:S(2)}) collective-permute-start(f32[4,4,32,128]{3,2,1,0:T(8,128)S(1)} %pass.1.rest_0_), channel_id=1, source_target_pairs={{0,64},{8,72},{16,80},{24,88},{32,96},{40,104},{48,112},{56,120},{... | collective-permute-start | bytes 786440 | tf_op jit(solution)/shard_map/ppermute | solution.py:600
  106.6 2.2 %collective-permute-done.22.rest_1_ = f32[4,4,32,128]{3,2,1,0:T(8,128)S(1)} collective-permute-done((f32[4,4,32,128]{3,2,1,0:T(8,128)S(1)}, f32[4,4,32,128]{3,2,1,0:T(8,128)S(1)}, u32[]{:S(2)}, u32[]{:S(2)}) %collective-permute-start.22) | collective-permute-done | bytes 262176 | tf_op jit(solution)/shard_map/ppermute | solution.py:600
  109.6 5.3 %collective-permute-done.23.rest_2_ = f32[4,4,32,128]{3,2,1,0:T(8,128)S(1)} collective-permute-done((f32[4,4,32,128]{3,2,1,0:T(8,128)S(1)}, f32[4,4,32,128]{3,2,1,0:T(8,128)S(1)}, u32[]{:S(2)}, u32[]{:S(2)}) %collective-permute-start.23) | collective-permute-done | bytes 262176 | tf_op jit(solution)/shard_map/ppermute | solution.py:600
  115.0 2.2 %collective-permute-done.24.rest_3_ = f32[4,4,32,128]{3,2,1,0:T(8,128)S(1)} collective-permute-done((f32[4,4,32,128]{3,2,1,0:T(8,128)S(1)}, f32[4,4,32,128]{3,2,1,0:T(8,128)S(1)}, u32[]{:S(2)}, u32[]{:S(2)}) %collective-permute-start.24) | collective-permute-done | bytes 262176 | tf_op jit(solution)/shard_map/ppermute | solution.py:600
  117.2 9.2 %collective-permute-done.20.rest_1_.rest_5_ = f32[2,8,64,128]{3,2,1,0:T(8,128)S(1)} collective-permute-done((f32[2,8,64,128]{3,2,1,0:T(8,128)S(1)}, f32[2,8,64,128]{3,2,1,0:T(8,128)S(1)}, u32[]{:S(2)}, u32[]{:S(2)}) %collective-permute-start.20) | collective-permute-done | bytes 524320 | tf_op jit(solution)/shard_map/ppermute | solution.py:591
  126.8 1.6 %collective-permute-start.25 = (f32[16,4,32,128]{3,2,1,0:T(8,128)S(1)}, f32[16,4,32,128]{3,2,1,0:T(8,128)S(1)}, u32[]{:S(2)}, u32[]{:S(2)}) collective-permute-start(f32[16,4,32,128]{3,2,1,0:T(8,128)S(1)} %bitcast.11), channel_id=1, source_target_pairs={{0,1},{1,0},{2,3},{3,2},{4,5},{5,4},{6,7},{7,6},{8,9},{9,8},{10,11... | collective-permute-start | bytes 3145736 | tf_op jit(solution)/shard_map/ppermute | solution.py:602
  128.4 1.7 %finish.1 = f32[1024,512]{1,0:T(8,128)} custom-call(f32[1024,512]{1,0:T(8,128)S(1)} %copy-done.3, f32[8,64,128]{2,1,0:T(8,128)S(1)} %get-tuple-element.61.keep, f32[4,8,64,128]{3,2,1,0:T(8,128)S(1)} %collective-permute-done.18.rest_3_.swapped, f32[2,8,64,128]{3,2,1,0:T(8,128)S(1)} %collective-permute-done.19.rest_0_.rest_4_, ...), custom_call_target="tpu_custom_call" | custom-call | flops 1048576 | bytes 8388608 | tf_op jit(solution)/shard_map/finish/pallas_call | solution.py:490
  (67 shorter events, 22.7 us)
Async XLA Ops:
  10.5 8.1 %collective-permute-start = (f32[30,256,128]{2,1,0:T(8,128)}, f32[30,256,128]{2,1,0:T(8,128)S(1)}, u32[]{:S(2)}, u32[]{:S(2)}) collective-permute-start(f32[30,256,128]{2,1,0:T(8,128)} %get-tuple-element.40), channel_id=1, source_target_pairs={{0,1},{1,0},{2,3},{3,2},{4,5},{5,4},{6,7},{7,6},{8,9},{9,8},{10,11... | collective-permute-start | bytes 11796488 | tf_op jit(solution)/shard_map/ppermute | solution.py:537
  17.7 10.9 %collective-permute-start.1 = (f32[16,4,32,128]{3,2,1,0:T(8,128)S(1)}, f32[16,4,32,128]{3,2,1,0:T(8,128)S(1)}, u32[]{:S(2)}, u32[]{:S(2)}) collective-permute-start(f32[16,4,32,128]{3,2,1,0:T(8,128)S(1)} %get-tuple-element.43), channel_id=1, source_target_pairs={{0,1},{1,0},{2,3},{3,2},{4,5},{5,4},{6,7},{7,6},{8,9},{9,8},{10,11... | collective-permute-start | bytes 3145736 | tf_op jit(solution)/shard_map/ppermute | solution.py:554
  25.3 21.0 %copy-start.6 = (f32[512,512]{1,0:T(8,128)S(1)}, f32[512,512]{1,0:T(8,128)}, u32[]{:S(2)}) copy-start(f32[512,512]{1,0:T(8,128)} %weight.1) | copy-start | bytes 3145732
  25.3 21.0 %copy-start.7 = (f32[8,256,128]{2,1,0:T(8,128)S(1)}, f32[8,256,128]{2,1,0:T(8,128)}, u32[]{:S(2)}) copy-start(f32[8,256,128]{2,1,0:T(8,128)} %get-tuple-element.38.other_local) | copy-start | bytes 3145732
  25.3 25.0 %collective-permute-start.5 = (f32[2,15,64,128]{3,2,1,0:T(8,128)S(1)}, f32[2,15,64,128]{3,2,1,0:T(8,128)S(1)}, u32[]{:S(2)}, u32[]{:S(2)}) collective-permute-start(f32[2,15,64,128]{3,2,1,0:T(8,128)S(1)} %get-tuple-element.52), channel_id=1, source_target_pairs={{0,2},{1,3},{2,0},{3,1},{4,6},{5,7},{6,4},{7,5},{8,10},{9,11},{10,... | collective-permute-start | bytes 2949128 | tf_op jit(solution)/shard_map/ppermute | solution.py:541
  26.7 24.1 %collective-permute-start.6 = (f32[2,15,64,128]{3,2,1,0:T(8,128)S(1)}, f32[2,15,64,128]{3,2,1,0:T(8,128)S(1)}, u32[]{:S(2)}, u32[]{:S(2)}) collective-permute-start(f32[2,15,64,128]{3,2,1,0:T(8,128)S(1)} %get-tuple-element.54), channel_id=1, source_target_pairs={{0,6},{1,7},{2,4},{3,5},{4,2},{5,3},{6,0},{7,1},{8,14},{9,15},{10,... | collective-permute-start | bytes 2949128 | tf_op jit(solution)/shard_map/ppermute | solution.py:542
  29.3 8.5 %collective-permute-start.2 = (f32[4,4,32,128]{3,2,1,0:T(8,128)S(1)}, f32[4,4,32,128]{3,2,1,0:T(8,128)S(1)}, u32[]{:S(2)}, u32[]{:S(2)}) collective-permute-start(f32[4,4,32,128]{3,2,1,0:T(8,128)S(1)} %get-tuple-element.46), channel_id=1, source_target_pairs={{0,32},{8,40},{16,48},{24,56},{32,64},{40,72},{48,80},{56,88},{64,... | collective-permute-start | bytes 786440 | tf_op jit(solution)/shard_map/ppermute | solution.py:557
  30.7 13.9 %collective-permute-start.3 = (f32[4,4,32,128]{3,2,1,0:T(8,128)S(1)}, f32[4,4,32,128]{3,2,1,0:T(8,128)S(1)}, u32[]{:S(2)}, u32[]{:S(2)}) collective-permute-start(f32[4,4,32,128]{3,2,1,0:T(8,128)S(1)} %get-tuple-element.47), channel_id=1, source_target_pairs={{0,64},{8,72},{16,80},{24,88},{32,96},{40,104},{48,112},{56,120},{... | collective-permute-start | bytes 786440 | tf_op jit(solution)/shard_map/ppermute | solution.py:557
  33.3 11.2 %collective-permute-start.4 = (f32[4,4,32,128]{3,2,1,0:T(8,128)S(1)}, f32[4,4,32,128]{3,2,1,0:T(8,128)S(1)}, u32[]{:S(2)}, u32[]{:S(2)}) collective-permute-start(f32[4,4,32,128]{3,2,1,0:T(8,128)S(1)} %get-tuple-element.48), channel_id=1, source_target_pairs={{0,96},{8,104},{16,112},{24,120},{32,0},{40,8},{48,16},{56,24},{64... | collective-permute-start | bytes 786440 | tf_op jit(solution)/shard_map/ppermute | solution.py:557
  44.6 5.8 %collective-permute-start.7 = (f32[4,32,128]{2,1,0:T(8,128)S(1)}, f32[4,32,128]{2,1,0:T(8,128)S(1)}, u32[]{:S(2)}, u32[]{:S(2)}) collective-permute-start(f32[4,32,128]{2,1,0:T(8,128)S(1)} %get-tuple-element.55), channel_id=1, source_target_pairs={{0,8},{8,16},{16,24},{24,0},{32,40},{40,48},{48,56},{56,32},{64,72... | collective-permute-start | bytes 196616 | tf_op jit(solution)/shard_map/ppermute | solution.py:561
  50.8 17.0 %copy-start.10 = (s32[32]{0:T(128)S(1)}, s32[32]{0:T(128)}, u32[]{:S(2)}) copy-start(s32[32]{0:T(128)} %get-tuple-element.50.places) | copy-start | bytes 388
  51.0 16.7 %collective-permute-start.8 = (f32[15,64,128]{2,1,0:T(8,128)S(1)}, f32[15,64,128]{2,1,0:T(8,128)S(1)}, u32[]{:S(2)}, u32[]{:S(2)}) collective-permute-start(f32[15,64,128]{2,1,0:T(8,128)S(1)} %get-tuple-element.57), channel_id=1, source_target_pairs={{0,6},{1,7},{2,4},{3,5},{4,2},{5,3},{6,0},{7,1},{8,14},{9,15},{10,... | collective-permute-start | bytes 1474568 | tf_op jit(solution)/shard_map/ppermute | solution.py:575
  52.9 14.9 %collective-permute-start.9 = (f32[15,64,128]{2,1,0:T(8,128)S(1)}, f32[15,64,128]{2,1,0:T(8,128)S(1)}, u32[]{:S(2)}, u32[]{:S(2)}) collective-permute-start(f32[15,64,128]{2,1,0:T(8,128)S(1)} %get-tuple-element.58), channel_id=1, source_target_pairs={{0,2},{1,3},{2,0},{3,1},{4,6},{5,7},{6,4},{7,5},{8,10},{9,11},{10,... | collective-permute-start | bytes 1474568 | tf_op jit(solution)/shard_map/ppermute | solution.py:576
  52.9 5.2 %collective-permute-start.10 = (f32[4,32,128]{2,1,0:T(8,128)S(1)}, f32[4,32,128]{2,1,0:T(8,128)S(1)}, u32[]{:S(2)}, u32[]{:S(2)}) collective-permute-start(f32[4,32,128]{2,1,0:T(8,128)S(1)} %get-tuple-element.59), channel_id=1, source_target_pairs={{0,16},{8,24},{16,0},{24,8},{32,48},{40,56},{48,32},{56,40},{64,80... | collective-permute-start | bytes 196616 | tf_op jit(solution)/shard_map/ppermute | solution.py:561
  56.5 3.4 %collective-permute-start.11 = (f32[4,32,128]{2,1,0:T(8,128)S(1)}, f32[4,32,128]{2,1,0:T(8,128)S(1)}, u32[]{:S(2)}, u32[]{:S(2)}) collective-permute-start(f32[4,32,128]{2,1,0:T(8,128)S(1)} %get-tuple-element.60), channel_id=1, source_target_pairs={{0,24},{8,0},{16,8},{24,16},{32,56},{40,32},{48,40},{56,48},{64,88... | collective-permute-start | bytes 196616 | tf_op jit(solution)/shard_map/ppermute | solution.py:561
  59.9 5.5 %collective-permute-start.12 = (f32[4,32,128]{2,1,0:T(8,128)S(1)}, f32[4,32,128]{2,1,0:T(8,128)S(1)}, u32[]{:S(2)}, u32[]{:S(2)}) collective-permute-start(f32[4,32,128]{2,1,0:T(8,128)S(1)} %sum_z.1.mine), channel_id=1, source_target_pairs={{0,2},{1,3},{2,0},{3,1},{4,6},{5,7},{6,4},{7,5},{8,10},{9,11},{10,... | collective-permute-start | bytes 196616 | tf_op jit(solution)/shard_map/ppermute | solution.py:579
  61.4 4.5 %collective-permute-start.13 = (f32[4,32,128]{2,1,0:T(8,128)S(1)}, f32[4,32,128]{2,1,0:T(8,128)S(1)}, u32[]{:S(2)}, u32[]{:S(2)}) collective-permute-start(f32[4,32,128]{2,1,0:T(8,128)S(1)} %sum_z.1.mine), channel_id=1, source_target_pairs={{0,6},{1,7},{2,4},{3,5},{4,2},{5,3},{6,0},{7,1},{8,14},{9,15},{10,... | collective-permute-start | bytes 196616 | tf_op jit(solution)/shard_map/ppermute | solution.py:579
  62.3 5.4 %collective-permute-start.14 = (f32[4,32,128]{2,1,0:T(8,128)S(1)}, f32[4,32,128]{2,1,0:T(8,128)S(1)}, u32[]{:S(2)}, u32[]{:S(2)}) collective-permute-start(f32[4,32,128]{2,1,0:T(8,128)S(1)} %sum_z.1.mine), channel_id=1, source_target_pairs={{0,4},{1,5},{2,6},{3,7},{4,0},{5,1},{6,2},{7,3},{8,12},{9,13},{10,... | collective-permute-start | bytes 196616 | tf_op jit(solution)/shard_map/ppermute | solution.py:579
  67.7 23.0 %copy-start.9 = (s32[16,32]{1,0:T(8,128)S(1)}, s32[16,32]{1,0:T(8,128)}, u32[]{:S(2)}) copy-start(s32[16,32]{1,0:T(8,128)} %target_ref.1) | copy-start | bytes 6148
  69.4 21.3 %all-to-all-start = ((f32[32,64,128]{2,1,0:T(8,128)}), f32[32,64,128]{2,1,0:T(8,128)S(1)}, u32[]{:S(2)}, u32[]{:S(2)}) async-start(f32[32,64,128]{2,1,0:T(8,128)} %third_sums.1), calls=%async_computation | async-start | bytes 2097152 | tf_op jit(solution)/shard_map/all_to_all | solution.py:583
  76.6 5.8 %collective-permute-start.15 = (f32[4,32,128]{2,1,0:T(8,128)S(1)}, f32[4,32,128]{2,1,0:T(8,128)S(1)}, u32[]{:S(2)}, u32[]{:S(2)}) collective-permute-start(f32[4,32,128]{2,1,0:T(8,128)S(1)} %sum_chips.1.after.rest_0_), channel_id=1, source_target_pairs={{0,8},{8,16},{16,24},{24,0},{32,40},{40,48},{48,56},{56,32},{64,72... | collective-permute-start | bytes 196616 | tf_op jit(solution)/shard_map/ppermute | solution.py:584
  78.0 9.8 %collective-permute-start.16 = (f32[4,32,128]{2,1,0:T(8,128)S(1)}, f32[4,32,128]{2,1,0:T(8,128)S(1)}, u32[]{:S(2)}, u32[]{:S(2)}) collective-permute-start(f32[4,32,128]{2,1,0:T(8,128)S(1)} %sum_chips.1.after.rest_0_), channel_id=1, source_target_pairs={{0,16},{8,24},{16,0},{24,8},{32,48},{40,56},{48,32},{56,40},{64,80... | collective-permute-start | bytes 196616 | tf_op jit(solution)/shard_map/ppermute | solution.py:584
  80.4 9.3 %collective-permute-start.17 = (f32[4,32,128]{2,1,0:T(8,128)S(1)}, f32[4,32,128]{2,1,0:T(8,128)S(1)}, u32[]{:S(2)}, u32[]{:S(2)}) collective-permute-start(f32[4,32,128]{2,1,0:T(8,128)S(1)} %sum_chips.1.after.rest_0_), channel_id=1, source_target_pairs={{0,24},{8,0},{16,8},{24,16},{32,56},{40,32},{48,40},{56,48},{64,88... | collective-permute-start | bytes 196616 | tf_op jit(solution)/shard_map/ppermute | solution.py:584
  92.4 7.5 %collective-permute-start.18 = (f32[4,8,64,128]{3,2,1,0:T(8,128)S(1)}, f32[4,8,64,128]{3,2,1,0:T(8,128)S(1)}, u32[]{:S(2)}, u32[]{:S(2)}) collective-permute-start(f32[4,8,64,128]{3,2,1,0:T(8,128)S(1)} %get-tuple-element.62), channel_id=1, source_target_pairs={{0,1},{1,0},{2,3},{3,2},{4,5},{5,4},{6,7},{7,6},{8,9},{9,8},{10,11... | collective-permute-start | bytes 3145736 | tf_op jit(solution)/shard_map/ppermute | solution.py:588
  100.0 28.4 %copy-start.3 = (f32[1024,512]{1,0:T(8,128)S(1)}, f32[1024,512]{1,0:T(8,128)}, u32[]{:S(2)}) copy-start(f32[1024,512]{1,0:T(8,128)} %copy-done.2) | copy-start | bytes 6291460
  100.0 8.8 %collective-permute-start.22 = (f32[4,4,32,128]{3,2,1,0:T(8,128)S(1)}, f32[4,4,32,128]{3,2,1,0:T(8,128)S(1)}, u32[]{:S(2)}, u32[]{:S(2)}) collective-permute-start(f32[4,4,32,128]{3,2,1,0:T(8,128)S(1)} %pass.1.rest_0_), channel_id=1, source_target_pairs={{0,32},{8,40},{16,48},{24,56},{32,64},{40,72},{48,80},{56,88},{64,... | collective-permute-start | bytes 786440 | tf_op jit(solution)/shard_map/ppermute | solution.py:600
  100.8 16.4 %collective-permute-start.19 = (f32[2,8,64,128]{3,2,1,0:T(8,128)S(1)}, f32[2,8,64,128]{3,2,1,0:T(8,128)S(1)}, u32[]{:S(2)}, u32[]{:S(2)}) collective-permute-start(f32[2,8,64,128]{3,2,1,0:T(8,128)S(1)} %get-tuple-element.66.rest_0_), channel_id=1, source_target_pairs={{0,2},{1,3},{2,4},{3,5},{4,6},{5,7},{6,0},{7,1},{8,10},{9,11},{10,... | collective-permute-start | bytes 1572872 | tf_op jit(solution)/shard_map/ppermute | solution.py:591
  100.8 25.6 %collective-permute-start.20 = (f32[2,8,64,128]{3,2,1,0:T(8,128)S(1)}, f32[2,8,64,128]{3,2,1,0:T(8,128)S(1)}, u32[]{:S(2)}, u32[]{:S(2)}) collective-permute-start(f32[2,8,64,128]{3,2,1,0:T(8,128)S(1)} %get-tuple-element.67), channel_id=1, source_target_pairs={{0,4},{1,5},{2,6},{3,7},{4,0},{5,1},{6,2},{7,3},{8,12},{9,13},{10,... | collective-permute-start | bytes 1572872 | tf_op jit(solution)/shard_map/ppermute | solution.py:591
  103.8 22.9 %collective-permute-start.21 = (f32[2,8,64,128]{3,2,1,0:T(8,128)S(1)}, f32[2,8,64,128]{3,2,1,0:T(8,128)S(1)}, u32[]{:S(2)}, u32[]{:S(2)}) collective-permute-start(f32[2,8,64,128]{3,2,1,0:T(8,128)S(1)} %get-tuple-element.68), channel_id=1, source_target_pairs={{0,6},{1,7},{2,0},{3,1},{4,2},{5,3},{6,4},{7,5},{8,14},{9,15},{10,... | collective-permute-start | bytes 1572872 | tf_op jit(solution)/shard_map/ppermute | solution.py:591
  104.1 10.9 %collective-permute-start.23 = (f32[4,4,32,128]{3,2,1,0:T(8,128)S(1)}, f32[4,4,32,128]{3,2,1,0:T(8,128)S(1)}, u32[]{:S(2)}, u32[]{:S(2)}) collective-permute-start(f32[4,4,32,128]{3,2,1,0:T(8,128)S(1)} %pass.1.rest_0_), channel_id=1, source_target_pairs={{0,64},{8,72},{16,80},{24,88},{32,96},{40,104},{48,112},{56,120},{... | collective-permute-start | bytes 786440 | tf_op jit(solution)/shard_map/ppermute | solution.py:600
  108.8 8.4 %collective-permute-start.24 = (f32[4,4,32,128]{3,2,1,0:T(8,128)S(1)}, f32[4,4,32,128]{3,2,1,0:T(8,128)S(1)}, u32[]{:S(2)}, u32[]{:S(2)}) collective-permute-start(f32[4,4,32,128]{3,2,1,0:T(8,128)S(1)} %pass.1.rest_0_), channel_id=1, source_target_pairs={{0,96},{8,104},{16,112},{24,120},{32,0},{40,8},{48,16},{56,24},{64... | collective-permute-start | bytes 786440 | tf_op jit(solution)/shard_map/ppermute | solution.py:600
  126.8 3.9 %collective-permute-start.25 = (f32[16,4,32,128]{3,2,1,0:T(8,128)S(1)}, f32[16,4,32,128]{3,2,1,0:T(8,128)S(1)}, u32[]{:S(2)}, u32[]{:S(2)}) collective-permute-start(f32[16,4,32,128]{3,2,1,0:T(8,128)S(1)} %bitcast.11), channel_id=1, source_target_pairs={{0,1},{1,0},{2,3},{3,2},{4,5},{5,4},{6,7},{7,6},{8,9},{9,8},{10,11... | collective-permute-start | bytes 3145736 | tf_op jit(solution)/shard_map/ppermute | solution.py:602
  (8 other events, 27.8 us)

commit v10 on v9

--- a/solution.py
+++ b/solution.py
@@ -250,8 +250,8 @@
     )
 
 
-def third_kernel(places, keep, recv_a, recv_b, after, out, total):
-    del after
+def third_kernel(places, keep, recv_a, recv_b, *rest):
+    out, total = rest[-2:]
     half = recv_a.shape[0]
     main = 2 * half
     total[0:half] = keep[0] + recv_a[...]
@@ -266,9 +266,9 @@
     return small(
         third_kernel,
         jax.ShapeDtypeStruct(shape, F32),
-        [places, keep, recv_a, recv_b, after],
+        [places, keep, recv_a, recv_b, *after],
         "third_sums",
-        [IN_SMEM] + [IN_VMEM] * 3 + [ANYWHERE],
+        [IN_SMEM] + [IN_VMEM] * 3 + [ANYWHERE] * len(after),
         scratch=[pltpu.VMEM(shape, F32)],
     )
 
@@ -561,25 +561,25 @@
         lax.ppermute(some, "group", along_z[k + 1]) for k, some in enumerate(sends)
     ]
 
+    keep, send_a, send_b = second_sums(keep_a, recv_a, keep_b, recv_b, terms[1:])
+    recv_a = lax.ppermute(send_a, "local", across)
+    recv_b = lax.ppermute(send_b, "local", pairs)
     base = small(
         self_kernel,
         jax.ShapeDtypeStruct(pre_grad.shape, F32),
-        [pre_grad, w_self, other_local, own_local, mine],
+        [pre_grad, w_self, other_local, own_local, keep],
         "self_rows",
         [IN_VMEM] * 4 + [ANYWHERE],
         scratch=[pltpu.VMEM((blocks, width, BLOCK), F32)],
         mebibytes=16,
         flops=6 * pre_grad.size * width,
     )
-    keep, send_a, send_b = second_sums(keep_a, recv_a, keep_b, recv_b, [base, terms[1]])
-    recv_a = lax.ppermute(send_a, "local", across)
-    recv_b = lax.ppermute(send_b, "local", pairs)
     share_shape = jax.ShapeDtypeStruct(mine.shape, F32)
     share = small(sum_kernel, share_shape, terms, "sum_z")
     terms = [share] + [lax.ppermute(share, "local", p) for p in (pairs, across, along_x[2])]
     scale = float(node_rows * groups * members) ** (-0.5)
     share = small(functools.partial(chips_kernel, scale), share_shape, terms, "sum_chips")
-    shares = third_sums(places, keep, recv_a, recv_b, share)
+    shares = third_sums(places, keep, recv_a, recv_b, [share, base])
     arrived = lax.all_to_all(shares, "group", split_axis=0, concat_axis=0, tiled=True)
     terms = [share] + [lax.ppermute(share, "group", along_z[k]) for k in range(1, 4)]
     row = gather(lambda g: g & 3, terms, "gather_z")

time: 132 us -> 136 us (1.030)
  waiting for transfers between devices: 51.7 us -> 55.3 us
  local copies, waits for them, and re-layouts: 0.25 us -> 2.53 us
    ppermute x3, waiting for transfers between devices: 4.38 us -> 10.5 us  [on_device(): lax.ppermute(share, 'local', p)]
    unnamed x26 -> x28, local copies, waits for them, and re-layouts: 0.25 us -> 2.53 us
    ppermute x3, waiting for transfers between devices: 4.78 us -> 3.25 us  [on_device(): lax.ppermute(some, 'group', along_z[k + 1])]
  transfers between devices with their start and end apart: 27 -> 27, of which waited for: 21 -> 18; matrix products, arithmetic and copies ran while one was open for 4% -> 4% of each run, Pallas kernels for 9% -> 8%
where the time goes in v10:
time: 136 us
  waiting for transfers between devices  55.3 us (41%)
  starting transfers between devices  46.6 us (34%)
  Pallas kernels  25.4 us (19%)
  matrix products  5.45 us (4%)
  local copies, waits for them, and re-layouts  2.53 us (2%)
    pallas_call x2, Pallas kernels, tile_sums(): pl.pallas_call(functools.partial(tile_kernel, own, blocks, main, over), o...  16.3 us
    ppermute x3, waiting for transfers between devices, on_device(): lax.ppermute(share, 'local', p)  10.5 us
    ppermute x3, waiting for transfers between devices, on_device(): rows = [row] + [lax.ppermute(row, 'group', along_y[k]) for k in range(1, 4)]  10.2 us
    ppermute x3, waiting for transfers between devices, on_device(): lax.ppermute(some, 'group', along_y[k + 1])  10.2 us
    ppermute x3, waiting for transfers between devices, on_device(): lax.ppermute(joined[k - 1], 'local', along_x[k])  9.52 us
    ppermute x3, waiting for transfers between devices, on_device(): lax.ppermute(share, 'group', along_z[k])  8.08 us
    pallas_call x14, Pallas kernels, small(): pl.pallas_call(kernel, out_shape=out_shape, in_specs=specs or [IN_VMEM] *...  7.35 us
    all_to_all x1, starting transfers between devices, on_device(): lax.all_to_all(shares, 'group', split_axis=0, concat_axis=0, tiled=True)  6.47 us
  transfers between devices with their start and end apart: 27, of which 18 were waited for; matrix products, arithmetic and copies ran while one was open for 4% of the time, Pallas kernels for 8%

profile of v10, /device:TPU:1, one launch (start us, length us, event | category | flops | bytes accessed | tf_op | source)
XLA Modules:
  0.0 136.2 jit_solution(17409084268565823575)
XLA Ops:
  0.6 9.8 %other_tile_sums.1 = (f32[1024,512]{1,0:T(8,128)}, f32[8,256,128]{2,1,0:T(8,128)}, f32[30,256,128]{2,1,0:T(8,128)}, s32[32]{0:T(128)}, s32[64]{0:T(128)}) custom-call(s32[64]{0:T(128)} %col_ref.1, s32[16,16]{1,0:T(8,128)} %count_ref.5, f32[1024,512]{1,0:T(8,128)} %rest_0_.1, f32[1024,512]{1,0:T(8,128)} %rest_1_.2, f32[512,512]{1,0:T(8,128)} %rest_1_.3, ...), custom_call_target="tpu_custom_call" | custom-call | flops 2415919104 | bytes 14680064 | tf_op jit(solution)/shard_map/other_tile_sums/pallas_call | solution.py:208
  10.5 1.5 %collective-permute-start = (f32[30,256,128]{2,1,0:T(8,128)}, f32[30,256,128]{2,1,0:T(8,128)S(1)}, u32[]{:S(2)}, u32[]{:S(2)}) collective-permute-start(f32[30,256,128]{2,1,0:T(8,128)} %get-tuple-element.40), channel_id=1, source_target_pairs={{0,1},{1,0},{2,3},{3,2},{4,5},{5,4},{6,7},{7,6},{8,9},{9,8},{10,11... | collective-permute-start | bytes 11796488 | tf_op jit(solution)/shard_map/ppermute | solution.py:537
  12.0 3.6 %convolution_bitcast_fusion.neigh_term = f32[512,512]{1,0:T(8,128)S(1)} fusion(f32[1024,512]{1,0:T(8,128)} %get-tuple-element.37.rest_0_.pre_grad, f32[1024,512]{1,0:T(8,128)S(1)} %copy-done), kind=kOutput, calls=%fused_computation | convolution fusion | flops 1610612736 | bytes 5242880 | tf_op jit(solution)/shard_map/dot_general | solution.py:548
  15.6 1.9 %convolution_bitcast_fusion.1.self_term = f32[512,512]{1,0:T(8,128)S(1)} fusion(f32[1024,512]{1,0:T(8,128)S(1)} %copy-done.1, f32[1024,512]{1,0:T(8,128)S(1)} %copy-done.13), kind=kOutput, calls=%fused_computation.1 | convolution fusion | flops 1610612736 | bytes 5242880 | tf_op jit(solution)/shard_map/dot_general | solution.py:545
  18.8 6.5 %own_tile_sums.1 = (f32[8,256,128]{2,1,0:T(8,128)S(1)}, s32[1]{0:T(128)}, f32[2,15,64,128]{3,2,1,0:T(8,128)S(1)}, f32[2,15,64,128]{3,2,1,0:T(8,128)S(1)}, f32[2,...) custom-call(s32[64]{0:T(128)S(1)} %copy-done.11, s32[16,16]{1,0:T(8,128)S(1)} %copy-done.9, ...), custom_call_target="tpu_custom_call" | custom-call | flops 2415919104 | bytes 14680064 | tf_op jit(solution)/shard_map/own_tile_sums/pallas_call | solution.py:208
  26.7 1.8 %collective-permute-start.2 = (f32[2,15,64,128]{3,2,1,0:T(8,128)S(1)}, f32[2,15,64,128]{3,2,1,0:T(8,128)S(1)}, u32[]{:S(2)}, u32[]{:S(2)}) collective-permute-start(f32[2,15,64,128]{3,2,1,0:T(8,128)S(1)} %get-tuple-element.45), channel_id=1, source_target_pairs={{0,6},{1,7},{2,4},{3,5},{4,2},{5,3},{6,0},{7,1},{8,14},{9,15},{10,... | collective-permute-start | bytes 2949128 | tf_op jit(solution)/shard_map/ppermute | solution.py:542
  30.6 2.6 %collective-permute-start.5 = (f32[4,4,32,128]{3,2,1,0:T(8,128)S(1)}, f32[4,4,32,128]{3,2,1,0:T(8,128)S(1)}, u32[]{:S(2)}, u32[]{:S(2)}) collective-permute-start(f32[4,4,32,128]{3,2,1,0:T(8,128)S(1)} %get-tuple-element.51), channel_id=1, source_target_pairs={{0,64},{8,72},{16,80},{24,88},{32,96},{40,104},{48,112},{56,120},{... | collective-permute-start | bytes 786440 | tf_op jit(solution)/shard_map/ppermute | solution.py:557
  34.3 3.4 %collective-permute-done.4.rest_1_ = f32[4,4,32,128]{3,2,1,0:T(8,128)S(1)} collective-permute-done((f32[4,4,32,128]{3,2,1,0:T(8,128)S(1)}, f32[4,4,32,128]{3,2,1,0:T(8,128)S(1)}, u32[]{:S(2)}, u32[]{:S(2)}) %collective-permute-start.4) | collective-permute-done | bytes 262176 | tf_op jit(solution)/shard_map/ppermute | solution.py:557
  37.8 6.7 %collective-permute-done.5.rest_2_ = f32[4,4,32,128]{3,2,1,0:T(8,128)S(1)} collective-permute-done((f32[4,4,32,128]{3,2,1,0:T(8,128)S(1)}, f32[4,4,32,128]{3,2,1,0:T(8,128)S(1)}, u32[]{:S(2)}, u32[]{:S(2)}) %collective-permute-start.5) | collective-permute-done | bytes 262176 | tf_op jit(solution)/shard_map/ppermute | solution.py:557
  44.6 1.7 %collective-permute-start.7 = (f32[4,32,128]{2,1,0:T(8,128)S(1)}, f32[4,32,128]{2,1,0:T(8,128)S(1)}, u32[]{:S(2)}, u32[]{:S(2)}) collective-permute-start(f32[4,32,128]{2,1,0:T(8,128)S(1)} %get-tuple-element.53), channel_id=1, source_target_pairs={{0,8},{8,16},{16,24},{24,0},{32,40},{40,48},{48,56},{56,32},{64,72... | collective-permute-start | bytes 196616 | tf_op jit(solution)/shard_map/ppermute | solution.py:561
  46.3 3.3 %collective-permute-start.8 = (f32[4,32,128]{2,1,0:T(8,128)S(1)}, f32[4,32,128]{2,1,0:T(8,128)S(1)}, u32[]{:S(2)}, u32[]{:S(2)}) collective-permute-start(f32[4,32,128]{2,1,0:T(8,128)S(1)} %get-tuple-element.54), channel_id=1, source_target_pairs={{0,16},{8,24},{16,0},{24,8},{32,48},{40,56},{48,32},{56,40},{64,80... | collective-permute-start | bytes 196616 | tf_op jit(solution)/shard_map/ppermute | solution.py:561
  50.3 1.7 %collective-permute-done.8.rest_1_.rest_2_ = f32[4,32,128]{2,1,0:T(8,128)S(1)} collective-permute-done((f32[4,32,128]{2,1,0:T(8,128)S(1)}, f32[4,32,128]{2,1,0:T(8,128)S(1)}, u32[]{:S(2)}, u32[]{:S(2)}) %collective-permute-start.8) | collective-permute-done | bytes 65568 | tf_op jit(solution)/shard_map/ppermute | solution.py:561
  52.0 1.5 %collective-permute-done.9.rest_2_.rest_3_ = f32[4,32,128]{2,1,0:T(8,128)S(1)} collective-permute-done((f32[4,32,128]{2,1,0:T(8,128)S(1)}, f32[4,32,128]{2,1,0:T(8,128)S(1)}, u32[]{:S(2)}, u32[]{:S(2)}) %collective-permute-start.9) | collective-permute-done | bytes 65568 | tf_op jit(solution)/shard_map/ppermute | solution.py:561
  54.7 1.5 %collective-permute-start.12 = (f32[4,32,128]{2,1,0:T(8,128)S(1)}, f32[4,32,128]{2,1,0:T(8,128)S(1)}, u32[]{:S(2)}, u32[]{:S(2)}) collective-permute-start(f32[4,32,128]{2,1,0:T(8,128)S(1)} %sum_z.1.mine), channel_id=1, source_target_pairs={{0,2},{1,3},{2,0},{3,1},{4,6},{5,7},{6,4},{7,5},{8,10},{9,11},{10,... | collective-permute-start | bytes 196616 | tf_op jit(solution)/shard_map/ppermute | solution.py:579
  56.3 1.8 %collective-permute-start.13 = (f32[4,32,128]{2,1,0:T(8,128)S(1)}, f32[4,32,128]{2,1,0:T(8,128)S(1)}, u32[]{:S(2)}, u32[]{:S(2)}) collective-permute-start(f32[4,32,128]{2,1,0:T(8,128)S(1)} %sum_z.1.mine), channel_id=1, source_target_pairs={{0,6},{1,7},{2,4},{3,5},{4,2},{5,3},{6,0},{7,1},{8,14},{9,15},{10,... | collective-permute-start | bytes 196616 | tf_op jit(solution)/shard_map/ppermute | solution.py:579
  58.2 7.9 %collective-permute-done.12.pair = f32[4,32,128]{2,1,0:T(8,128)S(1)} collective-permute-done((f32[4,32,128]{2,1,0:T(8,128)S(1)}, f32[4,32,128]{2,1,0:T(8,128)S(1)}, u32[]{:S(2)}, u32[]{:S(2)}) %collective-permute-start.12) | collective-permute-done | bytes 65568 | tf_op jit(solution)/shard_map/ppermute | solution.py:579
  66.7 2.0 %collective-permute-done.14.far_two = f32[4,32,128]{2,1,0:T(8,128)S(1)} collective-permute-done((f32[4,32,128]{2,1,0:T(8,128)S(1)}, f32[4,32,128]{2,1,0:T(8,128)S(1)}, u32[]{:S(2)}, u32[]{:S(2)}) %collective-permute-start.14) | collective-permute-done | bytes 65568 | tf_op jit(solution)/shard_map/ppermute | solution.py:579
  68.8 2.3 %self_rows.1.rest_1_.base = f32[1024,512]{1,0:T(8,128)S(1)} custom-call(f32[1024,512]{1,0:T(8,128)S(1)} %copy-done.1, f32[512,512]{1,0:T(8,128)S(1)} %copy-done.7, f32[8,256,128]{2,1,0:T(8,128)S(1)} %copy-done.8, f32[8,256,128]{2,1,0:T(8,128)S(1)} %get-tuple-element.41.own_local, f32[2,15,64,128]{3,2,1,0:T(8,128)S(1)} %get-tuple-element.56.after.keep), custom_call_target="tpu_custom_call" | custom-call | flops 1610612736 | bytes 6291456 | tf_op jit(solution)/shard_map/self_rows/pallas_call | solution.py:280
  74.1 6.5 %all-to-all-start = ((f32[32,64,128]{2,1,0:T(8,128)}), f32[32,64,128]{2,1,0:T(8,128)S(1)}, u32[]{:S(2)}, u32[]{:S(2)}) async-start(f32[32,64,128]{2,1,0:T(8,128)} %copy-done.5), calls=%async_computation | async-start | bytes 2097152 | tf_op jit(solution)/shard_map/all_to_all | solution.py:583
  81.9 2.4 %collective-permute-start.16 = (f32[4,32,128]{2,1,0:T(8,128)S(1)}, f32[4,32,128]{2,1,0:T(8,128)S(1)}, u32[]{:S(2)}, u32[]{:S(2)}) collective-permute-start(f32[4,32,128]{2,1,0:T(8,128)S(1)} %sum_chips.1.rest_0_), channel_id=1, source_target_pairs={{0,16},{8,24},{16,0},{24,8},{32,48},{40,56},{48,32},{56,40},{64,80... | collective-permute-start | bytes 196616 | tf_op jit(solution)/shard_map/ppermute | solution.py:584
  86.4 5.2 %collective-permute-done.16.rest_2_ = f32[4,32,128]{2,1,0:T(8,128)S(1)} collective-permute-done((f32[4,32,128]{2,1,0:T(8,128)S(1)}, f32[4,32,128]{2,1,0:T(8,128)S(1)}, u32[]{:S(2)}, u32[]{:S(2)}) %collective-permute-start.16) | collective-permute-done | bytes 65568 | tf_op jit(solution)/shard_map/ppermute | solution.py:584
  91.6 2.0 %collective-permute-done.17.rest_3_ = f32[4,32,128]{2,1,0:T(8,128)S(1)} collective-permute-done((f32[4,32,128]{2,1,0:T(8,128)S(1)}, f32[4,32,128]{2,1,0:T(8,128)S(1)}, u32[]{:S(2)}, u32[]{:S(2)}) %collective-permute-start.17) | collective-permute-done | bytes 65568 | tf_op jit(solution)/shard_map/ppermute | solution.py:584
  95.1 6.2 %collective-permute-start.18 = (f32[4,8,64,128]{3,2,1,0:T(8,128)S(1)}, f32[4,8,64,128]{3,2,1,0:T(8,128)S(1)}, u32[]{:S(2)}, u32[]{:S(2)}) collective-permute-start(f32[4,8,64,128]{3,2,1,0:T(8,128)S(1)} %get-tuple-element.62), channel_id=1, source_target_pairs={{0,1},{1,0},{2,3},{3,2},{4,5},{5,4},{6,7},{7,6},{8,9},{9,8},{10,11... | collective-permute-start | bytes 3145736 | tf_op jit(solution)/shard_map/ppermute | solution.py:588
  101.3 2.3 %collective-permute-done.18.rest_3_.swapped = f32[4,8,64,128]{3,2,1,0:T(8,128)S(1)} collective-permute-done((f32[4,8,64,128]{3,2,1,0:T(8,128)S(1)}, f32[4,8,64,128]{3,2,1,0:T(8,128)S(1)}, u32[]{:S(2)}, u32[]{:S(2)}) %collective-permute-start.18) | collective-permute-done | bytes 1048608 | tf_op jit(solution)/shard_map/ppermute | solution.py:588
  104.9 2.5 %collective-permute-start.20 = (f32[2,8,64,128]{3,2,1,0:T(8,128)S(1)}, f32[2,8,64,128]{3,2,1,0:T(8,128)S(1)}, u32[]{:S(2)}, u32[]{:S(2)}) collective-permute-start(f32[2,8,64,128]{3,2,1,0:T(8,128)S(1)} %get-tuple-element.67), channel_id=1, source_target_pairs={{0,4},{1,5},{2,6},{3,7},{4,0},{5,1},{6,2},{7,3},{8,12},{9,13},{10,... | collective-permute-start | bytes 1572872 | tf_op jit(solution)/shard_map/ppermute | solution.py:591
  107.7 2.2 %collective-permute-start.23 = (f32[4,4,32,128]{3,2,1,0:T(8,128)S(1)}, f32[4,4,32,128]{3,2,1,0:T(8,128)S(1)}, u32[]{:S(2)}, u32[]{:S(2)}) collective-permute-start(f32[4,4,32,128]{3,2,1,0:T(8,128)S(1)} %pass.1.rest_0_), channel_id=1, source_target_pairs={{0,64},{8,72},{16,80},{24,88},{32,96},{40,104},{48,112},{56,120},{... | collective-permute-start | bytes 786440 | tf_op jit(solution)/shard_map/ppermute | solution.py:600
  109.9 2.7 %collective-permute-done.22.rest_1_ = f32[4,4,32,128]{3,2,1,0:T(8,128)S(1)} collective-permute-done((f32[4,4,32,128]{3,2,1,0:T(8,128)S(1)}, f32[4,4,32,128]{3,2,1,0:T(8,128)S(1)}, u32[]{:S(2)}, u32[]{:S(2)}) %collective-permute-start.22) | collective-permute-done | bytes 262176 | tf_op jit(solution)/shard_map/ppermute | solution.py:600
  113.4 5.3 %collective-permute-done.23.rest_2_ = f32[4,4,32,128]{3,2,1,0:T(8,128)S(1)} collective-permute-done((f32[4,4,32,128]{3,2,1,0:T(8,128)S(1)}, f32[4,4,32,128]{3,2,1,0:T(8,128)S(1)}, u32[]{:S(2)}, u32[]{:S(2)}) %collective-permute-start.23) | collective-permute-done | bytes 262176 | tf_op jit(solution)/shard_map/ppermute | solution.py:600
  118.7 2.2 %collective-permute-done.24.rest_3_ = f32[4,4,32,128]{3,2,1,0:T(8,128)S(1)} collective-permute-done((f32[4,4,32,128]{3,2,1,0:T(8,128)S(1)}, f32[4,4,32,128]{3,2,1,0:T(8,128)S(1)}, u32[]{:S(2)}, u32[]{:S(2)}) %collective-permute-start.24) | collective-permute-done | bytes 262176 | tf_op jit(solution)/shard_map/ppermute | solution.py:600
  120.9 9.1 %collective-permute-done.20.rest_1_.rest_5_ = f32[2,8,64,128]{3,2,1,0:T(8,128)S(1)} collective-permute-done((f32[2,8,64,128]{3,2,1,0:T(8,128)S(1)}, f32[2,8,64,128]{3,2,1,0:T(8,128)S(1)}, u32[]{:S(2)}, u32[]{:S(2)}) %collective-permute-start.20) | collective-permute-done | bytes 524320 | tf_op jit(solution)/shard_map/ppermute | solution.py:591
  130.5 1.9 %collective-permute-start.25 = (f32[16,4,32,128]{3,2,1,0:T(8,128)S(1)}, f32[16,4,32,128]{3,2,1,0:T(8,128)S(1)}, u32[]{:S(2)}, u32[]{:S(2)}) collective-permute-start(f32[16,4,32,128]{3,2,1,0:T(8,128)S(1)} %bitcast.11), channel_id=1, source_target_pairs={{0,1},{1,0},{2,3},{3,2},{4,5},{5,4},{6,7},{7,6},{8,9},{9,8},{10,11... | collective-permute-start | bytes 3145736 | tf_op jit(solution)/shard_map/ppermute | solution.py:602
  132.4 1.7 %finish.1 = f32[1024,512]{1,0:T(8,128)} custom-call(f32[1024,512]{1,0:T(8,128)S(1)} %copy-done.3, f32[8,64,128]{2,1,0:T(8,128)S(1)} %get-tuple-element.61.keep, f32[4,8,64,128]{3,2,1,0:T(8,128)S(1)} %collective-permute-done.18.rest_3_.swapped, f32[2,8,64,128]{3,2,1,0:T(8,128)S(1)} %collective-permute-done.19.rest_0_.rest_4_, ...), custom_call_target="tpu_custom_call" | custom-call | flops 1048576 | bytes 8388608 | tf_op jit(solution)/shard_map/finish/pallas_call | solution.py:490
  (69 shorter events, 21.5 us)
Async XLA Ops:
  0.6 11.3 %copy-start = (f32[1024,512]{1,0:T(8,128)S(1)}, f32[1024,512]{1,0:T(8,128)}, u32[]{:S(2)}) copy-start(f32[1024,512]{1,0:T(8,128)} %param.11) | copy-start | bytes 6291460
  10.5 8.1 %collective-permute-start = (f32[30,256,128]{2,1,0:T(8,128)}, f32[30,256,128]{2,1,0:T(8,128)S(1)}, u32[]{:S(2)}, u32[]{:S(2)}) collective-permute-start(f32[30,256,128]{2,1,0:T(8,128)} %get-tuple-element.40), channel_id=1, source_target_pairs={{0,1},{1,0},{2,3},{3,2},{4,5},{5,4},{6,7},{7,6},{8,9},{9,8},{10,11... | collective-permute-start | bytes 11796488 | tf_op jit(solution)/shard_map/ppermute | solution.py:537
  17.7 10.8 %collective-permute-start.3 = (f32[16,4,32,128]{3,2,1,0:T(8,128)S(1)}, f32[16,4,32,128]{3,2,1,0:T(8,128)S(1)}, u32[]{:S(2)}, u32[]{:S(2)}) collective-permute-start(f32[16,4,32,128]{3,2,1,0:T(8,128)S(1)} %get-tuple-element.47), channel_id=1, source_target_pairs={{0,1},{1,0},{2,3},{3,2},{4,5},{5,4},{6,7},{7,6},{8,9},{9,8},{10,11... | collective-permute-start | bytes 3145736 | tf_op jit(solution)/shard_map/ppermute | solution.py:554
  25.3 28.2 %collective-permute-start.1 = (f32[2,15,64,128]{3,2,1,0:T(8,128)S(1)}, f32[2,15,64,128]{3,2,1,0:T(8,128)S(1)}, u32[]{:S(2)}, u32[]{:S(2)}) collective-permute-start(f32[2,15,64,128]{3,2,1,0:T(8,128)S(1)} %get-tuple-element.43), channel_id=1, source_target_pairs={{0,2},{1,3},{2,0},{3,1},{4,6},{5,7},{6,4},{7,5},{8,10},{9,11},{10,... | collective-permute-start | bytes 2949128 | tf_op jit(solution)/shard_map/ppermute | solution.py:541
  26.7 26.8 %collective-permute-start.2 = (f32[2,15,64,128]{3,2,1,0:T(8,128)S(1)}, f32[2,15,64,128]{3,2,1,0:T(8,128)S(1)}, u32[]{:S(2)}, u32[]{:S(2)}) collective-permute-start(f32[2,15,64,128]{3,2,1,0:T(8,128)S(1)} %get-tuple-element.45), channel_id=1, source_target_pairs={{0,6},{1,7},{2,4},{3,5},{4,2},{5,3},{6,0},{7,1},{8,14},{9,15},{10,... | collective-permute-start | bytes 2949128 | tf_op jit(solution)/shard_map/ppermute | solution.py:542
  29.3 8.5 %collective-permute-start.4 = (f32[4,4,32,128]{3,2,1,0:T(8,128)S(1)}, f32[4,4,32,128]{3,2,1,0:T(8,128)S(1)}, u32[]{:S(2)}, u32[]{:S(2)}) collective-permute-start(f32[4,4,32,128]{3,2,1,0:T(8,128)S(1)} %get-tuple-element.50), channel_id=1, source_target_pairs={{0,32},{8,40},{16,48},{24,56},{32,64},{40,72},{48,80},{56,88},{64,... | collective-permute-start | bytes 786440 | tf_op jit(solution)/shard_map/ppermute | solution.py:557
  30.6 13.9 %collective-permute-start.5 = (f32[4,4,32,128]{3,2,1,0:T(8,128)S(1)}, f32[4,4,32,128]{3,2,1,0:T(8,128)S(1)}, u32[]{:S(2)}, u32[]{:S(2)}) collective-permute-start(f32[4,4,32,128]{3,2,1,0:T(8,128)S(1)} %get-tuple-element.51), channel_id=1, source_target_pairs={{0,64},{8,72},{16,80},{24,88},{32,96},{40,104},{48,112},{56,120},{... | collective-permute-start | bytes 786440 | tf_op jit(solution)/shard_map/ppermute | solution.py:557
  33.3 11.2 %collective-permute-start.6 = (f32[4,4,32,128]{3,2,1,0:T(8,128)S(1)}, f32[4,4,32,128]{3,2,1,0:T(8,128)S(1)}, u32[]{:S(2)}, u32[]{:S(2)}) collective-permute-start(f32[4,4,32,128]{3,2,1,0:T(8,128)S(1)} %get-tuple-element.52), channel_id=1, source_target_pairs={{0,96},{8,104},{16,112},{24,120},{32,0},{40,8},{48,16},{56,24},{64... | collective-permute-start | bytes 786440 | tf_op jit(solution)/shard_map/ppermute | solution.py:557
  44.6 5.8 %collective-permute-start.7 = (f32[4,32,128]{2,1,0:T(8,128)S(1)}, f32[4,32,128]{2,1,0:T(8,128)S(1)}, u32[]{:S(2)}, u32[]{:S(2)}) collective-permute-start(f32[4,32,128]{2,1,0:T(8,128)S(1)} %get-tuple-element.53), channel_id=1, source_target_pairs={{0,8},{8,16},{16,24},{24,0},{32,40},{40,48},{48,56},{56,32},{64,72... | collective-permute-start | bytes 196616 | tf_op jit(solution)/shard_map/ppermute | solution.py:561
  46.3 5.8 %collective-permute-start.8 = (f32[4,32,128]{2,1,0:T(8,128)S(1)}, f32[4,32,128]{2,1,0:T(8,128)S(1)}, u32[]{:S(2)}, u32[]{:S(2)}) collective-permute-start(f32[4,32,128]{2,1,0:T(8,128)S(1)} %get-tuple-element.54), channel_id=1, source_target_pairs={{0,16},{8,24},{16,0},{24,8},{32,48},{40,56},{48,32},{56,40},{64,80... | collective-permute-start | bytes 196616 | tf_op jit(solution)/shard_map/ppermute | solution.py:561
  49.6 4.0 %collective-permute-start.9 = (f32[4,32,128]{2,1,0:T(8,128)S(1)}, f32[4,32,128]{2,1,0:T(8,128)S(1)}, u32[]{:S(2)}, u32[]{:S(2)}) collective-permute-start(f32[4,32,128]{2,1,0:T(8,128)S(1)} %get-tuple-element.55), channel_id=1, source_target_pairs={{0,24},{8,0},{16,8},{24,16},{32,56},{40,32},{48,40},{56,48},{64,88... | collective-permute-start | bytes 196616 | tf_op jit(solution)/shard_map/ppermute | solution.py:561
  53.5 15.2 %copy-start.7 = (f32[512,512]{1,0:T(8,128)S(1)}, f32[512,512]{1,0:T(8,128)}, u32[]{:S(2)}) copy-start(f32[512,512]{1,0:T(8,128)} %weight.1) | copy-start | bytes 3145732
  53.5 15.2 %copy-start.8 = (f32[8,256,128]{2,1,0:T(8,128)S(1)}, f32[8,256,128]{2,1,0:T(8,128)}, u32[]{:S(2)}) copy-start(f32[8,256,128]{2,1,0:T(8,128)} %get-tuple-element.38.other_local) | copy-start | bytes 3145732
  53.8 17.3 %collective-permute-start.10 = (f32[15,64,128]{2,1,0:T(8,128)S(1)}, f32[15,64,128]{2,1,0:T(8,128)S(1)}, u32[]{:S(2)}, u32[]{:S(2)}) collective-permute-start(f32[15,64,128]{2,1,0:T(8,128)S(1)} %get-tuple-element.58), channel_id=1, source_target_pairs={{0,6},{1,7},{2,4},{3,5},{4,2},{5,3},{6,0},{7,1},{8,14},{9,15},{10,... | collective-permute-start | bytes 1474568 | tf_op jit(solution)/shard_map/ppermute | solution.py:565
  54.7 16.3 %collective-permute-start.11 = (f32[15,64,128]{2,1,0:T(8,128)S(1)}, f32[15,64,128]{2,1,0:T(8,128)S(1)}, u32[]{:S(2)}, u32[]{:S(2)}) collective-permute-start(f32[15,64,128]{2,1,0:T(8,128)S(1)} %get-tuple-element.59), channel_id=1, source_target_pairs={{0,2},{1,3},{2,0},{3,1},{4,6},{5,7},{6,4},{7,5},{8,10},{9,11},{10,... | collective-permute-start | bytes 1474568 | tf_op jit(solution)/shard_map/ppermute | solution.py:566
  54.7 11.3 %collective-permute-start.12 = (f32[4,32,128]{2,1,0:T(8,128)S(1)}, f32[4,32,128]{2,1,0:T(8,128)S(1)}, u32[]{:S(2)}, u32[]{:S(2)}) collective-permute-start(f32[4,32,128]{2,1,0:T(8,128)S(1)} %sum_z.1.mine), channel_id=1, source_target_pairs={{0,2},{1,3},{2,0},{3,1},{4,6},{5,7},{6,4},{7,5},{8,10},{9,11},{10,... | collective-permute-start | bytes 196616 | tf_op jit(solution)/shard_map/ppermute | solution.py:579
  56.3 10.4 %collective-permute-start.13 = (f32[4,32,128]{2,1,0:T(8,128)S(1)}, f32[4,32,128]{2,1,0:T(8,128)S(1)}, u32[]{:S(2)}, u32[]{:S(2)}) collective-permute-start(f32[4,32,128]{2,1,0:T(8,128)S(1)} %sum_z.1.mine), channel_id=1, source_target_pairs={{0,6},{1,7},{2,4},{3,5},{4,2},{5,3},{6,0},{7,1},{8,14},{9,15},{10,... | collective-permute-start | bytes 196616 | tf_op jit(solution)/shard_map/ppermute | solution.py:579
  58.1 10.6 %collective-permute-start.14 = (f32[4,32,128]{2,1,0:T(8,128)S(1)}, f32[4,32,128]{2,1,0:T(8,128)S(1)}, u32[]{:S(2)}, u32[]{:S(2)}) collective-permute-start(f32[4,32,128]{2,1,0:T(8,128)S(1)} %sum_z.1.mine), channel_id=1, source_target_pairs={{0,4},{1,5},{2,6},{3,7},{4,0},{5,1},{6,2},{7,3},{8,12},{9,13},{10,... | collective-permute-start | bytes 196616 | tf_op jit(solution)/shard_map/ppermute | solution.py:579
  74.1 19.5 %copy-start.10 = (s32[16,32]{1,0:T(8,128)S(1)}, s32[16,32]{1,0:T(8,128)}, u32[]{:S(2)}) copy-start(s32[16,32]{1,0:T(8,128)} %target_ref.1) | copy-start | bytes 6148
  74.1 19.5 %all-to-all-start = ((f32[32,64,128]{2,1,0:T(8,128)}), f32[32,64,128]{2,1,0:T(8,128)S(1)}, u32[]{:S(2)}, u32[]{:S(2)}) async-start(f32[32,64,128]{2,1,0:T(8,128)} %copy-done.5), calls=%async_computation | async-start | bytes 2097152 | tf_op jit(solution)/shard_map/all_to_all | solution.py:583
  80.5 5.8 %collective-permute-start.15 = (f32[4,32,128]{2,1,0:T(8,128)S(1)}, f32[4,32,128]{2,1,0:T(8,128)S(1)}, u32[]{:S(2)}, u32[]{:S(2)}) collective-permute-start(f32[4,32,128]{2,1,0:T(8,128)S(1)} %sum_chips.1.rest_0_), channel_id=1, source_target_pairs={{0,8},{8,16},{16,24},{24,0},{32,40},{40,48},{48,56},{56,32},{64,72... | collective-permute-start | bytes 196616 | tf_op jit(solution)/shard_map/ppermute | solution.py:584
  81.9 9.7 %collective-permute-start.16 = (f32[4,32,128]{2,1,0:T(8,128)S(1)}, f32[4,32,128]{2,1,0:T(8,128)S(1)}, u32[]{:S(2)}, u32[]{:S(2)}) collective-permute-start(f32[4,32,128]{2,1,0:T(8,128)S(1)} %sum_chips.1.rest_0_), channel_id=1, source_target_pairs={{0,16},{8,24},{16,0},{24,8},{32,48},{40,56},{48,32},{56,40},{64,80... | collective-permute-start | bytes 196616 | tf_op jit(solution)/shard_map/ppermute | solution.py:584
  84.3 9.3 %collective-permute-start.17 = (f32[4,32,128]{2,1,0:T(8,128)S(1)}, f32[4,32,128]{2,1,0:T(8,128)S(1)}, u32[]{:S(2)}, u32[]{:S(2)}) collective-permute-start(f32[4,32,128]{2,1,0:T(8,128)S(1)} %sum_chips.1.rest_0_), channel_id=1, source_target_pairs={{0,24},{8,0},{16,8},{24,16},{32,56},{40,32},{48,40},{56,48},{64,88... | collective-permute-start | bytes 196616 | tf_op jit(solution)/shard_map/ppermute | solution.py:584
  95.1 8.5 %collective-permute-start.18 = (f32[4,8,64,128]{3,2,1,0:T(8,128)S(1)}, f32[4,8,64,128]{3,2,1,0:T(8,128)S(1)}, u32[]{:S(2)}, u32[]{:S(2)}) collective-permute-start(f32[4,8,64,128]{3,2,1,0:T(8,128)S(1)} %get-tuple-element.62), channel_id=1, source_target_pairs={{0,1},{1,0},{2,3},{3,2},{4,5},{5,4},{6,7},{7,6},{8,9},{9,8},{10,11... | collective-permute-start | bytes 3145736 | tf_op jit(solution)/shard_map/ppermute | solution.py:588
  103.7 28.7 %copy-start.3 = (f32[1024,512]{1,0:T(8,128)S(1)}, f32[1024,512]{1,0:T(8,128)}, u32[]{:S(2)}) copy-start(f32[1024,512]{1,0:T(8,128)} %copy-done.2) | copy-start | bytes 6291460
  103.7 8.8 %collective-permute-start.22 = (f32[4,4,32,128]{3,2,1,0:T(8,128)S(1)}, f32[4,4,32,128]{3,2,1,0:T(8,128)S(1)}, u32[]{:S(2)}, u32[]{:S(2)}) collective-permute-start(f32[4,4,32,128]{3,2,1,0:T(8,128)S(1)} %pass.1.rest_0_), channel_id=1, source_target_pairs={{0,32},{8,40},{16,48},{24,56},{32,64},{40,72},{48,80},{56,88},{64,... | collective-permute-start | bytes 786440 | tf_op jit(solution)/shard_map/ppermute | solution.py:600
  104.9 16.1 %collective-permute-start.19 = (f32[2,8,64,128]{3,2,1,0:T(8,128)S(1)}, f32[2,8,64,128]{3,2,1,0:T(8,128)S(1)}, u32[]{:S(2)}, u32[]{:S(2)}) collective-permute-start(f32[2,8,64,128]{3,2,1,0:T(8,128)S(1)} %get-tuple-element.66.rest_0_), channel_id=1, source_target_pairs={{0,2},{1,3},{2,4},{3,5},{4,6},{5,7},{6,0},{7,1},{8,10},{9,11},{10,... | collective-permute-start | bytes 1572872 | tf_op jit(solution)/shard_map/ppermute | solution.py:591
  104.9 25.2 %collective-permute-start.20 = (f32[2,8,64,128]{3,2,1,0:T(8,128)S(1)}, f32[2,8,64,128]{3,2,1,0:T(8,128)S(1)}, u32[]{:S(2)}, u32[]{:S(2)}) collective-permute-start(f32[2,8,64,128]{3,2,1,0:T(8,128)S(1)} %get-tuple-element.67), channel_id=1, source_target_pairs={{0,4},{1,5},{2,6},{3,7},{4,0},{5,1},{6,2},{7,3},{8,12},{9,13},{10,... | collective-permute-start | bytes 1572872 | tf_op jit(solution)/shard_map/ppermute | solution.py:591
  107.4 23.1 %collective-permute-start.21 = (f32[2,8,64,128]{3,2,1,0:T(8,128)S(1)}, f32[2,8,64,128]{3,2,1,0:T(8,128)S(1)}, u32[]{:S(2)}, u32[]{:S(2)}) collective-permute-start(f32[2,8,64,128]{3,2,1,0:T(8,128)S(1)} %get-tuple-element.68), channel_id=1, source_target_pairs={{0,6},{1,7},{2,0},{3,1},{4,2},{5,3},{6,4},{7,5},{8,14},{9,15},{10,... | collective-permute-start | bytes 1572872 | tf_op jit(solution)/shard_map/ppermute | solution.py:591
  107.7 11.1 %collective-permute-start.23 = (f32[4,4,32,128]{3,2,1,0:T(8,128)S(1)}, f32[4,4,32,128]{3,2,1,0:T(8,128)S(1)}, u32[]{:S(2)}, u32[]{:S(2)}) collective-permute-start(f32[4,4,32,128]{3,2,1,0:T(8,128)S(1)} %pass.1.rest_0_), channel_id=1, source_target_pairs={{0,64},{8,72},{16,80},{24,88},{32,96},{40,104},{48,112},{56,120},{... | collective-permute-start | bytes 786440 | tf_op jit(solution)/shard_map/ppermute | solution.py:600
  112.5 8.4 %collective-permute-start.24 = (f32[4,4,32,128]{3,2,1,0:T(8,128)S(1)}, f32[4,4,32,128]{3,2,1,0:T(8,128)S(1)}, u32[]{:S(2)}, u32[]{:S(2)}) collective-permute-start(f32[4,4,32,128]{3,2,1,0:T(8,128)S(1)} %pass.1.rest_0_), channel_id=1, source_target_pairs={{0,96},{8,104},{16,112},{24,120},{32,0},{40,8},{48,16},{56,24},{64... | collective-permute-start | bytes 786440 | tf_op jit(solution)/shard_map/ppermute | solution.py:600
  130.5 4.2 %collective-permute-start.25 = (f32[16,4,32,128]{3,2,1,0:T(8,128)S(1)}, f32[16,4,32,128]{3,2,1,0:T(8,128)S(1)}, u32[]{:S(2)}, u32[]{:S(2)}) collective-permute-start(f32[16,4,32,128]{3,2,1,0:T(8,128)S(1)} %bitcast.11), channel_id=1, source_target_pairs={{0,1},{1,0},{2,3},{3,2},{4,5},{5,4},{6,7},{7,6},{8,9},{9,8},{10,11... | collective-permute-start | bytes 3145736 | tf_op jit(solution)/shard_map/ppermute | solution.py:602
  (9 other events, 18.7 us)

commit v11 on v9

--- a/solution.py
+++ b/solution.py
@@ -576,11 +576,12 @@
     recv_b = lax.ppermute(send_b, "local", pairs)
     share_shape = jax.ShapeDtypeStruct(mine.shape, F32)
     share = small(sum_kernel, share_shape, terms, "sum_z")
+    shares = third_sums(places, keep, recv_a, recv_b, share)
+    arrived = lax.all_to_all(shares, "group", split_axis=0, concat_axis=0, tiled=True)
+    share = small(pass_kernel, share_shape, [share, shares], "pass", [IN_VMEM, ANYWHERE])
     terms = [share] + [lax.ppermute(share, "local", p) for p in (pairs, across, along_x[2])]
     scale = float(node_rows * groups * members) ** (-0.5)
     share = small(functools.partial(chips_kernel, scale), share_shape, terms, "sum_chips")
-    shares = third_sums(places, keep, recv_a, recv_b, share)
-    arrived = lax.all_to_all(shares, "group", split_axis=0, concat_axis=0, tiled=True)
     terms = [share] + [lax.ppermute(share, "group", along_z[k]) for k in range(1, 4)]
     row = gather(lambda g: g & 3, terms, "gather_z")
 

time: 132 us -> 130 us (0.985)
  starting transfers between devices: 47.4 us -> 43 us
  waiting for transfers between devices: 51.7 us -> 53.6 us
    ppermute x1, starting transfers between devices: 5.17 us -> 0.9 us  [on_device(): swapped = lax.ppermute(send, 'local', swap)]
    ppermute x1, waiting for transfers between devices: 0.01 us -> 3.26 us  [on_device(): recv_a = lax.ppermute(send_a, 'local', across)]
    ppermute x3, starting transfers between devices: 4.16 us -> 2.3 us  [on_device(): rows = [row] + [lax.ppermute(row, 'group', along_y[k]) for k in range(1, 4)]]
    ppermute x3, waiting for transfers between devices: 4.38 us -> 2.95 us  [on_device(): lax.ppermute(share, 'local', p)]
    pallas_call x14 -> x15, Pallas kernels: 8.45 us -> 8.49 us  [small(): pl.pallas_call(kernel, out_shape=out_shape, in_specs=specs or [IN_VMEM] *...]
  transfers between devices with their start and end apart: 27 -> 27, of which waited for: 21 -> 20; matrix products, arithmetic and copies ran while one was open for 4% -> 4% of each run, Pallas kernels for 9% -> 9%
where the time goes in v11:
time: 130 us
  waiting for transfers between devices  53.6 us (41%)
  starting transfers between devices  43 us (33%)
  Pallas kernels  26.5 us (20%)
  matrix products  5.45 us (4%)
    pallas_call x2, Pallas kernels, tile_sums(): pl.pallas_call(functools.partial(tile_kernel, own, blocks, main, over), o...  16.3 us
    ppermute x3, waiting for transfers between devices, on_device(): lax.ppermute(some, 'group', along_y[k + 1])  10.2 us
    ppermute x3, waiting for transfers between devices, on_device(): lax.ppermute(joined[k - 1], 'local', along_x[k])  9.81 us
    ppermute x3, waiting for transfers between devices, on_device(): rows = [row] + [lax.ppermute(row, 'group', along_y[k]) for k in range(1, 4)]  9.59 us
    pallas_call x15, Pallas kernels, small(): pl.pallas_call(kernel, out_shape=out_shape, in_specs=specs or [IN_VMEM] *...  8.49 us
    ppermute x3, waiting for transfers between devices, on_device(): lax.ppermute(share, 'group', along_z[k])  8.29 us
    all_to_all x1, starting transfers between devices, on_device(): lax.all_to_all(shares, 'group', split_axis=0, concat_axis=0, tiled=True)  7.9 us
    ppermute x3, starting transfers between devices, on_device(): lax.ppermute(some, 'group', along_z[k + 1])  5.71 us
  transfers between devices with their start and end apart: 27, of which 20 were waited for; matrix products, arithmetic and copies ran while one was open for 4% of the time, Pallas kernels for 9%

profile of v11, /device:TPU:1, one launch (start us, length us, event | category | flops | bytes accessed | tf_op | source)
XLA Modules:
  0.0 129.7 jit_solution(3353839731851462397)
XLA Ops:
  0.6 9.8 %other_tile_sums.1 = (f32[1024,512]{1,0:T(8,128)}, f32[8,256,128]{2,1,0:T(8,128)}, f32[30,256,128]{2,1,0:T(8,128)}, s32[32]{0:T(128)}, s32[64]{0:T(128)}) custom-call(s32[64]{0:T(128)} %col_ref.1, s32[16,16]{1,0:T(8,128)} %count_ref.5, f32[1024,512]{1,0:T(8,128)} %rest_0_.1, f32[1024,512]{1,0:T(8,128)} %rest_1_.2, f32[512,512]{1,0:T(8,128)} %rest_1_.3, ...), custom_call_target="tpu_custom_call" | custom-call | flops 2415919104 | bytes 14680064 | tf_op jit(solution)/shard_map/other_tile_sums/pallas_call | solution.py:208
  12.0 3.6 %convolution_bitcast_fusion.neigh_term = f32[512,512]{1,0:T(8,128)S(1)} fusion(f32[1024,512]{1,0:T(8,128)} %get-tuple-element.37.rest_0_.pre_grad, f32[1024,512]{1,0:T(8,128)S(1)} %copy-done), kind=kOutput, calls=%fused_computation | convolution fusion | flops 1610612736 | bytes 5242880 | tf_op jit(solution)/shard_map/dot_general | solution.py:548
  15.6 1.9 %convolution_bitcast_fusion.1.self_term = f32[512,512]{1,0:T(8,128)S(1)} fusion(f32[1024,512]{1,0:T(8,128)S(1)} %copy-done.1, f32[1024,512]{1,0:T(8,128)S(1)} %copy-done.12), kind=kOutput, calls=%fused_computation.1 | convolution fusion | flops 1610612736 | bytes 5242880 | tf_op jit(solution)/shard_map/dot_general | solution.py:545
  18.8 6.5 %own_tile_sums.1 = (f32[8,256,128]{2,1,0:T(8,128)S(1)}, s32[1]{0:T(128)}, f32[2,15,64,128]{3,2,1,0:T(8,128)S(1)}, f32[2,15,64,128]{3,2,1,0:T(8,128)S(1)}, f32[2,...) custom-call(s32[64]{0:T(128)S(1)} %copy-done.11, s32[16,16]{1,0:T(8,128)S(1)} %copy-done.8, ...), custom_call_target="tpu_custom_call" | custom-call | flops 2415919104 | bytes 14680064 | tf_op jit(solution)/shard_map/own_tile_sums/pallas_call | solution.py:208
  26.7 1.8 %collective-permute-start.6 = (f32[2,15,64,128]{3,2,1,0:T(8,128)S(1)}, f32[2,15,64,128]{3,2,1,0:T(8,128)S(1)}, u32[]{:S(2)}, u32[]{:S(2)}) collective-permute-start(f32[2,15,64,128]{3,2,1,0:T(8,128)S(1)} %get-tuple-element.54), channel_id=1, source_target_pairs={{0,6},{1,7},{2,4},{3,5},{4,2},{5,3},{6,0},{7,1},{8,14},{9,15},{10,... | collective-permute-start | bytes 2949128 | tf_op jit(solution)/shard_map/ppermute | solution.py:542
  30.7 2.6 %collective-permute-start.3 = (f32[4,4,32,128]{3,2,1,0:T(8,128)S(1)}, f32[4,4,32,128]{3,2,1,0:T(8,128)S(1)}, u32[]{:S(2)}, u32[]{:S(2)}) collective-permute-start(f32[4,4,32,128]{3,2,1,0:T(8,128)S(1)} %get-tuple-element.47), channel_id=1, source_target_pairs={{0,64},{8,72},{16,80},{24,88},{32,96},{40,104},{48,112},{56,120},{... | collective-permute-start | bytes 786440 | tf_op jit(solution)/shard_map/ppermute | solution.py:557
  34.4 3.4 %collective-permute-done.2.rest_1_ = f32[4,4,32,128]{3,2,1,0:T(8,128)S(1)} collective-permute-done((f32[4,4,32,128]{3,2,1,0:T(8,128)S(1)}, f32[4,4,32,128]{3,2,1,0:T(8,128)S(1)}, u32[]{:S(2)}, u32[]{:S(2)}) %collective-permute-start.2) | collective-permute-done | bytes 262176 | tf_op jit(solution)/shard_map/ppermute | solution.py:557
  37.8 6.7 %collective-permute-done.3.rest_2_ = f32[4,4,32,128]{3,2,1,0:T(8,128)S(1)} collective-permute-done((f32[4,4,32,128]{3,2,1,0:T(8,128)S(1)}, f32[4,4,32,128]{3,2,1,0:T(8,128)S(1)}, u32[]{:S(2)}, u32[]{:S(2)}) %collective-permute-start.3) | collective-permute-done | bytes 262176 | tf_op jit(solution)/shard_map/ppermute | solution.py:557
  44.6 1.7 %collective-permute-start.7 = (f32[4,32,128]{2,1,0:T(8,128)S(1)}, f32[4,32,128]{2,1,0:T(8,128)S(1)}, u32[]{:S(2)}, u32[]{:S(2)}) collective-permute-start(f32[4,32,128]{2,1,0:T(8,128)S(1)} %get-tuple-element.55), channel_id=1, source_target_pairs={{0,8},{8,16},{16,24},{24,0},{32,40},{40,48},{48,56},{56,32},{64,72... | collective-permute-start | bytes 196616 | tf_op jit(solution)/shard_map/ppermute | solution.py:561
  46.3 2.2 %self_rows.1.rest_0_.base = f32[1024,512]{1,0:T(8,128)S(1)} custom-call(f32[1024,512]{1,0:T(8,128)S(1)} %copy-done.1, f32[512,512]{1,0:T(8,128)S(1)} %copy-done.6, f32[8,256,128]{2,1,0:T(8,128)S(1)} %copy-done.7, f32[8,256,128]{2,1,0:T(8,128)S(1)} %get-tuple-element.41.own_local, f32[4,32,128]{2,1,0:T(8,128)S(1)} %get-tuple-element.49.after.rest_0_), custom_call_target="tpu_custom_call" | custom-call | flops 1610612736 | bytes 6291456 | tf_op jit(solution)/shard_map/self_rows/pallas_call | solution.py:280
  48.6 1.8 %collective-permute-done.7.rest_1_ = f32[4,32,128]{2,1,0:T(8,128)S(1)} collective-permute-done((f32[4,32,128]{2,1,0:T(8,128)S(1)}, f32[4,32,128]{2,1,0:T(8,128)S(1)}, u32[]{:S(2)}, u32[]{:S(2)}) %collective-permute-start.7) | collective-permute-done | bytes 65568 | tf_op jit(solution)/shard_map/ppermute | solution.py:561
  51.0 1.9 %collective-permute-start.8 = (f32[15,64,128]{2,1,0:T(8,128)S(1)}, f32[15,64,128]{2,1,0:T(8,128)S(1)}, u32[]{:S(2)}, u32[]{:S(2)}) collective-permute-start(f32[15,64,128]{2,1,0:T(8,128)S(1)} %get-tuple-element.57), channel_id=1, source_target_pairs={{0,6},{1,7},{2,4},{3,5},{4,2},{5,3},{6,0},{7,1},{8,14},{9,15},{10,... | collective-permute-start | bytes 1474568 | tf_op jit(solution)/shard_map/ppermute | solution.py:575
  52.9 3.6 %collective-permute-start.10 = (f32[4,32,128]{2,1,0:T(8,128)S(1)}, f32[4,32,128]{2,1,0:T(8,128)S(1)}, u32[]{:S(2)}, u32[]{:S(2)}) collective-permute-start(f32[4,32,128]{2,1,0:T(8,128)S(1)} %get-tuple-element.59), channel_id=1, source_target_pairs={{0,16},{8,24},{16,0},{24,8},{32,48},{40,56},{48,32},{56,40},{64,80... | collective-permute-start | bytes 196616 | tf_op jit(solution)/shard_map/ppermute | solution.py:561
  58.1 1.8 %collective-permute-done.11.rest_3_ = f32[4,32,128]{2,1,0:T(8,128)S(1)} collective-permute-done((f32[4,32,128]{2,1,0:T(8,128)S(1)}, f32[4,32,128]{2,1,0:T(8,128)S(1)}, u32[]{:S(2)}, u32[]{:S(2)}) %collective-permute-start.11) | collective-permute-done | bytes 65568 | tf_op jit(solution)/shard_map/ppermute | solution.py:561
  59.9 3.3 %collective-permute-done.8.recv_a = f32[15,64,128]{2,1,0:T(8,128)S(1)} collective-permute-done((f32[15,64,128]{2,1,0:T(8,128)S(1)}, f32[15,64,128]{2,1,0:T(8,128)S(1)}, u32[]{:S(2)}, u32[]{:S(2)}) %collective-permute-start.8) | collective-permute-done | bytes 491552 | tf_op jit(solution)/shard_map/ppermute | solution.py:575
  64.0 1.7 %third_sums.1.rest_0_ = f32[32,64,128]{2,1,0:T(8,128)} custom-call(s32[32]{0:T(128)S(1)} %copy-done.10, f32[2,15,64,128]{3,2,1,0:T(8,128)S(1)} %get-tuple-element.56.keep, f32[15,64,128]{2,1,0:T(8,128)S(1)} %collective-permute-done.8.recv_a, f32[15,64,128]{2,1,0:T(8,128)S(1)} %collective-permute-done.9.recv_b, f32[4,32,128]{2,1,0:T(8,128)S(1)} %sum_z.1.after.value), custom_call_target="tpu_custom_call" | custom-call | flops 245760 | bytes 2949120 | tf_op jit(solution)/shard_map/third_sums/pallas_call | solution.py:280
  65.7 7.9 %all-to-all-start = ((f32[32,64,128]{2,1,0:T(8,128)}), f32[32,64,128]{2,1,0:T(8,128)S(1)}, u32[]{:S(2)}, u32[]{:S(2)}) async-start(f32[32,64,128]{2,1,0:T(8,128)} %third_sums.1.rest_0_), calls=%async_computation | async-start | bytes 2097152 | tf_op jit(solution)/shard_map/all_to_all | solution.py:580
  75.3 1.7 %collective-permute-start.14 = (f32[4,32,128]{2,1,0:T(8,128)S(1)}, f32[4,32,128]{2,1,0:T(8,128)S(1)}, u32[]{:S(2)}, u32[]{:S(2)}) collective-permute-start(f32[4,32,128]{2,1,0:T(8,128)S(1)} %pass.2.mine), channel_id=1, source_target_pairs={{0,4},{1,5},{2,6},{3,7},{4,0},{5,1},{6,2},{7,3},{8,12},{9,13},{10,... | collective-permute-start | bytes 196616 | tf_op jit(solution)/shard_map/ppermute | solution.py:582
  78.3 1.6 %collective-permute-done.14.far_two = f32[4,32,128]{2,1,0:T(8,128)S(1)} collective-permute-done((f32[4,32,128]{2,1,0:T(8,128)S(1)}, f32[4,32,128]{2,1,0:T(8,128)S(1)}, u32[]{:S(2)}, u32[]{:S(2)}) %collective-permute-start.14) | collective-permute-done | bytes 65568 | tf_op jit(solution)/shard_map/ppermute | solution.py:582
  81.3 2.4 %collective-permute-start.16 = (f32[4,32,128]{2,1,0:T(8,128)S(1)}, f32[4,32,128]{2,1,0:T(8,128)S(1)}, u32[]{:S(2)}, u32[]{:S(2)}) collective-permute-start(f32[4,32,128]{2,1,0:T(8,128)S(1)} %sum_chips.1.rest_0_), channel_id=1, source_target_pairs={{0,16},{8,24},{16,0},{24,8},{32,48},{40,56},{48,32},{56,40},{64,80... | collective-permute-start | bytes 196616 | tf_op jit(solution)/shard_map/ppermute | solution.py:585
  84.9 5.9 %collective-permute-done.15.rest_1_ = f32[4,32,128]{2,1,0:T(8,128)S(1)} collective-permute-done((f32[4,32,128]{2,1,0:T(8,128)S(1)}, f32[4,32,128]{2,1,0:T(8,128)S(1)}, u32[]{:S(2)}, u32[]{:S(2)}) %collective-permute-start.15) | collective-permute-done | bytes 65568 | tf_op jit(solution)/shard_map/ppermute | solution.py:585
  90.8 2.4 %collective-permute-done.16.rest_2_ = f32[4,32,128]{2,1,0:T(8,128)S(1)} collective-permute-done((f32[4,32,128]{2,1,0:T(8,128)S(1)}, f32[4,32,128]{2,1,0:T(8,128)S(1)}, u32[]{:S(2)}, u32[]{:S(2)}) %collective-permute-start.16) | collective-permute-done | bytes 65568 | tf_op jit(solution)/shard_map/ppermute | solution.py:585
  93.2 1.7 %place.1 = (f32[4,8,64,128]{3,2,1,0:T(8,128)S(1)}, f32[8,64,128]{2,1,0:T(8,128)S(1)}, f32[8,64,128]{2,1,0:T(8,128)S(1)}, f32[8,64,128]{2,1,0:T(8,128)S(1)}, f32[8,64,128]{2,1,0:T(8,128)S(1)}) custom-call(s32[16,16]{1,0:T(8,128)S(1)} %copy-done.8, s32[16,32]{1,0:T(8,128)S(1)} %copy-done.9, f32[32,64,128]{2,1,0:T(8,128)S(1)} %all-to-all-done.arrived, ...), custom_call_target="tpu_custom_call" | custom-call | flops 262144 | bytes 3145728 | tf_op jit(solution)/shard_map/place/pallas_call | solution.py:280
  95.8 2.3 %collective-permute-done.18.rest_3_.swapped = f32[4,8,64,128]{3,2,1,0:T(8,128)S(1)} collective-permute-done((f32[4,8,64,128]{3,2,1,0:T(8,128)S(1)}, f32[4,8,64,128]{3,2,1,0:T(8,128)S(1)}, u32[]{:S(2)}, u32[]{:S(2)}) %collective-permute-start.18) | collective-permute-done | bytes 1048608 | tf_op jit(solution)/shard_map/ppermute | solution.py:589
  99.4 1.8 %collective-permute-start.20 = (f32[2,8,64,128]{3,2,1,0:T(8,128)S(1)}, f32[2,8,64,128]{3,2,1,0:T(8,128)S(1)}, u32[]{:S(2)}, u32[]{:S(2)}) collective-permute-start(f32[2,8,64,128]{3,2,1,0:T(8,128)S(1)} %get-tuple-element.67), channel_id=1, source_target_pairs={{0,4},{1,5},{2,6},{3,7},{4,0},{5,1},{6,2},{7,3},{8,12},{9,13},{10,... | collective-permute-start | bytes 1572872 | tf_op jit(solution)/shard_map/ppermute | solution.py:592
  102.6 2.2 %collective-permute-start.23 = (f32[4,4,32,128]{3,2,1,0:T(8,128)S(1)}, f32[4,4,32,128]{3,2,1,0:T(8,128)S(1)}, u32[]{:S(2)}, u32[]{:S(2)}) collective-permute-start(f32[4,4,32,128]{3,2,1,0:T(8,128)S(1)} %pass.3.rest_0_), channel_id=1, source_target_pairs={{0,64},{8,72},{16,80},{24,88},{32,96},{40,104},{48,112},{56,120},{... | collective-permute-start | bytes 786440 | tf_op jit(solution)/shard_map/ppermute | solution.py:601
  104.9 2.3 %collective-permute-done.22.rest_1_ = f32[4,4,32,128]{3,2,1,0:T(8,128)S(1)} collective-permute-done((f32[4,4,32,128]{3,2,1,0:T(8,128)S(1)}, f32[4,4,32,128]{3,2,1,0:T(8,128)S(1)}, u32[]{:S(2)}, u32[]{:S(2)}) %collective-permute-start.22) | collective-permute-done | bytes 262176 | tf_op jit(solution)/shard_map/ppermute | solution.py:601
  107.2 4.4 %collective-permute-done.23.rest_2_ = f32[4,4,32,128]{3,2,1,0:T(8,128)S(1)} collective-permute-done((f32[4,4,32,128]{3,2,1,0:T(8,128)S(1)}, f32[4,4,32,128]{3,2,1,0:T(8,128)S(1)}, u32[]{:S(2)}, u32[]{:S(2)}) %collective-permute-start.23) | collective-permute-done | bytes 262176 | tf_op jit(solution)/shard_map/ppermute | solution.py:601
  111.6 2.8 %collective-permute-done.24.rest_3_ = f32[4,4,32,128]{3,2,1,0:T(8,128)S(1)} collective-permute-done((f32[4,4,32,128]{3,2,1,0:T(8,128)S(1)}, f32[4,4,32,128]{3,2,1,0:T(8,128)S(1)}, u32[]{:S(2)}, u32[]{:S(2)}) %collective-permute-start.24) | collective-permute-done | bytes 262176 | tf_op jit(solution)/shard_map/ppermute | solution.py:601
  114.5 9.3 %collective-permute-done.20.rest_1_.rest_5_ = f32[2,8,64,128]{3,2,1,0:T(8,128)S(1)} collective-permute-done((f32[2,8,64,128]{3,2,1,0:T(8,128)S(1)}, f32[2,8,64,128]{3,2,1,0:T(8,128)S(1)}, u32[]{:S(2)}, u32[]{:S(2)}) %collective-permute-start.20) | collective-permute-done | bytes 524320 | tf_op jit(solution)/shard_map/ppermute | solution.py:592
  124.4 1.6 %collective-permute-start.25 = (f32[16,4,32,128]{3,2,1,0:T(8,128)S(1)}, f32[16,4,32,128]{3,2,1,0:T(8,128)S(1)}, u32[]{:S(2)}, u32[]{:S(2)}) collective-permute-start(f32[16,4,32,128]{3,2,1,0:T(8,128)S(1)} %bitcast.11), channel_id=1, source_target_pairs={{0,1},{1,0},{2,3},{3,2},{4,5},{5,4},{6,7},{7,6},{8,9},{9,8},{10,11... | collective-permute-start | bytes 3145736 | tf_op jit(solution)/shard_map/ppermute | solution.py:603
  126.0 1.7 %finish.1 = f32[1024,512]{1,0:T(8,128)} custom-call(f32[1024,512]{1,0:T(8,128)S(1)} %copy-done.3, f32[8,64,128]{2,1,0:T(8,128)S(1)} %get-tuple-element.61.keep, f32[4,8,64,128]{3,2,1,0:T(8,128)S(1)} %collective-permute-done.18.rest_3_.swapped, f32[2,8,64,128]{3,2,1,0:T(8,128)S(1)} %collective-permute-done.19.rest_0_.rest_4_, ...), custom_call_target="tpu_custom_call" | custom-call | flops 1048576 | bytes 8388608 | tf_op jit(solution)/shard_map/finish/pallas_call | solution.py:490
  (68 shorter events, 22.5 us)
Async XLA Ops:
  10.5 8.1 %collective-permute-start = (f32[30,256,128]{2,1,0:T(8,128)}, f32[30,256,128]{2,1,0:T(8,128)S(1)}, u32[]{:S(2)}, u32[]{:S(2)}) collective-permute-start(f32[30,256,128]{2,1,0:T(8,128)} %get-tuple-element.40), channel_id=1, source_target_pairs={{0,1},{1,0},{2,3},{3,2},{4,5},{5,4},{6,7},{7,6},{8,9},{9,8},{10,11... | collective-permute-start | bytes 11796488 | tf_op jit(solution)/shard_map/ppermute | solution.py:537
  17.7 10.9 %collective-permute-start.1 = (f32[16,4,32,128]{3,2,1,0:T(8,128)S(1)}, f32[16,4,32,128]{3,2,1,0:T(8,128)S(1)}, u32[]{:S(2)}, u32[]{:S(2)}) collective-permute-start(f32[16,4,32,128]{3,2,1,0:T(8,128)S(1)} %get-tuple-element.43), channel_id=1, source_target_pairs={{0,1},{1,0},{2,3},{3,2},{4,5},{5,4},{6,7},{7,6},{8,9},{9,8},{10,11... | collective-permute-start | bytes 3145736 | tf_op jit(solution)/shard_map/ppermute | solution.py:554
  25.3 21.0 %copy-start.6 = (f32[512,512]{1,0:T(8,128)S(1)}, f32[512,512]{1,0:T(8,128)}, u32[]{:S(2)}) copy-start(f32[512,512]{1,0:T(8,128)} %weight.1) | copy-start | bytes 3145732
  25.3 21.0 %copy-start.7 = (f32[8,256,128]{2,1,0:T(8,128)S(1)}, f32[8,256,128]{2,1,0:T(8,128)}, u32[]{:S(2)}) copy-start(f32[8,256,128]{2,1,0:T(8,128)} %get-tuple-element.38.other_local) | copy-start | bytes 3145732
  25.3 25.0 %collective-permute-start.5 = (f32[2,15,64,128]{3,2,1,0:T(8,128)S(1)}, f32[2,15,64,128]{3,2,1,0:T(8,128)S(1)}, u32[]{:S(2)}, u32[]{:S(2)}) collective-permute-start(f32[2,15,64,128]{3,2,1,0:T(8,128)S(1)} %get-tuple-element.52), channel_id=1, source_target_pairs={{0,2},{1,3},{2,0},{3,1},{4,6},{5,7},{6,4},{7,5},{8,10},{9,11},{10,... | collective-permute-start | bytes 2949128 | tf_op jit(solution)/shard_map/ppermute | solution.py:541
  26.7 24.1 %collective-permute-start.6 = (f32[2,15,64,128]{3,2,1,0:T(8,128)S(1)}, f32[2,15,64,128]{3,2,1,0:T(8,128)S(1)}, u32[]{:S(2)}, u32[]{:S(2)}) collective-permute-start(f32[2,15,64,128]{3,2,1,0:T(8,128)S(1)} %get-tuple-element.54), channel_id=1, source_target_pairs={{0,6},{1,7},{2,4},{3,5},{4,2},{5,3},{6,0},{7,1},{8,14},{9,15},{10,... | collective-permute-start | bytes 2949128 | tf_op jit(solution)/shard_map/ppermute | solution.py:542
  29.3 8.5 %collective-permute-start.2 = (f32[4,4,32,128]{3,2,1,0:T(8,128)S(1)}, f32[4,4,32,128]{3,2,1,0:T(8,128)S(1)}, u32[]{:S(2)}, u32[]{:S(2)}) collective-permute-start(f32[4,4,32,128]{3,2,1,0:T(8,128)S(1)} %get-tuple-element.46), channel_id=1, source_target_pairs={{0,32},{8,40},{16,48},{24,56},{32,64},{40,72},{48,80},{56,88},{64,... | collective-permute-start | bytes 786440 | tf_op jit(solution)/shard_map/ppermute | solution.py:557
  30.7 13.9 %collective-permute-start.3 = (f32[4,4,32,128]{3,2,1,0:T(8,128)S(1)}, f32[4,4,32,128]{3,2,1,0:T(8,128)S(1)}, u32[]{:S(2)}, u32[]{:S(2)}) collective-permute-start(f32[4,4,32,128]{3,2,1,0:T(8,128)S(1)} %get-tuple-element.47), channel_id=1, source_target_pairs={{0,64},{8,72},{16,80},{24,88},{32,96},{40,104},{48,112},{56,120},{... | collective-permute-start | bytes 786440 | tf_op jit(solution)/shard_map/ppermute | solution.py:557
  33.3 11.2 %collective-permute-start.4 = (f32[4,4,32,128]{3,2,1,0:T(8,128)S(1)}, f32[4,4,32,128]{3,2,1,0:T(8,128)S(1)}, u32[]{:S(2)}, u32[]{:S(2)}) collective-permute-start(f32[4,4,32,128]{3,2,1,0:T(8,128)S(1)} %get-tuple-element.48), channel_id=1, source_target_pairs={{0,96},{8,104},{16,112},{24,120},{32,0},{40,8},{48,16},{56,24},{64... | collective-permute-start | bytes 786440 | tf_op jit(solution)/shard_map/ppermute | solution.py:557
  44.6 5.8 %collective-permute-start.7 = (f32[4,32,128]{2,1,0:T(8,128)S(1)}, f32[4,32,128]{2,1,0:T(8,128)S(1)}, u32[]{:S(2)}, u32[]{:S(2)}) collective-permute-start(f32[4,32,128]{2,1,0:T(8,128)S(1)} %get-tuple-element.55), channel_id=1, source_target_pairs={{0,8},{8,16},{16,24},{24,0},{32,40},{40,48},{48,56},{56,32},{64,72... | collective-permute-start | bytes 196616 | tf_op jit(solution)/shard_map/ppermute | solution.py:561
  50.8 13.2 %copy-start.10 = (s32[32]{0:T(128)S(1)}, s32[32]{0:T(128)}, u32[]{:S(2)}) copy-start(s32[32]{0:T(128)} %get-tuple-element.50.places) | copy-start | bytes 388
  51.0 12.2 %collective-permute-start.8 = (f32[15,64,128]{2,1,0:T(8,128)S(1)}, f32[15,64,128]{2,1,0:T(8,128)S(1)}, u32[]{:S(2)}, u32[]{:S(2)}) collective-permute-start(f32[15,64,128]{2,1,0:T(8,128)S(1)} %get-tuple-element.57), channel_id=1, source_target_pairs={{0,6},{1,7},{2,4},{3,5},{4,2},{5,3},{6,0},{7,1},{8,14},{9,15},{10,... | collective-permute-start | bytes 1474568 | tf_op jit(solution)/shard_map/ppermute | solution.py:575
  52.9 11.1 %collective-permute-start.9 = (f32[15,64,128]{2,1,0:T(8,128)S(1)}, f32[15,64,128]{2,1,0:T(8,128)S(1)}, u32[]{:S(2)}, u32[]{:S(2)}) collective-permute-start(f32[15,64,128]{2,1,0:T(8,128)S(1)} %get-tuple-element.58), channel_id=1, source_target_pairs={{0,2},{1,3},{2,0},{3,1},{4,6},{5,7},{6,4},{7,5},{8,10},{9,11},{10,... | collective-permute-start | bytes 1474568 | tf_op jit(solution)/shard_map/ppermute | solution.py:576
  52.9 5.3 %collective-permute-start.10 = (f32[4,32,128]{2,1,0:T(8,128)S(1)}, f32[4,32,128]{2,1,0:T(8,128)S(1)}, u32[]{:S(2)}, u32[]{:S(2)}) collective-permute-start(f32[4,32,128]{2,1,0:T(8,128)S(1)} %get-tuple-element.59), channel_id=1, source_target_pairs={{0,16},{8,24},{16,0},{24,8},{32,48},{40,56},{48,32},{56,40},{64,80... | collective-permute-start | bytes 196616 | tf_op jit(solution)/shard_map/ppermute | solution.py:561
  56.5 3.4 %collective-permute-start.11 = (f32[4,32,128]{2,1,0:T(8,128)S(1)}, f32[4,32,128]{2,1,0:T(8,128)S(1)}, u32[]{:S(2)}, u32[]{:S(2)}) collective-permute-start(f32[4,32,128]{2,1,0:T(8,128)S(1)} %get-tuple-element.60), channel_id=1, source_target_pairs={{0,24},{8,0},{16,8},{24,16},{32,56},{40,32},{48,40},{56,48},{64,88... | collective-permute-start | bytes 196616 | tf_op jit(solution)/shard_map/ppermute | solution.py:561
  65.7 27.6 %copy-start.9 = (s32[16,32]{1,0:T(8,128)S(1)}, s32[16,32]{1,0:T(8,128)}, u32[]{:S(2)}) copy-start(s32[16,32]{1,0:T(8,128)} %target_ref.1) | copy-start | bytes 6148
  65.7 27.6 %all-to-all-start = ((f32[32,64,128]{2,1,0:T(8,128)}), f32[32,64,128]{2,1,0:T(8,128)S(1)}, u32[]{:S(2)}, u32[]{:S(2)}) async-start(f32[32,64,128]{2,1,0:T(8,128)} %third_sums.1.rest_0_), calls=%async_computation | async-start | bytes 2097152 | tf_op jit(solution)/shard_map/all_to_all | solution.py:580
  73.6 3.3 %collective-permute-start.12 = (f32[4,32,128]{2,1,0:T(8,128)S(1)}, f32[4,32,128]{2,1,0:T(8,128)S(1)}, u32[]{:S(2)}, u32[]{:S(2)}) collective-permute-start(f32[4,32,128]{2,1,0:T(8,128)S(1)} %pass.2.mine), channel_id=1, source_target_pairs={{0,2},{1,3},{2,0},{3,1},{4,6},{5,7},{6,4},{7,5},{8,10},{9,11},{10,... | collective-permute-start | bytes 196616 | tf_op jit(solution)/shard_map/ppermute | solution.py:582
  73.9 4.3 %collective-permute-start.13 = (f32[4,32,128]{2,1,0:T(8,128)S(1)}, f32[4,32,128]{2,1,0:T(8,128)S(1)}, u32[]{:S(2)}, u32[]{:S(2)}) collective-permute-start(f32[4,32,128]{2,1,0:T(8,128)S(1)} %pass.2.mine), channel_id=1, source_target_pairs={{0,6},{1,7},{2,4},{3,5},{4,2},{5,3},{6,0},{7,1},{8,14},{9,15},{10,... | collective-permute-start | bytes 196616 | tf_op jit(solution)/shard_map/ppermute | solution.py:582
  75.3 4.6 %collective-permute-start.14 = (f32[4,32,128]{2,1,0:T(8,128)S(1)}, f32[4,32,128]{2,1,0:T(8,128)S(1)}, u32[]{:S(2)}, u32[]{:S(2)}) collective-permute-start(f32[4,32,128]{2,1,0:T(8,128)S(1)} %pass.2.mine), channel_id=1, source_target_pairs={{0,4},{1,5},{2,6},{3,7},{4,0},{5,1},{6,2},{7,3},{8,12},{9,13},{10,... | collective-permute-start | bytes 196616 | tf_op jit(solution)/shard_map/ppermute | solution.py:582
  79.9 10.9 %collective-permute-start.15 = (f32[4,32,128]{2,1,0:T(8,128)S(1)}, f32[4,32,128]{2,1,0:T(8,128)S(1)}, u32[]{:S(2)}, u32[]{:S(2)}) collective-permute-start(f32[4,32,128]{2,1,0:T(8,128)S(1)} %sum_chips.1.rest_0_), channel_id=1, source_target_pairs={{0,8},{8,16},{16,24},{24,0},{32,40},{40,48},{48,56},{56,32},{64,72... | collective-permute-start | bytes 196616 | tf_op jit(solution)/shard_map/ppermute | solution.py:585
  81.3 11.9 %collective-permute-start.16 = (f32[4,32,128]{2,1,0:T(8,128)S(1)}, f32[4,32,128]{2,1,0:T(8,128)S(1)}, u32[]{:S(2)}, u32[]{:S(2)}) collective-permute-start(f32[4,32,128]{2,1,0:T(8,128)S(1)} %sum_chips.1.rest_0_), channel_id=1, source_target_pairs={{0,16},{8,24},{16,0},{24,8},{32,48},{40,56},{48,32},{56,40},{64,80... | collective-permute-start | bytes 196616 | tf_op jit(solution)/shard_map/ppermute | solution.py:585
  83.7 9.5 %collective-permute-start.17 = (f32[4,32,128]{2,1,0:T(8,128)S(1)}, f32[4,32,128]{2,1,0:T(8,128)S(1)}, u32[]{:S(2)}, u32[]{:S(2)}) collective-permute-start(f32[4,32,128]{2,1,0:T(8,128)S(1)} %sum_chips.1.rest_0_), channel_id=1, source_target_pairs={{0,24},{8,0},{16,8},{24,16},{32,56},{40,32},{48,40},{56,48},{64,88... | collective-permute-start | bytes 196616 | tf_op jit(solution)/shard_map/ppermute | solution.py:585
  94.9 3.2 %collective-permute-start.18 = (f32[4,8,64,128]{3,2,1,0:T(8,128)S(1)}, f32[4,8,64,128]{3,2,1,0:T(8,128)S(1)}, u32[]{:S(2)}, u32[]{:S(2)}) collective-permute-start(f32[4,8,64,128]{3,2,1,0:T(8,128)S(1)} %get-tuple-element.62), channel_id=1, source_target_pairs={{0,1},{1,0},{2,3},{3,2},{4,5},{5,4},{6,7},{7,6},{8,9},{9,8},{10,11... | collective-permute-start | bytes 3145736 | tf_op jit(solution)/shard_map/ppermute | solution.py:589
  98.3 27.7 %copy-start.3 = (f32[1024,512]{1,0:T(8,128)S(1)}, f32[1024,512]{1,0:T(8,128)}, u32[]{:S(2)}) copy-start(f32[1024,512]{1,0:T(8,128)} %copy-done.2) | copy-start | bytes 6291460
  98.3 8.9 %collective-permute-start.22 = (f32[4,4,32,128]{3,2,1,0:T(8,128)S(1)}, f32[4,4,32,128]{3,2,1,0:T(8,128)S(1)}, u32[]{:S(2)}, u32[]{:S(2)}) collective-permute-start(f32[4,4,32,128]{3,2,1,0:T(8,128)S(1)} %pass.3.rest_0_), channel_id=1, source_target_pairs={{0,32},{8,40},{16,48},{24,56},{32,64},{40,72},{48,80},{56,88},{64,... | collective-permute-start | bytes 786440 | tf_op jit(solution)/shard_map/ppermute | solution.py:601
  98.3 16.1 %collective-permute-start.19 = (f32[2,8,64,128]{3,2,1,0:T(8,128)S(1)}, f32[2,8,64,128]{3,2,1,0:T(8,128)S(1)}, u32[]{:S(2)}, u32[]{:S(2)}) collective-permute-start(f32[2,8,64,128]{3,2,1,0:T(8,128)S(1)} %get-tuple-element.66.rest_0_), channel_id=1, source_target_pairs={{0,2},{1,3},{2,4},{3,5},{4,6},{5,7},{6,0},{7,1},{8,10},{9,11},{10,... | collective-permute-start | bytes 1572872 | tf_op jit(solution)/shard_map/ppermute | solution.py:592
  99.4 24.4 %collective-permute-start.20 = (f32[2,8,64,128]{3,2,1,0:T(8,128)S(1)}, f32[2,8,64,128]{3,2,1,0:T(8,128)S(1)}, u32[]{:S(2)}, u32[]{:S(2)}) collective-permute-start(f32[2,8,64,128]{3,2,1,0:T(8,128)S(1)} %get-tuple-element.67), channel_id=1, source_target_pairs={{0,4},{1,5},{2,6},{3,7},{4,0},{5,1},{6,2},{7,3},{8,12},{9,13},{10,... | collective-permute-start | bytes 1572872 | tf_op jit(solution)/shard_map/ppermute | solution.py:592
  101.2 23.1 %collective-permute-start.21 = (f32[2,8,64,128]{3,2,1,0:T(8,128)S(1)}, f32[2,8,64,128]{3,2,1,0:T(8,128)S(1)}, u32[]{:S(2)}, u32[]{:S(2)}) collective-permute-start(f32[2,8,64,128]{3,2,1,0:T(8,128)S(1)} %get-tuple-element.68), channel_id=1, source_target_pairs={{0,6},{1,7},{2,0},{3,1},{4,2},{5,3},{6,4},{7,5},{8,14},{9,15},{10,... | collective-permute-start | bytes 1572872 | tf_op jit(solution)/shard_map/ppermute | solution.py:592
  102.6 9.0 %collective-permute-start.23 = (f32[4,4,32,128]{3,2,1,0:T(8,128)S(1)}, f32[4,4,32,128]{3,2,1,0:T(8,128)S(1)}, u32[]{:S(2)}, u32[]{:S(2)}) collective-permute-start(f32[4,4,32,128]{3,2,1,0:T(8,128)S(1)} %pass.3.rest_0_), channel_id=1, source_target_pairs={{0,64},{8,72},{16,80},{24,88},{32,96},{40,104},{48,112},{56,120},{... | collective-permute-start | bytes 786440 | tf_op jit(solution)/shard_map/ppermute | solution.py:601
  107.2 7.2 %collective-permute-start.24 = (f32[4,4,32,128]{3,2,1,0:T(8,128)S(1)}, f32[4,4,32,128]{3,2,1,0:T(8,128)S(1)}, u32[]{:S(2)}, u32[]{:S(2)}) collective-permute-start(f32[4,4,32,128]{3,2,1,0:T(8,128)S(1)} %pass.3.rest_0_), channel_id=1, source_target_pairs={{0,96},{8,104},{16,112},{24,120},{32,0},{40,8},{48,16},{56,24},{64... | collective-permute-start | bytes 786440 | tf_op jit(solution)/shard_map/ppermute | solution.py:601
  124.4 3.9 %collective-permute-start.25 = (f32[16,4,32,128]{3,2,1,0:T(8,128)S(1)}, f32[16,4,32,128]{3,2,1,0:T(8,128)S(1)}, u32[]{:S(2)}, u32[]{:S(2)}) collective-permute-start(f32[16,4,32,128]{3,2,1,0:T(8,128)S(1)} %bitcast.11), channel_id=1, source_target_pairs={{0,1},{1,0},{2,3},{3,2},{4,5},{5,4},{6,7},{7,6},{8,9},{9,8},{10,11... | collective-permute-start | bytes 3145736 | tf_op jit(solution)/shard_map/ppermute | solution.py:603
  (8 other events, 27.8 us)

commit v12 on v11

--- a/solution.py
+++ b/solution.py
@@ -12,9 +12,10 @@
 BLOCK = 128
 CHUNKS = 2
 MAIN = 30
-LIMIT_OTHER = 55
+LIMIT_OTHER = 52
 LIMIT_OWN = 20
 LIMIT_SMALL = 6
+AWAY = (0, 1, 3, 2)
 
 
 def split(x):
@@ -192,7 +193,7 @@
         out_shape = [
             jax.ShapeDtypeStruct((node_rows, feat), F32),
             local,
-            jax.ShapeDtypeStruct((main, width, BLOCK), F32),
+            pltpu.VMEM((main, width, BLOCK), F32),
             jax.ShapeDtypeStruct((main + over,), jnp.int32),
             jax.ShapeDtypeStruct(tile_col.shape, jnp.int32),
         ]
@@ -364,7 +365,8 @@
     out[...] = total
 
 
-def chips_kernel(scale, mine, pair, far_one, far_two, out):
+def chips_kernel(scale, mine, pair, far_one, far_two, after, out):
+    del after
     out[...] = ((mine[...] + pair[...]) + (far_one[...] + far_two[...])) * scale
 
 
@@ -469,7 +471,7 @@
     copies = []
     for b in range(blocks):
         for k, some in enumerate(pieces):
-            source = (chip - k // 2) & 3
+            source = (chip - AWAY[k // 2]) & 3
             side = source >> 1
             quarter = side * 2 + ((source + side) & 1)
             first = core if k % 2 == 0 else 1 - core
@@ -578,10 +580,15 @@
     share = small(sum_kernel, share_shape, terms, "sum_z")
     shares = third_sums(places, keep, recv_a, recv_b, share)
     arrived = lax.all_to_all(shares, "group", split_axis=0, concat_axis=0, tiled=True)
-    share = small(pass_kernel, share_shape, [share, shares], "pass", [IN_VMEM, ANYWHERE])
     terms = [share] + [lax.ppermute(share, "local", p) for p in (pairs, across, along_x[2])]
     scale = float(node_rows * groups * members) ** (-0.5)
-    share = small(functools.partial(chips_kernel, scale), share_shape, terms, "sum_chips")
+    share = small(
+        functools.partial(chips_kernel, scale),
+        share_shape,
+        [*terms, shares],
+        "sum_chips",
+        [IN_VMEM] * 4 + [ANYWHERE],
+    )
     terms = [share] + [lax.ppermute(share, "group", along_z[k]) for k in range(1, 4)]
     row = gather(lambda g: g & 3, terms, "gather_z")
 
@@ -589,7 +596,7 @@
     swapped = lax.ppermute(send, "local", swap)
     joined = jax.ShapeDtypeStruct((2,) + keeps[0].shape, F32)
     joined = small(join_kernel, [joined] * 3, [*keeps[1:], swapped], "join")
-    received = [lax.ppermute(joined[k - 1], "local", along_x[k]) for k in range(1, 4)]
+    received = [lax.ppermute(joined[k - 1], "local", along_x[k]) for k in AWAY[1:]]
 
     row = small(
         pass_kernel,

time: 130 us -> 129 us (level)
    pallas_call x15 -> x14, Pallas kernels: 8.49 us -> 8.38 us  [small(): pl.pallas_call(kernel, out_shape=out_shape, in_specs=specs or [IN_VMEM] *...]
  transfers between devices with their start and end apart: 27 -> 27, of which waited for: 20 -> 19; matrix products, arithmetic and copies ran while one was open for 4% -> 4% of each run, Pallas kernels for 9% -> 9%
where the time goes in v12:
time: 129 us; the launch traced here: 128 us
  waiting for transfers between devices  54 us (42%)
  starting transfers between devices  42.3 us (33%)
  Pallas kernels  25.4 us (20%)
  matrix products  5.41 us (4%)
    pallas_call x2, Pallas kernels, tile_sums(): pl.pallas_call(functools.partial(tile_kernel, own, blocks, main, over), o...  15.3 us
    ppermute x3, waiting for transfers between devices, on_device(): lax.ppermute(some, 'group', along_y[k + 1])  10.3 us
    ppermute x3, waiting for transfers between devices, on_device(): rows = [row] + [lax.ppermute(row, 'group', along_y[k]) for k in range(1, 4)]  10 us
    ppermute x3, waiting for transfers between devices, on_device(): lax.ppermute(joined[k - 1], 'local', along_x[k])  9.61 us
    pallas_call x14, Pallas kernels, small(): pl.pallas_call(kernel, out_shape=out_shape, in_specs=specs or [IN_VMEM] *...  8.38 us
    ppermute x3, waiting for transfers between devices, on_device(): lax.ppermute(share, 'group', along_z[k])  8.26 us
    all_to_all x1, starting transfers between devices, on_device(): lax.all_to_all(shares, 'group', split_axis=0, concat_axis=0, tiled=True)  7.9 us
    ppermute x3, starting transfers between devices, on_device(): lax.ppermute(some, 'group', along_z[k + 1])  5.74 us
  transfers between devices with their start and end apart: 27, of which 19 were waited for; matrix products, arithmetic and copies ran while one was open for 4% of the time, Pallas kernels for 9%

profile of v12, /device:TPU:1, one launch (start us, length us, event | category | flops | bytes accessed | tf_op | source)
XLA Modules:
  0.0 128.4 jit_solution(4849003362764143228)
XLA Ops:
  0.6 8.8 %other_tile_sums.1 = (f32[1024,512]{1,0:T(8,128)}, f32[8,256,128]{2,1,0:T(8,128)}, f32[30,256,128]{2,1,0:T(8,128)S(1)}, s32[32]{0:T(128)}, s32[64]{0:T(128)}) custom-call(s32[64]{0:T(128)} %col_ref.1, s32[16,16]{1,0:T(8,128)} %count_ref.5, f32[1024,512]{1,0:T(8,128)} %rest_0_.1, f32[1024,512]{1,0:T(8,128)} %rest_1_.2, f32[512,512]{1,0:T(8,128)} %rest_1_.3, ...), custom_call_target="tpu_custom_call" | custom-call | flops 2415919104 | bytes 14680064 | tf_op jit(solution)/shard_map/other_tile_sums/pallas_call | solution.py:209
  11.0 3.6 %convolution_bitcast_fusion.neigh_term = f32[512,512]{1,0:T(8,128)S(1)} fusion(f32[1024,512]{1,0:T(8,128)} %get-tuple-element.37.rest_0_.pre_grad, f32[1024,512]{1,0:T(8,128)S(1)} %copy-done), kind=kOutput, calls=%fused_computation | convolution fusion | flops 1610612736 | bytes 5242880 | tf_op jit(solution)/shard_map/dot_general | solution.py:550
  14.6 1.8 %convolution_bitcast_fusion.1.self_term = f32[512,512]{1,0:T(8,128)S(1)} fusion(f32[1024,512]{1,0:T(8,128)S(1)} %copy-done.1, f32[1024,512]{1,0:T(8,128)S(1)} %copy-done.12), kind=kOutput, calls=%fused_computation.1 | convolution fusion | flops 1610612736 | bytes 5242880 | tf_op jit(solution)/shard_map/dot_general | solution.py:547
  17.7 6.5 %own_tile_sums.1 = (f32[8,256,128]{2,1,0:T(8,128)S(1)}, s32[1]{0:T(128)}, f32[2,15,64,128]{3,2,1,0:T(8,128)S(1)}, f32[2,15,64,128]{3,2,1,0:T(8,128)S(1)}, f32[2,...) custom-call(s32[64]{0:T(128)S(1)} %copy-done.11, s32[16,16]{1,0:T(8,128)S(1)} %copy-done.8, ...), custom_call_target="tpu_custom_call" | custom-call | flops 2415919104 | bytes 14680064 | tf_op jit(solution)/shard_map/own_tile_sums/pallas_call | solution.py:209
  25.7 1.8 %collective-permute-start.6 = (f32[2,15,64,128]{3,2,1,0:T(8,128)S(1)}, f32[2,15,64,128]{3,2,1,0:T(8,128)S(1)}, u32[]{:S(2)}, u32[]{:S(2)}) collective-permute-start(f32[2,15,64,128]{3,2,1,0:T(8,128)S(1)} %get-tuple-element.54), channel_id=1, source_target_pairs={{0,6},{1,7},{2,4},{3,5},{4,2},{5,3},{6,0},{7,1},{8,14},{9,15},{10,... | collective-permute-start | bytes 2949128 | tf_op jit(solution)/shard_map/ppermute | solution.py:544
  29.6 2.6 %collective-permute-start.3 = (f32[4,4,32,128]{3,2,1,0:T(8,128)S(1)}, f32[4,4,32,128]{3,2,1,0:T(8,128)S(1)}, u32[]{:S(2)}, u32[]{:S(2)}) collective-permute-start(f32[4,4,32,128]{3,2,1,0:T(8,128)S(1)} %get-tuple-element.47), channel_id=1, source_target_pairs={{0,64},{8,72},{16,80},{24,88},{32,96},{40,104},{48,112},{56,120},{... | collective-permute-start | bytes 786440 | tf_op jit(solution)/shard_map/ppermute | solution.py:559
  33.3 3.6 %collective-permute-done.2.rest_1_ = f32[4,4,32,128]{3,2,1,0:T(8,128)S(1)} collective-permute-done((f32[4,4,32,128]{3,2,1,0:T(8,128)S(1)}, f32[4,4,32,128]{3,2,1,0:T(8,128)S(1)}, u32[]{:S(2)}, u32[]{:S(2)}) %collective-permute-start.2) | collective-permute-done | bytes 262176 | tf_op jit(solution)/shard_map/ppermute | solution.py:559
  37.0 6.7 %collective-permute-done.3.rest_2_ = f32[4,4,32,128]{3,2,1,0:T(8,128)S(1)} collective-permute-done((f32[4,4,32,128]{3,2,1,0:T(8,128)S(1)}, f32[4,4,32,128]{3,2,1,0:T(8,128)S(1)}, u32[]{:S(2)}, u32[]{:S(2)}) %collective-permute-start.3) | collective-permute-done | bytes 262176 | tf_op jit(solution)/shard_map/ppermute | solution.py:559
  43.7 1.7 %collective-permute-start.7 = (f32[4,32,128]{2,1,0:T(8,128)S(1)}, f32[4,32,128]{2,1,0:T(8,128)S(1)}, u32[]{:S(2)}, u32[]{:S(2)}) collective-permute-start(f32[4,32,128]{2,1,0:T(8,128)S(1)} %get-tuple-element.55), channel_id=1, source_target_pairs={{0,8},{8,16},{16,24},{24,0},{32,40},{40,48},{48,56},{56,32},{64,72... | collective-permute-start | bytes 196616 | tf_op jit(solution)/shard_map/ppermute | solution.py:563
  45.4 2.2 %self_rows.1.rest_0_.base = f32[1024,512]{1,0:T(8,128)S(1)} custom-call(f32[1024,512]{1,0:T(8,128)S(1)} %copy-done.1, f32[512,512]{1,0:T(8,128)S(1)} %copy-done.6, f32[8,256,128]{2,1,0:T(8,128)S(1)} %copy-done.7, f32[8,256,128]{2,1,0:T(8,128)S(1)} %get-tuple-element.41.own_local, f32[4,32,128]{2,1,0:T(8,128)S(1)} %get-tuple-element.49.after.rest_0_), custom_call_target="tpu_custom_call" | custom-call | flops 1610612736 | bytes 6291456 | tf_op jit(solution)/shard_map/self_rows/pallas_call | solution.py:281
  47.7 1.8 %collective-permute-done.7.rest_1_ = f32[4,32,128]{2,1,0:T(8,128)S(1)} collective-permute-done((f32[4,32,128]{2,1,0:T(8,128)S(1)}, f32[4,32,128]{2,1,0:T(8,128)S(1)}, u32[]{:S(2)}, u32[]{:S(2)}) %collective-permute-start.7) | collective-permute-done | bytes 65568 | tf_op jit(solution)/shard_map/ppermute | solution.py:563
  50.1 1.9 %collective-permute-start.8 = (f32[15,64,128]{2,1,0:T(8,128)S(1)}, f32[15,64,128]{2,1,0:T(8,128)S(1)}, u32[]{:S(2)}, u32[]{:S(2)}) collective-permute-start(f32[15,64,128]{2,1,0:T(8,128)S(1)} %get-tuple-element.57), channel_id=1, source_target_pairs={{0,6},{1,7},{2,4},{3,5},{4,2},{5,3},{6,0},{7,1},{8,14},{9,15},{10,... | collective-permute-start | bytes 1474568 | tf_op jit(solution)/shard_map/ppermute | solution.py:577
  52.0 3.6 %collective-permute-start.10 = (f32[4,32,128]{2,1,0:T(8,128)S(1)}, f32[4,32,128]{2,1,0:T(8,128)S(1)}, u32[]{:S(2)}, u32[]{:S(2)}) collective-permute-start(f32[4,32,128]{2,1,0:T(8,128)S(1)} %get-tuple-element.59), channel_id=1, source_target_pairs={{0,16},{8,24},{16,0},{24,8},{32,48},{40,56},{48,32},{56,40},{64,80... | collective-permute-start | bytes 196616 | tf_op jit(solution)/shard_map/ppermute | solution.py:563
  57.3 1.8 %collective-permute-done.11.rest_3_ = f32[4,32,128]{2,1,0:T(8,128)S(1)} collective-permute-done((f32[4,32,128]{2,1,0:T(8,128)S(1)}, f32[4,32,128]{2,1,0:T(8,128)S(1)}, u32[]{:S(2)}, u32[]{:S(2)}) %collective-permute-start.11) | collective-permute-done | bytes 65568 | tf_op jit(solution)/shard_map/ppermute | solution.py:563
  59.1 3.4 %collective-permute-done.8.recv_a = f32[15,64,128]{2,1,0:T(8,128)S(1)} collective-permute-done((f32[15,64,128]{2,1,0:T(8,128)S(1)}, f32[15,64,128]{2,1,0:T(8,128)S(1)}, u32[]{:S(2)}, u32[]{:S(2)}) %collective-permute-start.8) | collective-permute-done | bytes 491552 | tf_op jit(solution)/shard_map/ppermute | solution.py:577
  63.3 1.7 %third_sums.1.after = f32[32,64,128]{2,1,0:T(8,128)} custom-call(s32[32]{0:T(128)S(1)} %copy-done.10, f32[2,15,64,128]{3,2,1,0:T(8,128)S(1)} %get-tuple-element.56.keep, f32[15,64,128]{2,1,0:T(8,128)S(1)} %collective-permute-done.8.recv_a, f32[15,64,128]{2,1,0:T(8,128)S(1)} %collective-permute-done.9.recv_b, f32[4,32,128]{2,1,0:T(8,128)S(1)} %sum_z.1.after.mine), custom_call_target="tpu_custom_call" | custom-call | flops 245760 | bytes 2949120 | tf_op jit(solution)/shard_map/third_sums/pallas_call | solution.py:281
  65.0 7.9 %all-to-all-start = ((f32[32,64,128]{2,1,0:T(8,128)}), f32[32,64,128]{2,1,0:T(8,128)S(1)}, u32[]{:S(2)}, u32[]{:S(2)}) async-start(f32[32,64,128]{2,1,0:T(8,128)} %third_sums.1.after), calls=%async_computation | async-start | bytes 2097152 | tf_op jit(solution)/shard_map/all_to_all | solution.py:582
  74.6 1.7 %collective-permute-start.14 = (f32[4,32,128]{2,1,0:T(8,128)S(1)}, f32[4,32,128]{2,1,0:T(8,128)S(1)}, u32[]{:S(2)}, u32[]{:S(2)}) collective-permute-start(f32[4,32,128]{2,1,0:T(8,128)S(1)} %sum_z.1.after.mine), channel_id=1, source_target_pairs={{0,4},{1,5},{2,6},{3,7},{4,0},{5,1},{6,2},{7,3},{8,12},{9,13},{10,... | collective-permute-start | bytes 196616 | tf_op jit(solution)/shard_map/ppermute | solution.py:583
  77.6 1.6 %collective-permute-done.14.far_two = f32[4,32,128]{2,1,0:T(8,128)S(1)} collective-permute-done((f32[4,32,128]{2,1,0:T(8,128)S(1)}, f32[4,32,128]{2,1,0:T(8,128)S(1)}, u32[]{:S(2)}, u32[]{:S(2)}) %collective-permute-start.14) | collective-permute-done | bytes 65568 | tf_op jit(solution)/shard_map/ppermute | solution.py:583
  80.5 2.4 %collective-permute-start.16 = (f32[4,32,128]{2,1,0:T(8,128)S(1)}, f32[4,32,128]{2,1,0:T(8,128)S(1)}, u32[]{:S(2)}, u32[]{:S(2)}) collective-permute-start(f32[4,32,128]{2,1,0:T(8,128)S(1)} %sum_chips.1.rest_0_), channel_id=1, source_target_pairs={{0,16},{8,24},{16,0},{24,8},{32,48},{40,56},{48,32},{56,40},{64,80... | collective-permute-start | bytes 196616 | tf_op jit(solution)/shard_map/ppermute | solution.py:592
  84.1 6.1 %collective-permute-done.15.rest_1_ = f32[4,32,128]{2,1,0:T(8,128)S(1)} collective-permute-done((f32[4,32,128]{2,1,0:T(8,128)S(1)}, f32[4,32,128]{2,1,0:T(8,128)S(1)}, u32[]{:S(2)}, u32[]{:S(2)}) %collective-permute-start.15) | collective-permute-done | bytes 65568 | tf_op jit(solution)/shard_map/ppermute | solution.py:592
  90.3 2.1 %collective-permute-done.16.rest_2_ = f32[4,32,128]{2,1,0:T(8,128)S(1)} collective-permute-done((f32[4,32,128]{2,1,0:T(8,128)S(1)}, f32[4,32,128]{2,1,0:T(8,128)S(1)}, u32[]{:S(2)}, u32[]{:S(2)}) %collective-permute-start.16) | collective-permute-done | bytes 65568 | tf_op jit(solution)/shard_map/ppermute | solution.py:592
  92.4 1.6 %place.1 = (f32[4,8,64,128]{3,2,1,0:T(8,128)S(1)}, f32[8,64,128]{2,1,0:T(8,128)S(1)}, f32[8,64,128]{2,1,0:T(8,128)S(1)}, f32[8,64,128]{2,1,0:T(8,128)S(1)}, f32[8,64,128]{2,1,0:T(8,128)S(1)}) custom-call(s32[16,16]{1,0:T(8,128)S(1)} %copy-done.8, s32[16,32]{1,0:T(8,128)S(1)} %copy-done.9, f32[32,64,128]{2,1,0:T(8,128)S(1)} %all-to-all-done.arrived, ...), custom_call_target="tpu_custom_call" | custom-call | flops 262144 | bytes 3145728 | tf_op jit(solution)/shard_map/place/pallas_call | solution.py:281
  95.1 2.3 %collective-permute-done.18.rest_3_.swapped = f32[4,8,64,128]{3,2,1,0:T(8,128)S(1)} collective-permute-done((f32[4,8,64,128]{3,2,1,0:T(8,128)S(1)}, f32[4,8,64,128]{3,2,1,0:T(8,128)S(1)}, u32[]{:S(2)}, u32[]{:S(2)}) %collective-permute-start.18) | collective-permute-done | bytes 1048608 | tf_op jit(solution)/shard_map/ppermute | solution.py:596
  98.4 2.0 %collective-permute-start.20 = (f32[2,8,64,128]{3,2,1,0:T(8,128)S(1)}, f32[2,8,64,128]{3,2,1,0:T(8,128)S(1)}, u32[]{:S(2)}, u32[]{:S(2)}) collective-permute-start(f32[2,8,64,128]{3,2,1,0:T(8,128)S(1)} %get-tuple-element.67), channel_id=1, source_target_pairs={{0,6},{1,7},{2,0},{3,1},{4,2},{5,3},{6,4},{7,5},{8,14},{9,15},{10,... | collective-permute-start | bytes 1572872 | tf_op jit(solution)/shard_map/ppermute | solution.py:599
  101.0 2.3 %collective-permute-start.23 = (f32[4,4,32,128]{3,2,1,0:T(8,128)S(1)}, f32[4,4,32,128]{3,2,1,0:T(8,128)S(1)}, u32[]{:S(2)}, u32[]{:S(2)}) collective-permute-start(f32[4,4,32,128]{3,2,1,0:T(8,128)S(1)} %pass.1.rest_0_), channel_id=1, source_target_pairs={{0,64},{8,72},{16,80},{24,88},{32,96},{40,104},{48,112},{56,120},{... | collective-permute-start | bytes 786440 | tf_op jit(solution)/shard_map/ppermute | solution.py:608
  103.3 3.6 %collective-permute-done.22.rest_1_ = f32[4,4,32,128]{3,2,1,0:T(8,128)S(1)} collective-permute-done((f32[4,4,32,128]{3,2,1,0:T(8,128)S(1)}, f32[4,4,32,128]{3,2,1,0:T(8,128)S(1)}, u32[]{:S(2)}, u32[]{:S(2)}) %collective-permute-start.22) | collective-permute-done | bytes 262176 | tf_op jit(solution)/shard_map/ppermute | solution.py:608
  106.9 4.5 %collective-permute-done.23.rest_2_ = f32[4,4,32,128]{3,2,1,0:T(8,128)S(1)} collective-permute-done((f32[4,4,32,128]{3,2,1,0:T(8,128)S(1)}, f32[4,4,32,128]{3,2,1,0:T(8,128)S(1)}, u32[]{:S(2)}, u32[]{:S(2)}) %collective-permute-start.23) | collective-permute-done | bytes 262176 | tf_op jit(solution)/shard_map/ppermute | solution.py:608
  111.4 1.9 %collective-permute-done.24.rest_3_ = f32[4,4,32,128]{3,2,1,0:T(8,128)S(1)} collective-permute-done((f32[4,4,32,128]{3,2,1,0:T(8,128)S(1)}, f32[4,4,32,128]{3,2,1,0:T(8,128)S(1)}, u32[]{:S(2)}, u32[]{:S(2)}) %collective-permute-start.24) | collective-permute-done | bytes 262176 | tf_op jit(solution)/shard_map/ppermute | solution.py:608
  113.3 9.6 %collective-permute-done.21.rest_2_.rest_6_ = f32[2,8,64,128]{3,2,1,0:T(8,128)S(1)} collective-permute-done((f32[2,8,64,128]{3,2,1,0:T(8,128)S(1)}, f32[2,8,64,128]{3,2,1,0:T(8,128)S(1)}, u32[]{:S(2)}, u32[]{:S(2)}) %collective-permute-start.21) | collective-permute-done | bytes 524320 | tf_op jit(solution)/shard_map/ppermute | solution.py:599
  123.0 1.6 %collective-permute-start.25 = (f32[16,4,32,128]{3,2,1,0:T(8,128)S(1)}, f32[16,4,32,128]{3,2,1,0:T(8,128)S(1)}, u32[]{:S(2)}, u32[]{:S(2)}) collective-permute-start(f32[16,4,32,128]{3,2,1,0:T(8,128)S(1)} %bitcast.11), channel_id=1, source_target_pairs={{0,1},{1,0},{2,3},{3,2},{4,5},{5,4},{6,7},{7,6},{8,9},{9,8},{10,11... | collective-permute-start | bytes 3145736 | tf_op jit(solution)/shard_map/ppermute | solution.py:610
  124.7 1.7 %finish.1 = f32[1024,512]{1,0:T(8,128)} custom-call(f32[1024,512]{1,0:T(8,128)S(1)} %copy-done.3, f32[8,64,128]{2,1,0:T(8,128)S(1)} %get-tuple-element.61.keep, f32[4,8,64,128]{3,2,1,0:T(8,128)S(1)} %collective-permute-done.18.rest_3_.swapped, f32[2,8,64,128]{3,2,1,0:T(8,128)S(1)} %collective-permute-done.19.rest_0_.rest_4_, ...), custom_call_target="tpu_custom_call" | custom-call | flops 1048576 | bytes 8388608 | tf_op jit(solution)/shard_map/finish/pallas_call | solution.py:492
  (67 shorter events, 20.9 us)
Async XLA Ops:
  9.5 7.9 %collective-permute-start = (f32[30,256,128]{2,1,0:T(8,128)S(1)}, f32[30,256,128]{2,1,0:T(8,128)S(1)}, u32[]{:S(2)}, u32[]{:S(2)}) collective-permute-start(f32[30,256,128]{2,1,0:T(8,128)S(1)} %get-tuple-element.40), channel_id=1, source_target_pairs={{0,1},{1,0},{2,3},{3,2},{4,5},{5,4},{6,7},{7,6},{8,9},{9,8},{10,11... | collective-permute-start | bytes 11796488 | tf_op jit(solution)/shard_map/ppermute | solution.py:539
  16.6 10.9 %collective-permute-start.1 = (f32[16,4,32,128]{3,2,1,0:T(8,128)S(1)}, f32[16,4,32,128]{3,2,1,0:T(8,128)S(1)}, u32[]{:S(2)}, u32[]{:S(2)}) collective-permute-start(f32[16,4,32,128]{3,2,1,0:T(8,128)S(1)} %get-tuple-element.43), channel_id=1, source_target_pairs={{0,1},{1,0},{2,3},{3,2},{4,5},{5,4},{6,7},{7,6},{8,9},{9,8},{10,11... | collective-permute-start | bytes 3145736 | tf_op jit(solution)/shard_map/ppermute | solution.py:556
  24.3 21.2 %copy-start.6 = (f32[512,512]{1,0:T(8,128)S(1)}, f32[512,512]{1,0:T(8,128)}, u32[]{:S(2)}) copy-start(f32[512,512]{1,0:T(8,128)} %weight.1) | copy-start | bytes 3145732
  24.3 21.2 %copy-start.7 = (f32[8,256,128]{2,1,0:T(8,128)S(1)}, f32[8,256,128]{2,1,0:T(8,128)}, u32[]{:S(2)}) copy-start(f32[8,256,128]{2,1,0:T(8,128)} %get-tuple-element.38.other_local) | copy-start | bytes 3145732
  24.3 25.2 %collective-permute-start.5 = (f32[2,15,64,128]{3,2,1,0:T(8,128)S(1)}, f32[2,15,64,128]{3,2,1,0:T(8,128)S(1)}, u32[]{:S(2)}, u32[]{:S(2)}) collective-permute-start(f32[2,15,64,128]{3,2,1,0:T(8,128)S(1)} %get-tuple-element.52), channel_id=1, source_target_pairs={{0,2},{1,3},{2,0},{3,1},{4,6},{5,7},{6,4},{7,5},{8,10},{9,11},{10,... | collective-permute-start | bytes 2949128 | tf_op jit(solution)/shard_map/ppermute | solution.py:543
  25.7 24.2 %collective-permute-start.6 = (f32[2,15,64,128]{3,2,1,0:T(8,128)S(1)}, f32[2,15,64,128]{3,2,1,0:T(8,128)S(1)}, u32[]{:S(2)}, u32[]{:S(2)}) collective-permute-start(f32[2,15,64,128]{3,2,1,0:T(8,128)S(1)} %get-tuple-element.54), channel_id=1, source_target_pairs={{0,6},{1,7},{2,4},{3,5},{4,2},{5,3},{6,0},{7,1},{8,14},{9,15},{10,... | collective-permute-start | bytes 2949128 | tf_op jit(solution)/shard_map/ppermute | solution.py:544
  28.3 8.7 %collective-permute-start.2 = (f32[4,4,32,128]{3,2,1,0:T(8,128)S(1)}, f32[4,4,32,128]{3,2,1,0:T(8,128)S(1)}, u32[]{:S(2)}, u32[]{:S(2)}) collective-permute-start(f32[4,4,32,128]{3,2,1,0:T(8,128)S(1)} %get-tuple-element.46), channel_id=1, source_target_pairs={{0,32},{8,40},{16,48},{24,56},{32,64},{40,72},{48,80},{56,88},{64,... | collective-permute-start | bytes 786440 | tf_op jit(solution)/shard_map/ppermute | solution.py:559
  29.6 14.0 %collective-permute-start.3 = (f32[4,4,32,128]{3,2,1,0:T(8,128)S(1)}, f32[4,4,32,128]{3,2,1,0:T(8,128)S(1)}, u32[]{:S(2)}, u32[]{:S(2)}) collective-permute-start(f32[4,4,32,128]{3,2,1,0:T(8,128)S(1)} %get-tuple-element.47), channel_id=1, source_target_pairs={{0,64},{8,72},{16,80},{24,88},{32,96},{40,104},{48,112},{56,120},{... | collective-permute-start | bytes 786440 | tf_op jit(solution)/shard_map/ppermute | solution.py:559
  32.3 11.4 %collective-permute-start.4 = (f32[4,4,32,128]{3,2,1,0:T(8,128)S(1)}, f32[4,4,32,128]{3,2,1,0:T(8,128)S(1)}, u32[]{:S(2)}, u32[]{:S(2)}) collective-permute-start(f32[4,4,32,128]{3,2,1,0:T(8,128)S(1)} %get-tuple-element.48), channel_id=1, source_target_pairs={{0,96},{8,104},{16,112},{24,120},{32,0},{40,8},{48,16},{56,24},{64... | collective-permute-start | bytes 786440 | tf_op jit(solution)/shard_map/ppermute | solution.py:559
  43.7 5.8 %collective-permute-start.7 = (f32[4,32,128]{2,1,0:T(8,128)S(1)}, f32[4,32,128]{2,1,0:T(8,128)S(1)}, u32[]{:S(2)}, u32[]{:S(2)}) collective-permute-start(f32[4,32,128]{2,1,0:T(8,128)S(1)} %get-tuple-element.55), channel_id=1, source_target_pairs={{0,8},{8,16},{16,24},{24,0},{32,40},{40,48},{48,56},{56,32},{64,72... | collective-permute-start | bytes 196616 | tf_op jit(solution)/shard_map/ppermute | solution.py:563
  49.9 13.4 %copy-start.10 = (s32[32]{0:T(128)S(1)}, s32[32]{0:T(128)}, u32[]{:S(2)}) copy-start(s32[32]{0:T(128)} %get-tuple-element.50.places) | copy-start | bytes 388
  50.1 12.4 %collective-permute-start.8 = (f32[15,64,128]{2,1,0:T(8,128)S(1)}, f32[15,64,128]{2,1,0:T(8,128)S(1)}, u32[]{:S(2)}, u32[]{:S(2)}) collective-permute-start(f32[15,64,128]{2,1,0:T(8,128)S(1)} %get-tuple-element.57), channel_id=1, source_target_pairs={{0,6},{1,7},{2,4},{3,5},{4,2},{5,3},{6,0},{7,1},{8,14},{9,15},{10,... | collective-permute-start | bytes 1474568 | tf_op jit(solution)/shard_map/ppermute | solution.py:577
  52.0 11.3 %collective-permute-start.9 = (f32[15,64,128]{2,1,0:T(8,128)S(1)}, f32[15,64,128]{2,1,0:T(8,128)S(1)}, u32[]{:S(2)}, u32[]{:S(2)}) collective-permute-start(f32[15,64,128]{2,1,0:T(8,128)S(1)} %get-tuple-element.58), channel_id=1, source_target_pairs={{0,2},{1,3},{2,0},{3,1},{4,6},{5,7},{6,4},{7,5},{8,10},{9,11},{10,... | collective-permute-start | bytes 1474568 | tf_op jit(solution)/shard_map/ppermute | solution.py:578
  52.0 5.3 %collective-permute-start.10 = (f32[4,32,128]{2,1,0:T(8,128)S(1)}, f32[4,32,128]{2,1,0:T(8,128)S(1)}, u32[]{:S(2)}, u32[]{:S(2)}) collective-permute-start(f32[4,32,128]{2,1,0:T(8,128)S(1)} %get-tuple-element.59), channel_id=1, source_target_pairs={{0,16},{8,24},{16,0},{24,8},{32,48},{40,56},{48,32},{56,40},{64,80... | collective-permute-start | bytes 196616 | tf_op jit(solution)/shard_map/ppermute | solution.py:563
  55.6 3.4 %collective-permute-start.11 = (f32[4,32,128]{2,1,0:T(8,128)S(1)}, f32[4,32,128]{2,1,0:T(8,128)S(1)}, u32[]{:S(2)}, u32[]{:S(2)}) collective-permute-start(f32[4,32,128]{2,1,0:T(8,128)S(1)} %get-tuple-element.60), channel_id=1, source_target_pairs={{0,24},{8,0},{16,8},{24,16},{32,56},{40,32},{48,40},{56,48},{64,88... | collective-permute-start | bytes 196616 | tf_op jit(solution)/shard_map/ppermute | solution.py:563
  65.0 27.5 %copy-start.9 = (s32[16,32]{1,0:T(8,128)S(1)}, s32[16,32]{1,0:T(8,128)}, u32[]{:S(2)}) copy-start(s32[16,32]{1,0:T(8,128)} %target_ref.1) | copy-start | bytes 6148
  65.0 27.4 %all-to-all-start = ((f32[32,64,128]{2,1,0:T(8,128)}), f32[32,64,128]{2,1,0:T(8,128)S(1)}, u32[]{:S(2)}, u32[]{:S(2)}) async-start(f32[32,64,128]{2,1,0:T(8,128)} %third_sums.1.after), calls=%async_computation | async-start | bytes 2097152 | tf_op jit(solution)/shard_map/all_to_all | solution.py:582
  72.9 3.3 %collective-permute-start.12 = (f32[4,32,128]{2,1,0:T(8,128)S(1)}, f32[4,32,128]{2,1,0:T(8,128)S(1)}, u32[]{:S(2)}, u32[]{:S(2)}) collective-permute-start(f32[4,32,128]{2,1,0:T(8,128)S(1)} %sum_z.1.after.mine), channel_id=1, source_target_pairs={{0,2},{1,3},{2,0},{3,1},{4,6},{5,7},{6,4},{7,5},{8,10},{9,11},{10,... | collective-permute-start | bytes 196616 | tf_op jit(solution)/shard_map/ppermute | solution.py:583
  73.3 4.3 %collective-permute-start.13 = (f32[4,32,128]{2,1,0:T(8,128)S(1)}, f32[4,32,128]{2,1,0:T(8,128)S(1)}, u32[]{:S(2)}, u32[]{:S(2)}) collective-permute-start(f32[4,32,128]{2,1,0:T(8,128)S(1)} %sum_z.1.after.mine), channel_id=1, source_target_pairs={{0,6},{1,7},{2,4},{3,5},{4,2},{5,3},{6,0},{7,1},{8,14},{9,15},{10,... | collective-permute-start | bytes 196616 | tf_op jit(solution)/shard_map/ppermute | solution.py:583
  74.6 4.6 %collective-permute-start.14 = (f32[4,32,128]{2,1,0:T(8,128)S(1)}, f32[4,32,128]{2,1,0:T(8,128)S(1)}, u32[]{:S(2)}, u32[]{:S(2)}) collective-permute-start(f32[4,32,128]{2,1,0:T(8,128)S(1)} %sum_z.1.after.mine), channel_id=1, source_target_pairs={{0,4},{1,5},{2,6},{3,7},{4,0},{5,1},{6,2},{7,3},{8,12},{9,13},{10,... | collective-permute-start | bytes 196616 | tf_op jit(solution)/shard_map/ppermute | solution.py:583
  79.2 11.1 %collective-permute-start.15 = (f32[4,32,128]{2,1,0:T(8,128)S(1)}, f32[4,32,128]{2,1,0:T(8,128)S(1)}, u32[]{:S(2)}, u32[]{:S(2)}) collective-permute-start(f32[4,32,128]{2,1,0:T(8,128)S(1)} %sum_chips.1.rest_0_), channel_id=1, source_target_pairs={{0,8},{8,16},{16,24},{24,0},{32,40},{40,48},{48,56},{56,32},{64,72... | collective-permute-start | bytes 196616 | tf_op jit(solution)/shard_map/ppermute | solution.py:592
  80.5 11.8 %collective-permute-start.16 = (f32[4,32,128]{2,1,0:T(8,128)S(1)}, f32[4,32,128]{2,1,0:T(8,128)S(1)}, u32[]{:S(2)}, u32[]{:S(2)}) collective-permute-start(f32[4,32,128]{2,1,0:T(8,128)S(1)} %sum_chips.1.rest_0_), channel_id=1, source_target_pairs={{0,16},{8,24},{16,0},{24,8},{32,48},{40,56},{48,32},{56,40},{64,80... | collective-permute-start | bytes 196616 | tf_op jit(solution)/shard_map/ppermute | solution.py:592
  82.9 9.4 %collective-permute-start.17 = (f32[4,32,128]{2,1,0:T(8,128)S(1)}, f32[4,32,128]{2,1,0:T(8,128)S(1)}, u32[]{:S(2)}, u32[]{:S(2)}) collective-permute-start(f32[4,32,128]{2,1,0:T(8,128)S(1)} %sum_chips.1.rest_0_), channel_id=1, source_target_pairs={{0,24},{8,0},{16,8},{24,16},{32,56},{40,32},{48,40},{56,48},{64,88... | collective-permute-start | bytes 196616 | tf_op jit(solution)/shard_map/ppermute | solution.py:592
  94.0 3.4 %collective-permute-start.18 = (f32[4,8,64,128]{3,2,1,0:T(8,128)S(1)}, f32[4,8,64,128]{3,2,1,0:T(8,128)S(1)}, u32[]{:S(2)}, u32[]{:S(2)}) collective-permute-start(f32[4,8,64,128]{3,2,1,0:T(8,128)S(1)} %get-tuple-element.62), channel_id=1, source_target_pairs={{0,1},{1,0},{2,3},{3,2},{4,5},{5,4},{6,7},{7,6},{8,9},{9,8},{10,11... | collective-permute-start | bytes 3145736 | tf_op jit(solution)/shard_map/ppermute | solution.py:596
  97.5 27.1 %copy-start.3 = (f32[1024,512]{1,0:T(8,128)S(1)}, f32[1024,512]{1,0:T(8,128)}, u32[]{:S(2)}) copy-start(f32[1024,512]{1,0:T(8,128)} %copy-done.2) | copy-start | bytes 6291460
  97.5 9.4 %collective-permute-start.22 = (f32[4,4,32,128]{3,2,1,0:T(8,128)S(1)}, f32[4,4,32,128]{3,2,1,0:T(8,128)S(1)}, u32[]{:S(2)}, u32[]{:S(2)}) collective-permute-start(f32[4,4,32,128]{3,2,1,0:T(8,128)S(1)} %pass.1.rest_0_), channel_id=1, source_target_pairs={{0,32},{8,40},{16,48},{24,56},{32,64},{40,72},{48,80},{56,88},{64,... | collective-permute-start | bytes 786440 | tf_op jit(solution)/shard_map/ppermute | solution.py:608
  97.6 15.7 %collective-permute-start.19 = (f32[2,8,64,128]{3,2,1,0:T(8,128)S(1)}, f32[2,8,64,128]{3,2,1,0:T(8,128)S(1)}, u32[]{:S(2)}, u32[]{:S(2)}) collective-permute-start(f32[2,8,64,128]{3,2,1,0:T(8,128)S(1)} %get-tuple-element.66.rest_0_), channel_id=1, source_target_pairs={{0,2},{1,3},{2,4},{3,5},{4,6},{5,7},{6,0},{7,1},{8,10},{9,11},{10,... | collective-permute-start | bytes 1572872 | tf_op jit(solution)/shard_map/ppermute | solution.py:599
  98.4 15.0 %collective-permute-start.20 = (f32[2,8,64,128]{3,2,1,0:T(8,128)S(1)}, f32[2,8,64,128]{3,2,1,0:T(8,128)S(1)}, u32[]{:S(2)}, u32[]{:S(2)}) collective-permute-start(f32[2,8,64,128]{3,2,1,0:T(8,128)S(1)} %get-tuple-element.67), channel_id=1, source_target_pairs={{0,6},{1,7},{2,0},{3,1},{4,2},{5,3},{6,4},{7,5},{8,14},{9,15},{10,... | collective-permute-start | bytes 1572872 | tf_op jit(solution)/shard_map/ppermute | solution.py:599
  100.4 22.6 %collective-permute-start.21 = (f32[2,8,64,128]{3,2,1,0:T(8,128)S(1)}, f32[2,8,64,128]{3,2,1,0:T(8,128)S(1)}, u32[]{:S(2)}, u32[]{:S(2)}) collective-permute-start(f32[2,8,64,128]{3,2,1,0:T(8,128)S(1)} %get-tuple-element.68), channel_id=1, source_target_pairs={{0,4},{1,5},{2,6},{3,7},{4,0},{5,1},{6,2},{7,3},{8,12},{9,13},{10,... | collective-permute-start | bytes 1572872 | tf_op jit(solution)/shard_map/ppermute | solution.py:599
  101.0 10.4 %collective-permute-start.23 = (f32[4,4,32,128]{3,2,1,0:T(8,128)S(1)}, f32[4,4,32,128]{3,2,1,0:T(8,128)S(1)}, u32[]{:S(2)}, u32[]{:S(2)}) collective-permute-start(f32[4,4,32,128]{3,2,1,0:T(8,128)S(1)} %pass.1.rest_0_), channel_id=1, source_target_pairs={{0,64},{8,72},{16,80},{24,88},{32,96},{40,104},{48,112},{56,120},{... | collective-permute-start | bytes 786440 | tf_op jit(solution)/shard_map/ppermute | solution.py:608
  106.9 6.4 %collective-permute-start.24 = (f32[4,4,32,128]{3,2,1,0:T(8,128)S(1)}, f32[4,4,32,128]{3,2,1,0:T(8,128)S(1)}, u32[]{:S(2)}, u32[]{:S(2)}) collective-permute-start(f32[4,4,32,128]{3,2,1,0:T(8,128)S(1)} %pass.1.rest_0_), channel_id=1, source_target_pairs={{0,96},{8,104},{16,112},{24,120},{32,0},{40,8},{48,16},{56,24},{64... | collective-permute-start | bytes 786440 | tf_op jit(solution)/shard_map/ppermute | solution.py:608
  123.0 3.9 %collective-permute-start.25 = (f32[16,4,32,128]{3,2,1,0:T(8,128)S(1)}, f32[16,4,32,128]{3,2,1,0:T(8,128)S(1)}, u32[]{:S(2)}, u32[]{:S(2)}) collective-permute-start(f32[16,4,32,128]{3,2,1,0:T(8,128)S(1)} %bitcast.11), channel_id=1, source_target_pairs={{0,1},{1,0},{2,3},{3,2},{4,5},{5,4},{6,7},{7,6},{8,9},{9,8},{10,11... | collective-permute-start | bytes 3145736 | tf_op jit(solution)/shard_map/ppermute | solution.py:610
  (8 other events, 26.7 us)

commit v13 on v12

--- a/solution.py
+++ b/solution.py
@@ -12,7 +12,7 @@
 BLOCK = 128
 CHUNKS = 2
 MAIN = 30
-LIMIT_OTHER = 52
+LIMIT_OTHER = 51
 LIMIT_OWN = 20
 LIMIT_SMALL = 6
 AWAY = (0, 1, 3, 2)
@@ -182,7 +182,7 @@
     blocks = node_rows // BLOCK
     some = main // 2
     anywhere = pl.BlockSpec(memory_space=pl.ANY)
-    local = jax.ShapeDtypeStruct((blocks, width, BLOCK), F32)
+    local = pltpu.VMEM((blocks, width, BLOCK), F32)
     piece = jax.ShapeDtypeStruct((2, some, width // 4, BLOCK), F32)
     if own:
         args = [pre_grad, weight, tile_vals, recv]
@@ -578,9 +578,9 @@
     recv_b = lax.ppermute(send_b, "local", pairs)
     share_shape = jax.ShapeDtypeStruct(mine.shape, F32)
     share = small(sum_kernel, share_shape, terms, "sum_z")
-    shares = third_sums(places, keep, recv_a, recv_b, share)
+    terms = [share] + [lax.ppermute(share, "local", p) for p in (pairs, across, along_x[2])]
+    shares = third_sums(places, keep, recv_a, recv_b, terms[1])
     arrived = lax.all_to_all(shares, "group", split_axis=0, concat_axis=0, tiled=True)
-    terms = [share] + [lax.ppermute(share, "local", p) for p in (pairs, across, along_x[2])]
     scale = float(node_rows * groups * members) ** (-0.5)
     share = small(
         functools.partial(chips_kernel, scale),

time: 129 us -> 129 us (level)
    ppermute x3, waiting for transfers between devices: 2.95 us -> 7.54 us  [on_device(): lax.ppermute(share, 'local', p)]
    ppermute x1, waiting for transfers between devices: 3.45 us -> 0.01 us  [on_device(): recv_a = lax.ppermute(send_a, 'local', across)]
    ppermute x3, waiting for transfers between devices: 9.61 us -> 7.96 us  [on_device(): lax.ppermute(joined[k - 1], 'local', along_x[k])]
    ppermute x3, waiting for transfers between devices: 10 us -> 11.6 us  [on_device(): rows = [row] + [lax.ppermute(row, 'group', along_y[k]) for k in range(1, 4)]]
  transfers between devices with their start and end apart: 27 -> 27, of which waited for: 19 -> 18; matrix products, arithmetic and copies ran while one was open for 4% -> 4% of each run, Pallas kernels for 9% -> 9%
where the time goes in v13:
time: 129 us
  waiting for transfers between devices  54.1 us (42%)
  starting transfers between devices  43.3 us (34%)
  Pallas kernels  24.5 us (19%)
  matrix products  5.42 us (4%)
    pallas_call x2, Pallas kernels, tile_sums(): pl.pallas_call(functools.partial(tile_kernel, own, blocks, main, over), o...  14.4 us
    ppermute x3, waiting for transfers between devices, on_device(): rows = [row] + [lax.ppermute(row, 'group', along_y[k]) for k in range(1, 4)]  11.6 us
    ppermute x3, waiting for transfers between devices, on_device(): lax.ppermute(some, 'group', along_y[k + 1])  10.3 us
    pallas_call x14, Pallas kernels, small(): pl.pallas_call(kernel, out_shape=out_shape, in_specs=specs or [IN_VMEM] *...  8.43 us
    ppermute x3, waiting for transfers between devices, on_device(): lax.ppermute(share, 'group', along_z[k])  8.12 us
    ppermute x3, waiting for transfers between devices, on_device(): lax.ppermute(joined[k - 1], 'local', along_x[k])  7.96 us
    all_to_all x1, starting transfers between devices, on_device(): lax.all_to_all(shares, 'group', split_axis=0, concat_axis=0, tiled=True)  7.9 us
    ppermute x3, waiting for transfers between devices, on_device(): lax.ppermute(share, 'local', p)  7.54 us
  transfers between devices with their start and end apart: 27, of which 18 were waited for; matrix products, arithmetic and copies ran while one was open for 4% of the time, Pallas kernels for 9%

profile of v13, /device:TPU:1, one launch (start us, length us, event | category | flops | bytes accessed | tf_op | source)
XLA Modules:
  0.0 128.7 jit_solution(16760126920056075193)
XLA Ops:
  0.6 7.9 %other_tile_sums.1 = (f32[1024,512]{1,0:T(8,128)}, f32[8,256,128]{2,1,0:T(8,128)S(1)}, f32[30,256,128]{2,1,0:T(8,128)S(1)}, s32[32]{0:T(128)}, s32[64]{0:T(128)}) custom-call(s32[64]{0:T(128)} %col_ref.1, s32[16,16]{1,0:T(8,128)} %count_ref.5, f32[1024,512]{1,0:T(8,128)} %rest_0_.1, f32[1024,512]{1,0:T(8,128)} %rest_1_.2, f32[512,512]{1,0:T(8,128)} %rest_1_.3, ...), custom_call_target="tpu_custom_call" | custom-call | flops 2415919104 | bytes 14680064 | tf_op jit(solution)/shard_map/other_tile_sums/pallas_call | solution.py:209
  10.1 3.6 %convolution_bitcast_fusion.neigh_term = f32[512,512]{1,0:T(8,128)S(1)} fusion(f32[1024,512]{1,0:T(8,128)} %get-tuple-element.37.rest_0_.pre_grad, f32[1024,512]{1,0:T(8,128)S(1)} %copy-done), kind=kOutput, calls=%fused_computation | convolution fusion | flops 1610612736 | bytes 5242880 | tf_op jit(solution)/shard_map/dot_general | solution.py:550
  13.7 1.8 %convolution_bitcast_fusion.1.self_term = f32[512,512]{1,0:T(8,128)S(1)} fusion(f32[1024,512]{1,0:T(8,128)S(1)} %copy-done.1, f32[1024,512]{1,0:T(8,128)S(1)} %copy-done.11), kind=kOutput, calls=%fused_computation.1 | convolution fusion | flops 1610612736 | bytes 5242880 | tf_op jit(solution)/shard_map/dot_general | solution.py:547
  16.9 6.5 %own_tile_sums.1 = (f32[8,256,128]{2,1,0:T(8,128)S(1)}, s32[1]{0:T(128)}, f32[2,15,64,128]{3,2,1,0:T(8,128)S(1)}, f32[2,15,64,128]{3,2,1,0:T(8,128)S(1)}, f32[2,...) custom-call(s32[64]{0:T(128)S(1)} %copy-done.10, s32[16,16]{1,0:T(8,128)S(1)} %copy-done.7, ...), custom_call_target="tpu_custom_call" | custom-call | flops 2415919104 | bytes 14680064 | tf_op jit(solution)/shard_map/own_tile_sums/pallas_call | solution.py:209
  24.8 1.8 %collective-permute-start.6 = (f32[2,15,64,128]{3,2,1,0:T(8,128)S(1)}, f32[2,15,64,128]{3,2,1,0:T(8,128)S(1)}, u32[]{:S(2)}, u32[]{:S(2)}) collective-permute-start(f32[2,15,64,128]{3,2,1,0:T(8,128)S(1)} %get-tuple-element.54), channel_id=1, source_target_pairs={{0,6},{1,7},{2,4},{3,5},{4,2},{5,3},{6,0},{7,1},{8,14},{9,15},{10,... | collective-permute-start | bytes 2949128 | tf_op jit(solution)/shard_map/ppermute | solution.py:544
  28.7 2.6 %collective-permute-start.3 = (f32[4,4,32,128]{3,2,1,0:T(8,128)S(1)}, f32[4,4,32,128]{3,2,1,0:T(8,128)S(1)}, u32[]{:S(2)}, u32[]{:S(2)}) collective-permute-start(f32[4,4,32,128]{3,2,1,0:T(8,128)S(1)} %get-tuple-element.47), channel_id=1, source_target_pairs={{0,64},{8,72},{16,80},{24,88},{32,96},{40,104},{48,112},{56,120},{... | collective-permute-start | bytes 786440 | tf_op jit(solution)/shard_map/ppermute | solution.py:559
  32.4 3.6 %collective-permute-done.2.rest_1_ = f32[4,4,32,128]{3,2,1,0:T(8,128)S(1)} collective-permute-done((f32[4,4,32,128]{3,2,1,0:T(8,128)S(1)}, f32[4,4,32,128]{3,2,1,0:T(8,128)S(1)}, u32[]{:S(2)}, u32[]{:S(2)}) %collective-permute-start.2) | collective-permute-done | bytes 262176 | tf_op jit(solution)/shard_map/ppermute | solution.py:559
  36.1 6.7 %collective-permute-done.3.rest_2_ = f32[4,4,32,128]{3,2,1,0:T(8,128)S(1)} collective-permute-done((f32[4,4,32,128]{3,2,1,0:T(8,128)S(1)}, f32[4,4,32,128]{3,2,1,0:T(8,128)S(1)}, u32[]{:S(2)}, u32[]{:S(2)}) %collective-permute-start.3) | collective-permute-done | bytes 262176 | tf_op jit(solution)/shard_map/ppermute | solution.py:559
  42.8 1.7 %collective-permute-start.7 = (f32[4,32,128]{2,1,0:T(8,128)S(1)}, f32[4,32,128]{2,1,0:T(8,128)S(1)}, u32[]{:S(2)}, u32[]{:S(2)}) collective-permute-start(f32[4,32,128]{2,1,0:T(8,128)S(1)} %get-tuple-element.55), channel_id=1, source_target_pairs={{0,8},{8,16},{16,24},{24,0},{32,40},{40,48},{48,56},{56,32},{64,72... | collective-permute-start | bytes 196616 | tf_op jit(solution)/shard_map/ppermute | solution.py:563
  44.5 2.2 %self_rows.1.rest_0_.base = f32[1024,512]{1,0:T(8,128)S(1)} custom-call(f32[1024,512]{1,0:T(8,128)S(1)} %copy-done.1, f32[512,512]{1,0:T(8,128)S(1)} %copy-done.6, f32[8,256,128]{2,1,0:T(8,128)S(1)} %get-tuple-element.38.other_local, f32[8,256,128]{2,1,0:T(8,128)S(1)} %get-tuple-element.41.own_local, f32[4,32,128]{2,1,0:T(8,128)S(1)} %get-tuple-element.49.after.rest_0_), custom_call_target="tpu_custom_call" | custom-call | flops 1610612736 | bytes 6291456 | tf_op jit(solution)/shard_map/self_rows/pallas_call | solution.py:281
  46.8 1.8 %collective-permute-done.7.rest_1_ = f32[4,32,128]{2,1,0:T(8,128)S(1)} collective-permute-done((f32[4,32,128]{2,1,0:T(8,128)S(1)}, f32[4,32,128]{2,1,0:T(8,128)S(1)}, u32[]{:S(2)}, u32[]{:S(2)}) %collective-permute-start.7) | collective-permute-done | bytes 65568 | tf_op jit(solution)/shard_map/ppermute | solution.py:563
  49.2 1.9 %collective-permute-start.8 = (f32[15,64,128]{2,1,0:T(8,128)S(1)}, f32[15,64,128]{2,1,0:T(8,128)S(1)}, u32[]{:S(2)}, u32[]{:S(2)}) collective-permute-start(f32[15,64,128]{2,1,0:T(8,128)S(1)} %get-tuple-element.57), channel_id=1, source_target_pairs={{0,6},{1,7},{2,4},{3,5},{4,2},{5,3},{6,0},{7,1},{8,14},{9,15},{10,... | collective-permute-start | bytes 1474568 | tf_op jit(solution)/shard_map/ppermute | solution.py:577
  51.1 3.6 %collective-permute-start.10 = (f32[4,32,128]{2,1,0:T(8,128)S(1)}, f32[4,32,128]{2,1,0:T(8,128)S(1)}, u32[]{:S(2)}, u32[]{:S(2)}) collective-permute-start(f32[4,32,128]{2,1,0:T(8,128)S(1)} %get-tuple-element.59), channel_id=1, source_target_pairs={{0,16},{8,24},{16,0},{24,8},{32,48},{40,56},{48,32},{56,40},{64,80... | collective-permute-start | bytes 196616 | tf_op jit(solution)/shard_map/ppermute | solution.py:563
  56.4 1.8 %collective-permute-done.11.rest_3_ = f32[4,32,128]{2,1,0:T(8,128)S(1)} collective-permute-done((f32[4,32,128]{2,1,0:T(8,128)S(1)}, f32[4,32,128]{2,1,0:T(8,128)S(1)}, u32[]{:S(2)}, u32[]{:S(2)}) %collective-permute-start.11) | collective-permute-done | bytes 65568 | tf_op jit(solution)/shard_map/ppermute | solution.py:563
  58.2 1.5 %collective-permute-start.12 = (f32[4,32,128]{2,1,0:T(8,128)S(1)}, f32[4,32,128]{2,1,0:T(8,128)S(1)}, u32[]{:S(2)}, u32[]{:S(2)}) collective-permute-start(f32[4,32,128]{2,1,0:T(8,128)S(1)} %sum_z.1.mine), channel_id=1, source_target_pairs={{0,2},{1,3},{2,0},{3,1},{4,6},{5,7},{6,4},{7,5},{8,10},{9,11},{10,... | collective-permute-start | bytes 196616 | tf_op jit(solution)/shard_map/ppermute | solution.py:581
  59.7 4.1 %collective-permute-done.12.after.pair = f32[4,32,128]{2,1,0:T(8,128)S(1)} collective-permute-done((f32[4,32,128]{2,1,0:T(8,128)S(1)}, f32[4,32,128]{2,1,0:T(8,128)S(1)}, u32[]{:S(2)}, u32[]{:S(2)}) %collective-permute-start.12) | collective-permute-done | bytes 65568 | tf_op jit(solution)/shard_map/ppermute | solution.py:581
  63.8 1.7 %third_sums.1.after = f32[32,64,128]{2,1,0:T(8,128)} custom-call(s32[32]{0:T(128)S(1)} %copy-done.9, f32[2,15,64,128]{3,2,1,0:T(8,128)S(1)} %get-tuple-element.56.keep, f32[15,64,128]{2,1,0:T(8,128)S(1)} %collective-permute-done.8.recv_a, f32[15,64,128]{2,1,0:T(8,128)S(1)} %collective-permute-done.9.recv_b, f32[4,32,128]{2,1,0:T(8,128)S(1)} %collective-permute-done.12.after.pair), custom_call_target="tpu_custom_call" | custom-call | flops 245760 | bytes 2949120 | tf_op jit(solution)/shard_map/third_sums/pallas_call | solution.py:281
  65.5 7.9 %all-to-all-start = ((f32[32,64,128]{2,1,0:T(8,128)}), f32[32,64,128]{2,1,0:T(8,128)S(1)}, u32[]{:S(2)}, u32[]{:S(2)}) async-start(f32[32,64,128]{2,1,0:T(8,128)} %third_sums.1.after), calls=%async_computation | async-start | bytes 2097152 | tf_op jit(solution)/shard_map/all_to_all | solution.py:583
  75.6 2.3 %collective-permute-done.13.far_one = f32[4,32,128]{2,1,0:T(8,128)S(1)} collective-permute-done((f32[4,32,128]{2,1,0:T(8,128)S(1)}, f32[4,32,128]{2,1,0:T(8,128)S(1)}, u32[]{:S(2)}, u32[]{:S(2)}) %collective-permute-start.13) | collective-permute-done | bytes 65568 | tf_op jit(solution)/shard_map/ppermute | solution.py:581
  80.4 2.4 %collective-permute-start.16 = (f32[4,32,128]{2,1,0:T(8,128)S(1)}, f32[4,32,128]{2,1,0:T(8,128)S(1)}, u32[]{:S(2)}, u32[]{:S(2)}) collective-permute-start(f32[4,32,128]{2,1,0:T(8,128)S(1)} %sum_chips.1.rest_0_), channel_id=1, source_target_pairs={{0,16},{8,24},{16,0},{24,8},{32,48},{40,56},{48,32},{56,40},{64,80... | collective-permute-start | bytes 196616 | tf_op jit(solution)/shard_map/ppermute | solution.py:592
  84.0 6.6 %collective-permute-done.15.rest_1_ = f32[4,32,128]{2,1,0:T(8,128)S(1)} collective-permute-done((f32[4,32,128]{2,1,0:T(8,128)S(1)}, f32[4,32,128]{2,1,0:T(8,128)S(1)}, u32[]{:S(2)}, u32[]{:S(2)}) %collective-permute-start.15) | collective-permute-done | bytes 65568 | tf_op jit(solution)/shard_map/ppermute | solution.py:592
  92.1 1.6 %place.1 = (f32[4,8,64,128]{3,2,1,0:T(8,128)S(1)}, f32[8,64,128]{2,1,0:T(8,128)S(1)}, f32[8,64,128]{2,1,0:T(8,128)S(1)}, f32[8,64,128]{2,1,0:T(8,128)S(1)}, f32[8,64,128]{2,1,0:T(8,128)S(1)}) custom-call(s32[16,16]{1,0:T(8,128)S(1)} %copy-done.7, s32[16,32]{1,0:T(8,128)S(1)} %copy-done.8, f32[32,64,128]{2,1,0:T(8,128)S(1)} %all-to-all-done.arrived, ...), custom_call_target="tpu_custom_call" | custom-call | flops 262144 | bytes 3145728 | tf_op jit(solution)/shard_map/place/pallas_call | solution.py:281
  93.8 1.6 %collective-permute-start.18 = (f32[4,8,64,128]{3,2,1,0:T(8,128)S(1)}, f32[4,8,64,128]{3,2,1,0:T(8,128)S(1)}, u32[]{:S(2)}, u32[]{:S(2)}) collective-permute-start(f32[4,8,64,128]{3,2,1,0:T(8,128)S(1)} %get-tuple-element.62), channel_id=1, source_target_pairs={{0,1},{1,0},{2,3},{3,2},{4,5},{5,4},{6,7},{7,6},{8,9},{9,8},{10,11... | collective-permute-start | bytes 3145736 | tf_op jit(solution)/shard_map/ppermute | solution.py:596
  95.4 2.3 %collective-permute-done.18.rest_3_.swapped = f32[4,8,64,128]{3,2,1,0:T(8,128)S(1)} collective-permute-done((f32[4,8,64,128]{3,2,1,0:T(8,128)S(1)}, f32[4,8,64,128]{3,2,1,0:T(8,128)S(1)}, u32[]{:S(2)}, u32[]{:S(2)}) %collective-permute-start.18) | collective-permute-done | bytes 1048608 | tf_op jit(solution)/shard_map/ppermute | solution.py:596
  98.3 2.3 %collective-permute-start.20 = (f32[2,8,64,128]{3,2,1,0:T(8,128)S(1)}, f32[2,8,64,128]{3,2,1,0:T(8,128)S(1)}, u32[]{:S(2)}, u32[]{:S(2)}) collective-permute-start(f32[2,8,64,128]{3,2,1,0:T(8,128)S(1)} %get-tuple-element.67), channel_id=1, source_target_pairs={{0,6},{1,7},{2,0},{3,1},{4,2},{5,3},{6,4},{7,5},{8,14},{9,15},{10,... | collective-permute-start | bytes 1572872 | tf_op jit(solution)/shard_map/ppermute | solution.py:599
  100.7 2.6 %collective-permute-start.23 = (f32[4,4,32,128]{3,2,1,0:T(8,128)S(1)}, f32[4,4,32,128]{3,2,1,0:T(8,128)S(1)}, u32[]{:S(2)}, u32[]{:S(2)}) collective-permute-start(f32[4,4,32,128]{3,2,1,0:T(8,128)S(1)} %pass.1.rest_0_), channel_id=1, source_target_pairs={{0,64},{8,72},{16,80},{24,88},{32,96},{40,104},{48,112},{56,120},{... | collective-permute-start | bytes 786440 | tf_op jit(solution)/shard_map/ppermute | solution.py:608
  103.2 3.4 %collective-permute-done.22.rest_1_ = f32[4,4,32,128]{3,2,1,0:T(8,128)S(1)} collective-permute-done((f32[4,4,32,128]{3,2,1,0:T(8,128)S(1)}, f32[4,4,32,128]{3,2,1,0:T(8,128)S(1)}, u32[]{:S(2)}, u32[]{:S(2)}) %collective-permute-start.22) | collective-permute-done | bytes 262176 | tf_op jit(solution)/shard_map/ppermute | solution.py:608
  106.9 5.3 %collective-permute-done.23.rest_2_ = f32[4,4,32,128]{3,2,1,0:T(8,128)S(1)} collective-permute-done((f32[4,4,32,128]{3,2,1,0:T(8,128)S(1)}, f32[4,4,32,128]{3,2,1,0:T(8,128)S(1)}, u32[]{:S(2)}, u32[]{:S(2)}) %collective-permute-start.23) | collective-permute-done | bytes 262176 | tf_op jit(solution)/shard_map/ppermute | solution.py:608
  112.2 2.8 %collective-permute-done.24.rest_3_ = f32[4,4,32,128]{3,2,1,0:T(8,128)S(1)} collective-permute-done((f32[4,4,32,128]{3,2,1,0:T(8,128)S(1)}, f32[4,4,32,128]{3,2,1,0:T(8,128)S(1)}, u32[]{:S(2)}, u32[]{:S(2)}) %collective-permute-start.24) | collective-permute-done | bytes 262176 | tf_op jit(solution)/shard_map/ppermute | solution.py:608
  115.1 8.0 %collective-permute-done.21.rest_2_.rest_6_ = f32[2,8,64,128]{3,2,1,0:T(8,128)S(1)} collective-permute-done((f32[2,8,64,128]{3,2,1,0:T(8,128)S(1)}, f32[2,8,64,128]{3,2,1,0:T(8,128)S(1)}, u32[]{:S(2)}, u32[]{:S(2)}) %collective-permute-start.21) | collective-permute-done | bytes 524320 | tf_op jit(solution)/shard_map/ppermute | solution.py:599
  123.1 1.9 %collective-permute-start.25 = (f32[16,4,32,128]{3,2,1,0:T(8,128)S(1)}, f32[16,4,32,128]{3,2,1,0:T(8,128)S(1)}, u32[]{:S(2)}, u32[]{:S(2)}) collective-permute-start(f32[16,4,32,128]{3,2,1,0:T(8,128)S(1)} %bitcast.11), channel_id=1, source_target_pairs={{0,1},{1,0},{2,3},{3,2},{4,5},{5,4},{6,7},{7,6},{8,9},{9,8},{10,11... | collective-permute-start | bytes 3145736 | tf_op jit(solution)/shard_map/ppermute | solution.py:610
  125.0 1.7 %finish.1 = f32[1024,512]{1,0:T(8,128)} custom-call(f32[1024,512]{1,0:T(8,128)S(1)} %copy-done.3, f32[8,64,128]{2,1,0:T(8,128)S(1)} %get-tuple-element.61.keep, f32[4,8,64,128]{3,2,1,0:T(8,128)S(1)} %collective-permute-done.18.rest_3_.swapped, f32[2,8,64,128]{3,2,1,0:T(8,128)S(1)} %collective-permute-done.19.rest_0_.rest_4_, ...), custom_call_target="tpu_custom_call" | custom-call | flops 1048576 | bytes 8388608 | tf_op jit(solution)/shard_map/finish/pallas_call | solution.py:492
  (65 shorter events, 20.2 us)
Async XLA Ops:
  0.6 9.4 %copy-start = (f32[1024,512]{1,0:T(8,128)S(1)}, f32[1024,512]{1,0:T(8,128)}, u32[]{:S(2)}) copy-start(f32[1024,512]{1,0:T(8,128)} %param.11) | copy-start | bytes 6291460
  8.6 7.9 %collective-permute-start = (f32[30,256,128]{2,1,0:T(8,128)S(1)}, f32[30,256,128]{2,1,0:T(8,128)S(1)}, u32[]{:S(2)}, u32[]{:S(2)}) collective-permute-start(f32[30,256,128]{2,1,0:T(8,128)S(1)} %get-tuple-element.40), channel_id=1, source_target_pairs={{0,1},{1,0},{2,3},{3,2},{4,5},{5,4},{6,7},{7,6},{8,9},{9,8},{10,11... | collective-permute-start | bytes 11796488 | tf_op jit(solution)/shard_map/ppermute | solution.py:539
  15.7 10.8 %collective-permute-start.1 = (f32[16,4,32,128]{3,2,1,0:T(8,128)S(1)}, f32[16,4,32,128]{3,2,1,0:T(8,128)S(1)}, u32[]{:S(2)}, u32[]{:S(2)}) collective-permute-start(f32[16,4,32,128]{3,2,1,0:T(8,128)S(1)} %get-tuple-element.43), channel_id=1, source_target_pairs={{0,1},{1,0},{2,3},{3,2},{4,5},{5,4},{6,7},{7,6},{8,9},{9,8},{10,11... | collective-permute-start | bytes 3145736 | tf_op jit(solution)/shard_map/ppermute | solution.py:556
  23.4 21.1 %copy-start.6 = (f32[512,512]{1,0:T(8,128)S(1)}, f32[512,512]{1,0:T(8,128)}, u32[]{:S(2)}) copy-start(f32[512,512]{1,0:T(8,128)} %weight.1) | copy-start | bytes 3145732
  23.4 25.2 %collective-permute-start.5 = (f32[2,15,64,128]{3,2,1,0:T(8,128)S(1)}, f32[2,15,64,128]{3,2,1,0:T(8,128)S(1)}, u32[]{:S(2)}, u32[]{:S(2)}) collective-permute-start(f32[2,15,64,128]{3,2,1,0:T(8,128)S(1)} %get-tuple-element.52), channel_id=1, source_target_pairs={{0,2},{1,3},{2,0},{3,1},{4,6},{5,7},{6,4},{7,5},{8,10},{9,11},{10,... | collective-permute-start | bytes 2949128 | tf_op jit(solution)/shard_map/ppermute | solution.py:543
  24.8 24.2 %collective-permute-start.6 = (f32[2,15,64,128]{3,2,1,0:T(8,128)S(1)}, f32[2,15,64,128]{3,2,1,0:T(8,128)S(1)}, u32[]{:S(2)}, u32[]{:S(2)}) collective-permute-start(f32[2,15,64,128]{3,2,1,0:T(8,128)S(1)} %get-tuple-element.54), channel_id=1, source_target_pairs={{0,6},{1,7},{2,4},{3,5},{4,2},{5,3},{6,0},{7,1},{8,14},{9,15},{10,... | collective-permute-start | bytes 2949128 | tf_op jit(solution)/shard_map/ppermute | solution.py:544
  27.4 8.7 %collective-permute-start.2 = (f32[4,4,32,128]{3,2,1,0:T(8,128)S(1)}, f32[4,4,32,128]{3,2,1,0:T(8,128)S(1)}, u32[]{:S(2)}, u32[]{:S(2)}) collective-permute-start(f32[4,4,32,128]{3,2,1,0:T(8,128)S(1)} %get-tuple-element.46), channel_id=1, source_target_pairs={{0,32},{8,40},{16,48},{24,56},{32,64},{40,72},{48,80},{56,88},{64,... | collective-permute-start | bytes 786440 | tf_op jit(solution)/shard_map/ppermute | solution.py:559
  28.7 14.0 %collective-permute-start.3 = (f32[4,4,32,128]{3,2,1,0:T(8,128)S(1)}, f32[4,4,32,128]{3,2,1,0:T(8,128)S(1)}, u32[]{:S(2)}, u32[]{:S(2)}) collective-permute-start(f32[4,4,32,128]{3,2,1,0:T(8,128)S(1)} %get-tuple-element.47), channel_id=1, source_target_pairs={{0,64},{8,72},{16,80},{24,88},{32,96},{40,104},{48,112},{56,120},{... | collective-permute-start | bytes 786440 | tf_op jit(solution)/shard_map/ppermute | solution.py:559
  31.4 11.4 %collective-permute-start.4 = (f32[4,4,32,128]{3,2,1,0:T(8,128)S(1)}, f32[4,4,32,128]{3,2,1,0:T(8,128)S(1)}, u32[]{:S(2)}, u32[]{:S(2)}) collective-permute-start(f32[4,4,32,128]{3,2,1,0:T(8,128)S(1)} %get-tuple-element.48), channel_id=1, source_target_pairs={{0,96},{8,104},{16,112},{24,120},{32,0},{40,8},{48,16},{56,24},{64... | collective-permute-start | bytes 786440 | tf_op jit(solution)/shard_map/ppermute | solution.py:559
  42.8 5.8 %collective-permute-start.7 = (f32[4,32,128]{2,1,0:T(8,128)S(1)}, f32[4,32,128]{2,1,0:T(8,128)S(1)}, u32[]{:S(2)}, u32[]{:S(2)}) collective-permute-start(f32[4,32,128]{2,1,0:T(8,128)S(1)} %get-tuple-element.55), channel_id=1, source_target_pairs={{0,8},{8,16},{16,24},{24,0},{32,40},{40,48},{48,56},{56,32},{64,72... | collective-permute-start | bytes 196616 | tf_op jit(solution)/shard_map/ppermute | solution.py:563
  49.0 14.8 %copy-start.9 = (s32[32]{0:T(128)S(1)}, s32[32]{0:T(128)}, u32[]{:S(2)}) copy-start(s32[32]{0:T(128)} %get-tuple-element.50.places) | copy-start | bytes 388
  49.2 14.6 %collective-permute-start.8 = (f32[15,64,128]{2,1,0:T(8,128)S(1)}, f32[15,64,128]{2,1,0:T(8,128)S(1)}, u32[]{:S(2)}, u32[]{:S(2)}) collective-permute-start(f32[15,64,128]{2,1,0:T(8,128)S(1)} %get-tuple-element.57), channel_id=1, source_target_pairs={{0,6},{1,7},{2,4},{3,5},{4,2},{5,3},{6,0},{7,1},{8,14},{9,15},{10,... | collective-permute-start | bytes 1474568 | tf_op jit(solution)/shard_map/ppermute | solution.py:577
  51.1 12.7 %collective-permute-start.9 = (f32[15,64,128]{2,1,0:T(8,128)S(1)}, f32[15,64,128]{2,1,0:T(8,128)S(1)}, u32[]{:S(2)}, u32[]{:S(2)}) collective-permute-start(f32[15,64,128]{2,1,0:T(8,128)S(1)} %get-tuple-element.58), channel_id=1, source_target_pairs={{0,2},{1,3},{2,0},{3,1},{4,6},{5,7},{6,4},{7,5},{8,10},{9,11},{10,... | collective-permute-start | bytes 1474568 | tf_op jit(solution)/shard_map/ppermute | solution.py:578
  51.1 5.3 %collective-permute-start.10 = (f32[4,32,128]{2,1,0:T(8,128)S(1)}, f32[4,32,128]{2,1,0:T(8,128)S(1)}, u32[]{:S(2)}, u32[]{:S(2)}) collective-permute-start(f32[4,32,128]{2,1,0:T(8,128)S(1)} %get-tuple-element.59), channel_id=1, source_target_pairs={{0,16},{8,24},{16,0},{24,8},{32,48},{40,56},{48,32},{56,40},{64,80... | collective-permute-start | bytes 196616 | tf_op jit(solution)/shard_map/ppermute | solution.py:563
  54.7 3.4 %collective-permute-start.11 = (f32[4,32,128]{2,1,0:T(8,128)S(1)}, f32[4,32,128]{2,1,0:T(8,128)S(1)}, u32[]{:S(2)}, u32[]{:S(2)}) collective-permute-start(f32[4,32,128]{2,1,0:T(8,128)S(1)} %get-tuple-element.60), channel_id=1, source_target_pairs={{0,24},{8,0},{16,8},{24,16},{32,56},{40,32},{48,40},{56,48},{64,88... | collective-permute-start | bytes 196616 | tf_op jit(solution)/shard_map/ppermute | solution.py:563
  58.2 5.7 %collective-permute-start.12 = (f32[4,32,128]{2,1,0:T(8,128)S(1)}, f32[4,32,128]{2,1,0:T(8,128)S(1)}, u32[]{:S(2)}, u32[]{:S(2)}) collective-permute-start(f32[4,32,128]{2,1,0:T(8,128)S(1)} %sum_z.1.mine), channel_id=1, source_target_pairs={{0,2},{1,3},{2,0},{3,1},{4,6},{5,7},{6,4},{7,5},{8,10},{9,11},{10,... | collective-permute-start | bytes 196616 | tf_op jit(solution)/shard_map/ppermute | solution.py:581
  65.5 26.6 %copy-start.8 = (s32[16,32]{1,0:T(8,128)S(1)}, s32[16,32]{1,0:T(8,128)}, u32[]{:S(2)}) copy-start(s32[16,32]{1,0:T(8,128)} %target_ref.1) | copy-start | bytes 6148
  65.5 26.6 %all-to-all-start = ((f32[32,64,128]{2,1,0:T(8,128)}), f32[32,64,128]{2,1,0:T(8,128)S(1)}, u32[]{:S(2)}, u32[]{:S(2)}) async-start(f32[32,64,128]{2,1,0:T(8,128)} %third_sums.1.after), calls=%async_computation | async-start | bytes 2097152 | tf_op jit(solution)/shard_map/all_to_all | solution.py:583
  73.4 4.4 %collective-permute-start.13 = (f32[4,32,128]{2,1,0:T(8,128)S(1)}, f32[4,32,128]{2,1,0:T(8,128)S(1)}, u32[]{:S(2)}, u32[]{:S(2)}) collective-permute-start(f32[4,32,128]{2,1,0:T(8,128)S(1)} %sum_z.1.mine), channel_id=1, source_target_pairs={{0,6},{1,7},{2,4},{3,5},{4,2},{5,3},{6,0},{7,1},{8,14},{9,15},{10,... | collective-permute-start | bytes 196616 | tf_op jit(solution)/shard_map/ppermute | solution.py:581
  74.4 4.6 %collective-permute-start.14 = (f32[4,32,128]{2,1,0:T(8,128)S(1)}, f32[4,32,128]{2,1,0:T(8,128)S(1)}, u32[]{:S(2)}, u32[]{:S(2)}) collective-permute-start(f32[4,32,128]{2,1,0:T(8,128)S(1)} %sum_z.1.mine), channel_id=1, source_target_pairs={{0,4},{1,5},{2,6},{3,7},{4,0},{5,1},{6,2},{7,3},{8,12},{9,13},{10,... | collective-permute-start | bytes 196616 | tf_op jit(solution)/shard_map/ppermute | solution.py:581
  79.0 11.5 %collective-permute-start.15 = (f32[4,32,128]{2,1,0:T(8,128)S(1)}, f32[4,32,128]{2,1,0:T(8,128)S(1)}, u32[]{:S(2)}, u32[]{:S(2)}) collective-permute-start(f32[4,32,128]{2,1,0:T(8,128)S(1)} %sum_chips.1.rest_0_), channel_id=1, source_target_pairs={{0,8},{8,16},{16,24},{24,0},{32,40},{40,48},{48,56},{56,32},{64,72... | collective-permute-start | bytes 196616 | tf_op jit(solution)/shard_map/ppermute | solution.py:592
  80.4 11.7 %collective-permute-start.16 = (f32[4,32,128]{2,1,0:T(8,128)S(1)}, f32[4,32,128]{2,1,0:T(8,128)S(1)}, u32[]{:S(2)}, u32[]{:S(2)}) collective-permute-start(f32[4,32,128]{2,1,0:T(8,128)S(1)} %sum_chips.1.rest_0_), channel_id=1, source_target_pairs={{0,16},{8,24},{16,0},{24,8},{32,48},{40,56},{48,32},{56,40},{64,80... | collective-permute-start | bytes 196616 | tf_op jit(solution)/shard_map/ppermute | solution.py:592
  82.8 9.3 %collective-permute-start.17 = (f32[4,32,128]{2,1,0:T(8,128)S(1)}, f32[4,32,128]{2,1,0:T(8,128)S(1)}, u32[]{:S(2)}, u32[]{:S(2)}) collective-permute-start(f32[4,32,128]{2,1,0:T(8,128)S(1)} %sum_chips.1.rest_0_), channel_id=1, source_target_pairs={{0,24},{8,0},{16,8},{24,16},{32,56},{40,32},{48,40},{56,48},{64,88... | collective-permute-start | bytes 196616 | tf_op jit(solution)/shard_map/ppermute | solution.py:592
  93.8 3.9 %collective-permute-start.18 = (f32[4,8,64,128]{3,2,1,0:T(8,128)S(1)}, f32[4,8,64,128]{3,2,1,0:T(8,128)S(1)}, u32[]{:S(2)}, u32[]{:S(2)}) collective-permute-start(f32[4,8,64,128]{3,2,1,0:T(8,128)S(1)} %get-tuple-element.62), channel_id=1, source_target_pairs={{0,1},{1,0},{2,3},{3,2},{4,5},{5,4},{6,7},{7,6},{8,9},{9,8},{10,11... | collective-permute-start | bytes 3145736 | tf_op jit(solution)/shard_map/ppermute | solution.py:596
  97.8 27.1 %copy-start.3 = (f32[1024,512]{1,0:T(8,128)S(1)}, f32[1024,512]{1,0:T(8,128)}, u32[]{:S(2)}) copy-start(f32[1024,512]{1,0:T(8,128)} %copy-done.2) | copy-start | bytes 6291460
  97.8 8.8 %collective-permute-start.22 = (f32[4,4,32,128]{3,2,1,0:T(8,128)S(1)}, f32[4,4,32,128]{3,2,1,0:T(8,128)S(1)}, u32[]{:S(2)}, u32[]{:S(2)}) collective-permute-start(f32[4,4,32,128]{3,2,1,0:T(8,128)S(1)} %pass.1.rest_0_), channel_id=1, source_target_pairs={{0,32},{8,40},{16,48},{24,56},{32,64},{40,72},{48,80},{56,88},{64,... | collective-permute-start | bytes 786440 | tf_op jit(solution)/shard_map/ppermute | solution.py:608
  97.9 17.1 %collective-permute-start.19 = (f32[2,8,64,128]{3,2,1,0:T(8,128)S(1)}, f32[2,8,64,128]{3,2,1,0:T(8,128)S(1)}, u32[]{:S(2)}, u32[]{:S(2)}) collective-permute-start(f32[2,8,64,128]{3,2,1,0:T(8,128)S(1)} %get-tuple-element.66.rest_0_), channel_id=1, source_target_pairs={{0,2},{1,3},{2,4},{3,5},{4,6},{5,7},{6,0},{7,1},{8,10},{9,11},{10,... | collective-permute-start | bytes 1572872 | tf_op jit(solution)/shard_map/ppermute | solution.py:599
  98.3 16.7 %collective-permute-start.20 = (f32[2,8,64,128]{3,2,1,0:T(8,128)S(1)}, f32[2,8,64,128]{3,2,1,0:T(8,128)S(1)}, u32[]{:S(2)}, u32[]{:S(2)}) collective-permute-start(f32[2,8,64,128]{3,2,1,0:T(8,128)S(1)} %get-tuple-element.67), channel_id=1, source_target_pairs={{0,6},{1,7},{2,0},{3,1},{4,2},{5,3},{6,4},{7,5},{8,14},{9,15},{10,... | collective-permute-start | bytes 1572872 | tf_op jit(solution)/shard_map/ppermute | solution.py:599
  100.7 22.3 %collective-permute-start.21 = (f32[2,8,64,128]{3,2,1,0:T(8,128)S(1)}, f32[2,8,64,128]{3,2,1,0:T(8,128)S(1)}, u32[]{:S(2)}, u32[]{:S(2)}) collective-permute-start(f32[2,8,64,128]{3,2,1,0:T(8,128)S(1)} %get-tuple-element.68), channel_id=1, source_target_pairs={{0,4},{1,5},{2,6},{3,7},{4,0},{5,1},{6,2},{7,3},{8,12},{9,13},{10,... | collective-permute-start | bytes 1572872 | tf_op jit(solution)/shard_map/ppermute | solution.py:599
  100.7 11.6 %collective-permute-start.23 = (f32[4,4,32,128]{3,2,1,0:T(8,128)S(1)}, f32[4,4,32,128]{3,2,1,0:T(8,128)S(1)}, u32[]{:S(2)}, u32[]{:S(2)}) collective-permute-start(f32[4,4,32,128]{3,2,1,0:T(8,128)S(1)} %pass.1.rest_0_), channel_id=1, source_target_pairs={{0,64},{8,72},{16,80},{24,88},{32,96},{40,104},{48,112},{56,120},{... | collective-permute-start | bytes 786440 | tf_op jit(solution)/shard_map/ppermute | solution.py:608
  106.7 8.4 %collective-permute-start.24 = (f32[4,4,32,128]{3,2,1,0:T(8,128)S(1)}, f32[4,4,32,128]{3,2,1,0:T(8,128)S(1)}, u32[]{:S(2)}, u32[]{:S(2)}) collective-permute-start(f32[4,4,32,128]{3,2,1,0:T(8,128)S(1)} %pass.1.rest_0_), channel_id=1, source_target_pairs={{0,96},{8,104},{16,112},{24,120},{32,0},{40,8},{48,16},{56,24},{64... | collective-permute-start | bytes 786440 | tf_op jit(solution)/shard_map/ppermute | solution.py:608
  123.1 4.1 %collective-permute-start.25 = (f32[16,4,32,128]{3,2,1,0:T(8,128)S(1)}, f32[16,4,32,128]{3,2,1,0:T(8,128)S(1)}, u32[]{:S(2)}, u32[]{:S(2)}) collective-permute-start(f32[16,4,32,128]{3,2,1,0:T(8,128)S(1)} %bitcast.11), channel_id=1, source_target_pairs={{0,1},{1,0},{2,3},{3,2},{4,5},{5,4},{6,7},{7,6},{8,9},{9,8},{10,11... | collective-permute-start | bytes 3145736 | tf_op jit(solution)/shard_map/ppermute | solution.py:610
  (7 other events, 16.3 us)

commit v14 on v12

--- a/solution.py
+++ b/solution.py
@@ -573,7 +573,7 @@
         mebibytes=16,
         flops=6 * pre_grad.size * width,
     )
-    keep, send_a, send_b = second_sums(keep_a, recv_a, keep_b, recv_b, [base, terms[1]])
+    keep, send_a, send_b = second_sums(keep_a, recv_a, keep_b, recv_b, [base])
     recv_a = lax.ppermute(send_a, "local", across)
     recv_b = lax.ppermute(send_b, "local", pairs)
     share_shape = jax.ShapeDtypeStruct(mine.shape, F32)

time: 129 us -> 129 us (level)
    ppermute x1, waiting for transfers between devices: 0.43 us -> 2.2 us  [on_device(): recv_b = lax.ppermute(send_b, 'local', across)]
    ppermute x1, waiting for transfers between devices: 0.01 us -> 1.71 us  [on_device(): recv_a = lax.ppermute(send_a, 'local', pairs)]
  transfers between devices with their start and end apart: 27 -> 27, of which waited for: 19 -> 20; matrix products, arithmetic and copies ran while one was open for 4% -> 4% of each run, Pallas kernels for 9% -> 9%
where the time goes in v14:
time: 129 us
  waiting for transfers between devices  55 us (43%)
  starting transfers between devices  41.2 us (32%)
  Pallas kernels  25.7 us (20%)
  matrix products  5.41 us (4%)
    pallas_call x2, Pallas kernels, tile_sums(): pl.pallas_call(functools.partial(tile_kernel, own, blocks, main, over), o...  15.3 us
    ppermute x3, waiting for transfers between devices, on_device(): lax.ppermute(some, 'group', along_y[k + 1])  10.3 us
    ppermute x3, waiting for transfers between devices, on_device(): rows = [row] + [lax.ppermute(row, 'group', along_y[k]) for k in range(1, 4)]  10.2 us
    ppermute x3, waiting for transfers between devices, on_device(): lax.ppermute(joined[k - 1], 'local', along_x[k])  9.86 us
    pallas_call x14, Pallas kernels, small(): pl.pallas_call(kernel, out_shape=out_shape, in_specs=specs or [IN_VMEM] *...  8.67 us
    ppermute x3, waiting for transfers between devices, on_device(): lax.ppermute(share, 'group', along_z[k])  8.26 us
    all_to_all x1, starting transfers between devices, on_device(): lax.all_to_all(shares, 'group', split_axis=0, concat_axis=0, tiled=True)  7.9 us
    ppermute x3, starting transfers between devices, on_device(): lax.ppermute(some, 'group', along_z[k + 1])  5.07 us
  transfers between devices with their start and end apart: 27, of which 20 were waited for; matrix products, arithmetic and copies ran while one was open for 4% of the time, Pallas kernels for 9%

profile of v14, /device:TPU:1, one launch (start us, length us, event | category | flops | bytes accessed | tf_op | source)
XLA Modules:
  0.0 128.7 jit_solution(15985721172833554162)
XLA Ops:
  0.6 8.8 %other_tile_sums.1 = (f32[1024,512]{1,0:T(8,128)}, f32[8,256,128]{2,1,0:T(8,128)}, f32[30,256,128]{2,1,0:T(8,128)S(1)}, s32[32]{0:T(128)}, s32[64]{0:T(128)}) custom-call(s32[64]{0:T(128)} %col_ref.1, s32[16,16]{1,0:T(8,128)} %count_ref.5, f32[1024,512]{1,0:T(8,128)} %rest_0_.1, f32[1024,512]{1,0:T(8,128)} %rest_1_.2, f32[512,512]{1,0:T(8,128)} %rest_1_.3, ...), custom_call_target="tpu_custom_call" | custom-call | flops 2415919104 | bytes 14680064 | tf_op jit(solution)/shard_map/other_tile_sums/pallas_call | solution.py:209
  11.0 3.6 %convolution_bitcast_fusion.neigh_term = f32[512,512]{1,0:T(8,128)S(1)} fusion(f32[1024,512]{1,0:T(8,128)} %get-tuple-element.37.rest_0_.pre_grad, f32[1024,512]{1,0:T(8,128)S(1)} %copy-done), kind=kOutput, calls=%fused_computation | convolution fusion | flops 1610612736 | bytes 5242880 | tf_op jit(solution)/shard_map/dot_general | solution.py:550
  14.6 1.8 %convolution_bitcast_fusion.1.self_term = f32[512,512]{1,0:T(8,128)S(1)} fusion(f32[1024,512]{1,0:T(8,128)S(1)} %copy-done.1, f32[1024,512]{1,0:T(8,128)S(1)} %copy-done.12), kind=kOutput, calls=%fused_computation.1 | convolution fusion | flops 1610612736 | bytes 5242880 | tf_op jit(solution)/shard_map/dot_general | solution.py:547
  17.7 6.5 %own_tile_sums.1 = (f32[8,256,128]{2,1,0:T(8,128)S(1)}, s32[1]{0:T(128)}, f32[2,15,64,128]{3,2,1,0:T(8,128)S(1)}, f32[2,15,64,128]{3,2,1,0:T(8,128)S(1)}, f32[2,...) custom-call(s32[64]{0:T(128)S(1)} %copy-done.11, s32[16,16]{1,0:T(8,128)S(1)} %copy-done.8, ...), custom_call_target="tpu_custom_call" | custom-call | flops 2415919104 | bytes 14680064 | tf_op jit(solution)/shard_map/own_tile_sums/pallas_call | solution.py:209
  25.7 1.8 %collective-permute-start.6 = (f32[2,15,64,128]{3,2,1,0:T(8,128)S(1)}, f32[2,15,64,128]{3,2,1,0:T(8,128)S(1)}, u32[]{:S(2)}, u32[]{:S(2)}) collective-permute-start(f32[2,15,64,128]{3,2,1,0:T(8,128)S(1)} %get-tuple-element.54), channel_id=1, source_target_pairs={{0,6},{1,7},{2,4},{3,5},{4,2},{5,3},{6,0},{7,1},{8,14},{9,15},{10,... | collective-permute-start | bytes 2949128 | tf_op jit(solution)/shard_map/ppermute | solution.py:544
  29.6 2.6 %collective-permute-start.3 = (f32[4,4,32,128]{3,2,1,0:T(8,128)S(1)}, f32[4,4,32,128]{3,2,1,0:T(8,128)S(1)}, u32[]{:S(2)}, u32[]{:S(2)}) collective-permute-start(f32[4,4,32,128]{3,2,1,0:T(8,128)S(1)} %get-tuple-element.47), channel_id=1, source_target_pairs={{0,64},{8,72},{16,80},{24,88},{32,96},{40,104},{48,112},{56,120},{... | collective-permute-start | bytes 786440 | tf_op jit(solution)/shard_map/ppermute | solution.py:559
  33.3 3.6 %collective-permute-done.2.rest_1_ = f32[4,4,32,128]{3,2,1,0:T(8,128)S(1)} collective-permute-done((f32[4,4,32,128]{3,2,1,0:T(8,128)S(1)}, f32[4,4,32,128]{3,2,1,0:T(8,128)S(1)}, u32[]{:S(2)}, u32[]{:S(2)}) %collective-permute-start.2) | collective-permute-done | bytes 262176 | tf_op jit(solution)/shard_map/ppermute | solution.py:559
  37.0 6.7 %collective-permute-done.3.rest_2_ = f32[4,4,32,128]{3,2,1,0:T(8,128)S(1)} collective-permute-done((f32[4,4,32,128]{3,2,1,0:T(8,128)S(1)}, f32[4,4,32,128]{3,2,1,0:T(8,128)S(1)}, u32[]{:S(2)}, u32[]{:S(2)}) %collective-permute-start.3) | collective-permute-done | bytes 262176 | tf_op jit(solution)/shard_map/ppermute | solution.py:559
  43.7 2.2 %self_rows.1.rest_0_.base = f32[1024,512]{1,0:T(8,128)S(1)} custom-call(f32[1024,512]{1,0:T(8,128)S(1)} %copy-done.1, f32[512,512]{1,0:T(8,128)S(1)} %copy-done.6, f32[8,256,128]{2,1,0:T(8,128)S(1)} %copy-done.7, f32[8,256,128]{2,1,0:T(8,128)S(1)} %get-tuple-element.41.own_local, f32[4,32,128]{2,1,0:T(8,128)S(1)} %get-tuple-element.49.after.rest_0_), custom_call_target="tpu_custom_call" | custom-call | flops 1610612736 | bytes 6291456 | tf_op jit(solution)/shard_map/self_rows/pallas_call | solution.py:281
  46.0 1.7 %collective-permute-done.5.recv_a = f32[2,15,64,128]{3,2,1,0:T(8,128)S(1)} collective-permute-done((f32[2,15,64,128]{3,2,1,0:T(8,128)S(1)}, f32[2,15,64,128]{3,2,1,0:T(8,128)S(1)}, u32[]{:S(2)}, u32[]{:S(2)}) %collective-permute-start.5) | collective-permute-done | bytes 983072 | tf_op jit(solution)/shard_map/ppermute | solution.py:543
  47.7 2.2 %collective-permute-done.6.recv_b = f32[2,15,64,128]{3,2,1,0:T(8,128)S(1)} collective-permute-done((f32[2,15,64,128]{3,2,1,0:T(8,128)S(1)}, f32[2,15,64,128]{3,2,1,0:T(8,128)S(1)}, u32[]{:S(2)}, u32[]{:S(2)}) %collective-permute-start.6) | collective-permute-done | bytes 983072 | tf_op jit(solution)/shard_map/ppermute | solution.py:544
  50.1 1.9 %collective-permute-start.7 = (f32[15,64,128]{2,1,0:T(8,128)S(1)}, f32[15,64,128]{2,1,0:T(8,128)S(1)}, u32[]{:S(2)}, u32[]{:S(2)}) collective-permute-start(f32[15,64,128]{2,1,0:T(8,128)S(1)} %get-tuple-element.56), channel_id=1, source_target_pairs={{0,6},{1,7},{2,4},{3,5},{4,2},{5,3},{6,0},{7,1},{8,14},{9,15},{10,... | collective-permute-start | bytes 1474568 | tf_op jit(solution)/shard_map/ppermute | solution.py:577
  52.0 3.6 %collective-permute-start.10 = (f32[4,32,128]{2,1,0:T(8,128)S(1)}, f32[4,32,128]{2,1,0:T(8,128)S(1)}, u32[]{:S(2)}, u32[]{:S(2)}) collective-permute-start(f32[4,32,128]{2,1,0:T(8,128)S(1)} %get-tuple-element.59), channel_id=1, source_target_pairs={{0,16},{8,24},{16,0},{24,8},{32,48},{40,56},{48,32},{56,40},{64,80... | collective-permute-start | bytes 196616 | tf_op jit(solution)/shard_map/ppermute | solution.py:563
  57.3 1.8 %collective-permute-done.11.rest_3_ = f32[4,32,128]{2,1,0:T(8,128)S(1)} collective-permute-done((f32[4,32,128]{2,1,0:T(8,128)S(1)}, f32[4,32,128]{2,1,0:T(8,128)S(1)}, u32[]{:S(2)}, u32[]{:S(2)}) %collective-permute-start.11) | collective-permute-done | bytes 65568 | tf_op jit(solution)/shard_map/ppermute | solution.py:563
  59.0 1.6 %collective-permute-done.9.rest_1_ = f32[4,32,128]{2,1,0:T(8,128)S(1)} collective-permute-done((f32[4,32,128]{2,1,0:T(8,128)S(1)}, f32[4,32,128]{2,1,0:T(8,128)S(1)}, u32[]{:S(2)}, u32[]{:S(2)}) %collective-permute-start.9) | collective-permute-done | bytes 65568 | tf_op jit(solution)/shard_map/ppermute | solution.py:563
  60.7 2.3 %collective-permute-done.7.recv_a = f32[15,64,128]{2,1,0:T(8,128)S(1)} collective-permute-done((f32[15,64,128]{2,1,0:T(8,128)S(1)}, f32[15,64,128]{2,1,0:T(8,128)S(1)}, u32[]{:S(2)}, u32[]{:S(2)}) %collective-permute-start.7) | collective-permute-done | bytes 491552 | tf_op jit(solution)/shard_map/ppermute | solution.py:577
  63.3 1.7 %third_sums.1.after = f32[32,64,128]{2,1,0:T(8,128)} custom-call(s32[32]{0:T(128)S(1)} %copy-done.10, f32[2,15,64,128]{3,2,1,0:T(8,128)S(1)} %get-tuple-element.55.keep, f32[15,64,128]{2,1,0:T(8,128)S(1)} %collective-permute-done.7.recv_a, f32[15,64,128]{2,1,0:T(8,128)S(1)} %collective-permute-done.8.recv_b, f32[4,32,128]{2,1,0:T(8,128)S(1)} %sum_z.1.after.mine), custom_call_target="tpu_custom_call" | custom-call | flops 245760 | bytes 2949120 | tf_op jit(solution)/shard_map/third_sums/pallas_call | solution.py:281
  65.0 7.9 %all-to-all-start = ((f32[32,64,128]{2,1,0:T(8,128)}), f32[32,64,128]{2,1,0:T(8,128)S(1)}, u32[]{:S(2)}, u32[]{:S(2)}) async-start(f32[32,64,128]{2,1,0:T(8,128)} %third_sums.1.after), calls=%async_computation | async-start | bytes 2097152 | tf_op jit(solution)/shard_map/all_to_all | solution.py:582
  74.6 1.7 %collective-permute-start.14 = (f32[4,32,128]{2,1,0:T(8,128)S(1)}, f32[4,32,128]{2,1,0:T(8,128)S(1)}, u32[]{:S(2)}, u32[]{:S(2)}) collective-permute-start(f32[4,32,128]{2,1,0:T(8,128)S(1)} %sum_z.1.after.mine), channel_id=1, source_target_pairs={{0,4},{1,5},{2,6},{3,7},{4,0},{5,1},{6,2},{7,3},{8,12},{9,13},{10,... | collective-permute-start | bytes 196616 | tf_op jit(solution)/shard_map/ppermute | solution.py:583
  77.6 1.6 %collective-permute-done.14.far_two = f32[4,32,128]{2,1,0:T(8,128)S(1)} collective-permute-done((f32[4,32,128]{2,1,0:T(8,128)S(1)}, f32[4,32,128]{2,1,0:T(8,128)S(1)}, u32[]{:S(2)}, u32[]{:S(2)}) %collective-permute-start.14) | collective-permute-done | bytes 65568 | tf_op jit(solution)/shard_map/ppermute | solution.py:583
  80.5 2.4 %collective-permute-start.16 = (f32[4,32,128]{2,1,0:T(8,128)S(1)}, f32[4,32,128]{2,1,0:T(8,128)S(1)}, u32[]{:S(2)}, u32[]{:S(2)}) collective-permute-start(f32[4,32,128]{2,1,0:T(8,128)S(1)} %sum_chips.1.rest_0_), channel_id=1, source_target_pairs={{0,16},{8,24},{16,0},{24,8},{32,48},{40,56},{48,32},{56,40},{64,80... | collective-permute-start | bytes 196616 | tf_op jit(solution)/shard_map/ppermute | solution.py:592
  84.1 6.1 %collective-permute-done.15.rest_1_ = f32[4,32,128]{2,1,0:T(8,128)S(1)} collective-permute-done((f32[4,32,128]{2,1,0:T(8,128)S(1)}, f32[4,32,128]{2,1,0:T(8,128)S(1)}, u32[]{:S(2)}, u32[]{:S(2)}) %collective-permute-start.15) | collective-permute-done | bytes 65568 | tf_op jit(solution)/shard_map/ppermute | solution.py:592
  90.3 2.1 %collective-permute-done.16.rest_2_ = f32[4,32,128]{2,1,0:T(8,128)S(1)} collective-permute-done((f32[4,32,128]{2,1,0:T(8,128)S(1)}, f32[4,32,128]{2,1,0:T(8,128)S(1)}, u32[]{:S(2)}, u32[]{:S(2)}) %collective-permute-start.16) | collective-permute-done | bytes 65568 | tf_op jit(solution)/shard_map/ppermute | solution.py:592
  92.4 1.9 %place.1 = (f32[4,8,64,128]{3,2,1,0:T(8,128)S(1)}, f32[8,64,128]{2,1,0:T(8,128)S(1)}, f32[8,64,128]{2,1,0:T(8,128)S(1)}, f32[8,64,128]{2,1,0:T(8,128)S(1)}, f32[8,64,128]{2,1,0:T(8,128)S(1)}) custom-call(s32[16,16]{1,0:T(8,128)S(1)} %copy-done.8, s32[16,32]{1,0:T(8,128)S(1)} %copy-done.9, f32[32,64,128]{2,1,0:T(8,128)S(1)} %all-to-all-done.arrived, ...), custom_call_target="tpu_custom_call" | custom-call | flops 262144 | bytes 3145728 | tf_op jit(solution)/shard_map/place/pallas_call | solution.py:281
  95.4 2.3 %collective-permute-done.18.rest_3_.swapped = f32[4,8,64,128]{3,2,1,0:T(8,128)S(1)} collective-permute-done((f32[4,8,64,128]{3,2,1,0:T(8,128)S(1)}, f32[4,8,64,128]{3,2,1,0:T(8,128)S(1)}, u32[]{:S(2)}, u32[]{:S(2)}) %collective-permute-start.18) | collective-permute-done | bytes 1048608 | tf_op jit(solution)/shard_map/ppermute | solution.py:596
  98.4 2.2 %collective-permute-start.20 = (f32[2,8,64,128]{3,2,1,0:T(8,128)S(1)}, f32[2,8,64,128]{3,2,1,0:T(8,128)S(1)}, u32[]{:S(2)}, u32[]{:S(2)}) collective-permute-start(f32[2,8,64,128]{3,2,1,0:T(8,128)S(1)} %get-tuple-element.67), channel_id=1, source_target_pairs={{0,6},{1,7},{2,0},{3,1},{4,2},{5,3},{6,4},{7,5},{8,14},{9,15},{10,... | collective-permute-start | bytes 1572872 | tf_op jit(solution)/shard_map/ppermute | solution.py:599
  101.0 2.4 %collective-permute-start.23 = (f32[4,4,32,128]{3,2,1,0:T(8,128)S(1)}, f32[4,4,32,128]{3,2,1,0:T(8,128)S(1)}, u32[]{:S(2)}, u32[]{:S(2)}) collective-permute-start(f32[4,4,32,128]{3,2,1,0:T(8,128)S(1)} %pass.1.rest_0_), channel_id=1, source_target_pairs={{0,64},{8,72},{16,80},{24,88},{32,96},{40,104},{48,112},{56,120},{... | collective-permute-start | bytes 786440 | tf_op jit(solution)/shard_map/ppermute | solution.py:608
  103.4 4.0 %collective-permute-done.22.rest_1_ = f32[4,4,32,128]{3,2,1,0:T(8,128)S(1)} collective-permute-done((f32[4,4,32,128]{3,2,1,0:T(8,128)S(1)}, f32[4,4,32,128]{3,2,1,0:T(8,128)S(1)}, u32[]{:S(2)}, u32[]{:S(2)}) %collective-permute-start.22) | collective-permute-done | bytes 262176 | tf_op jit(solution)/shard_map/ppermute | solution.py:608
  107.4 4.1 %collective-permute-done.23.rest_2_ = f32[4,4,32,128]{3,2,1,0:T(8,128)S(1)} collective-permute-done((f32[4,4,32,128]{3,2,1,0:T(8,128)S(1)}, f32[4,4,32,128]{3,2,1,0:T(8,128)S(1)}, u32[]{:S(2)}, u32[]{:S(2)}) %collective-permute-start.23) | collective-permute-done | bytes 262176 | tf_op jit(solution)/shard_map/ppermute | solution.py:608
  111.5 2.1 %collective-permute-done.24.rest_3_ = f32[4,4,32,128]{3,2,1,0:T(8,128)S(1)} collective-permute-done((f32[4,4,32,128]{3,2,1,0:T(8,128)S(1)}, f32[4,4,32,128]{3,2,1,0:T(8,128)S(1)}, u32[]{:S(2)}, u32[]{:S(2)}) %collective-permute-start.24) | collective-permute-done | bytes 262176 | tf_op jit(solution)/shard_map/ppermute | solution.py:608
  113.6 9.9 %collective-permute-done.21.rest_2_.rest_6_ = f32[2,8,64,128]{3,2,1,0:T(8,128)S(1)} collective-permute-done((f32[2,8,64,128]{3,2,1,0:T(8,128)S(1)}, f32[2,8,64,128]{3,2,1,0:T(8,128)S(1)}, u32[]{:S(2)}, u32[]{:S(2)}) %collective-permute-start.21) | collective-permute-done | bytes 524320 | tf_op jit(solution)/shard_map/ppermute | solution.py:599
  124.9 1.7 %finish.1 = f32[1024,512]{1,0:T(8,128)} custom-call(f32[1024,512]{1,0:T(8,128)S(1)} %copy-done.3, f32[8,64,128]{2,1,0:T(8,128)S(1)} %get-tuple-element.61.keep, f32[4,8,64,128]{3,2,1,0:T(8,128)S(1)} %collective-permute-done.18.rest_3_.swapped, f32[2,8,64,128]{3,2,1,0:T(8,128)S(1)} %collective-permute-done.19.rest_0_.rest_4_, ...), custom_call_target="tpu_custom_call" | custom-call | flops 1048576 | bytes 8388608 | tf_op jit(solution)/shard_map/finish/pallas_call | solution.py:492
  (67 shorter events, 20.9 us)
Async XLA Ops:
  9.5 7.9 %collective-permute-start = (f32[30,256,128]{2,1,0:T(8,128)S(1)}, f32[30,256,128]{2,1,0:T(8,128)S(1)}, u32[]{:S(2)}, u32[]{:S(2)}) collective-permute-start(f32[30,256,128]{2,1,0:T(8,128)S(1)} %get-tuple-element.40), channel_id=1, source_target_pairs={{0,1},{1,0},{2,3},{3,2},{4,5},{5,4},{6,7},{7,6},{8,9},{9,8},{10,11... | collective-permute-start | bytes 11796488 | tf_op jit(solution)/shard_map/ppermute | solution.py:539
  16.6 10.9 %collective-permute-start.1 = (f32[16,4,32,128]{3,2,1,0:T(8,128)S(1)}, f32[16,4,32,128]{3,2,1,0:T(8,128)S(1)}, u32[]{:S(2)}, u32[]{:S(2)}) collective-permute-start(f32[16,4,32,128]{3,2,1,0:T(8,128)S(1)} %get-tuple-element.43), channel_id=1, source_target_pairs={{0,1},{1,0},{2,3},{3,2},{4,5},{5,4},{6,7},{7,6},{8,9},{9,8},{10,11... | collective-permute-start | bytes 3145736 | tf_op jit(solution)/shard_map/ppermute | solution.py:556
  24.3 19.5 %copy-start.6 = (f32[512,512]{1,0:T(8,128)S(1)}, f32[512,512]{1,0:T(8,128)}, u32[]{:S(2)}) copy-start(f32[512,512]{1,0:T(8,128)} %weight.1) | copy-start | bytes 3145732
  24.3 19.5 %copy-start.7 = (f32[8,256,128]{2,1,0:T(8,128)S(1)}, f32[8,256,128]{2,1,0:T(8,128)}, u32[]{:S(2)}) copy-start(f32[8,256,128]{2,1,0:T(8,128)} %get-tuple-element.38.other_local) | copy-start | bytes 3145732
  24.3 23.4 %collective-permute-start.5 = (f32[2,15,64,128]{3,2,1,0:T(8,128)S(1)}, f32[2,15,64,128]{3,2,1,0:T(8,128)S(1)}, u32[]{:S(2)}, u32[]{:S(2)}) collective-permute-start(f32[2,15,64,128]{3,2,1,0:T(8,128)S(1)} %get-tuple-element.52), channel_id=1, source_target_pairs={{0,2},{1,3},{2,0},{3,1},{4,6},{5,7},{6,4},{7,5},{8,10},{9,11},{10,... | collective-permute-start | bytes 2949128 | tf_op jit(solution)/shard_map/ppermute | solution.py:543
  25.7 24.2 %collective-permute-start.6 = (f32[2,15,64,128]{3,2,1,0:T(8,128)S(1)}, f32[2,15,64,128]{3,2,1,0:T(8,128)S(1)}, u32[]{:S(2)}, u32[]{:S(2)}) collective-permute-start(f32[2,15,64,128]{3,2,1,0:T(8,128)S(1)} %get-tuple-element.54), channel_id=1, source_target_pairs={{0,6},{1,7},{2,4},{3,5},{4,2},{5,3},{6,0},{7,1},{8,14},{9,15},{10,... | collective-permute-start | bytes 2949128 | tf_op jit(solution)/shard_map/ppermute | solution.py:544
  28.3 8.7 %collective-permute-start.2 = (f32[4,4,32,128]{3,2,1,0:T(8,128)S(1)}, f32[4,4,32,128]{3,2,1,0:T(8,128)S(1)}, u32[]{:S(2)}, u32[]{:S(2)}) collective-permute-start(f32[4,4,32,128]{3,2,1,0:T(8,128)S(1)} %get-tuple-element.46), channel_id=1, source_target_pairs={{0,32},{8,40},{16,48},{24,56},{32,64},{40,72},{48,80},{56,88},{64,... | collective-permute-start | bytes 786440 | tf_op jit(solution)/shard_map/ppermute | solution.py:559
  29.6 14.0 %collective-permute-start.3 = (f32[4,4,32,128]{3,2,1,0:T(8,128)S(1)}, f32[4,4,32,128]{3,2,1,0:T(8,128)S(1)}, u32[]{:S(2)}, u32[]{:S(2)}) collective-permute-start(f32[4,4,32,128]{3,2,1,0:T(8,128)S(1)} %get-tuple-element.47), channel_id=1, source_target_pairs={{0,64},{8,72},{16,80},{24,88},{32,96},{40,104},{48,112},{56,120},{... | collective-permute-start | bytes 786440 | tf_op jit(solution)/shard_map/ppermute | solution.py:559
  32.3 11.4 %collective-permute-start.4 = (f32[4,4,32,128]{3,2,1,0:T(8,128)S(1)}, f32[4,4,32,128]{3,2,1,0:T(8,128)S(1)}, u32[]{:S(2)}, u32[]{:S(2)}) collective-permute-start(f32[4,4,32,128]{3,2,1,0:T(8,128)S(1)} %get-tuple-element.48), channel_id=1, source_target_pairs={{0,96},{8,104},{16,112},{24,120},{32,0},{40,8},{48,16},{56,24},{64... | collective-permute-start | bytes 786440 | tf_op jit(solution)/shard_map/ppermute | solution.py:559
  49.9 13.4 %copy-start.10 = (s32[32]{0:T(128)S(1)}, s32[32]{0:T(128)}, u32[]{:S(2)}) copy-start(s32[32]{0:T(128)} %get-tuple-element.50.places) | copy-start | bytes 388
  50.1 12.9 %collective-permute-start.7 = (f32[15,64,128]{2,1,0:T(8,128)S(1)}, f32[15,64,128]{2,1,0:T(8,128)S(1)}, u32[]{:S(2)}, u32[]{:S(2)}) collective-permute-start(f32[15,64,128]{2,1,0:T(8,128)S(1)} %get-tuple-element.56), channel_id=1, source_target_pairs={{0,6},{1,7},{2,4},{3,5},{4,2},{5,3},{6,0},{7,1},{8,14},{9,15},{10,... | collective-permute-start | bytes 1474568 | tf_op jit(solution)/shard_map/ppermute | solution.py:577
  52.0 11.3 %collective-permute-start.8 = (f32[15,64,128]{2,1,0:T(8,128)S(1)}, f32[15,64,128]{2,1,0:T(8,128)S(1)}, u32[]{:S(2)}, u32[]{:S(2)}) collective-permute-start(f32[15,64,128]{2,1,0:T(8,128)S(1)} %get-tuple-element.57), channel_id=1, source_target_pairs={{0,2},{1,3},{2,0},{3,1},{4,6},{5,7},{6,4},{7,5},{8,10},{9,11},{10,... | collective-permute-start | bytes 1474568 | tf_op jit(solution)/shard_map/ppermute | solution.py:578
  52.0 5.3 %collective-permute-start.10 = (f32[4,32,128]{2,1,0:T(8,128)S(1)}, f32[4,32,128]{2,1,0:T(8,128)S(1)}, u32[]{:S(2)}, u32[]{:S(2)}) collective-permute-start(f32[4,32,128]{2,1,0:T(8,128)S(1)} %get-tuple-element.59), channel_id=1, source_target_pairs={{0,16},{8,24},{16,0},{24,8},{32,48},{40,56},{48,32},{56,40},{64,80... | collective-permute-start | bytes 196616 | tf_op jit(solution)/shard_map/ppermute | solution.py:563
  55.6 3.4 %collective-permute-start.11 = (f32[4,32,128]{2,1,0:T(8,128)S(1)}, f32[4,32,128]{2,1,0:T(8,128)S(1)}, u32[]{:S(2)}, u32[]{:S(2)}) collective-permute-start(f32[4,32,128]{2,1,0:T(8,128)S(1)} %get-tuple-element.60), channel_id=1, source_target_pairs={{0,24},{8,0},{16,8},{24,16},{32,56},{40,32},{48,40},{56,48},{64,88... | collective-permute-start | bytes 196616 | tf_op jit(solution)/shard_map/ppermute | solution.py:563
  56.1 4.6 %collective-permute-start.9 = (f32[4,32,128]{2,1,0:T(8,128)S(1)}, f32[4,32,128]{2,1,0:T(8,128)S(1)}, u32[]{:S(2)}, u32[]{:S(2)}) collective-permute-start(f32[4,32,128]{2,1,0:T(8,128)S(1)} %get-tuple-element.58), channel_id=1, source_target_pairs={{0,8},{8,16},{16,24},{24,0},{32,40},{40,48},{48,56},{56,32},{64,72... | collective-permute-start | bytes 196616 | tf_op jit(solution)/shard_map/ppermute | solution.py:563
  65.0 27.5 %copy-start.9 = (s32[16,32]{1,0:T(8,128)S(1)}, s32[16,32]{1,0:T(8,128)}, u32[]{:S(2)}) copy-start(s32[16,32]{1,0:T(8,128)} %target_ref.1) | copy-start | bytes 6148
  65.0 27.4 %all-to-all-start = ((f32[32,64,128]{2,1,0:T(8,128)}), f32[32,64,128]{2,1,0:T(8,128)S(1)}, u32[]{:S(2)}, u32[]{:S(2)}) async-start(f32[32,64,128]{2,1,0:T(8,128)} %third_sums.1.after), calls=%async_computation | async-start | bytes 2097152 | tf_op jit(solution)/shard_map/all_to_all | solution.py:582
  72.9 3.3 %collective-permute-start.12 = (f32[4,32,128]{2,1,0:T(8,128)S(1)}, f32[4,32,128]{2,1,0:T(8,128)S(1)}, u32[]{:S(2)}, u32[]{:S(2)}) collective-permute-start(f32[4,32,128]{2,1,0:T(8,128)S(1)} %sum_z.1.after.mine), channel_id=1, source_target_pairs={{0,2},{1,3},{2,0},{3,1},{4,6},{5,7},{6,4},{7,5},{8,10},{9,11},{10,... | collective-permute-start | bytes 196616 | tf_op jit(solution)/shard_map/ppermute | solution.py:583
  73.3 4.3 %collective-permute-start.13 = (f32[4,32,128]{2,1,0:T(8,128)S(1)}, f32[4,32,128]{2,1,0:T(8,128)S(1)}, u32[]{:S(2)}, u32[]{:S(2)}) collective-permute-start(f32[4,32,128]{2,1,0:T(8,128)S(1)} %sum_z.1.after.mine), channel_id=1, source_target_pairs={{0,6},{1,7},{2,4},{3,5},{4,2},{5,3},{6,0},{7,1},{8,14},{9,15},{10,... | collective-permute-start | bytes 196616 | tf_op jit(solution)/shard_map/ppermute | solution.py:583
  74.6 4.6 %collective-permute-start.14 = (f32[4,32,128]{2,1,0:T(8,128)S(1)}, f32[4,32,128]{2,1,0:T(8,128)S(1)}, u32[]{:S(2)}, u32[]{:S(2)}) collective-permute-start(f32[4,32,128]{2,1,0:T(8,128)S(1)} %sum_z.1.after.mine), channel_id=1, source_target_pairs={{0,4},{1,5},{2,6},{3,7},{4,0},{5,1},{6,2},{7,3},{8,12},{9,13},{10,... | collective-permute-start | bytes 196616 | tf_op jit(solution)/shard_map/ppermute | solution.py:583
  79.2 11.1 %collective-permute-start.15 = (f32[4,32,128]{2,1,0:T(8,128)S(1)}, f32[4,32,128]{2,1,0:T(8,128)S(1)}, u32[]{:S(2)}, u32[]{:S(2)}) collective-permute-start(f32[4,32,128]{2,1,0:T(8,128)S(1)} %sum_chips.1.rest_0_), channel_id=1, source_target_pairs={{0,8},{8,16},{16,24},{24,0},{32,40},{40,48},{48,56},{56,32},{64,72... | collective-permute-start | bytes 196616 | tf_op jit(solution)/shard_map/ppermute | solution.py:592
  80.5 11.8 %collective-permute-start.16 = (f32[4,32,128]{2,1,0:T(8,128)S(1)}, f32[4,32,128]{2,1,0:T(8,128)S(1)}, u32[]{:S(2)}, u32[]{:S(2)}) collective-permute-start(f32[4,32,128]{2,1,0:T(8,128)S(1)} %sum_chips.1.rest_0_), channel_id=1, source_target_pairs={{0,16},{8,24},{16,0},{24,8},{32,48},{40,56},{48,32},{56,40},{64,80... | collective-permute-start | bytes 196616 | tf_op jit(solution)/shard_map/ppermute | solution.py:592
  82.9 9.4 %collective-permute-start.17 = (f32[4,32,128]{2,1,0:T(8,128)S(1)}, f32[4,32,128]{2,1,0:T(8,128)S(1)}, u32[]{:S(2)}, u32[]{:S(2)}) collective-permute-start(f32[4,32,128]{2,1,0:T(8,128)S(1)} %sum_chips.1.rest_0_), channel_id=1, source_target_pairs={{0,24},{8,0},{16,8},{24,16},{32,56},{40,32},{48,40},{56,48},{64,88... | collective-permute-start | bytes 196616 | tf_op jit(solution)/shard_map/ppermute | solution.py:592
  94.3 3.3 %collective-permute-start.18 = (f32[4,8,64,128]{3,2,1,0:T(8,128)S(1)}, f32[4,8,64,128]{3,2,1,0:T(8,128)S(1)}, u32[]{:S(2)}, u32[]{:S(2)}) collective-permute-start(f32[4,8,64,128]{3,2,1,0:T(8,128)S(1)} %get-tuple-element.62), channel_id=1, source_target_pairs={{0,1},{1,0},{2,3},{3,2},{4,5},{5,4},{6,7},{7,6},{8,9},{9,8},{10,11... | collective-permute-start | bytes 3145736 | tf_op jit(solution)/shard_map/ppermute | solution.py:596
  97.8 27.1 %copy-start.3 = (f32[1024,512]{1,0:T(8,128)S(1)}, f32[1024,512]{1,0:T(8,128)}, u32[]{:S(2)}) copy-start(f32[1024,512]{1,0:T(8,128)} %copy-done.2) | copy-start | bytes 6291460
  97.8 9.6 %collective-permute-start.22 = (f32[4,4,32,128]{3,2,1,0:T(8,128)S(1)}, f32[4,4,32,128]{3,2,1,0:T(8,128)S(1)}, u32[]{:S(2)}, u32[]{:S(2)}) collective-permute-start(f32[4,4,32,128]{3,2,1,0:T(8,128)S(1)} %pass.1.rest_0_), channel_id=1, source_target_pairs={{0,32},{8,40},{16,48},{24,56},{32,64},{40,72},{48,80},{56,88},{64,... | collective-permute-start | bytes 786440 | tf_op jit(solution)/shard_map/ppermute | solution.py:608
  97.9 15.7 %collective-permute-start.19 = (f32[2,8,64,128]{3,2,1,0:T(8,128)S(1)}, f32[2,8,64,128]{3,2,1,0:T(8,128)S(1)}, u32[]{:S(2)}, u32[]{:S(2)}) collective-permute-start(f32[2,8,64,128]{3,2,1,0:T(8,128)S(1)} %get-tuple-element.66.rest_0_), channel_id=1, source_target_pairs={{0,2},{1,3},{2,4},{3,5},{4,6},{5,7},{6,0},{7,1},{8,10},{9,11},{10,... | collective-permute-start | bytes 1572872 | tf_op jit(solution)/shard_map/ppermute | solution.py:599
  98.4 15.2 %collective-permute-start.20 = (f32[2,8,64,128]{3,2,1,0:T(8,128)S(1)}, f32[2,8,64,128]{3,2,1,0:T(8,128)S(1)}, u32[]{:S(2)}, u32[]{:S(2)}) collective-permute-start(f32[2,8,64,128]{3,2,1,0:T(8,128)S(1)} %get-tuple-element.67), channel_id=1, source_target_pairs={{0,6},{1,7},{2,0},{3,1},{4,2},{5,3},{6,4},{7,5},{8,14},{9,15},{10,... | collective-permute-start | bytes 1572872 | tf_op jit(solution)/shard_map/ppermute | solution.py:599
  100.6 22.8 %collective-permute-start.21 = (f32[2,8,64,128]{3,2,1,0:T(8,128)S(1)}, f32[2,8,64,128]{3,2,1,0:T(8,128)S(1)}, u32[]{:S(2)}, u32[]{:S(2)}) collective-permute-start(f32[2,8,64,128]{3,2,1,0:T(8,128)S(1)} %get-tuple-element.68), channel_id=1, source_target_pairs={{0,4},{1,5},{2,6},{3,7},{4,0},{5,1},{6,2},{7,3},{8,12},{9,13},{10,... | collective-permute-start | bytes 1572872 | tf_op jit(solution)/shard_map/ppermute | solution.py:599
  101.0 10.5 %collective-permute-start.23 = (f32[4,4,32,128]{3,2,1,0:T(8,128)S(1)}, f32[4,4,32,128]{3,2,1,0:T(8,128)S(1)}, u32[]{:S(2)}, u32[]{:S(2)}) collective-permute-start(f32[4,4,32,128]{3,2,1,0:T(8,128)S(1)} %pass.1.rest_0_), channel_id=1, source_target_pairs={{0,64},{8,72},{16,80},{24,88},{32,96},{40,104},{48,112},{56,120},{... | collective-permute-start | bytes 786440 | tf_op jit(solution)/shard_map/ppermute | solution.py:608
  107.4 6.2 %collective-permute-start.24 = (f32[4,4,32,128]{3,2,1,0:T(8,128)S(1)}, f32[4,4,32,128]{3,2,1,0:T(8,128)S(1)}, u32[]{:S(2)}, u32[]{:S(2)}) collective-permute-start(f32[4,4,32,128]{3,2,1,0:T(8,128)S(1)} %pass.1.rest_0_), channel_id=1, source_target_pairs={{0,96},{8,104},{16,112},{24,120},{32,0},{40,8},{48,16},{56,24},{64... | collective-permute-start | bytes 786440 | tf_op jit(solution)/shard_map/ppermute | solution.py:608
  123.5 3.7 %collective-permute-start.25 = (f32[16,4,32,128]{3,2,1,0:T(8,128)S(1)}, f32[16,4,32,128]{3,2,1,0:T(8,128)S(1)}, u32[]{:S(2)}, u32[]{:S(2)}) collective-permute-start(f32[16,4,32,128]{3,2,1,0:T(8,128)S(1)} %bitcast.11), channel_id=1, source_target_pairs={{0,1},{1,0},{2,3},{3,2},{4,5},{5,4},{6,7},{7,6},{8,9},{9,8},{10,11... | collective-permute-start | bytes 3145736 | tf_op jit(solution)/shard_map/ppermute | solution.py:610
  (8 other events, 28.4 us)
